TPU v7x, 32 devices: a whole 2x2x4 slice. The times are simulated.
32 devices in a mesh: ctx: 8 (over z, y), fsdp: 4 (over x, core).
Axes of the slice: x: 2, y: 2, z: 4, core: 2. Of those that a mesh axis runs over, the one named last changes fastest.
Arguments:
- tokens: bfloat16 [4, 1024, 2048], P('fsdp', 'ctx'), may hold values from -6 to 6
- attn_gain: float32 [2048], replicated, may hold values from 0.1 to 1.9
- w_query: bfloat16 [2048, 2048], P('fsdp'), may hold values from -0.125 to 0.125
- w_key: bfloat16 [2048, 2048], P('fsdp'), may hold values from -0.125 to 0.125
- w_value: bfloat16 [2048, 2048], P('fsdp'), may hold values from -0.125 to 0.125
- query_gain: float32 [128], replicated, may hold values from 0.1 to 1.9
- key_gain: float32 [128], replicated, may hold values from 0.1 to 1.9
- w_out: bfloat16 [2048, 2048], P('fsdp'), may hold values from -2.53125 to 2.53125
- ffn_gain: float32 [2048], replicated, may hold values from 0.1 to 1.9
- w_router: bfloat16 [2048, 16], P('fsdp'), may hold values from -0.06591797 to 0.06591797
- w_gate: bfloat16 [2048, 16, 1024], P('fsdp', 'ctx'), may hold values from -0.125 to 0.125
- w_up: bfloat16 [2048, 16, 1024], P('fsdp', 'ctx'), may hold values from -0.125 to 0.125
- w_down: bfloat16 [2048, 16, 1024], P('fsdp', 'ctx'), may hold values from -0.75 to 0.75
- routes: int32 [4, 1024, 8], P('fsdp', 'ctx'), may hold values from 0 to 15, all different within a row; in each aligned block of 128 rows (0 to 127, 128 to 255, ..., all dimensions but the last counted through in order) at most 80 rows name the same one
- cotangent: bfloat16 [4, 1024, 2048], P('fsdp', 'ctx'), may hold values from -8 to 8
Outputs:
- out: bfloat16 [4, 1024, 2048], P('fsdp', 'ctx')
- d_tokens: float32 [4, 1024, 2048], P('fsdp', 'ctx')
- d_attn_gain: float32 [2048], replicated
- d_query: float32 [2048, 2048], P('fsdp')
- d_key: float32 [2048, 2048], P('fsdp')
- d_value: float32 [2048, 2048], P('fsdp')
- d_query_gain: float32 [128], replicated
- d_key_gain: float32 [128], replicated
- d_out_proj: float32 [2048, 2048], P('fsdp')
- d_ffn_gain: float32 [2048], replicated
- d_router: float32 [2048, 16], P('fsdp')
- d_gate: float32 [2048, 16, 1024], P('fsdp', 'ctx')
- d_up: float32 [2048, 16, 1024], P('fsdp', 'ctx')
- d_down: float32 [2048, 16, 1024], P('fsdp', 'ctx')
Inputs may be any that keep to these rules, and one draw needn't show every extreme that they name: `routes`: each token names 8 different experts; in each aligned block of 128 tokens (the tokens of one device) no expert is named more than 80 times, and in some blocks one is named exactly 80 times.
All inputs are finite; a program needn't handle non-finite values.
Results may differ from a plain program's by a relative error of at most 0.025.
Values may be sent and summed in bfloat16 or wider, within the bound.
No kernel may reach another device: no remote copies, remote signals or barrier semaphores. Data moves between devices by JAX's collectives and lax.ppermute only.
A program may use at most 384 MiB of HBM per device.

v0:
```python
import jax
import jax.numpy as jnp
from jax import lax
from jax.sharding import PartitionSpec as P

EPSILON = 1e-06
ROPE_BASE = 10000.0
NEG_LARGE = -1e30


def rms_norm(values, gain_vec):
    factor = lax.rsqrt(jnp.mean(values * values, axis=-1, keepdims=True) + EPSILON)
    return values * factor * gain_vec


def rope_turn(values, places):
    half_dim = values.shape[-1] // 2
    frequency = ROPE_BASE ** (-jnp.arange(half_dim, dtype=jnp.float32) * 2.0 / values.shape[-1])
    angles = places.astype(jnp.float32)[:, None, None] * frequency[None, None, :]
    cosine = jnp.cos(angles)
    sine_part = jnp.sin(angles)
    first_half = values[..., :half_dim]
    second_half = values[..., half_dim:]
    return jnp.concatenate(
        [
            first_half * cosine - second_half * sine_part,
            second_half * cosine + first_half * sine_part,
        ],
        axis=-1,
    )


def head_path(projected, gain_vec, places, head_count):
    split_heads = projected.reshape(projected.shape[0], head_count, -1)
    return rope_turn(rms_norm(split_heads, gain_vec), places)


def swiglu(gate_part, up_part):
    return jax.nn.silu(gate_part) * up_part


def block_number(length):
    number = 1
    while length // number > 1024 and length % (2 * number) == 0:
        number = number * 2
    return number


def attend_fold(queries, scale, carry, piece):
    head_count = queries.shape[1]
    head_dim = queries.shape[2]
    keys_piece, values_piece = piece
    length = keys_piece.shape[0]
    number = block_number(length)
    key_blocks = keys_piece.reshape(number, length // number, head_count, head_dim)
    value_blocks = values_piece.reshape(number, length // number, head_count, head_dim)

    def attend_step(state, block):
        running_max, running_sum, running_acc = state
        key_block, value_block = block
        scores = (
            jnp.einsum("qhd,khd->hqk", queries, key_block, preferred_element_type=jnp.float32)
            * scale
        )
        new_max = jnp.maximum(running_max, jnp.max(scores, axis=-1))
        weights = jnp.exp(scores - new_max[..., None])
        shrink = jnp.exp(running_max - new_max)
        running_sum = running_sum * shrink + jnp.sum(weights, axis=-1)
        running_acc = running_acc * shrink[..., None] + jnp.einsum(
            "hqk,khd->hqd",
            weights.astype(jnp.bfloat16),
            value_block,
            preferred_element_type=jnp.float32,
        )
        return ((new_max, running_sum, running_acc), None)

    carry, ignored = lax.scan(attend_step, carry, (key_blocks, value_blocks))
    return carry


def key_side_fold(queries, grad_out, log_total, delta, scale, carry, piece):
    head_count = queries.shape[1]
    head_dim = queries.shape[2]
    grad_query, keys_all, values_all = carry
    keys_piece, values_piece = piece
    length = keys_piece.shape[0]
    number = block_number(length)
    key_blocks = keys_piece.reshape(number, length // number, head_count, head_dim)
    value_blocks = values_piece.reshape(number, length // number, head_count, head_dim)

    def key_step(accum, block):
        key_block, value_block = block
        scores = (
            jnp.einsum("qhd,khd->hqk", queries, key_block, preferred_element_type=jnp.float32)
            * scale
        )
        probs = jnp.exp(scores - log_total[..., None])
        grad_val = jnp.einsum(
            "hqk,qhd->khd", probs.astype(jnp.bfloat16), grad_out, preferred_element_type=jnp.float32
        )
        grad_probs = jnp.einsum(
            "qhd,khd->hqk", grad_out, value_block, preferred_element_type=jnp.float32
        )
        grad_scores = (probs * (grad_probs - delta[..., None])).astype(jnp.bfloat16)
        grad_k = (
            jnp.einsum("hqk,qhd->khd", grad_scores, queries, preferred_element_type=jnp.float32)
            * scale
        )
        accum = (
            accum
            + jnp.einsum("hqk,khd->qhd", grad_scores, key_block, preferred_element_type=jnp.float32)
            * scale
        )
        return (accum, (grad_k, grad_val))

    grad_query, (key_parts, value_parts) = lax.scan(
        key_step, grad_query, (key_blocks, value_blocks)
    )
    width = head_count * head_dim
    keys_all = key_parts.reshape(length, width)
    values_all = value_parts.reshape(length, width)
    return (grad_query, keys_all, values_all)


def body(
    tokens,
    attn_gain,
    w_query,
    w_key,
    w_value,
    query_gain,
    key_gain,
    w_out,
    ffn_gain,
    w_router,
    w_gate,
    w_up,
    w_down,
    routes,
    cotangent,
):
    ctx_size = lax.axis_size("ctx")
    fsdp_size = lax.axis_size("fsdp")
    local_rows = tokens.shape[1]
    width = tokens.shape[2]
    head_dim = query_gain.shape[0]
    head_count = width // head_dim
    local_experts = w_gate.shape[1]
    expert_total = local_experts * ctx_size
    top_count = routes.shape[2]
    capacity = 5 * local_rows * top_count // (4 * expert_total)
    seq_length = local_rows * ctx_size
    scale = head_dim ** (-0.5)
    places = lax.axis_index("ctx") * local_rows + jnp.arange(local_rows, dtype=jnp.int32)
    source = tokens[0].astype(jnp.float32)
    route_local = routes[0]
    route_rows = route_local.reshape(-1)
    expert_ids = jnp.arange(expert_total, dtype=jnp.int32)
    member = (route_rows[:, None] == expert_ids[None, :]).astype(jnp.int32)
    ranking = jnp.cumsum(member, axis=0) - 1
    target = route_rows * capacity + jnp.sum(ranking * member, axis=1)
    owner = jnp.arange(local_rows * top_count, dtype=jnp.int32) // top_count
    choose_table = (route_local[:, :, None] == expert_ids[None, None, :]).astype(jnp.float32)

    def forward_pass():
        query_w, key_w, value_w = (
            lax.all_gather(w_query, "fsdp", axis=0, tiled=True),
            lax.all_gather(w_key, "fsdp", axis=0, tiled=True),
            lax.all_gather(w_value, "fsdp", axis=0, tiled=True),
        )
        out_w, router_w, gate_w, up_w, down_w = (
            lax.all_gather(w_out, "fsdp", axis=0, tiled=True),
            lax.all_gather(w_router, "fsdp", axis=0, tiled=True),
            lax.all_gather(w_gate, "fsdp", axis=0, tiled=True),
            lax.all_gather(w_up, "fsdp", axis=0, tiled=True),
            lax.all_gather(w_down, "fsdp", axis=0, tiled=True),
        )
        normed = rms_norm(source, attn_gain).astype(jnp.bfloat16)
        query_pre = jnp.dot(normed, query_w, preferred_element_type=jnp.float32)
        key_pre = jnp.dot(normed, key_w, preferred_element_type=jnp.float32)
        value_low = jnp.dot(normed, value_w, preferred_element_type=jnp.float32).astype(
            jnp.bfloat16
        )
        query_low = head_path(query_pre, query_gain, places, head_count).astype(jnp.bfloat16)
        key_low = head_path(key_pre, key_gain, places, head_count).astype(jnp.bfloat16)
        start_state = (
            jnp.full((head_count, local_rows), NEG_LARGE, jnp.float32),
            jnp.zeros((head_count, local_rows), jnp.float32),
            jnp.zeros((head_count, local_rows, head_dim), jnp.float32),
        )
        final_max, final_sum, final_acc = attend_fold(
            query_low,
            scale,
            start_state,
            (
                lax.all_gather(key_low.reshape(local_rows, width), "ctx", axis=0, tiled=True),
                lax.all_gather(value_low, "ctx", axis=0, tiled=True),
            ),
        )
        attended = final_acc / final_sum[..., None]
        log_total = final_max + jnp.log(final_sum)
        mixed_full = jnp.transpose(attended, (1, 0, 2)).reshape(local_rows, width)
        mixed_low = mixed_full.astype(jnp.bfloat16)
        hidden = source + jnp.dot(mixed_low, out_w, preferred_element_type=jnp.float32)
        ffn_in = rms_norm(hidden, ffn_gain).astype(jnp.bfloat16)
        logits = jnp.dot(ffn_in, router_w, preferred_element_type=jnp.float32)
        chosen = jnp.einsum("tke,te->tk", choose_table, logits, precision=lax.Precision.HIGHEST)
        gates = jax.nn.softmax(chosen, axis=-1)
        send = (
            jnp.zeros((expert_total * capacity, width), jnp.bfloat16).at[target].set(ffn_in[owner])
        )
        send = send.reshape(ctx_size, local_experts, capacity, width)
        arrived = lax.all_to_all(send, "ctx", split_axis=0, concat_axis=0, tiled=True)
        gate_pre = jnp.einsum("nesd,def->nesf", arrived, gate_w, preferred_element_type=jnp.float32)
        up_pre = jnp.einsum("nesd,def->nesf", arrived, up_w, preferred_element_type=jnp.float32)
        act_low = swiglu(gate_pre, up_pre).astype(jnp.bfloat16)
        result = jnp.einsum(
            "nesf,def->nesd", act_low, down_w, preferred_element_type=jnp.float32
        ).astype(jnp.bfloat16)
        arrived, gate_pre, up_pre, expert_low = (arrived, gate_pre, up_pre, result)
        returned = lax.all_to_all(expert_low, "ctx", split_axis=0, concat_axis=0, tiled=True)
        picked = returned.reshape(expert_total * capacity, width)[target].reshape(
            local_rows, top_count, width
        )
        output = hidden + jnp.sum(gates[..., None] * picked.astype(jnp.float32), axis=1)
        return {
            "query_w": query_w,
            "key_w": key_w,
            "value_w": value_w,
            "out_w": out_w,
            "router_w": router_w,
            "gate_w": gate_w,
            "up_w": up_w,
            "down_w": down_w,
            "normed": normed,
            "query_pre": query_pre,
            "key_pre": key_pre,
            "value_low": value_low,
            "query_low": query_low,
            "key_low": key_low,
            "log_total": log_total,
            "mixed_full": mixed_full,
            "mixed_low": mixed_low,
            "hidden": hidden,
            "ffn_in": ffn_in,
            "gates": gates,
            "arrived": arrived,
            "gate_pre": gate_pre,
            "up_pre": up_pre,
            "picked": picked,
            "output": output,
        }

    first_pass = forward_pass()
    output = first_pass["output"]
    saved = forward_pass()
    grad_out = cotangent[0].astype(jnp.float32)
    gates = saved["gates"]
    picked = saved["picked"]
    d_gates = jnp.sum(grad_out[:, None, :] * picked.astype(jnp.float32), axis=-1)
    grad_expert = (
        (gates[..., None] * grad_out[:, None, :])
        .astype(jnp.bfloat16)
        .reshape(local_rows * top_count, width)
    )
    send_back = (
        jnp.zeros((expert_total * capacity, width), jnp.bfloat16).at[target].set(grad_expert)
    )
    send_back = send_back.reshape(ctx_size, local_experts, capacity, width)
    grad_slots = lax.all_to_all(send_back, "ctx", split_axis=0, concat_axis=0, tiled=True)
    act_low = swiglu(saved["gate_pre"], saved["up_pre"]).astype(jnp.bfloat16)
    grad_act = jnp.einsum(
        "nesd,def->nesf", grad_slots, saved["down_w"], preferred_element_type=jnp.float32
    )
    d_down_w = jnp.einsum("nesd,nesf->def", grad_slots, act_low, preferred_element_type=jnp.float32)
    ignored, swiglu_back = jax.vjp(swiglu, saved["gate_pre"], saved["up_pre"])
    grad_gate_pre, grad_up_pre = swiglu_back(grad_act)
    grad_gate_low = grad_gate_pre.astype(jnp.bfloat16)
    grad_up_low = grad_up_pre.astype(jnp.bfloat16)
    d_gate_w = jnp.einsum(
        "nesd,nesf->def", saved["arrived"], grad_gate_low, preferred_element_type=jnp.float32
    )
    d_up_w = jnp.einsum(
        "nesd,nesf->def", saved["arrived"], grad_up_low, preferred_element_type=jnp.float32
    )
    grad_arrived = (
        jnp.einsum(
            "nesf,def->nesd", grad_gate_low, saved["gate_w"], preferred_element_type=jnp.float32
        )
        + jnp.einsum(
            "nesf,def->nesd", grad_up_low, saved["up_w"], preferred_element_type=jnp.float32
        )
    ).astype(jnp.bfloat16)
    grad_back = lax.all_to_all(grad_arrived, "ctx", split_axis=0, concat_axis=0, tiled=True)
    grad_rows = grad_back.reshape(expert_total * capacity, width)[target].reshape(
        local_rows, top_count, width
    )
    grad_ffn_in = jnp.sum(grad_rows.astype(jnp.float32), axis=1)
    grad_chosen = gates * (d_gates - jnp.sum(gates * d_gates, axis=-1, keepdims=True))
    grad_logits = jnp.einsum(
        "tke,tk->te", choose_table, grad_chosen, precision=lax.Precision.HIGHEST
    )
    router_full = saved["router_w"].astype(jnp.float32)
    grad_ffn_in = grad_ffn_in + jnp.einsum(
        "te,de->td", grad_logits, router_full, precision=lax.Precision.HIGHEST
    )
    d_router_w = jnp.einsum(
        "td,te->de",
        saved["ffn_in"].astype(jnp.float32),
        grad_logits,
        precision=lax.Precision.HIGHEST,
    )
    ignored, norm_two_back = jax.vjp(rms_norm, saved["hidden"], ffn_gain)
    grad_hidden_norm, d_ffn_gain = norm_two_back(grad_ffn_in)
    grad_hidden = grad_out + grad_hidden_norm
    grad_proj = grad_hidden.astype(jnp.bfloat16)
    d_out_w = jnp.einsum(
        "td,te->de", saved["mixed_low"], grad_proj, preferred_element_type=jnp.float32
    )
    grad_mixed = jnp.einsum(
        "te,de->td", grad_proj, saved["out_w"], preferred_element_type=jnp.float32
    ).astype(jnp.bfloat16)
    grad_heads = grad_mixed.reshape(local_rows, head_count, head_dim)
    delta = jnp.sum(
        grad_heads.astype(jnp.float32)
        * saved["mixed_full"].reshape(local_rows, head_count, head_dim),
        axis=-1,
    ).T
    query_low = saved["query_low"]
    key_low = saved["key_low"]
    value_low = saved["value_low"]
    start_grads = (
        jnp.zeros((local_rows, head_count, head_dim), jnp.float32),
        jnp.zeros((seq_length, width), jnp.float32),
        jnp.zeros((seq_length, width), jnp.float32),
    )
    grad_query, keys_all, values_all = key_side_fold(
        query_low,
        grad_heads,
        saved["log_total"],
        delta,
        scale,
        start_grads,
        (
            lax.all_gather(key_low.reshape(local_rows, width), "ctx", axis=0, tiled=True),
            lax.all_gather(value_low, "ctx", axis=0, tiled=True),
        ),
    )
    grad_key_flat, grad_value_flat = (
        lax.psum_scatter(
            keys_all.astype(jnp.bfloat16), "ctx", scatter_dimension=0, tiled=True
        ).astype(jnp.float32),
        lax.psum_scatter(
            values_all.astype(jnp.bfloat16), "ctx", scatter_dimension=0, tiled=True
        ).astype(jnp.float32),
    )
    grad_key = grad_key_flat.reshape(local_rows, head_count, head_dim)
    ignored, query_back = jax.vjp(
        lambda projected, gain_vec: head_path(projected, gain_vec, places, head_count),
        saved["query_pre"],
        query_gain,
    )
    grad_query_pre, d_query_gain = query_back(grad_query)
    ignored, key_back = jax.vjp(
        lambda projected, gain_vec: head_path(projected, gain_vec, places, head_count),
        saved["key_pre"],
        key_gain,
    )
    grad_key_pre, d_key_gain = key_back(grad_key)
    grad_query_low = grad_query_pre.astype(jnp.bfloat16)
    grad_key_low = grad_key_pre.astype(jnp.bfloat16)
    grad_value_low = grad_value_flat.astype(jnp.bfloat16)
    normed = saved["normed"]
    d_query_w = jnp.einsum("td,te->de", normed, grad_query_low, preferred_element_type=jnp.float32)
    d_key_w = jnp.einsum("td,te->de", normed, grad_key_low, preferred_element_type=jnp.float32)
    d_value_w = jnp.einsum("td,te->de", normed, grad_value_low, preferred_element_type=jnp.float32)
    grad_normed = (
        jnp.einsum(
            "te,de->td", grad_query_low, saved["query_w"], preferred_element_type=jnp.float32
        )
        + jnp.einsum("te,de->td", grad_key_low, saved["key_w"], preferred_element_type=jnp.float32)
        + jnp.einsum(
            "te,de->td", grad_value_low, saved["value_w"], preferred_element_type=jnp.float32
        )
    )
    ignored, norm_one_back = jax.vjp(rms_norm, source, attn_gain)
    grad_source, d_attn_gain = norm_one_back(grad_normed)
    d_tokens = grad_hidden + grad_source
    gain_grads = jnp.concatenate([d_attn_gain, d_query_gain, d_key_gain, d_ffn_gain])
    tiled = jnp.broadcast_to(gain_grads[None, :], (fsdp_size, gain_grads.shape[0]))
    shards = (
        lax.psum_scatter(
            d_query_w.astype(jnp.bfloat16), "fsdp", scatter_dimension=0, tiled=True
        ).astype(jnp.float32),
        lax.psum_scatter(
            d_key_w.astype(jnp.bfloat16), "fsdp", scatter_dimension=0, tiled=True
        ).astype(jnp.float32),
        lax.psum_scatter(
            d_value_w.astype(jnp.bfloat16), "fsdp", scatter_dimension=0, tiled=True
        ).astype(jnp.float32),
        lax.psum_scatter(
            d_out_w.astype(jnp.bfloat16), "fsdp", scatter_dimension=0, tiled=True
        ).astype(jnp.float32),
        lax.psum_scatter(
            d_router_w.astype(jnp.bfloat16), "fsdp", scatter_dimension=0, tiled=True
        ).astype(jnp.float32),
        lax.psum_scatter(
            d_gate_w.astype(jnp.bfloat16), "fsdp", scatter_dimension=0, tiled=True
        ).astype(jnp.float32),
        lax.psum_scatter(
            d_up_w.astype(jnp.bfloat16), "fsdp", scatter_dimension=0, tiled=True
        ).astype(jnp.float32),
        lax.psum_scatter(
            d_down_w.astype(jnp.bfloat16), "fsdp", scatter_dimension=0, tiled=True
        ).astype(jnp.float32),
        lax.psum_scatter(
            tiled.astype(jnp.bfloat16), "fsdp", scatter_dimension=0, tiled=True
        ).astype(jnp.float32),
    )
    summed = (
        lax.psum(shards[0].astype(jnp.bfloat16), "ctx").astype(jnp.float32),
        lax.psum(shards[1].astype(jnp.bfloat16), "ctx").astype(jnp.float32),
        lax.psum(shards[2].astype(jnp.bfloat16), "ctx").astype(jnp.float32),
        lax.psum(shards[3].astype(jnp.bfloat16), "ctx").astype(jnp.float32),
        lax.psum(shards[4].astype(jnp.bfloat16), "ctx").astype(jnp.float32),
        lax.psum(shards[8][0].astype(jnp.bfloat16), "ctx").astype(jnp.float32),
    )
    query_part, key_part, value_part, out_part, router_part, gains_total = summed
    gate_part, up_part, down_part = (shards[5], shards[6], shards[7])
    return (
        output[None].astype(jnp.bfloat16),
        d_tokens[None],
        gains_total[:width],
        query_part,
        key_part,
        value_part,
        gains_total[width : width + head_dim],
        gains_total[width + head_dim : width + 2 * head_dim],
        out_part,
        gains_total[width + 2 * head_dim :],
        router_part,
        gate_part,
        up_part,
        down_part,
    )


def solution(mesh):
    placed = (
        P("fsdp", "ctx", None),
        P(),
        P("fsdp", None),
        P("fsdp", None),
        P("fsdp", None),
        P(),
        P(),
        P("fsdp", None),
        P(),
        P("fsdp", None),
        P("fsdp", "ctx", None),
        P("fsdp", "ctx", None),
        P("fsdp", "ctx", None),
        P("fsdp", "ctx", None),
        P("fsdp", "ctx", None),
    )
    return jax.shard_map(
        body,
        mesh=mesh,
        in_specs=placed,
        out_specs=(
            P("fsdp", "ctx", None),
            P("fsdp", "ctx", None),
            P(),
            P("fsdp", None),
            P("fsdp", None),
            P("fsdp", None),
            P(),
            P(),
            P("fsdp", None),
            P(),
            P("fsdp", None),
            P("fsdp", "ctx", None),
            P("fsdp", "ctx", None),
            P("fsdp", "ctx", None),
        ),
        check_vma=False,
    )
```

profile of v0, /device:TPU:0, one launch (start us, length us, event | category | flops | bytes accessed | tf_op | source)
XLA Modules:
  0.0 1994.8 jit_solution(16803237976775698070)
XLA Ops:
  9.9 60.7 %all-gather.10.cloned.1.call-done = bf16[2048,2048]{1,0:T(8,128)(2,1)} async-done(((bf16[512,2048]{1,0:T(8,128)(2,1)}), bf16[2048,2048]{1,0:T(8,128)(2,1)}) %all-gather.10.cloned.1.call-update) | async-done | bytes 8388624 | tf_op jit(solution)/shard_map/all_gather | solution.py:167
  70.6 12.4 copy.70
  83.0 47.5 %all-gather.12.cloned.1.call-done = bf16[2048,2048]{1,0:T(8,128)(2,1)} async-done(((bf16[512,2048]{1,0:T(8,128)(2,1)}), bf16[2048,2048]{1,0:T(8,128)(2,1)}) %all-gather.12.cloned.1.call-update) | async-done | bytes 8388624 | tf_op jit(solution)/shard_map/all_gather | solution.py:168
  130.5 12.4 copy.71
  142.9 6.4 multiply_reduce_fusion.10
  154.3 36.1 %all-gather.16.cloned.1.call-done = bf16[2048,2048]{1,0:T(8,128)(2,1)} async-done(((bf16[512,2048]{1,0:T(8,128)(2,1)}), bf16[2048,2048]{1,0:T(8,128)(2,1)}) %all-gather.16.cloned.1.call-update) | async-done | bytes 8388624 | tf_op jit(solution)/shard_map/all_gather | solution.py:169
  190.4 5.5 convolution_convert_fusion.5
  202.5 4.5 reduce-window.6
  207.8 5.2 all_gather.48
  213.2 54.7 %all-gather.14.cloned.1.call-done = bf16[1024,2048]{0,1:T(8,128)(2,1)} async-done(((bf16[128,2048]{0,1:T(8,128)(2,1)}), bf16[1024,2048]{0,1:T(8,128)(2,1)}) %all-gather.14.cloned.1.call-update) | async-done | bytes 4194320 | tf_op jit(solution)/shard_map/all_gather | solution.py:196
  277.4 64.7 %all-gather.18.cloned.1.call-done = bf16[1024,2048]{1,0:T(8,128)(2,1)} async-done(((bf16[128,2048]{1,0:T(8,128)(2,1)}), bf16[1024,2048]{1,0:T(8,128)(2,1)}) %all-gather.18.cloned.1.call-update) | async-done | bytes 4194320 | tf_op jit(solution)/shard_map/all_gather | solution.py:197
  342.1 8.0 fusion.135
  350.0 50.0 %all-gather.20.cloned.1.call-done = bf16[2048,2048]{1,0:T(8,128)(2,1)} async-done(((bf16[512,2048]{1,0:T(8,128)(2,1)}), bf16[2048,2048]{1,0:T(8,128)(2,1)}) %all-gather.20.cloned.1.call-update) | async-done | bytes 8388624 | tf_op jit(solution)/shard_map/all_gather | solution.py:172
  400.1 4.8 multiply_reduce_fusion.8
  406.4 10.0 scatter_custom_fusion.1
  416.5 5.5 all-to-all-start.2
  426.0 23.3 %scatter_custom_fusion = bf16[1280,2048]{1,0:T(8,128)(2,1)} fusion(s32[1024]{0:T(1024)S(1)} %bitcast.316, bf16[128,2048]{1,0:T(8,128)(2,1)S(1)} %multiply_convert_fusion.2, s32[1024]{0:T(1024)S(1)} %broadcast_clamp_fusion.1, bf16[]{:T(256)} %constant.108.clone.1), kind=kCustom, calls=%fused_computation.68 | custom fusion | bytes 5242882 | tf_op jit(solution)/shard_map/scatter | solution.py:210
  449.3 88.9 %all-to-all-done.2 = bf16[8,2,80,2048]{3,2,1,0:T(8,128)(2,1)} async-done(((bf16[8,2,80,2048]{3,2,1,0:T(8,128)(2,1)}), bf16[8,2,80,2048]{3,2,1,0:T(8,128)(2,1)}, u32[]{:S(2)}, u32[]{:S(2)}) %all-to-all-start.2) | async-done | bytes 5242912 | tf_op jit(solution)/shard_map/all_to_all | solution.py:270
  538.2 4.6 all-to-all-start
  542.9 11.4 fusion.13
  554.3 103.8 %all-to-all-done = bf16[8,2,80,2048]{3,2,1,0:T(8,128)(2,1)} async-done(((bf16[8,2,80,2048]{3,2,1,0:T(8,128)(2,1)}), bf16[8,2,80,2048]{3,2,1,0:T(8,128)(2,1)}, u32[]{:S(2)}, u32[]{:S(2)}) %all-to-all-start) | async-done | bytes 5242912 | tf_op jit(solution)/shard_map/all_to_all | solution.py:213
  658.1 11.5 fusion.7
  669.6 15.1 fusion.23
  684.7 10.4 convert_bitcast_fusion
  697.9 5.1 all-to-all-start.1
  703.0 12.1 fusion.5
  715.1 11.2 fusion.24
  729.1 88.8 %all-to-all-done.1 = bf16[8,2,80,2048]{3,2,1,0:T(8,128)(2,1)} async-done(((bf16[8,2,80,2048]{3,2,1,0:T(8,128)(2,1)}), bf16[8,2,80,2048]{3,2,1,0:T(8,128)(2,1)}, u32[]{:S(2)}, u32[]{:S(2)}) %all-to-all-start.1) | async-done | bytes 5242912 | tf_op jit(solution)/shard_map/all_to_all | solution.py:221
  817.8 4.6 all-to-all-start.3
  822.6 12.0 gather_fusion
  834.5 5.8 fusion.1
  841.3 96.1 %all-to-all-done.3 = bf16[8,2,80,2048]{3,2,1,0:T(8,128)(2,1)} async-done(((bf16[8,2,80,2048]{3,2,1,0:T(8,128)(2,1)}), bf16[8,2,80,2048]{3,2,1,0:T(8,128)(2,1)}, u32[]{:S(2)}, u32[]{:S(2)}) %all-to-all-start.3) | async-done | bytes 5242912 | tf_op jit(solution)/shard_map/all_to_all | solution.py:294
  937.4 12.1 gather_fusion.1
  949.6 5.2 convert_reduce_fusion
  956.9 6.3 convolution_convert_fusion.4
  963.5 7.2 fusion.61
  970.7 6.5 copy.113
  977.4 6.2 multiply_convert_fusion.1
  988.9 6.5 copy.111
  995.7 5.6 convolution_convert_fusion
  1001.4 62.0 %reduce-scatter.33.cloned.1.call-done = bf16[128,2048]{1,0:T(8,128)(2,1)} async-done(((bf16[1024,2048]{1,0:T(8,128)(2,1)}), bf16[128,2048]{1,0:T(8,128)(2,1)}) %reduce-scatter.33.cloned.1.call-update) | async-done | bytes 524304
  1063.4 6.8 convolution_convert_fusion.1
  1070.3 5.7 fusion.71
  1076.0 79.9 %reduce-scatter.31.cloned.1.call-done = bf16[128,2048]{1,0:T(8,128)(2,1)} async-done(((bf16[1024,2048]{1,0:T(8,128)(2,1)}), bf16[128,2048]{1,0:T(8,128)(2,1)}) %reduce-scatter.31.cloned.1.call-update) | async-done | bytes 524304
  1161.2 6.6 convolution_convert_fusion.2
  1172.6 5.8 convolution_convert_fusion.3
  1178.5 11.8 fusion.4
  1190.4 12.0 fusion.2
  1202.7 11.9 fusion.3
  1216.7 13.2 reduce-scatter.21.cloned.1.call-done
  1229.9 74.5 %reduce-scatter.19.cloned.1.call-done = bf16[512,2048]{1,0:T(8,128)(2,1)} async-done(((bf16[2048,2048]{1,0:T(8,128)(2,1)}), bf16[512,2048]{1,0:T(8,128)(2,1)}) %reduce-scatter.19.cloned.1.call-update) | async-done | bytes 2097168 | tf_op jit(solution)/shard_map/reduce_scatter | solution.py:398
  1304.4 74.2 %reduce-scatter.17.cloned.1.call-done = bf16[512,2048]{1,0:T(8,128)(2,1)} async-done(((bf16[2048,2048]{1,0:T(8,128)(2,1)}), bf16[512,2048]{1,0:T(8,128)(2,1)}) %reduce-scatter.17.cloned.1.call-update) | async-done | bytes 2097168 | tf_op jit(solution)/shard_map/reduce_scatter | solution.py:395
  1378.6 74.3 %reduce-scatter.15.cloned.1.call-done = bf16[512,2048]{1,0:T(8,128)(2,1)} async-done(((bf16[2048,2048]{1,0:T(8,128)(2,1)}), bf16[512,2048]{1,0:T(8,128)(2,1)}) %reduce-scatter.15.cloned.1.call-update) | async-done | bytes 2097168 | tf_op jit(solution)/shard_map/reduce_scatter | solution.py:392
  1453.6 73.6 %reduce-scatter.29.cloned.1.call-done = bf16[512,2,1024]{0,2,1:T(8,128)(2,1)} async-done(((bf16[2048,2,1024]{0,2,1:T(8,128)(2,1)}), bf16[512,2,1024]{0,2,1:T(8,128)(2,1)}) %reduce-scatter.29.cloned.1.call-update) | async-done | bytes 2097168 | tf_op jit(solution)/shard_map/reduce_scatter | solution.py:413
  1527.1 6.5 copy.97
  1533.6 67.9 %reduce-scatter.25.cloned.1.call-done = bf16[512,2,1024]{0,2,1:T(8,128)(2,1)} async-done(((bf16[2048,2,1024]{0,2,1:T(8,128)(2,1)}), bf16[512,2,1024]{0,2,1:T(8,128)(2,1)}) %reduce-scatter.25.cloned.1.call-update) | async-done | bytes 2097168 | tf_op jit(solution)/shard_map/reduce_scatter | solution.py:407
  1601.5 6.5 copy.95
  1607.9 67.7 %reduce-scatter.27.cloned.1.call-done = bf16[512,2,1024]{0,2,1:T(8,128)(2,1)} async-done(((bf16[2048,2,1024]{0,2,1:T(8,128)(2,1)}), bf16[512,2,1024]{0,2,1:T(8,128)(2,1)}) %reduce-scatter.27.cloned.1.call-update) | async-done | bytes 2097168 | tf_op jit(solution)/shard_map/reduce_scatter | solution.py:410
  1675.7 6.5 copy.96
  1682.1 6.5 fusion.137
  1688.6 6.5 convolution_add_fusion.2
  1698.3 10.5 all-reduce.4
  1709.5 39.7 %all-reduce.5 = (bf16[4352]{0:T(1024)(128)(2,1)S(1)}, bf16[512,16]{0,1:T(8,128)(2,1)S(1)}) all-reduce(bf16[4352]{0:T(1024)(128)(2,1)S(1)} %dynamic-slice_reduce_fusion, bf16[512,16]{0,1:T(8,128)(2,1)} %reduce-scatter.23.cloned.1.call-done), channel_id=1, replica_groups=mesh['ctx'=8,'fsdp'=4] {'ctx'}, use_global_device_ids=true, to_apply=%region_29.30 | all-reduce | flops 12544 | bytes 50176 | tf_op jit(solution)/shard_map/psum | solution.py:426
  1752.3 223.6 %all-reduce.9.cloned.1.call-done = (bf16[512,2048]{1,0:T(8,128)(2,1)}, bf16[512,2048]{1,0:T(8,128)(2,1)}, bf16[512,2048]{1,0:T(8,128)(2,1)}, bf16[512,2048]{1,0:T(8,128)(2,1)}) async-done(((bf16[512,2048]{1,0:T(8,128)(2,1)}, bf16[512,2048]{1,0:T(8,128)(2,1)}, bf16[512,2048]{1,0:T(8,128)(2,1)}, bf16[512,2048]{1,0:T(8,128)(2,1)}), (bf16[512,2048]{1,0:T(8,128)(2,1)}, bf16[512,2048]{1,0:T(8,128)(2,1)}, ...) | async-done | bytes 8388624 | tf_op jit(solution)/shard_map/psum | solution.py:421
  (245 shorter events, 76.5 us)
Async XLA Ops:
  7.2 63.4 %all-gather.10.cloned.1.call-start = ((), (), s32[]{:S(2)}) async-start(), calls=%async_computation.14 | async-start | bytes 10485760 | tf_op jit(solution)/shard_map/all_gather | solution.py:167
  7.9 122.6 %all-gather.12.cloned.1.call-start = ((), (), s32[]{:S(2)}) async-start(), calls=%async_computation.15 | async-start | bytes 10485760 | tf_op jit(solution)/shard_map/all_gather | solution.py:168
  8.7 181.7 %all-gather.16.cloned.1.call-start = ((), (), s32[]{:S(2)}) async-start(), calls=%async_computation.17 | async-start | bytes 10485760 | tf_op jit(solution)/shard_map/all_gather | solution.py:169
  9.4 258.5 %all-gather.14.cloned.1.call-start = ((), (), s32[]{:S(2)}) async-start(), calls=%async_computation.16 | async-start | bytes 4718592 | tf_op jit(solution)/shard_map/all_gather | solution.py:196
  9.7 73.3 %copy-start.53 = (f32[128]{0:T(128)}, f32[128]{0:T(128)S(1)}, u32[]{:S(2)}) copy-start(f32[128]{0:T(128)S(1)} %fusion.85) | copy-start | bytes 1540
  9.7 180.7 %copy-start.41 = (f32[128]{0:T(128)}, f32[128]{0:T(128)S(1)}, u32[]{:S(2)}) copy-start(f32[128]{0:T(128)S(1)} %fusion.123) | copy-start | bytes 1540
  9.9 143.1 %copy-start.31 = (f32[128,64]{0,1:T(8,128)}, f32[128,64]{0,1:T(8,128)S(1)}, u32[]{:S(2)}) copy-start(f32[128,64]{0,1:T(8,128)S(1)} %get-tuple-element.160) | copy-start | bytes 98308
  9.9 143.0 %copy-start.33 = (f32[128,64]{0,1:T(8,128)}, f32[128,64]{0,1:T(8,128)S(1)}, u32[]{:S(2)}) copy-start(f32[128,64]{0,1:T(8,128)S(1)} %get-tuple-element.161) | copy-start | bytes 98308
  130.5 12.4 copy-start.21
  142.9 6.5 copy-start.3
  153.3 114.6 %copy-start.17 = (bf16[128,16,64]{0,2,1:T(8,128)(2,1)}, bf16[128,16,64]{0,2,1:T(8,128)(2,1)S(1)}, u32[]{:S(2)}) copy-start(bf16[128,16,64]{0,2,1:T(8,128)(2,1)S(1)} %get-tuple-element.144) | copy-start | bytes 786436
  153.3 114.6 %copy-start.19 = (bf16[128,16,64]{0,2,1:T(8,128)(2,1)}, bf16[128,16,64]{0,2,1:T(8,128)(2,1)S(1)}, u32[]{:S(2)}) copy-start(bf16[128,16,64]{0,2,1:T(8,128)(2,1)S(1)} %get-tuple-element.145) | copy-start | bytes 786436
  154.2 42.3 %copy-start.29 = (bf16[512,2,1024]{2,1,0:T(2,128)(2,1)S(1)}, bf16[512,2,1024]{2,1,0:T(2,128)(2,1)}, u32[]{:S(2)}) copy-start(bf16[512,2,1024]{2,1,0:T(2,128)(2,1)} %param.27) | copy-start | bytes 6291460
  154.2 187.8 %all-gather.18.cloned.1.call-start = ((), (), s32[]{:S(2)}) async-start(), calls=%async_computation.18 | async-start | bytes 4718592 | tf_op jit(solution)/shard_map/all_gather | solution.py:197
  195.9 204.2 %all-gather.20.cloned.1.call-start = ((), (), s32[]{:S(2)}) async-start(), calls=%async_computation.19 | async-start | bytes 10485760 | tf_op jit(solution)/shard_map/all_gather | solution.py:172
  196.5 346.4 %all-gather.26.cloned.1.call-start = ((), (), s32[]{:S(2)}) async-start(), calls=%async_computation.22 | async-start | bytes 10485760 | tf_op jit(solution)/shard_map/all_gather | solution.py:176
  198.5 9.3 copy-start.48
  198.5 14.6 copy-start.26
  198.5 355.8 %all-gather.24.cloned.1.call-start = ((), (), s32[]{:S(2)}) async-start(), calls=%async_computation.21 | async-start | bytes 10485760 | tf_op jit(solution)/shard_map/all_gather | solution.py:175
  350.0 54.8 %copy-start.9 = (bf16[128,16,128]{0,2,1:T(8,128)(2,1)}, bf16[128,16,128]{0,2,1:T(8,128)(2,1)S(1)}, u32[]{:S(2)}) copy-start(bf16[128,16,128]{0,2,1:T(8,128)(2,1)S(1)} %get-tuple-element.168) | copy-start | bytes 1572868
  400.1 4.8 copy-start.40
  405.0 21.0 %copy-start.11 = (bf16[128,2048]{1,0:T(8,128)(2,1)}, bf16[128,2048]{1,0:T(8,128)(2,1)S(1)}, u32[]{:S(2)}) copy-start(bf16[128,2048]{1,0:T(8,128)(2,1)S(1)} %multiply_convert_fusion.2) | copy-start | bytes 1572868
  416.5 121.7 %all-to-all-start.2 = ((bf16[8,2,80,2048]{3,2,1,0:T(8,128)(2,1)}), bf16[8,2,80,2048]{3,2,1,0:T(8,128)(2,1)}, u32[]{:S(2)}, u32[]{:S(2)}) async-start(bf16[8,2,80,2048]{3,2,1,0:T(8,128)(2,1)} %bitcast.285), calls=%async_computation.2 | async-start | bytes 10485760 | tf_op jit(solution)/shard_map/all_to_all | solution.py:270
  422.0 247.6 %all-gather.22.cloned.1.call-start = ((), (), s32[]{:S(2)}) async-start(), calls=%async_computation.20 | async-start | bytes 10485760 | tf_op jit(solution)/shard_map/all_gather | solution.py:174
  538.2 119.9 %all-to-all-start = ((bf16[8,2,80,2048]{3,2,1,0:T(8,128)(2,1)}), bf16[8,2,80,2048]{3,2,1,0:T(8,128)(2,1)}, u32[]{:S(2)}, u32[]{:S(2)}) async-start(bf16[8,2,80,2048]{3,2,1,0:T(8,128)(2,1)} %bitcast.286), calls=%async_computation | async-start | bytes 10485760 | tf_op jit(solution)/shard_map/all_to_all | solution.py:213
  684.7 10.4 copy-start.56
  697.9 120.0 %all-to-all-start.1 = ((bf16[8,2,80,2048]{3,2,1,0:T(8,128)(2,1)}), bf16[8,2,80,2048]{3,2,1,0:T(8,128)(2,1)}, u32[]{:S(2)}, u32[]{:S(2)}) async-start(bf16[8,2,80,2048]{3,2,1,0:T(8,128)(2,1)} %copy.86), calls=%async_computation.1 | async-start | bytes 10485760 | tf_op jit(solution)/shard_map/all_to_all | solution.py:221
  817.8 119.6 %all-to-all-start.3 = ((bf16[8,2,80,2048]{3,2,1,0:T(8,128)(2,1)}), bf16[8,2,80,2048]{3,2,1,0:T(8,128)(2,1)}, u32[]{:S(2)}, u32[]{:S(2)}) async-start(bf16[8,2,80,2048]{3,2,1,0:T(8,128)(2,1)} %copy.88), calls=%async_computation.3 | async-start | bytes 10485760 | tf_op jit(solution)/shard_map/all_to_all | solution.py:294
  822.5 240.9 %reduce-scatter.33.cloned.1.call-start = ((), (), s32[]{:S(2)}) async-start(), calls=%async_computation.32 | async-start | bytes 4718592
  949.6 6.1 copy-start.16
  949.6 6.1 copy-start.27
  956.9 6.6 copy-start.39
  970.7 6.6 copy-start.30
  977.2 178.7 %reduce-scatter.31.cloned.1.call-start = ((), (), s32[]{:S(2)}) async-start(), calls=%async_computation.31 | async-start | bytes 4718592
  977.4 8.2 copy-start.18
  977.4 8.2 copy-start.20
  988.9 6.8 copy-start.10
  995.4 234.5 %reduce-scatter.21.cloned.1.call-start = ((), (), s32[]{:S(2)}) async-start(), calls=%async_computation.26 | async-start | bytes 10485760 | tf_op jit(solution)/shard_map/reduce_scatter | solution.py:401
  1001.3 62.1 %copy-start.2 = (bf16[1,128,2048]{2,1,0:T(8,128)(2,1)S(1)}, bf16[1,128,2048]{2,1,0:T(8,128)(2,1)}, u32[]{:S(2)}) copy-start(bf16[1,128,2048]{2,1,0:T(8,128)(2,1)} %param.15) | copy-start | bytes 1572868
  1001.3 62.1 %copy-start.22 = (f32[2048]{0:T(1024)S(1)}, f32[2048]{0:T(1024)}, u32[]{:S(2)}) copy-start(f32[2048]{0:T(1024)} %param.16) | copy-start | bytes 24580
  1001.3 62.1 %copy-start.42 = (f32[128]{0:T(128)S(1)}, f32[128]{0:T(128)}, u32[]{:S(2)}) copy-start(f32[128]{0:T(128)} %copy-done.41) | copy-start | bytes 1540
  1001.4 303.0 %reduce-scatter.19.cloned.1.call-start = ((), (), s32[]{:S(2)}) async-start(), calls=%async_computation.25 | async-start | bytes 10485760 | tf_op jit(solution)/shard_map/reduce_scatter | solution.py:398
  1070.3 87.1 %copy-start.32 = (f32[128,64]{0,1:T(8,128)S(1)}, f32[128,64]{0,1:T(8,128)}, u32[]{:S(2)}) copy-start(f32[128,64]{0,1:T(8,128)} %copy-done.31) | copy-start | bytes 98308
  1070.3 87.1 %copy-start.34 = (f32[128,64]{0,1:T(8,128)S(1)}, f32[128,64]{0,1:T(8,128)}, u32[]{:S(2)}) copy-start(f32[128,64]{0,1:T(8,128)} %copy-done.33) | copy-start | bytes 98308
  1070.3 308.3 %reduce-scatter.17.cloned.1.call-start = ((), (), s32[]{:S(2)}) async-start(), calls=%async_computation.24 | async-start | bytes 10485760 | tf_op jit(solution)/shard_map/reduce_scatter | solution.py:395
  1076.0 83.7 %copy-start.8 = (f32[128,16,128]{0,2,1:T(8,128)S(1)}, f32[128,16,128]{0,2,1:T(8,128)}, u32[]{:S(2)}) copy-start(f32[128,16,128]{0,2,1:T(8,128)} %copy-done.7) | copy-start | bytes 3145732
  1076.0 83.7 %copy-start.38 = (f32[128,16]{0,1:T(8,128)S(1)}, f32[128,16]{0,1:T(8,128)}, u32[]{:S(2)}) copy-start(f32[128,16]{0,1:T(8,128)} %copy-done.37) | copy-start | bytes 24580
  1076.0 83.7 %copy-start.50 = (f32[128]{0:T(128)S(1)}, f32[128]{0:T(128)}, u32[]{:S(2)}) copy-start(f32[128]{0:T(128)} %param.21) | copy-start | bytes 1540
  1076.0 84.1 %copy-start.46 = (f32[128,16]{0,1:T(8,128)S(1)}, f32[128,16]{0,1:T(8,128)}, u32[]{:S(2)}) copy-start(f32[128,16]{0,1:T(8,128)} %copy-done.45) | copy-start | bytes 24580
  1159.7 8.7 copy-start.13
  1167.9 285.0 %reduce-scatter.15.cloned.1.call-start = ((), (), s32[]{:S(2)}) async-start(), calls=%async_computation.23 | async-start | bytes 10485760 | tf_op jit(solution)/shard_map/reduce_scatter | solution.py:392
  1178.5 348.7 %reduce-scatter.29.cloned.1.call-start = ((), (), s32[]{:S(2)}) async-start(), calls=%async_computation.30 | async-start | bytes 10485760 | tf_op jit(solution)/shard_map/reduce_scatter | solution.py:413
  1190.4 411.1 %reduce-scatter.25.cloned.1.call-start = ((), (), s32[]{:S(2)}) async-start(), calls=%async_computation.28 | async-start | bytes 10485760 | tf_op jit(solution)/shard_map/reduce_scatter | solution.py:407
  1202.5 473.2 %reduce-scatter.27.cloned.1.call-start = ((), (), s32[]{:S(2)}) async-start(), calls=%async_computation.29 | async-start | bytes 10485760 | tf_op jit(solution)/shard_map/reduce_scatter | solution.py:410
  1214.6 238.4 %copy-start.55 = (u32[32]{0:T(128)S(1)}, u32[32]{0:T(128)}, u32[]{:S(2)}) copy-start(u32[32]{0:T(128)} %constant.134) | copy-start | bytes 388
  1214.6 494.9 %reduce-scatter.23.cloned.1.call-start = ((), (), s32[]{:S(2)}) async-start(), calls=%async_computation.27 | async-start | bytes 81920 | tf_op jit(solution)/shard_map/reduce_scatter | solution.py:404
  1216.6 759.2 %all-reduce.9.cloned.1.call-start = ((), (), s32[]{:S(2)}) async-start(), calls=%async_computation.33 | async-start | bytes 16777216 | tf_op jit(solution)/shard_map/psum | solution.py:421
  1682.1 6.5 copy-start.15
  1682.1 13.0 slice-start
  1688.6 6.5 slice-start.1
  1688.6 6.5 copy-start.28
  1695.1 54.7 %copy-start.54 = (f32[128]{0:T(128)S(1)}, f32[128]{0:T(128)}, u32[]{:S(2)}) copy-start(f32[128]{0:T(128)} %copy-done.53) | copy-start | bytes 1540
  1975.9 6.8 copy-start.24
  1980.2 5.1 copy-start.23
  (19 other events, 41.1 us)
Sparse Core Ops, SparseCore 0:
  9.6 60.9 all-gather.9
  72.2 58.2 all-gather.11
  132.0 58.2 all-gather.15
  192.8 75.0 all-gather.13
  270.4 71.5 all-gather.17
  343.5 56.5 all-gather.19
  402.2 58.2 all-gather.25
  462.6 58.2 all-gather.23
  523.1 58.2 all-gather.21
  977.3 86.0 reduce-scatter.32
  1068.1 87.8 reduce-scatter.30
  1158.4 71.4 reduce-scatter.20
  1232.6 71.6 reduce-scatter.18
  1306.8 71.7 reduce-scatter.16
  1381.2 71.6 reduce-scatter.14
  1455.4 71.7 reduce-scatter.28
  1529.7 71.6 reduce-scatter.24
  1603.9 71.7 reduce-scatter.26
  1678.8 19.4 reduce-scatter.22
  1702.7 273.1 all-reduce.8
where the time goes:
time: 2010 us; the launch traced here: 1990 us
  waiting for transfers between devices  1500 us (75%)
  matrix products  211 us (10%)
  local copies, waits for them, and re-layouts  133 us (7%)
  blocking collectives  55.5 us (3%)
  other arithmetic  52.8 us (3%)
  starting transfers between devices  21.9 us (1%)
    psum x1, waiting for transfers between devices, body(): lax.psum(shards[0].astype(jnp.bfloat16), 'ctx').astype(jnp.float32)  224 us
    unnamed x22, waiting for transfers between devices  145 us
    all_to_all x1, waiting for transfers between devices, forward_pass(): lax.all_to_all(send, 'ctx', split_axis=0, concat_axis=0, tiled=True)  104 us
    all_to_all x1, waiting for transfers between devices, body(): lax.all_to_all(grad_arrived, 'ctx', split_axis=0, concat_axis=0, tiled=True)  96.1 us
    all_to_all x1, waiting for transfers between devices, body(): lax.all_to_all(send_back, 'ctx', split_axis=0, concat_axis=0, tiled=True)  88.9 us
    all_to_all x1, waiting for transfers between devices, forward_pass(): lax.all_to_all(expert_low, 'ctx', split_axis=0, concat_axis=0, tiled=True)  88.8 us
    reduce_scatter x1, waiting for transfers between devices, body(): lax.psum_scatter(d_value_w.astype(jnp.bfloat16), 'fsdp', scatter_dimensio...  74.5 us
    reduce_scatter x1, waiting for transfers between devices, body(): lax.psum_scatter(d_query_w.astype(jnp.bfloat16), 'fsdp', scatter_dimensio...  74.3 us
  transfers between devices with their start and end apart: 24, of which 20 were waited for; matrix products, arithmetic and copies ran while one was open for 15% of the time, Pallas kernels for 0%

commit v1 on v0

v1 whole, which is shorter than its diff:
```python
import functools

import jax
import jax.numpy as jnp
import numpy as np
from jax import lax
from jax.experimental import pallas as pl
from jax.experimental.pallas import tpu as pltpu
from jax.sharding import PartitionSpec as P

EPSILON = 1e-06
ROPE_BASE = 10000.0
BF = jnp.bfloat16
F32 = jnp.float32


def dot(a, b, contract=((1,), (0,)), precision=None):
    return lax.dot_general(a, b, (contract, ((), ())), precision=precision, preferred_element_type=F32)


def dot_nt(a, b):
    return dot(a, b, ((1,), (1,)))


def dot_tn(a, b):
    return dot(a, b, ((0,), (0,)))


def head_norm(v, gain):
    factor = lax.rsqrt(jnp.mean(v * v, axis=-1, keepdims=True) + EPSILON)
    return v * factor * gain, factor


def turn(v, cosine, sine):
    return v * cosine + pltpu.roll(v, v.shape[-1] // 2, 1) * sine


def head_back(grad, v, gain, cosine, sine):
    grad = turn(grad, cosine, -sine)
    factor = lax.rsqrt(jnp.mean(v * v, axis=-1, keepdims=True) + EPSILON)
    gain_grad = jnp.sum(grad * v * factor, axis=0, keepdims=True)
    inner = grad * gain
    return factor * inner - v * (factor * factor * factor) * jnp.mean(inner * v, axis=-1, keepdims=True), gain_grad


def rows_of(ref):
    block = ref[...]
    return block.reshape(-1, block.shape[-1])


def attend_kernel(q_ref, k_ref, v_ref, qg_ref, kg_ref, cos_ref, sin_ref, o_ref, keys, values_t):
    step = pl.program_id(1)

    @pl.when(step == 0)
    def _():
        normed, _unused = head_norm(rows_of(k_ref).astype(F32), kg_ref[...])
        keys[...] = turn(normed, cos_ref[...], sin_ref[...]).astype(BF)
        values_t[...] = rows_of(v_ref).astype(F32).T.astype(BF)

    queries = rows_of(q_ref).astype(F32)
    number, head_dim = queries.shape
    here = pl.ds(pl.multiple_of(step * number, number), number)
    normed, _unused = head_norm(queries, qg_ref[...])
    queries = turn(normed, cos_ref[here, :], sin_ref[here, :]).astype(BF)
    weights = jnp.exp(dot_nt(keys[...], queries) * (head_dim**-0.5))
    total = jnp.sum(weights, axis=0, keepdims=True)
    mixed = dot(values_t[...], weights.astype(BF)) / total
    o_ref[...] = mixed.T.astype(BF).reshape(o_ref.shape)


def attend_back_kernel(
    q_ref, k_ref, v_ref, m_ref, qg_ref, kg_ref, cos_ref, sin_ref,
    g_ref, gain_ref, keys, keys_t, key_acc, value_acc,
):
    pair = pl.program_id(0)
    step = pl.program_id(1)
    last = pl.num_programs(1) - 1

    @pl.when((pair == 0) & (step == 0))
    def _():
        gain_ref[...] = jnp.zeros_like(gain_ref)

    @pl.when(step == 0)
    def _():
        normed, _unused = head_norm(rows_of(k_ref).astype(F32), kg_ref[...])
        turned = turn(normed, cos_ref[...], sin_ref[...])
        keys[...] = turned.astype(BF)
        keys_t[...] = turned.T.astype(BF)
        key_acc[...] = jnp.zeros_like(key_acc)
        value_acc[...] = jnp.zeros_like(value_acc)

    query_pre = rows_of(q_ref).astype(F32)
    grad_mixed = rows_of(m_ref)
    number, head_dim = query_pre.shape
    scale = head_dim**-0.5
    here = pl.ds(pl.multiple_of(step * number, number), number)
    cosine, sine = cos_ref[here, :], sin_ref[here, :]
    normed, _unused = head_norm(query_pre, qg_ref[...])
    queries = turn(normed, cosine, sine).astype(BF)
    weights = jnp.exp(dot_nt(keys[...], queries) * scale)
    probs = weights * (1.0 / jnp.sum(weights, axis=0, keepdims=True))
    value_acc[...] += dot(probs.astype(BF), grad_mixed)
    weighted = probs * dot_nt(rows_of(v_ref), grad_mixed)
    delta = jnp.sum(weighted, axis=0, keepdims=True)
    grad_scores = (weighted - probs * delta).astype(BF)
    key_acc[...] += dot(grad_scores, queries)
    grad_query = dot(keys_t[...], grad_scores).T * scale
    grad_query, gain_grad = head_back(grad_query, query_pre, qg_ref[...], cosine, sine)
    rows = g_ref.shape[2]
    blocks = number // rows
    g_ref[pl.ds(step * blocks, blocks), 0] = grad_query.astype(BF).reshape(blocks, rows, head_dim)
    gain_ref[0:1, :] += gain_grad

    @pl.when(step == last)
    def _():
        grad_key, gain_grad = head_back(
            key_acc[...] * scale, rows_of(k_ref).astype(F32), kg_ref[...], cos_ref[...], sin_ref[...]
        )
        g_ref[:, 1] = grad_key.astype(BF).reshape(-1, rows, head_dim)
        g_ref[:, 2] = value_acc[...].astype(BF).reshape(-1, rows, head_dim)
        gain_ref[1:2, :] += gain_grad


def attention_specs(shape):
    blocks, pairs, rows, head_dim = shape
    at_once = max(1, 256 // rows)
    while blocks % at_once:
        at_once -= 1
    pairs //= 3
    part = pl.BlockSpec((at_once, 1, rows, head_dim), lambda p, i: (i, p, 0, 0))
    three = [
        pl.BlockSpec((at_once, 1, rows, head_dim), lambda p, i: (i, 3 * p, 0, 0)),
        pl.BlockSpec((blocks, 1, rows, head_dim), lambda p, i: (0, 3 * p + 1, 0, 0)),
        pl.BlockSpec((blocks, 1, rows, head_dim), lambda p, i: (0, 3 * p + 2, 0, 0)),
    ]
    gain = pl.BlockSpec((1, head_dim), lambda p, i: (0, 0))
    table = pl.BlockSpec((blocks * rows, head_dim), lambda p, i: (0, 0))
    params = pltpu.CompilerParams(
        dimension_semantics=("arbitrary", "arbitrary"),
        vmem_limit_bytes=(24 if blocks * rows <= 1024 else 56) * 2**20,
    )
    return part, three, gain, table, (pairs, blocks // at_once), params


def attend(qkv, query_gain, key_gain, cosine, sine):
    part, three, gain, table, grid, params = attention_specs(qkv.shape)
    blocks, _unused, rows, head_dim = qkv.shape
    length = blocks * rows
    work = grid[0] * length * length
    return pl.pallas_call(
        attend_kernel,
        grid=grid,
        in_specs=[*three, gain, gain, table, table],
        out_specs=part,
        out_shape=jax.ShapeDtypeStruct((blocks, grid[0], rows, head_dim), BF),
        scratch_shapes=[pltpu.VMEM((length, head_dim), BF), pltpu.VMEM((head_dim, length), BF)],
        compiler_params=params,
        cost_estimate=pl.CostEstimate(flops=4 * work * head_dim, bytes_accessed=3 * qkv.size, transcendentals=work),
        name="attend",
    )(qkv, qkv, qkv, query_gain, key_gain, cosine, sine)


def attend_back(qkv, grad_mixed, query_gain, key_gain, cosine, sine):
    part, three, gain, table, grid, params = attention_specs(qkv.shape)
    blocks, _unused, rows, head_dim = qkv.shape
    length = blocks * rows
    work = grid[0] * length * length
    return pl.pallas_call(
        attend_back_kernel,
        grid=grid,
        in_specs=[*three, part, gain, gain, table, table],
        out_specs=[
            pl.BlockSpec((blocks, 3, rows, head_dim), lambda p, i: (0, p, 0, 0)),
            pl.BlockSpec((8, head_dim), lambda p, i: (0, 0)),
        ],
        out_shape=[jax.ShapeDtypeStruct(qkv.shape, BF), jax.ShapeDtypeStruct((8, head_dim), F32)],
        scratch_shapes=[
            pltpu.VMEM((length, head_dim), BF),
            pltpu.VMEM((head_dim, length), BF),
            pltpu.VMEM((length, head_dim), F32),
            pltpu.VMEM((length, head_dim), F32),
        ],
        compiler_params=params,
        cost_estimate=pl.CostEstimate(flops=10 * work * head_dim, bytes_accessed=5 * qkv.size, transcendentals=work),
        name="attend_back",
    )(qkv, qkv, qkv, grad_mixed, query_gain, key_gain, cosine, sine)


def swap(v, mask):
    size = lax.axis_size("fsdp")
    return lax.ppermute(v, "fsdp", [(i, i ^ mask) for i in range(size)])


def ring_order(size):
    if size == 8:
        return [0, 2, 4, 6, 7, 5, 3, 1]
    return list(range(size))


def ring_send(v, direction):
    order = ring_order(lax.axis_size("ctx"))
    size = len(order)
    return lax.ppermute(v, "ctx", [(order[i], order[(i + direction) % size]) for i in range(size)])


def ring_gather(v):
    size = lax.axis_size("ctx")
    far, half = size // 2, v.shape[0] // 2
    found = {0: v}
    right, left = v, v
    for step in range(1, far):
        right, left = ring_send(right, 1), ring_send(left, -1)
        found[size - step], found[step] = right, left
    found[far] = jnp.concatenate([ring_send(right[:half], 1), ring_send(left[half:], -1)])
    return found


def ring_scatter(term, watch=None):
    size = lax.axis_size("ctx")
    far = size // 2
    first = term(far)
    half = first.shape[0] // 2
    right, left = ring_send(first[:half].astype(BF), 1), ring_send(first[half:].astype(BF), -1)
    if watch is not None:
        watch += [right, left]
    for offset in range(far - 1, 0, -1):
        ahead, behind = term(offset), term(size - offset)
        if offset == far - 1:
            ahead = jnp.concatenate([ahead[:half] + right.astype(F32), ahead[half:]])
            behind = jnp.concatenate([behind[:half], behind[half:] + left.astype(F32)])
        else:
            ahead, behind = ahead + right.astype(F32), behind + left.astype(F32)
        right, left = ring_send(ahead.astype(BF), 1), ring_send(behind.astype(BF), -1)
    return term(0) + right.astype(F32) + left.astype(F32)


def after(v, *others):
    return lax.optimization_barrier((v, *others))[0]


class Order:
    def __init__(self, first):
        self.last = first

    def __call__(self, *values):
        self.last, *values = lax.optimization_barrier((self.last, *values))
        return values[0] if len(values) == 1 else values


def sum_all(v):
    for axis in ("fsdp", "ctx"):
        size = lax.axis_size(axis)
        mask = 1
        while mask < size:
            v = v + lax.ppermute(v, axis, [(i, i ^ mask) for i in range(size)])
            mask *= 2
    return v


def body(
    tokens, attn_gain, w_query, w_key, w_value, query_gain, key_gain, w_out,
    ffn_gain, w_router, w_gate, w_up, w_down, routes, cotangent,
):
    ctx_size = lax.axis_size("ctx")
    parts = lax.axis_size("fsdp")
    mine = lax.axis_index("fsdp")
    place = lax.axis_index("ctx")
    rows = tokens.shape[1]
    width = tokens.shape[2]
    slab = w_query.shape[0]
    head_dim = query_gain.shape[0]
    own_heads = width // head_dim // parts
    own_experts = w_gate.shape[1]
    hidden_units = w_gate.shape[2]
    experts = own_experts * ctx_size
    seq_length = rows * ctx_size
    order = ring_order(ctx_size)
    ring_place = jnp.asarray(np.argsort(np.array(order)), jnp.int32)[place]
    ring_table = jnp.asarray(order, jnp.int32)

    pairs = own_heads * parts
    per = max(1, pairs // ctx_size)
    repeats = max(1, ctx_size // pairs)

    def to_pairs(v, kinds):
        v = v.reshape(parts, rows, kinds, own_heads, head_dim).transpose(3, 0, 2, 1, 4)
        v = v.reshape(pairs // per, per * kinds, rows, head_dim)
        if repeats > 1:
            v = jnp.repeat(v, repeats, axis=0)
        return lax.all_to_all(v, "ctx", split_axis=0, concat_axis=0, tiled=True)

    def from_pairs(v):
        v = lax.all_to_all(v, "ctx", split_axis=0, concat_axis=0, tiled=True)
        if repeats > 1:
            v = v[::repeats]
        kinds = v.shape[1] // per
        v = v.reshape(own_heads, -1, per, kinds, rows, head_dim).transpose(1, 2, 4, 3, 0, 5)
        return v.reshape(parts * rows, kinds * own_heads * head_dim)

    def block(v, index, size, axis):
        return lax.dynamic_slice_in_dim(v, index * size, size, axis)

    def assemble(pieces, axis):
        size = pieces[0].shape[axis]
        shape = list(pieces[0].shape)
        shape[axis] = size * parts
        whole = jnp.zeros(shape, pieces[0].dtype)
        for mask, piece in enumerate(pieces):
            whole = lax.dynamic_update_slice_in_dim(whole, piece, (mine ^ mask) * size, axis)
        return whole

    def fsdp_gather(v, axis):
        across = swap(v, 2)
        return assemble([v, swap(v, 1), across, swap(across, 1)], axis)

    def fsdp_scatter(term):
        near = swap(term(mine ^ 1).astype(BF), 1)
        far = swap(term(mine ^ 3).astype(BF), 1)
        far = (term(mine ^ 2) + far.astype(F32)).astype(BF)
        return term(mine) + near.astype(F32) + swap(far, 2).astype(F32)

    half = head_dim // 2
    frequency = ROPE_BASE ** (-jnp.arange(half, dtype=F32) * 2.0 / head_dim)
    angles = jnp.arange(seq_length, dtype=jnp.int32).astype(F32)[:, None] * frequency[None, :]
    cosine, sine = jnp.cos(angles), jnp.sin(angles)
    cosine = jnp.concatenate([cosine, cosine], axis=1)
    sine = jnp.concatenate([-sine, sine], axis=1)
    q_gain, k_gain = query_gain[None, :], key_gain[None, :]

    source = tokens[0].astype(F32)
    factor_one = lax.rsqrt(jnp.mean(source * source, axis=-1, keepdims=True) + EPSILON)
    normed = (source * factor_one * attn_gain).astype(BF)
    in_order = Order(jnp.zeros((), F32))
    normed = in_order(normed)
    w_query, w_key, w_value, w_router, w_gate, w_up, w_down, routes = after(
        (w_query, w_key, w_value, w_router, w_gate, w_up, w_down, routes), normed
    )
    normed_all = fsdp_gather(normed, 0)
    normed_slab = block(normed_all, mine, slab, 1)
    own_width = own_heads * head_dim
    projections = [
        jnp.concatenate([block(w, mine ^ mask, own_width, 1) for w in (w_query, w_key, w_value)], axis=1)
        for mask in range(parts)
    ]
    near, far = [swap(dot(normed_slab, projections[mask]).astype(BF), 1) for mask in (1, 3)]
    far = in_order((dot(normed_slab, projections[2]) + far.astype(F32)).astype(BF))
    cot_low = after(cotangent[0], far)
    own = dot(normed_slab, projections[0]) + near.astype(F32)
    qkv = in_order(to_pairs((own + swap(far, 2).astype(F32)).astype(BF), 3))

    gate_w = lax.all_gather(w_gate.reshape(slab, -1), "fsdp", axis=0, tiled=True)
    up_w = lax.all_gather(w_up.reshape(slab, -1), "fsdp", axis=0, tiled=True)
    down_w = lax.all_gather(w_down.reshape(slab, -1), "fsdp", axis=0, tiled=True)
    router_w = fsdp_gather(w_router, 0)
    routes_all = lax.all_to_all(
        jnp.broadcast_to(routes, (ctx_size, *routes.shape[1:])), "ctx", split_axis=0, concat_axis=0, tiled=True
    )
    cot_blocks = ring_gather(cot_low)

    mixed_low = attend(qkv, q_gain, k_gain, cosine, sine)
    mixed = in_order(from_pairs(mixed_low))
    hidden = source + fsdp_scatter(lambda index: dot(block(mixed, index, rows, 0), w_out))
    factor_two = lax.rsqrt(jnp.mean(hidden * hidden, axis=-1, keepdims=True) + EPSILON)
    ffn_in = in_order((hidden * factor_two * ffn_gain).astype(BF))

    expert_ids = jnp.arange(experts, dtype=jnp.int32)

    def gates_of(rows_in, named):
        logits = dot(rows_in, router_w)
        chosen = jnp.any(named[:, :, None] == expert_ids[None, None, :], axis=1)
        high = jnp.max(jnp.where(chosen, logits, -1e30), axis=-1, keepdims=True)
        weights = jnp.where(chosen, jnp.exp(jnp.where(chosen, logits - high, 0.0)), 0.0)
        return weights / jnp.sum(weights, axis=-1, keepdims=True)

    def at_offset(offset):
        return ring_table[(ring_place + offset) % ctx_size]

    columns = lax.broadcasted_iota(jnp.int32, (1, own_experts * hidden_units), 1) // hidden_units

    def spread(per_expert):
        out = per_expert[:, 0:1]
        for index in range(1, own_experts):
            out = jnp.where(columns == index, per_expert[:, index : index + 1], out)
        return out

    def per_expert_sum(v):
        return jnp.stack(
            [jnp.sum(v[:, i * hidden_units : (i + 1) * hidden_units], axis=1) for i in range(own_experts)]
        )

    ffn_blocks = ring_gather(ffn_in)
    offsets = [0] + [o for step in range(1, ctx_size // 2) for o in (step, ctx_size - step)] + [ctx_size // 2]
    cots = jnp.concatenate([cot_blocks[o] for o in offsets])
    cots, down_w = after((cots, down_w), ffn_in)
    grad_act = in_order(dot(cots, down_w))
    inputs = in_order(jnp.concatenate([ffn_blocks[o] for o in offsets]))
    named = jnp.concatenate([routes_all[at_offset(o)] for o in offsets])
    gates = lax.dynamic_slice_in_dim(gates_of(inputs, named), place * own_experts, own_experts, 1)
    wide_gates = spread(gates)
    gate_pre = dot(inputs, gate_w)
    up_pre = dot(inputs, up_w)
    sigmoid = jax.nn.sigmoid(gate_pre)
    silu = gate_pre * sigmoid
    acts = (silu * up_pre).astype(BF).astype(F32)
    d_gates = per_expert_sum(acts * grad_act).reshape(own_experts, ctx_size, rows)
    grad_act = wide_gates * grad_act
    up_grads = (grad_act * silu).astype(BF)
    gate_grads = (grad_act * up_pre * (sigmoid * (1.0 + gate_pre * (1.0 - sigmoid)))).astype(BF)
    acts = (wide_gates * acts).astype(BF)
    grad_rows = dot_nt(gate_grads, gate_w) + dot_nt(up_grads, up_w)
    grad_rows = in_order(grad_rows)

    def term_of(terms):
        return lambda offset: terms[offsets.index(offset) * rows :][:rows]

    watch = []
    grad_ffn_in = ring_scatter(term_of(grad_rows), watch)
    acts = after(acts, *watch)
    weighted = dot_nt(acts, down_w)
    back_index = jnp.asarray(np.argsort(np.array(offsets)), jnp.int32)
    by_place = jnp.asarray(np.argsort(np.array(order)), jnp.int32)
    d_gates = d_gates[:, back_index[(by_place - ring_place) % ctx_size], :].transpose(1, 0, 2)
    d_gates = lax.all_to_all(d_gates, "ctx", split_axis=0, concat_axis=0, tiled=True)
    d_gates = d_gates.reshape(experts, rows).T

    def weight_grad(left, right):
        grad = dot_tn(left, after(right, *watch)).astype(BF)
        return lax.psum_scatter(grad, "fsdp", scatter_dimension=0, tiled=True)

    expert_grads = [weight_grad(cots, acts), weight_grad(inputs, gate_grads), weight_grad(inputs, up_grads)]

    gates = gates_of(ffn_in, routes[0])
    grad_logits = gates * (d_gates - jnp.sum(gates * d_gates, axis=-1, keepdims=True))
    grad_ffn_in = grad_ffn_in + dot(
        grad_logits, router_w.astype(F32), ((1,), (1,)), precision=lax.Precision.HIGHEST
    )
    d_router = dot(grad_logits, ffn_in.astype(F32), ((0,), (0,)), precision=lax.Precision.HIGHEST)
    d_router = block(sum_all(d_router), mine, slab, 1).T
    d_ffn_gain = jnp.sum(grad_ffn_in * hidden * factor_two, axis=0)
    inner = grad_ffn_in * ffn_gain
    grad_hidden = (
        cot_low.astype(F32)
        + factor_two * inner
        - hidden * (factor_two * factor_two * factor_two) * jnp.mean(inner * hidden, axis=-1, keepdims=True)
    )

    output = hidden + ring_scatter(term_of(after(weighted, grad_ffn_in)))
    grad_hidden = in_order(grad_hidden)

    grad_proj = fsdp_gather(grad_hidden.astype(BF), 0)
    grad_mixed = in_order(to_pairs(dot_nt(grad_proj, w_out).astype(BF), 1))
    grads, head_gains = attend_back(qkv, grad_mixed, q_gain, k_gain, cosine, sine)
    if repeats > 1:
        head_gains = jnp.where(place % repeats == 0, head_gains, 0.0)
    grads = in_order(from_pairs(grads))
    across = swap(grads, 2)
    grad_normed = sum(
        dot_nt(piece, projections[mask])
        for mask, piece in enumerate([grads, swap(grads, 1), across, swap(across, 1)])
    ).astype(BF)
    grad_normed = assemble(
        [block(grad_normed, mine, rows, 0)]
        + [swap(block(grad_normed, mine ^ mask, rows, 0), mask) for mask in range(1, parts)],
        1,
    ).astype(F32)
    d_attn_gain = jnp.sum(grad_normed * source * factor_one, axis=0)
    inner = grad_normed * attn_gain
    d_tokens = (
        grad_hidden
        + factor_one * inner
        - source * (factor_one * factor_one * factor_one) * jnp.mean(inner * source, axis=-1, keepdims=True)
    )

    own_rows = slab // ctx_size

    def gather_rows(pieces, count):
        pieces = ring_gather(pieces)
        wholes = [jnp.zeros((slab, width), F32) for _ in range(count)]
        for offset, piece in pieces.items():
            at = ((ring_place + offset) % ctx_size) * own_rows
            for index in range(count):
                part = piece[index * own_rows : (index + 1) * own_rows].astype(F32)
                wholes[index] = lax.dynamic_update_slice_in_dim(wholes[index], part, at, 0)
        return wholes

    grad = dot_tn(mixed, grad_proj)
    d_out = ring_scatter(lambda offset: block(grad, (ring_place + offset) % ctx_size, own_rows, 0))
    (d_out,) = gather_rows(d_out.astype(BF), 1)

    all_grads = dot_tn(normed_all, grads).reshape(parts, ctx_size, own_rows, -1)
    total = ring_scatter(
        lambda offset: block(all_grads, (ring_place + offset) % ctx_size, 1, 1).reshape(parts * own_rows, -1)
    )
    total = total.astype(BF).reshape(parts, own_rows, -1)
    pieces = [block(total, mine ^ mask, 1, 0)[0] for mask in range(parts)]
    pieces = [piece if mask == 0 else swap(piece, mask) for mask, piece in enumerate(pieces)]
    pieces = [
        jnp.concatenate([piece[:, kind * own_width : (kind + 1) * own_width] for kind in range(3)]) for piece in pieces
    ]
    pieces = assemble(pieces, 1)
    d_down, d_gate, d_up = [
        grad.astype(F32).reshape(slab, own_experts, hidden_units) for grad in after(expert_grads, pieces)
    ]
    d_query, d_key, d_value = gather_rows(pieces, 3)
    gains = jnp.concatenate([d_attn_gain, head_gains[0], head_gains[1], d_ffn_gain])
    gains = sum_all(gains.reshape(-1, 128)).reshape(-1)
    return (
        output[None].astype(BF),
        d_tokens[None],
        gains[:width],
        d_query,
        d_key,
        d_value,
        gains[width : width + head_dim],
        gains[width + head_dim : width + 2 * head_dim],
        d_out,
        gains[width + 2 * head_dim :],
        d_router,
        d_gate,
        d_up,
        d_down,
    )


def solution(mesh):
    token_split = P("fsdp", "ctx", None)
    row_split = P("fsdp", None)
    return jax.shard_map(
        body,
        mesh=mesh,
        in_specs=(
            token_split, P(), row_split, row_split, row_split, P(), P(), row_split,
            P(), row_split, token_split, token_split, token_split, token_split, token_split,
        ),
        out_specs=(
            token_split, token_split, P(), row_split, row_split, row_split, P(), P(),
            row_split, P(), row_split, token_split, token_split, token_split,
        ),
        check_vma=False,
    )
```

time: 2010 us -> 892 us (0.44)
  waiting for transfers between devices: 1500 us -> 316 us
  starting transfers between devices: 21.9 us -> 143 us
  blocking collectives: 55.5 us -> 0 us
  matrix products: 211 us -> 172 us
  Pallas kernels: 0 us -> 24.4 us
  between operations: 15.5 us -> 38.3 us
    reduce_scatter x8 -> x3, waiting for transfers between devices: 445 us -> 0.01 us  [weight_grad(): return lax.psum_scatter(grad, 'fsdp', scatter_dimension=0, tiled=True)]
    all_to_all x4 -> x6, waiting for transfers between devices: 377 us -> 3.31 us  [the longest x2 3.3 us: to_pairs(): return lax.all_to_all(v, 'ctx', split_axis=0, concat_axis=0, tiled=True)]
    all_gather x9 -> x3, waiting for transfers between devices: 314 us -> 0.02 us  [the longest x1 0.02 us: body(): lax.all_gather(w_down.reshape(slab, -1), 'fsdp', axis=0, tiled=True)]
    ppermute x0 -> x98, waiting for transfers between devices: none -> 313 us  [the longest x64 201 us: ring_send(): lax.ppermute(v, 'ctx', [(order[i], order[(i + direction) % size]) for i i...]
    psum x1 -> x0, waiting for transfers between devices: 224 us -> none  [body(): lax.psum(shards[0].astype(jnp.bfloat16), 'ctx').astype(jnp.float32)]
    unnamed x22 -> x6, waiting for transfers between devices: 145 us -> 0.1 us
    ppermute x0 -> x98, starting transfers between devices: none -> 114 us  [the longest x64 86.8 us: ring_send(): lax.ppermute(v, 'ctx', [(order[i], order[(i + direction) % size]) for i i...]
    psum x1 -> x0, blocking collectives: 39.7 us -> none  [body(): lax.psum(shards[8][0].astype(jnp.bfloat16), 'ctx').astype(jnp.float32)]
  transfers between devices with their start and end apart: 24 -> 110, of which waited for: 20 -> 46; matrix products, arithmetic and copies ran while one was open for 15% -> 29% of each run, Pallas kernels for 0% -> 3%
where the time goes in v1:
time: 892 us; the launch traced here: 881 us
  waiting for transfers between devices  316 us (35%)
  matrix products  172 us (19%)
  starting transfers between devices  143 us (16%)
  local copies, waits for them, and re-layouts  114 us (13%)
  other arithmetic  72 us (8%)
  between operations  38.3 us (4%)
  Pallas kernels  24.4 us (3%)
    ppermute x64, waiting for transfers between devices, ring_send(): lax.ppermute(v, 'ctx', [(order[i], order[(i + direction) % size]) for i i...  201 us
    dot_general x28, matrix products, dot(): lax.dot_general(a, b, (contract, ((), ())), precision=precision, preferre...  172 us
    ppermute x24, waiting for transfers between devices, swap(): return lax.ppermute(v, 'fsdp', [(i, i ^ mask) for i in range(size)])  104 us
    ppermute x64, starting transfers between devices, ring_send(): lax.ppermute(v, 'ctx', [(order[i], order[(i + direction) % size]) for i i...  86.8 us
    unnamed x149, local copies, waits for them, and re-layouts  35.4 us
    dynamic_update_slice x18, other arithmetic, gather_rows(): wholes[index] = lax.dynamic_update_slice_in_dim(wholes[index], part, at, 0)  20.3 us
    reshape x3, local copies, waits for them, and re-layouts, body(): grad.astype(F32).reshape(slab, own_experts, hidden_units)  19.7 us
  transfers between devices with their start and end apart: 110, of which 46 were waited for; matrix products, arithmetic and copies ran while one was open for 29% of the time, Pallas kernels for 3%

profile of v1, /device:TPU:0, one launch (start us, length us, event | category | flops | bytes accessed | tf_op | source)
XLA Modules:
  0.0 880.8 jit_solution(7363832928379223828)
XLA Ops:
  11.0 3.5 copy.56
  14.5 3.5 copy.54
  21.1 4.4 constant_dynamic-slice_fusion.28
  27.9 11.0 %collective-permute-done.1 = bf16[128,2048]{1,0:T(8,128)(2,1)} collective-permute-done((bf16[128,2048]{1,0:T(8,128)(2,1)S(1)}, bf16[128,2048]{1,0:T(8,128)(2,1)}, u32[]{:S(2)}, u32[]{:S(2)}) %collective-permute-start.1) | collective-permute-done | bytes 524320 | tf_op jit(solution)/shard_map/ppermute | solution.py:191
  58.8 5.9 all-to-all-start.2
  64.7 47.0 %collective-permute-done.5 = bf16[512,1536]{1,0:T(8,128)(2,1)} collective-permute-done((bf16[512,1536]{1,0:T(8,128)(2,1)}, bf16[512,1536]{1,0:T(8,128)(2,1)}, u32[]{:S(2)}, u32[]{:S(2)}) %collective-permute-start.5) | collective-permute-done | bytes 1572896 | tf_op jit(solution)/shard_map/ppermute | solution.py:191
  111.8 5.3 fusion.3
  117.1 3.9 reshape.239
  124.0 5.9 all-to-all-start
  131.5 3.5 copy.55
  167.8 9.2 %attend.1 = bf16[8,2,128,128]{3,2,1,0:T(8,128)(2,1)S(1)} custom-call(bf16[8,6,128,128]{3,2,1,0:T(8,128)(2,1)} %all-to-all-done.q_ref.k_ref.v_ref, bf16[8,6,128,128]{3,2,1,0:T(8,128)(2,1)} %all-to-all-done.q_ref.k_ref.v_ref, bf16[8,6,128,128]{3,2,1,0:T(8,128)(2,1)} %all-to-all-done.q_ref.k_ref.v_ref, f32[1,128]{1,0:T(1,128)S(1)} %bitcast.195, ...), custom_call_target="tpu_custom_call" | custom-call | flops 1073741824 | bytes 2359296 | tf_op jit(solution)/shard_map/attend/pallas_call | solution.py:150
  177.8 4.2 all-to-all-start.1
  189.9 13.4 %collective-permute-done.22 = bf16[128,2048]{1,0:T(8,128)(2,1)} collective-permute-done((bf16[128,2048]{1,0:T(8,128)(2,1)}, bf16[128,2048]{1,0:T(8,128)(2,1)}, u32[]{:S(2)}, u32[]{:S(2)}) %collective-permute-start.22) | collective-permute-done | bytes 524320 | tf_op jit(solution)/shard_map/ppermute | solution.py:203
  203.3 4.3 collective-permute-start.25
  223.6 6.5 collective-permute-done.8
  237.9 7.1 collective-permute-done.9
  247.8 9.9 %collective-permute-done.11 = bf16[128,2048]{1,0:T(8,128)(2,1)S(1)} collective-permute-done((bf16[128,2048]{1,0:T(8,128)(2,1)S(1)}, bf16[128,2048]{1,0:T(8,128)(2,1)S(1)}, u32[]{:S(2)}, u32[]{:S(2)}) %collective-permute-start.11) | collective-permute-done | bytes 524320 | tf_op jit(solution)/shard_map/ppermute | solution.py:203
  259.9 11.3 %collective-permute-done.14 = bf16[128,2048]{1,0:T(8,128)(2,1)S(1)} collective-permute-done((bf16[128,2048]{1,0:T(8,128)(2,1)S(1)}, bf16[128,2048]{1,0:T(8,128)(2,1)S(1)}, u32[]{:S(2)}, u32[]{:S(2)}) %collective-permute-start.14) | collective-permute-done | bytes 524320 | tf_op jit(solution)/shard_map/ppermute | solution.py:203
  273.5 4.2 collective-permute-done.15
  281.6 14.8 %fusion.101 = f32[1024,2048]{1,0:T(8,128)} fusion(bf16[1024,2048]{1,0:T(8,128)(2,1)} %constant_dynamic-update-slice_fusion.17, bf16[2048,2048]{1,0:T(8,128)(2,1)} %all-gather.8.cloned.1.call-done), kind=kOutput, calls=%fused_computation.338 | convolution fusion | flops 8589934592 | bytes 20971520 | tf_op jit(solution)/shard_map/dot_general | solution.py:18
  296.5 14.4 %fusion.100 = f32[1024,2048]{1,0:T(8,128)} fusion(bf16[1024,2048]{1,0:T(8,128)(2,1)} %copy-done.17, bf16[2048,2048]{1,0:T(8,128)(2,1)} %all-gather.4.cloned.1.call-done), kind=kOutput, calls=%fused_computation.337 | convolution fusion | flops 8589934592 | bytes 20971520 | tf_op jit(solution)/shard_map/dot_general | solution.py:18
  310.9 24.1 %convert_multiply_fusion = (f32[1024,2048]{1,0:T(8,128)}, bf16[1024,2048]{1,0:T(8,128)(2,1)}, bf16[1024,2048]{1,0:T(8,128)(2,1)}, bf16[1024,2048]{1,0:T(8,128)(2,1)}) fusion(f32[1024,2048]{1,0:T(8,128)} %fusion.101, f32[1024,2048]{1,0:T(8,128)} %fusion.100, f32[1024]{0:T(1024)S(1)} %bitcast.234, f32[1024]{0:T(1024)S(1)} %bitcast.232, ...), kind=kOutput, calls=%fused_computation.4 | convolution fusion | flops 8629780480 | bytes 50341888 | tf_op jit(solution)/shard_map/dot_general | solution.py:18
  335.0 14.8 %fusion.102 = f32[1024,2048]{1,0:T(8,128)} fusion(bf16[1024,2048]{1,0:T(8,128)(2,1)} %get-tuple-element.53, bf16[2048,2048]{1,0:T(8,128)(2,1)} %all-gather.4.cloned.1.call-done), kind=kOutput, calls=%fused_computation.339 | convolution fusion | flops 8589934592 | bytes 20971520 | tf_op jit(solution)/shard_map/dot_general | solution.py:18
  349.8 12.8 %convolution_add_fusion = f32[1024,2048]{1,0:T(8,128)S(1)} fusion(f32[1024,2048]{1,0:T(8,128)} %fusion.102, bf16[1024,2048]{1,0:T(8,128)(2,1)S(1)} %copy-done.60, bf16[2048,2048]{1,0:T(8,128)(2,1)} %all-gather.6.cloned.1.call-done), kind=kOutput, calls=%fused_computation.16 | convolution fusion | flops 8592031744 | bytes 29360128 | tf_op jit(solution)/shard_map/dot_general | solution.py:18
  363.3 3.6 copy-done.6
  369.6 4.5 collective-permute-done.28
  375.7 13.7 %convolution_convert_fusion = bf16[2048,2048]{1,0:T(8,128)(2,1)} fusion(bf16[1024,2048]{1,0:T(8,128)(2,1)S(1)} %copy-done.18, bf16[1024,2048]{1,0:T(8,128)(2,1)} %get-tuple-element.54), kind=kOutput, calls=%fused_computation.11 | convolution fusion | flops 8594128896 | bytes 16777216 | tf_op jit(solution)/shard_map/dot_general | solution.py:18
  397.5 5.8 slice_reduce_fusion.1
  404.5 3.7 all-to-all-start.3
  414.5 14.1 %convolution_convert_fusion.1 = bf16[2048,2048]{1,0:T(8,128)(2,1)} fusion(bf16[1024,2048]{1,0:T(8,128)(2,1)} %copy-done.17, bf16[1024,2048]{1,0:T(8,128)(2,1)} %get-tuple-element.53), kind=kOutput, calls=%fused_computation.12 | convolution fusion | flops 8594128896 | bytes 16777216 | tf_op jit(solution)/shard_map/dot_general | solution.py:18
  433.9 5.3 fusion
  439.3 7.4 collective-permute-done.34
  450.2 12.6 %fusion.103 = f32[1024,2048]{1,0:T(8,128)S(1)} fusion(bf16[1024,2048]{1,0:T(8,128)(2,1)} %fusion, bf16[2048,2048]{1,0:T(8,128)(2,1)} %all-gather.8.cloned.1.call-done), kind=kOutput, calls=%fused_computation.340 | convolution fusion | flops 8589934592 | bytes 20971520 | tf_op jit(solution)/shard_map/dot_general | solution.py:18
  468.0 5.5 collective-permute-done.36
  476.7 8.7 collective-permute-done.37
  487.4 7.9 collective-permute-done.38
  497.7 7.2 collective-permute-done.42
  507.0 7.2 collective-permute-done.43
  520.2 19.2 %collective-permute-done.45 = bf16[128,2048]{1,0:T(8,128)(2,1)} collective-permute-done((bf16[128,2048]{1,0:T(8,128)(2,1)}, bf16[128,2048]{1,0:T(8,128)(2,1)}, u32[]{:S(2)}, u32[]{:S(2)}) %collective-permute-start.45) | collective-permute-done | bytes 524320 | tf_op jit(solution)/shard_map/ppermute | solution.py:191
  551.1 3.7 collective-permute-done.77
  561.9 3.4 collective-permute-done.78
  569.1 5.6 collective-permute-done.96
  583.2 3.7 convolution_convert_fusion.7
  590.8 4.2 all-to-all-start.4
  599.0 14.0 %convolution_convert_fusion.2 = bf16[2048,2048]{1,0:T(8,128)(2,1)} fusion(bf16[1024,2048]{1,0:T(8,128)(2,1)} %constant_dynamic-update-slice_fusion.17, bf16[1024,2048]{1,0:T(8,128)(2,1)} %fusion), kind=kOutput, calls=%fused_computation.13 | convolution fusion | flops 8594128896 | bytes 16777216 | tf_op jit(solution)/shard_map/dot_general | solution.py:18
  620.6 15.2 %attend_back.1 = (bf16[8,6,128,128]{3,2,1,0:T(8,128)(2,1)S(1)}, f32[8,128]{1,0:T(8,128)S(1)}) custom-call(bf16[8,6,128,128]{3,2,1,0:T(8,128)(2,1)} %all-to-all-done.q_ref.k_ref.v_ref, bf16[8,6,128,128]{3,2,1,0:T(8,128)(2,1)} %all-to-all-done.q_ref.k_ref.v_ref, bf16[8,6,128,128]{3,2,1,0:T(8,128)(2,1)} %all-to-all-done.q_ref.k_ref.v_ref, ...), custom_call_target="tpu_custom_call" | custom-call | flops 2684354560 | bytes 3932160 | tf_op jit(solution)/shard_map/attend_back/pallas_call | solution.py:168
  637.0 4.6 all-to-all-start.5
  646.4 22.8 %collective-permute-done.87 = bf16[64,2048]{1,0:T(8,128)(2,1)S(1)} collective-permute-done((bf16[64,2048]{1,0:T(8,128)(2,1)}, bf16[64,2048]{1,0:T(8,128)(2,1)S(1)}, u32[]{:S(2)}, u32[]{:S(2)}) %collective-permute-start.87) | collective-permute-done | bytes 262176 | tf_op jit(solution)/shard_map/ppermute | solution.py:203
  669.2 9.6 %collective-permute-start.89 = (bf16[64,2048]{1,0:T(8,128)(2,1)S(1)}, bf16[64,2048]{1,0:T(8,128)(2,1)S(1)}, u32[]{:S(2)}, u32[]{:S(2)}) collective-permute-start(bf16[64,2048]{1,0:T(8,128)(2,1)S(1)} %collective-permute-done.87), channel_id=1, source_target_pairs={{0,8},{8,16},{16,24},{24,28},{28,20},{20,12},{12,4},{4,0},{1,9},{9... | collective-permute-start | bytes 786440 | tf_op jit(solution)/shard_map/ppermute | solution.py:203
  689.2 3.8 copy.59
  693.0 3.8 reshape.250
  696.8 5.5 fusion.104
  704.9 7.4 collective-permute-done.58
  716.0 12.2 %collective-permute-done.59 = bf16[256,1536]{1,0:T(8,128)(2,1)} collective-permute-done((bf16[256,1536]{1,0:T(8,128)(2,1)S(1)}, bf16[256,1536]{1,0:T(8,128)(2,1)}, u32[]{:S(2)}, u32[]{:S(2)}) %collective-permute-start.59) | collective-permute-done | bytes 786464 | tf_op jit(solution)/shard_map/ppermute | solution.py:203
  736.1 12.2 %collective-permute-done.60 = bf16[256,1536]{1,0:T(8,128)(2,1)S(1)} collective-permute-done((bf16[256,1536]{1,0:T(8,128)(2,1)S(1)}, bf16[256,1536]{1,0:T(8,128)(2,1)S(1)}, u32[]{:S(2)}, u32[]{:S(2)}) %collective-permute-start.60) | collective-permute-done | bytes 786464 | tf_op jit(solution)/shard_map/ppermute | solution.py:203
  752.4 5.3 collective-permute-done.48
  765.8 5.7 collective-permute-done.67
  771.5 3.4 collective-permute-done.68
  811.9 13.3 %collective-permute-done.71 = bf16[192,2048]{1,0:T(8,128)(2,1)S(1)} collective-permute-done((bf16[192,2048]{1,0:T(8,128)(2,1)S(1)}, bf16[192,2048]{1,0:T(8,128)(2,1)S(1)}, u32[]{:S(2)}, u32[]{:S(2)}) %collective-permute-start.71) | collective-permute-done | bytes 786464 | tf_op jit(solution)/shard_map/ppermute | solution.py:203
  829.6 13.2 %collective-permute-done.73 = bf16[192,2048]{1,0:T(8,128)(2,1)S(1)} collective-permute-done((bf16[192,2048]{1,0:T(8,128)(2,1)S(1)}, bf16[192,2048]{1,0:T(8,128)(2,1)S(1)}, u32[]{:S(2)}, u32[]{:S(2)}) %collective-permute-start.73) | collective-permute-done | bytes 786464 | tf_op jit(solution)/shard_map/ppermute | solution.py:203
  847.4 3.3 collective-permute-done.75
  853.8 6.6 reshape.267
  860.4 6.6 reshape.269
  866.9 6.6 reshape.271
  (504 shorter events, 275.7 us)
Async XLA Ops:
  7.2 274.4 %all-gather.8.cloned.1.call-start = ((), (), s32[]{:S(2)}) async-start(), calls=%async_computation.11 | async-start | bytes 10485760 | tf_op jit(solution)/shard_map/all_gather | solution.py:353
  14.5 282.0 %all-gather.4.cloned.1.call-start = ((), (), s32[]{:S(2)}) async-start(), calls=%async_computation.9 | async-start | bytes 10485760 | tf_op jit(solution)/shard_map/all_gather | solution.py:351
  18.1 20.7 %collective-permute-start.1 = (bf16[128,2048]{1,0:T(8,128)(2,1)S(1)}, bf16[128,2048]{1,0:T(8,128)(2,1)}, u32[]{:S(2)}, u32[]{:S(2)}) collective-permute-start(bf16[128,2048]{1,0:T(8,128)(2,1)S(1)} %fusion.18), channel_id=1, source_target_pairs={{0,2},{1,3},{2,0},{3,1},{4,6},{5,7},{6,4},{7,5},{8,10},{9,11},{10,... | collective-permute-start | bytes 1572872 | tf_op jit(solution)/shard_map/ppermute | solution.py:191
  21.1 19.1 %collective-permute-start = (bf16[128,2048]{1,0:T(8,128)(2,1)S(1)}, bf16[128,2048]{1,0:T(8,128)(2,1)}, u32[]{:S(2)}, u32[]{:S(2)}) collective-permute-start(bf16[128,2048]{1,0:T(8,128)(2,1)S(1)} %fusion.18), channel_id=1, source_target_pairs={{0,1},{1,0},{2,3},{3,2},{4,5},{5,4},{6,7},{7,6},{8,9},{9,8},{10,11... | collective-permute-start | bytes 1572872 | tf_op jit(solution)/shard_map/ppermute | solution.py:191
  55.6 56.1 %collective-permute-start.5 = (bf16[512,1536]{1,0:T(8,128)(2,1)}, bf16[512,1536]{1,0:T(8,128)(2,1)}, u32[]{:S(2)}, u32[]{:S(2)}) collective-permute-start(bf16[512,1536]{1,0:T(8,128)(2,1)} %fusion.4), channel_id=1, source_target_pairs={{0,2},{1,3},{2,0},{3,1},{4,6},{5,7},{6,4},{7,5},{8,10},{9,11},{10,... | collective-permute-start | bytes 4718600 | tf_op jit(solution)/shard_map/ppermute | solution.py:191
  58.8 65.2 %all-to-all-start.2 = ((s32[8,128,8]{1,2,0:T(8,128)}), s32[8,128,8]{1,2,0:T(8,128)S(1)}, u32[]{:S(2)}, u32[]{:S(2)}) async-start(s32[8,128,8]{1,2,0:T(8,128)} %broadcast_in_dim.96), calls=%async_computation.2 | async-start | bytes 65536 | tf_op jit(solution)/shard_map/all_to_all | solution.py:355
  124.0 43.9 %all-to-all-start = ((bf16[8,6,128,128]{3,2,1,0:T(8,128)(2,1)}), bf16[8,6,128,128]{3,2,1,0:T(8,128)(2,1)}, u32[]{:S(2)}, u32[]{:S(2)}) async-start(bf16[8,6,128,128]{3,2,1,0:T(8,128)(2,1)} %bitcast.206), calls=%async_computation | async-start | bytes 3145728 | tf_op jit(solution)/shard_map/all_to_all | solution.py:290
  129.9 181.0 %all-gather.6.cloned.1.call-start = ((), (), s32[]{:S(2)}) async-start(), calls=%async_computation.10 | async-start | bytes 10485760 | tf_op jit(solution)/shard_map/all_gather | solution.py:352
  129.9 31.2 %collective-permute-start.17 = (bf16[512,16]{0,1:T(8,128)(2,1)S(1)}, bf16[512,16]{0,1:T(8,128)(2,1)S(1)}, u32[]{:S(2)}, u32[]{:S(2)}) collective-permute-start(bf16[512,16]{0,1:T(8,128)(2,1)S(1)} %copy-done.52), channel_id=1, source_target_pairs={{0,1},{1,0},{2,3},{3,2},{4,5},{5,4},{6,7},{7,6},{8,9},{9,8},{10,11... | collective-permute-start | bytes 49160 | tf_op jit(solution)/shard_map/ppermute | solution.py:191
  130.0 30.9 %collective-permute-start.18 = (bf16[512,16]{0,1:T(8,128)(2,1)S(1)}, bf16[512,16]{0,1:T(8,128)(2,1)S(1)}, u32[]{:S(2)}, u32[]{:S(2)}) collective-permute-start(bf16[512,16]{0,1:T(8,128)(2,1)S(1)} %copy-done.52), channel_id=1, source_target_pairs={{0,2},{1,3},{2,0},{3,1},{4,6},{5,7},{6,4},{7,5},{8,10},{9,11},{10,... | collective-permute-start | bytes 49160 | tf_op jit(solution)/shard_map/ppermute | solution.py:191
  162.2 19.9 %collective-permute-start.20 = (bf16[128,2048]{1,0:T(8,128)(2,1)}, bf16[128,2048]{1,0:T(8,128)(2,1)}, u32[]{:S(2)}, u32[]{:S(2)}) collective-permute-start(bf16[128,2048]{1,0:T(8,128)(2,1)} %bitcast.219), channel_id=1, source_target_pairs={{0,4},{8,0},{16,8},{24,16},{28,24},{20,28},{12,20},{4,12},{1,5},{9... | collective-permute-start | bytes 1572872 | tf_op jit(solution)/shard_map/ppermute | solution.py:203
  164.3 19.8 %collective-permute-start.21 = (bf16[128,2048]{1,0:T(8,128)(2,1)}, bf16[128,2048]{1,0:T(8,128)(2,1)}, u32[]{:S(2)}, u32[]{:S(2)}) collective-permute-start(bf16[128,2048]{1,0:T(8,128)(2,1)} %bitcast.220), channel_id=1, source_target_pairs={{0,8},{8,16},{16,24},{24,28},{28,20},{20,12},{12,4},{4,0},{1,9},{9... | collective-permute-start | bytes 1572872 | tf_op jit(solution)/shard_map/ppermute | solution.py:203
  177.8 29.8 %all-to-all-start.1 = ((bf16[8,2,128,128]{3,2,1,0:T(8,128)(2,1)}), bf16[8,2,128,128]{3,2,1,0:T(8,128)(2,1)}, u32[]{:S(2)}, u32[]{:S(2)}) async-start(bf16[8,2,128,128]{3,2,1,0:T(8,128)(2,1)} %copy-done.1), calls=%async_computation.1 | async-start | bytes 1048576 | tf_op jit(solution)/shard_map/all_to_all | solution.py:293
  182.0 671.8 %reduce-scatter.8.cloned.1.call-start = ((), (), s32[]{:S(2)}) async-start(), calls=%async_computation.14 | async-start | bytes 10485760 | tf_op jit(solution)/shard_map/reduce_scatter | solution.py:428
  182.1 21.1 %collective-permute-start.22 = (bf16[128,2048]{1,0:T(8,128)(2,1)}, bf16[128,2048]{1,0:T(8,128)(2,1)}, u32[]{:S(2)}, u32[]{:S(2)}) collective-permute-start(bf16[128,2048]{1,0:T(8,128)(2,1)} %collective-permute-done.20), channel_id=1, source_target_pairs={{0,4},{8,0},{16,8},{24,16},{28,24},{20,28},{12,20},{4,12},{1,5},{9... | collective-permute-start | bytes 1572872 | tf_op jit(solution)/shard_map/ppermute | solution.py:203
  184.0 19.3 %collective-permute-start.23 = (bf16[128,2048]{1,0:T(8,128)(2,1)}, bf16[128,2048]{1,0:T(8,128)(2,1)}, u32[]{:S(2)}, u32[]{:S(2)}) collective-permute-start(bf16[128,2048]{1,0:T(8,128)(2,1)} %collective-permute-done.21), channel_id=1, source_target_pairs={{0,8},{8,16},{16,24},{24,28},{28,20},{20,12},{12,4},{4,0},{1,9},{9... | collective-permute-start | bytes 1572872 | tf_op jit(solution)/shard_map/ppermute | solution.py:203
  203.3 17.8 %collective-permute-start.24 = (bf16[128,2048]{1,0:T(8,128)(2,1)}, bf16[128,2048]{1,0:T(8,128)(2,1)}, u32[]{:S(2)}, u32[]{:S(2)}) collective-permute-start(bf16[128,2048]{1,0:T(8,128)(2,1)} %collective-permute-done.22), channel_id=1, source_target_pairs={{0,4},{8,0},{16,8},{24,16},{28,24},{20,28},{12,20},{4,12},{1,5},{9... | collective-permute-start | bytes 1572872 | tf_op jit(solution)/shard_map/ppermute | solution.py:203
  203.3 15.4 %collective-permute-start.25 = (bf16[128,2048]{1,0:T(8,128)(2,1)}, bf16[128,2048]{1,0:T(8,128)(2,1)}, u32[]{:S(2)}, u32[]{:S(2)}) collective-permute-start(bf16[128,2048]{1,0:T(8,128)(2,1)} %collective-permute-done.23), channel_id=1, source_target_pairs={{0,8},{8,16},{16,24},{24,28},{28,20},{20,12},{12,4},{4,0},{1,9},{9... | collective-permute-start | bytes 1572872 | tf_op jit(solution)/shard_map/ppermute | solution.py:203
  213.1 17.1 %collective-permute-start.8 = (bf16[128,2048]{1,0:T(8,128)(2,1)S(1)}, bf16[128,2048]{1,0:T(8,128)(2,1)S(1)}, u32[]{:S(2)}, u32[]{:S(2)}) collective-permute-start(bf16[128,2048]{1,0:T(8,128)(2,1)S(1)} %add_convert_fusion.5), channel_id=1, source_target_pairs={{0,2},{1,3},{2,0},{3,1},{4,6},{5,7},{6,4},{7,5},{8,10},{9,11},{10,... | collective-permute-start | bytes 1572872 | tf_op jit(solution)/shard_map/ppermute | solution.py:191
  219.6 17.5 %collective-permute-start.26 = (bf16[64,2048]{1,0:T(8,128)(2,1)S(1)}, bf16[64,2048]{1,0:T(8,128)(2,1)S(1)}, u32[]{:S(2)}, u32[]{:S(2)}) collective-permute-start(bf16[64,2048]{1,0:T(8,128)(2,1)S(1)} %slice.452), channel_id=1, source_target_pairs={{0,8},{8,16},{16,24},{24,28},{28,20},{20,12},{12,4},{4,0},{1,9},{9... | collective-permute-start | bytes 786440 | tf_op jit(solution)/shard_map/ppermute | solution.py:203
  222.1 24.9 %collective-permute-start.27 = (bf16[64,2048]{1,0:T(8,128)(2,1)S(1)}, bf16[64,2048]{1,0:T(8,128)(2,1)S(1)}, u32[]{:S(2)}, u32[]{:S(2)}) collective-permute-start(bf16[64,2048]{1,0:T(8,128)(2,1)S(1)} %slice.453), channel_id=1, source_target_pairs={{0,4},{8,0},{16,8},{24,16},{28,24},{20,28},{12,20},{4,12},{1,5},{9... | collective-permute-start | bytes 786440 | tf_op jit(solution)/shard_map/ppermute | solution.py:203
  231.3 13.7 %collective-permute-start.9 = (bf16[128,2048]{1,0:T(8,128)(2,1)S(1)}, bf16[128,2048]{1,0:T(8,128)(2,1)S(1)}, u32[]{:S(2)}, u32[]{:S(2)}) collective-permute-start(bf16[128,2048]{1,0:T(8,128)(2,1)S(1)} %multiply_convert_fusion.3), channel_id=1, source_target_pairs={{0,4},{8,0},{16,8},{24,16},{28,24},{20,28},{12,20},{4,12},{1,5},{9... | collective-permute-start | bytes 1572872 | tf_op jit(solution)/shard_map/ppermute | solution.py:203
  232.8 13.6 %collective-permute-start.10 = (bf16[128,2048]{1,0:T(8,128)(2,1)S(1)}, bf16[128,2048]{1,0:T(8,128)(2,1)S(1)}, u32[]{:S(2)}, u32[]{:S(2)}) collective-permute-start(bf16[128,2048]{1,0:T(8,128)(2,1)S(1)} %multiply_convert_fusion.3), channel_id=1, source_target_pairs={{0,8},{8,16},{16,24},{24,28},{28,20},{20,12},{12,4},{4,0},{1,9},{9... | collective-permute-start | bytes 1572872 | tf_op jit(solution)/shard_map/ppermute | solution.py:203
  257.7 14.1 %collective-permute-start.13 = (bf16[128,2048]{1,0:T(8,128)(2,1)S(1)}, bf16[128,2048]{1,0:T(8,128)(2,1)S(1)}, u32[]{:S(2)}, u32[]{:S(2)}) collective-permute-start(bf16[128,2048]{1,0:T(8,128)(2,1)S(1)} %collective-permute-done.11), channel_id=1, source_target_pairs={{0,4},{8,0},{16,8},{24,16},{28,24},{20,28},{12,20},{4,12},{1,5},{9... | collective-permute-start | bytes 1572872 | tf_op jit(solution)/shard_map/ppermute | solution.py:203
  396.1 16.0 %collective-permute-start.30 = (bf16[128,2048]{1,0:T(8,128)(2,1)}, bf16[128,2048]{1,0:T(8,128)(2,1)}, u32[]{:S(2)}, u32[]{:S(2)}) collective-permute-start(bf16[128,2048]{1,0:T(8,128)(2,1)} %pad_maximum_fusion.16), channel_id=1, source_target_pairs={{0,8},{8,16},{16,24},{24,28},{28,20},{20,12},{12,4},{4,0},{1,9},{9... | collective-permute-start | bytes 1572872 | tf_op jit(solution)/shard_map/ppermute | solution.py:203
  404.5 34.7 %all-to-all-start.3 = ((f32[8,2,128]{2,1,0:T(2,128)}), f32[8,2,128]{2,1,0:T(2,128)S(1)}, u32[]{:S(2)}, u32[]{:S(2)}) async-start(f32[8,2,128]{2,1,0:T(2,128)} %gather_fusion.1), calls=%async_computation.3 | async-start | bytes 16384 | tf_op jit(solution)/shard_map/all_to_all | solution.py:423
  408.2 445.6 %reduce-scatter.6.cloned.1.call-start = ((), (), s32[]{:S(2)}) async-start(), calls=%async_computation.13 | async-start | bytes 10485760 | tf_op jit(solution)/shard_map/reduce_scatter | solution.py:428
  410.1 18.5 %collective-permute-start.33 = (bf16[128,2048]{1,0:T(8,128)(2,1)}, bf16[128,2048]{1,0:T(8,128)(2,1)}, u32[]{:S(2)}, u32[]{:S(2)}) collective-permute-start(bf16[128,2048]{1,0:T(8,128)(2,1)} %pad_maximum_fusion.17), channel_id=1, source_target_pairs={{0,4},{8,0},{16,8},{24,16},{28,24},{20,28},{12,20},{4,12},{1,5},{9... | collective-permute-start | bytes 1572872 | tf_op jit(solution)/shard_map/ppermute | solution.py:203
  414.5 14.1 %collective-permute-start.31 = (bf16[128,2048]{1,0:T(8,128)(2,1)}, bf16[128,2048]{1,0:T(8,128)(2,1)}, u32[]{:S(2)}, u32[]{:S(2)}) collective-permute-start(bf16[128,2048]{1,0:T(8,128)(2,1)} %fusion.25), channel_id=1, source_target_pairs={{0,8},{8,16},{16,24},{24,28},{28,20},{20,12},{12,4},{4,0},{1,9},{9... | collective-permute-start | bytes 1572872 | tf_op jit(solution)/shard_map/ppermute | solution.py:203
  431.8 14.9 %collective-permute-start.34 = (bf16[128,2048]{1,0:T(8,128)(2,1)}, bf16[128,2048]{1,0:T(8,128)(2,1)}, u32[]{:S(2)}, u32[]{:S(2)}) collective-permute-start(bf16[128,2048]{1,0:T(8,128)(2,1)} %get-tuple-element.90), channel_id=1, source_target_pairs={{0,4},{8,0},{16,8},{24,16},{28,24},{20,28},{12,20},{4,12},{1,5},{9... | collective-permute-start | bytes 1572872 | tf_op jit(solution)/shard_map/ppermute | solution.py:203
  439.2 23.6 %collective-permute-start.32 = (bf16[128,2048]{1,0:T(8,128)(2,1)}, bf16[128,2048]{1,0:T(8,128)(2,1)S(1)}, u32[]{:S(2)}, u32[]{:S(2)}) collective-permute-start(bf16[128,2048]{1,0:T(8,128)(2,1)} %get-tuple-element.89), channel_id=1, source_target_pairs={{0,8},{8,16},{16,24},{24,28},{28,20},{20,12},{12,4},{4,0},{1,9},{9... | collective-permute-start | bytes 1572872 | tf_op jit(solution)/shard_map/ppermute | solution.py:203
  448.2 14.6 %collective-permute-start.35 = (bf16[128,2048]{1,0:T(8,128)(2,1)S(1)}, bf16[128,2048]{1,0:T(8,128)(2,1)S(1)}, u32[]{:S(2)}, u32[]{:S(2)}) collective-permute-start(bf16[128,2048]{1,0:T(8,128)(2,1)S(1)} %fusion.24), channel_id=1, source_target_pairs={{0,4},{8,0},{16,8},{24,16},{28,24},{20,28},{12,20},{4,12},{1,5},{9... | collective-permute-start | bytes 1572872 | tf_op jit(solution)/shard_map/ppermute | solution.py:203
  518.6 20.8 %collective-permute-start.45 = (bf16[128,2048]{1,0:T(8,128)(2,1)}, bf16[128,2048]{1,0:T(8,128)(2,1)}, u32[]{:S(2)}, u32[]{:S(2)}) collective-permute-start(bf16[128,2048]{1,0:T(8,128)(2,1)} %get-tuple-element.67), channel_id=1, source_target_pairs={{0,2},{1,3},{2,0},{3,1},{4,6},{5,7},{6,4},{7,5},{8,10},{9,11},{10,... | collective-permute-start | bytes 1572872 | tf_op jit(solution)/shard_map/ppermute | solution.py:191
  519.3 20.8 %collective-permute-start.44 = (bf16[128,2048]{1,0:T(8,128)(2,1)}, bf16[128,2048]{1,0:T(8,128)(2,1)}, u32[]{:S(2)}, u32[]{:S(2)}) collective-permute-start(bf16[128,2048]{1,0:T(8,128)(2,1)} %get-tuple-element.67), channel_id=1, source_target_pairs={{0,1},{1,0},{2,3},{3,2},{4,5},{5,4},{6,7},{7,6},{8,9},{9,8},{10,11... | collective-permute-start | bytes 1572872 | tf_op jit(solution)/shard_map/ppermute | solution.py:191
  519.6 19.8 %collective-permute-start.93 = (f32[16,2048]{1,0:T(8,128)S(1)}, f32[16,2048]{1,0:T(8,128)S(1)}, u32[]{:S(2)}, u32[]{:S(2)}) collective-permute-start(f32[16,2048]{1,0:T(8,128)S(1)} %fusion.75), channel_id=1, source_target_pairs={{0,1},{1,0},{2,3},{3,2},{4,5},{5,4},{6,7},{7,6},{8,9},{9,8},{10,11... | collective-permute-start | bytes 393224 | tf_op jit(solution)/shard_map/ppermute | solution.py:255
  539.4 18.7 %collective-permute-start.94 = (f32[16,2048]{1,0:T(8,128)S(1)}, f32[16,2048]{1,0:T(8,128)}, u32[]{:S(2)}, u32[]{:S(2)}) collective-permute-start(f32[16,2048]{1,0:T(8,128)S(1)} %add.636), channel_id=1, source_target_pairs={{0,2},{1,3},{2,0},{3,1},{4,6},{5,7},{6,4},{7,5},{8,10},{9,11},{10,... | collective-permute-start | bytes 393224 | tf_op jit(solution)/shard_map/ppermute | solution.py:255
  559.9 18.3 %collective-permute-start.82 = (bf16[64,2048]{1,0:T(8,128)(2,1)}, bf16[64,2048]{1,0:T(8,128)(2,1)}, u32[]{:S(2)}, u32[]{:S(2)}) collective-permute-start(bf16[64,2048]{1,0:T(8,128)(2,1)} %pad_maximum_fusion.22), channel_id=1, source_target_pairs={{0,4},{8,0},{16,8},{24,16},{28,24},{20,28},{12,20},{4,12},{1,5},{9... | collective-permute-start | bytes 786440 | tf_op jit(solution)/shard_map/ppermute | solution.py:203
  576.2 36.7 %collective-permute-start.97 = (f32[16,2048]{1,0:T(8,128)}, f32[16,2048]{1,0:T(8,128)}, u32[]{:S(2)}, u32[]{:S(2)}) collective-permute-start(f32[16,2048]{1,0:T(8,128)} %add.639), channel_id=1, source_target_pairs={{0,16},{4,20},{8,24},{12,28},{16,0},{20,4},{24,8},{28,12},{1,17},{... | collective-permute-start | bytes 393224 | tf_op jit(solution)/shard_map/ppermute | solution.py:255
  580.4 16.4 %collective-permute-start.83 = (bf16[64,2048]{1,0:T(8,128)(2,1)}, bf16[64,2048]{1,0:T(8,128)(2,1)}, u32[]{:S(2)}, u32[]{:S(2)}) collective-permute-start(bf16[64,2048]{1,0:T(8,128)(2,1)} %get-tuple-element.94), channel_id=1, source_target_pairs={{0,4},{8,0},{16,8},{24,16},{28,24},{20,28},{12,20},{4,12},{1,5},{9... | collective-permute-start | bytes 786440 | tf_op jit(solution)/shard_map/ppermute | solution.py:203
  590.8 23.6 %all-to-all-start.4 = ((bf16[8,2,128,128]{3,2,1,0:T(8,128)(2,1)}), bf16[8,2,128,128]{3,2,1,0:T(8,128)(2,1)}, u32[]{:S(2)}, u32[]{:S(2)}) async-start(bf16[8,2,128,128]{3,2,1,0:T(8,128)(2,1)} %bitcast.217), calls=%async_computation.4 | async-start | bytes 1048576 | tf_op jit(solution)/shard_map/all_to_all | solution.py:290
  595.0 258.8 %reduce-scatter.4.cloned.1.call-start = ((), (), s32[]{:S(2)}) async-start(), calls=%async_computation.12 | async-start | bytes 10485760 | tf_op jit(solution)/shard_map/reduce_scatter | solution.py:428
  595.0 19.4 %collective-permute-start.80 = (bf16[64,2048]{1,0:T(8,128)(2,1)}, bf16[64,2048]{1,0:T(8,128)(2,1)S(1)}, u32[]{:S(2)}, u32[]{:S(2)}) collective-permute-start(bf16[64,2048]{1,0:T(8,128)(2,1)} %get-tuple-element.93), channel_id=1, source_target_pairs={{0,8},{8,16},{16,24},{24,28},{28,20},{20,12},{12,4},{4,0},{1,9},{9... | collective-permute-start | bytes 786440 | tf_op jit(solution)/shard_map/ppermute | solution.py:203
  598.7 15.6 %collective-permute-start.84 = (bf16[64,2048]{1,0:T(8,128)(2,1)}, bf16[64,2048]{1,0:T(8,128)(2,1)}, u32[]{:S(2)}, u32[]{:S(2)}) collective-permute-start(bf16[64,2048]{1,0:T(8,128)(2,1)} %add_convert_fusion.7), channel_id=1, source_target_pairs={{0,4},{8,0},{16,8},{24,16},{28,24},{20,28},{12,20},{4,12},{1,5},{9... | collective-permute-start | bytes 786440 | tf_op jit(solution)/shard_map/ppermute | solution.py:203
  616.8 24.8 %collective-permute-start.85 = (bf16[64,2048]{1,0:T(8,128)(2,1)}, bf16[64,2048]{1,0:T(8,128)(2,1)}, u32[]{:S(2)}, u32[]{:S(2)}) collective-permute-start(bf16[64,2048]{1,0:T(8,128)(2,1)} %get-tuple-element.65), channel_id=1, source_target_pairs={{0,8},{8,16},{16,24},{24,28},{28,20},{20,12},{12,4},{4,0},{1,9},{9... | collective-permute-start | bytes 786440 | tf_op jit(solution)/shard_map/ppermute | solution.py:203
  618.8 24.9 %collective-permute-start.86 = (bf16[64,2048]{1,0:T(8,128)(2,1)}, bf16[64,2048]{1,0:T(8,128)(2,1)S(1)}, u32[]{:S(2)}, u32[]{:S(2)}) collective-permute-start(bf16[64,2048]{1,0:T(8,128)(2,1)} %get-tuple-element.65), channel_id=1, source_target_pairs={{0,4},{8,0},{16,8},{24,16},{28,24},{20,28},{12,20},{4,12},{1,5},{9... | collective-permute-start | bytes 786440 | tf_op jit(solution)/shard_map/ppermute | solution.py:203
  637.0 52.2 %all-to-all-start.5 = ((bf16[8,6,128,128]{3,2,1,0:T(8,128)(2,1)}), bf16[8,6,128,128]{3,2,1,0:T(8,128)(2,1)}, u32[]{:S(2)}, u32[]{:S(2)}) async-start(bf16[8,6,128,128]{3,2,1,0:T(8,128)(2,1)} %copy-done.2), calls=%async_computation.5 | async-start | bytes 3145728 | tf_op jit(solution)/shard_map/all_to_all | solution.py:293
  641.6 27.6 %collective-permute-start.87 = (bf16[64,2048]{1,0:T(8,128)(2,1)}, bf16[64,2048]{1,0:T(8,128)(2,1)S(1)}, u32[]{:S(2)}, u32[]{:S(2)}) collective-permute-start(bf16[64,2048]{1,0:T(8,128)(2,1)} %collective-permute-done.85), channel_id=1, source_target_pairs={{0,8},{8,16},{16,24},{24,28},{28,20},{20,12},{12,4},{4,0},{1,9},{9... | collective-permute-start | bytes 786440 | tf_op jit(solution)/shard_map/ppermute | solution.py:203
  643.7 35.1 %collective-permute-start.88 = (bf16[64,2048]{1,0:T(8,128)(2,1)S(1)}, bf16[64,2048]{1,0:T(8,128)(2,1)S(1)}, u32[]{:S(2)}, u32[]{:S(2)}) collective-permute-start(bf16[64,2048]{1,0:T(8,128)(2,1)S(1)} %collective-permute-done.86), channel_id=1, source_target_pairs={{0,4},{8,0},{16,8},{24,16},{28,24},{20,28},{12,20},{4,12},{1,5},{9... | collective-permute-start | bytes 786440 | tf_op jit(solution)/shard_map/ppermute | solution.py:203
  669.2 13.5 %collective-permute-start.89 = (bf16[64,2048]{1,0:T(8,128)(2,1)S(1)}, bf16[64,2048]{1,0:T(8,128)(2,1)S(1)}, u32[]{:S(2)}, u32[]{:S(2)}) collective-permute-start(bf16[64,2048]{1,0:T(8,128)(2,1)S(1)} %collective-permute-done.87), channel_id=1, source_target_pairs={{0,8},{8,16},{16,24},{24,28},{28,20},{20,12},{12,4},{4,0},{1,9},{9... | collective-permute-start | bytes 786440 | tf_op jit(solution)/shard_map/ppermute | solution.py:203
  683.4 49.7 %collective-permute-start.91 = (bf16[32,2048]{1,0:T(8,128)(2,1)}, bf16[32,2048]{1,0:T(8,128)(2,1)}, u32[]{:S(2)}, u32[]{:S(2)}) collective-permute-start(bf16[32,2048]{1,0:T(8,128)(2,1)} %slice.515), channel_id=1, source_target_pairs={{0,8},{8,16},{16,24},{24,28},{28,20},{20,12},{12,4},{4,0},{1,9},{9... | collective-permute-start | bytes 393224 | tf_op jit(solution)/shard_map/ppermute | solution.py:203
  686.5 47.8 %collective-permute-start.92 = (bf16[32,2048]{1,0:T(8,128)(2,1)}, bf16[32,2048]{1,0:T(8,128)(2,1)}, u32[]{:S(2)}, u32[]{:S(2)}) collective-permute-start(bf16[32,2048]{1,0:T(8,128)(2,1)} %slice.516), channel_id=1, source_target_pairs={{0,4},{8,0},{16,8},{24,16},{28,24},{20,28},{12,20},{4,12},{1,5},{9... | collective-permute-start | bytes 393224 | tf_op jit(solution)/shard_map/ppermute | solution.py:203
  712.4 15.8 %collective-permute-start.59 = (bf16[256,1536]{1,0:T(8,128)(2,1)S(1)}, bf16[256,1536]{1,0:T(8,128)(2,1)}, u32[]{:S(2)}, u32[]{:S(2)}) collective-permute-start(bf16[256,1536]{1,0:T(8,128)(2,1)S(1)} %pad_maximum_fusion.4), channel_id=1, source_target_pairs={{0,8},{8,16},{16,24},{24,28},{28,20},{20,12},{12,4},{4,0},{1,9},{9... | collective-permute-start | bytes 2359304 | tf_op jit(solution)/shard_map/ppermute | solution.py:203
  713.8 16.9 %collective-permute-start.63 = (bf16[256,1536]{1,0:T(8,128)(2,1)S(1)}, bf16[256,1536]{1,0:T(8,128)(2,1)}, u32[]{:S(2)}, u32[]{:S(2)}) collective-permute-start(bf16[256,1536]{1,0:T(8,128)(2,1)S(1)} %pad_maximum_fusion.5), channel_id=1, source_target_pairs={{0,4},{8,0},{16,8},{24,16},{28,24},{20,28},{12,20},{4,12},{1,5},{9... | collective-permute-start | bytes 2359304 | tf_op jit(solution)/shard_map/ppermute | solution.py:203
  716.0 41.7 %collective-permute-start.47 = (bf16[512,1536]{1,0:T(8,128)(2,1)S(1)}, bf16[512,1536]{1,0:T(8,128)(2,1)S(1)}, u32[]{:S(2)}, u32[]{:S(2)}) collective-permute-start(bf16[512,1536]{1,0:T(8,128)(2,1)S(1)} %copy-done.24), channel_id=1, source_target_pairs={{0,1},{1,0},{2,3},{3,2},{4,5},{5,4},{6,7},{7,6},{8,9},{9,8},{10,11... | collective-permute-start | bytes 4718600 | tf_op jit(solution)/shard_map/ppermute | solution.py:191
  728.3 29.4 %collective-permute-start.48 = (bf16[512,1536]{1,0:T(8,128)(2,1)S(1)}, bf16[512,1536]{1,0:T(8,128)(2,1)S(1)}, u32[]{:S(2)}, u32[]{:S(2)}) collective-permute-start(bf16[512,1536]{1,0:T(8,128)(2,1)S(1)} %copy-done.24), channel_id=1, source_target_pairs={{0,2},{1,3},{2,0},{3,1},{4,6},{5,7},{6,4},{7,5},{8,10},{9,11},{10,... | collective-permute-start | bytes 4718600 | tf_op jit(solution)/shard_map/ppermute | solution.py:191
  730.7 17.5 %collective-permute-start.60 = (bf16[256,1536]{1,0:T(8,128)(2,1)S(1)}, bf16[256,1536]{1,0:T(8,128)(2,1)S(1)}, u32[]{:S(2)}, u32[]{:S(2)}) collective-permute-start(bf16[256,1536]{1,0:T(8,128)(2,1)S(1)} %fusion.7), channel_id=1, source_target_pairs={{0,8},{8,16},{16,24},{24,28},{28,20},{20,12},{12,4},{4,0},{1,9},{9... | collective-permute-start | bytes 2359304 | tf_op jit(solution)/shard_map/ppermute | solution.py:203
  733.1 17.5 %collective-permute-start.64 = (bf16[256,1536]{1,0:T(8,128)(2,1)S(1)}, bf16[256,1536]{1,0:T(8,128)(2,1)S(1)}, u32[]{:S(2)}, u32[]{:S(2)}) collective-permute-start(bf16[256,1536]{1,0:T(8,128)(2,1)S(1)} %fusion.5), channel_id=1, source_target_pairs={{0,4},{8,0},{16,8},{24,16},{28,24},{20,28},{12,20},{4,12},{1,5},{9... | collective-permute-start | bytes 2359304 | tf_op jit(solution)/shard_map/ppermute | solution.py:203
  757.7 17.3 %collective-permute-start.49 = (bf16[512,1536]{1,0:T(8,128)(2,1)S(1)}, bf16[512,1536]{1,0:T(8,128)(2,1)S(1)}, u32[]{:S(2)}, u32[]{:S(2)}) collective-permute-start(bf16[512,1536]{1,0:T(8,128)(2,1)S(1)} %collective-permute-done.48), channel_id=1, source_target_pairs={{0,1},{1,0},{2,3},{3,2},{4,5},{5,4},{6,7},{7,6},{8,9},{9,8},{10,11... | collective-permute-start | bytes 4718600 | tf_op jit(solution)/shard_map/ppermute | solution.py:191
  777.5 30.0 %collective-permute-start.69 = (bf16[192,2048]{1,0:T(8,128)(2,1)S(1)}, bf16[192,2048]{1,0:T(8,128)(2,1)S(1)}, u32[]{:S(2)}, u32[]{:S(2)}) collective-permute-start(bf16[192,2048]{1,0:T(8,128)(2,1)S(1)} %maximum_dynamic-update-slice_fusion.3), channel_id=1, source_target_pairs={{0,8},{8,16},{16,24},{24,28},{28,20},{20,12},{12,4},{4,0},{1,9},{9... | collective-permute-start | bytes 2359304 | tf_op jit(solution)/shard_map/ppermute | solution.py:203
  779.3 30.0 %collective-permute-start.70 = (bf16[192,2048]{1,0:T(8,128)(2,1)S(1)}, bf16[192,2048]{1,0:T(8,128)(2,1)S(1)}, u32[]{:S(2)}, u32[]{:S(2)}) collective-permute-start(bf16[192,2048]{1,0:T(8,128)(2,1)S(1)} %maximum_dynamic-update-slice_fusion.3), channel_id=1, source_target_pairs={{0,4},{8,0},{16,8},{24,16},{28,24},{20,28},{12,20},{4,12},{1,5},{9... | collective-permute-start | bytes 2359304 | tf_op jit(solution)/shard_map/ppermute | solution.py:203
  807.5 17.7 %collective-permute-start.71 = (bf16[192,2048]{1,0:T(8,128)(2,1)S(1)}, bf16[192,2048]{1,0:T(8,128)(2,1)S(1)}, u32[]{:S(2)}, u32[]{:S(2)}) collective-permute-start(bf16[192,2048]{1,0:T(8,128)(2,1)S(1)} %collective-permute-done.69), channel_id=1, source_target_pairs={{0,8},{8,16},{16,24},{24,28},{28,20},{20,12},{12,4},{4,0},{1,9},{9... | collective-permute-start | bytes 2359304 | tf_op jit(solution)/shard_map/ppermute | solution.py:203
  809.3 17.7 %collective-permute-start.72 = (bf16[192,2048]{1,0:T(8,128)(2,1)S(1)}, bf16[192,2048]{1,0:T(8,128)(2,1)S(1)}, u32[]{:S(2)}, u32[]{:S(2)}) collective-permute-start(bf16[192,2048]{1,0:T(8,128)(2,1)S(1)} %collective-permute-done.70), channel_id=1, source_target_pairs={{0,4},{8,0},{16,8},{24,16},{28,24},{20,28},{12,20},{4,12},{1,5},{9... | collective-permute-start | bytes 2359304 | tf_op jit(solution)/shard_map/ppermute | solution.py:203
  825.2 17.6 %collective-permute-start.73 = (bf16[192,2048]{1,0:T(8,128)(2,1)S(1)}, bf16[192,2048]{1,0:T(8,128)(2,1)S(1)}, u32[]{:S(2)}, u32[]{:S(2)}) collective-permute-start(bf16[192,2048]{1,0:T(8,128)(2,1)S(1)} %collective-permute-done.71), channel_id=1, source_target_pairs={{0,8},{8,16},{16,24},{24,28},{28,20},{20,12},{12,4},{4,0},{1,9},{9... | collective-permute-start | bytes 2359304 | tf_op jit(solution)/shard_map/ppermute | solution.py:203
  827.0 17.7 %collective-permute-start.74 = (bf16[192,2048]{1,0:T(8,128)(2,1)S(1)}, bf16[192,2048]{1,0:T(8,128)(2,1)S(1)}, u32[]{:S(2)}, u32[]{:S(2)}) collective-permute-start(bf16[192,2048]{1,0:T(8,128)(2,1)S(1)} %collective-permute-done.72), channel_id=1, source_target_pairs={{0,4},{8,0},{16,8},{24,16},{28,24},{20,28},{12,20},{4,12},{1,5},{9... | collective-permute-start | bytes 2359304 | tf_op jit(solution)/shard_map/ppermute | solution.py:203
  (107 other events, 1351.2 us)
Sparse Core Ops, SparseCore 0:
  14.6 83.3 all-gather.7
  100.2 59.9 all-gather.3
  162.3 61.4 all-gather.5
  389.5 70.7 reduce-scatter.7
  462.9 85.0 reduce-scatter.5
  613.1 72.8 reduce-scatter.3

commit v2 on v1

v2 whole, which is shorter than its diff:
```python
import functools

import jax
import jax.numpy as jnp
import numpy as np
from jax import lax
from jax.experimental import pallas as pl
from jax.experimental.pallas import tpu as pltpu
from jax.sharding import PartitionSpec as P

EPSILON = 1e-06
ROPE_BASE = 10000.0
BF = jnp.bfloat16
F32 = jnp.float32
LONG = pl.CostEstimate(flops=10**12, bytes_accessed=10**9, transcendentals=0)
MEDIUM = pl.CostEstimate(flops=2 * 10**10, bytes_accessed=5 * 10**7, transcendentals=0)
SMALL = pl.CostEstimate(flops=1, bytes_accessed=1, transcendentals=0)


def dot(a, b, contract=((1,), (0,)), precision=None):
    return lax.dot_general(a, b, (contract, ((), ())), precision=precision, preferred_element_type=F32)


def dot_nt(a, b):
    return dot(a, b, ((1,), (1,)))


def dot_tn(a, b):
    return dot(a, b, ((0,), (0,)))


def head_norm(v, gain):
    factor = lax.rsqrt(jnp.mean(v * v, axis=-1, keepdims=True) + EPSILON)
    return v * factor * gain, factor


def turn(v, cosine, sine):
    return v * cosine + pltpu.roll(v, v.shape[-1] // 2, 1) * sine


def head_back(grad, v, gain, cosine, sine):
    grad = turn(grad, cosine, -sine)
    factor = lax.rsqrt(jnp.mean(v * v, axis=-1, keepdims=True) + EPSILON)
    gain_grad = jnp.sum(grad * v * factor, axis=0, keepdims=True)
    inner = grad * gain
    return factor * inner - v * (factor * factor * factor) * jnp.mean(inner * v, axis=-1, keepdims=True), gain_grad


def rows_of(ref):
    block = ref[...]
    return block.reshape(-1, block.shape[-1])


def attend_kernel(q_ref, k_ref, v_ref, qg_ref, kg_ref, cos_ref, sin_ref, o_ref, keys, values_t):
    step = pl.program_id(1)

    @pl.when(step == 0)
    def _():
        normed, _unused = head_norm(rows_of(k_ref).astype(F32), kg_ref[...])
        keys[...] = turn(normed, cos_ref[...], sin_ref[...]).astype(BF)
        values_t[...] = rows_of(v_ref).astype(F32).T.astype(BF)

    queries = rows_of(q_ref).astype(F32)
    number, head_dim = queries.shape
    here = pl.ds(pl.multiple_of(step * number, number), number)
    normed, _unused = head_norm(queries, qg_ref[...])
    queries = turn(normed, cos_ref[here, :], sin_ref[here, :]).astype(BF)
    weights = jnp.exp(dot_nt(keys[...], queries) * (head_dim**-0.5))
    total = jnp.sum(weights, axis=0, keepdims=True)
    mixed = dot(values_t[...], weights.astype(BF)) / total
    o_ref[...] = mixed.T.astype(BF).reshape(o_ref.shape)


def attend_back_kernel(
    q_ref, k_ref, v_ref, m_ref, qg_ref, kg_ref, cos_ref, sin_ref,
    g_ref, gain_ref, keys, keys_t, key_acc, value_acc,
):
    pair = pl.program_id(0)
    step = pl.program_id(1)
    last = pl.num_programs(1) - 1

    @pl.when((pair == 0) & (step == 0))
    def _():
        gain_ref[...] = jnp.zeros_like(gain_ref)

    @pl.when(step == 0)
    def _():
        normed, _unused = head_norm(rows_of(k_ref).astype(F32), kg_ref[...])
        turned = turn(normed, cos_ref[...], sin_ref[...])
        keys[...] = turned.astype(BF)
        keys_t[...] = turned.T.astype(BF)
        key_acc[...] = jnp.zeros_like(key_acc)
        value_acc[...] = jnp.zeros_like(value_acc)

    query_pre = rows_of(q_ref).astype(F32)
    grad_mixed = rows_of(m_ref)
    number, head_dim = query_pre.shape
    scale = head_dim**-0.5
    here = pl.ds(pl.multiple_of(step * number, number), number)
    cosine, sine = cos_ref[here, :], sin_ref[here, :]
    normed, _unused = head_norm(query_pre, qg_ref[...])
    queries = turn(normed, cosine, sine).astype(BF)
    weights = jnp.exp(dot_nt(keys[...], queries) * scale)
    probs = weights * (1.0 / jnp.sum(weights, axis=0, keepdims=True))
    value_acc[...] += dot(probs.astype(BF), grad_mixed)
    weighted = probs * dot_nt(rows_of(v_ref), grad_mixed)
    delta = jnp.sum(weighted, axis=0, keepdims=True)
    grad_scores = (weighted - probs * delta).astype(BF)
    key_acc[...] += dot(grad_scores, queries)
    grad_query = dot(keys_t[...], grad_scores).T * scale
    grad_query, gain_grad = head_back(grad_query, query_pre, qg_ref[...], cosine, sine)
    rows = g_ref.shape[2]
    blocks = number // rows
    g_ref[pl.ds(step * blocks, blocks), 0] = grad_query.astype(BF).reshape(blocks, rows, head_dim)
    gain_ref[0:1, :] += gain_grad

    @pl.when(step == last)
    def _():
        grad_key, gain_grad = head_back(
            key_acc[...] * scale, rows_of(k_ref).astype(F32), kg_ref[...], cos_ref[...], sin_ref[...]
        )
        g_ref[:, 1] = grad_key.astype(BF).reshape(-1, rows, head_dim)
        g_ref[:, 2] = value_acc[...].astype(BF).reshape(-1, rows, head_dim)
        gain_ref[1:2, :] += gain_grad


def attention_specs(shape):
    blocks, pairs, rows, head_dim = shape
    at_once = max(1, 256 // rows)
    while blocks % at_once:
        at_once -= 1
    pairs //= 3
    part = pl.BlockSpec((at_once, 1, rows, head_dim), lambda p, i: (i, p, 0, 0))
    three = [
        pl.BlockSpec((at_once, 1, rows, head_dim), lambda p, i: (i, 3 * p, 0, 0)),
        pl.BlockSpec((blocks, 1, rows, head_dim), lambda p, i: (0, 3 * p + 1, 0, 0)),
        pl.BlockSpec((blocks, 1, rows, head_dim), lambda p, i: (0, 3 * p + 2, 0, 0)),
    ]
    gain = pl.BlockSpec((1, head_dim), lambda p, i: (0, 0))
    table = pl.BlockSpec((blocks * rows, head_dim), lambda p, i: (0, 0))
    params = pltpu.CompilerParams(
        dimension_semantics=("arbitrary", "arbitrary"),
        vmem_limit_bytes=(24 if blocks * rows <= 1024 else 56) * 2**20,
    )
    return part, three, gain, table, (pairs, blocks // at_once), params


def attend(qkv, query_gain, key_gain, cosine, sine):
    part, three, gain, table, grid, params = attention_specs(qkv.shape)
    blocks, _unused, rows, head_dim = qkv.shape
    length = blocks * rows
    return pl.pallas_call(
        attend_kernel,
        grid=grid,
        in_specs=[*three, gain, gain, table, table],
        out_specs=part,
        out_shape=jax.ShapeDtypeStruct((blocks, grid[0], rows, head_dim), BF),
        scratch_shapes=[pltpu.VMEM((length, head_dim), BF), pltpu.VMEM((head_dim, length), BF)],
        compiler_params=params,
        cost_estimate=MEDIUM,
        name="attend",
    )(qkv, qkv, qkv, query_gain, key_gain, cosine, sine)


def attend_back(qkv, grad_mixed, query_gain, key_gain, cosine, sine):
    part, three, gain, table, grid, params = attention_specs(qkv.shape)
    blocks, _unused, rows, head_dim = qkv.shape
    length = blocks * rows
    return pl.pallas_call(
        attend_back_kernel,
        grid=grid,
        in_specs=[*three, part, gain, gain, table, table],
        out_specs=[
            pl.BlockSpec((blocks, 3, rows, head_dim), lambda p, i: (0, p, 0, 0)),
            pl.BlockSpec((8, head_dim), lambda p, i: (0, 0)),
        ],
        out_shape=[jax.ShapeDtypeStruct(qkv.shape, BF), jax.ShapeDtypeStruct((8, head_dim), F32)],
        scratch_shapes=[
            pltpu.VMEM((length, head_dim), BF),
            pltpu.VMEM((head_dim, length), BF),
            pltpu.VMEM((length, head_dim), F32),
            pltpu.VMEM((length, head_dim), F32),
        ],
        compiler_params=params,
        cost_estimate=LONG,
        name="attend_back",
    )(qkv, qkv, qkv, grad_mixed, query_gain, key_gain, cosine, sine)


def stack_blocks(block_refs, out_ref):
    rows = block_refs[0].shape[0]
    for index, block_ref in enumerate(block_refs):
        out_ref[index * rows : (index + 1) * rows, :] = block_ref[...]


def stacked_kernel(w_ref, *refs):
    *block_refs, o_ref, rows_ref = refs

    @pl.when(pl.program_id(0) == 0)
    def _():
        stack_blocks(block_refs, rows_ref)

    o_ref[...] = dot(rows_ref[...], w_ref[...])


def stacked_matmul(blocks, weight):
    rows, depth = len(blocks) * blocks[0].shape[0], weight.shape[0]
    wide = min(512, weight.shape[1])
    return pl.pallas_call(
        stacked_kernel,
        grid=(weight.shape[1] // wide,),
        in_specs=[pl.BlockSpec((depth, wide), lambda n: (0, n))]
        + [pl.BlockSpec(block.shape, lambda n: (0, 0)) for block in blocks],
        out_specs=[pl.BlockSpec((rows, wide), lambda n: (0, n)), pl.BlockSpec((rows, depth), lambda n: (0, 0))],
        out_shape=[jax.ShapeDtypeStruct((rows, weight.shape[1]), F32), jax.ShapeDtypeStruct((rows, depth), BF)],
        compiler_params=pltpu.CompilerParams(dimension_semantics=("arbitrary",), vmem_limit_bytes=56 * 2**20),
        cost_estimate=LONG,
        name="stacked_matmul",
    )(weight, *blocks)


def routed_gates(logits, routes):
    columns = lax.broadcasted_iota(jnp.int32, logits.shape, 1)
    chosen = columns == routes[:, 0:1]
    for index in range(1, routes.shape[1]):
        chosen = chosen | (columns == routes[:, index : index + 1])
    high = jnp.max(jnp.where(chosen, logits, -1e30), axis=-1, keepdims=True)
    weights = jnp.where(chosen, jnp.exp(jnp.where(chosen, logits - high, 0.0)), 0.0)
    return weights / jnp.sum(weights, axis=-1, keepdims=True)


def expert_kernel(table_ref, router_ref, routes_ref, gate_w_ref, up_w_ref, grad_ref, *refs, per, place, at):
    *block_refs, act_ref, gate_ref, up_ref, d_gates_ref, x_ref, gates_ref = refs
    step = pl.program_id(0)

    @pl.when(step == 0)
    def _():
        stack_blocks(block_refs, x_ref)
        routes = jnp.concatenate([routes_ref[table_ref[at + index]] for index in range(len(block_refs))], axis=0)
        gates = routed_gates(dot(x_ref[...], router_ref[...]), routes)
        columns = lax.broadcasted_iota(jnp.int32, gates.shape, 1)
        count = gates_ref.shape[0]
        for index in range(count):
            here = columns == table_ref[place] * count + index
            gates_ref[index] = jnp.sum(jnp.where(here, gates, 0.0), axis=1, keepdims=True)

    @pl.when(step % per == 0)
    def _():
        d_gates_ref[...] = jnp.zeros_like(d_gates_ref)

    gate_pre = dot(x_ref[...], gate_w_ref[...])
    up_pre = dot(x_ref[...], up_w_ref[...])
    grad_act = grad_ref[...]
    gates = gates_ref[step // per]
    sigmoid = 1.0 / (1.0 + jnp.exp(-gate_pre))
    silu = gate_pre * sigmoid
    act = (silu * up_pre).astype(BF).astype(F32)
    d_gates_ref[0] += jnp.sum(act * grad_act, axis=1, keepdims=True)
    grad_act = grad_act * gates
    act_ref[...] = (act * gates).astype(BF)
    up_ref[...] = (grad_act * silu).astype(BF)
    gate_ref[...] = (grad_act * up_pre * (sigmoid * (1.0 + gate_pre * (1.0 - sigmoid)))).astype(BF)


def expert_units(table, place, at, group, blocks, routes, router_w, gate_w, up_w, grad_act, count):
    rows, width = len(blocks) * blocks[0].shape[0], blocks[0].shape[1]
    units = gate_w.shape[1]
    wide = min(512, units // count)
    per = units // wide // count
    weight = pl.BlockSpec((width, wide), lambda n: (0, n))
    tile = pl.BlockSpec((rows, wide), lambda n: (0, n))
    out = jax.ShapeDtypeStruct((rows, units), BF)
    return pl.pallas_call(
        functools.partial(expert_kernel, per=per, place=place, at=at),
        grid=(units // wide,),
        in_specs=[
            pl.BlockSpec(memory_space=pltpu.SMEM),
            pl.BlockSpec(router_w.shape, lambda n: (0, 0)),
            pl.BlockSpec(routes.shape, lambda n: (0, 0, 0)),
            weight,
            weight,
            pl.BlockSpec((rows, wide), lambda n: (group, n)),
        ]
        + [pl.BlockSpec(block.shape, lambda n: (0, 0)) for block in blocks],
        out_specs=[
            tile,
            tile,
            tile,
            pl.BlockSpec((1, rows, 1), lambda n: (n // per, 0, 0)),
            pl.BlockSpec((rows, width), lambda n: (0, 0)),
        ],
        out_shape=[
            out, out, out, jax.ShapeDtypeStruct((count, rows, 1), F32), jax.ShapeDtypeStruct((rows, width), BF),
        ],
        scratch_shapes=[pltpu.VMEM((count, rows, 1), F32)],
        compiler_params=pltpu.CompilerParams(dimension_semantics=("arbitrary",), vmem_limit_bytes=58 * 2**20),
        cost_estimate=LONG,
        name="expert_units",
    )(table, router_w, routes, gate_w, up_w, grad_act, *blocks)


def grouped(call, blocks, *arrays):
    size, rows = 8, blocks[0].shape[0]
    results = []
    for first in range(0, len(blocks), size):
        some = blocks[first : first + size]
        results.append(call(first, some, *[v[first * rows : (first + len(some)) * rows] for v in arrays]))
    if len(results) == 1:
        return results[0]
    return [jnp.concatenate(parts, axis=1 if parts[0].ndim == 3 else 0) for parts in zip(*results)]


def expert_rows_kernel(gate_ref, up_ref, gate_w_ref, up_w_ref, o_ref):
    o_ref[...] = (dot_nt(gate_ref[...], gate_w_ref[...]) + dot_nt(up_ref[...], up_w_ref[...])).astype(BF)


def expert_rows(gate_grads, up_grads, gate_w, up_w):
    rows, units = gate_grads.shape
    width = gate_w.shape[0]
    wide = min(512, width)
    whole = pl.BlockSpec((rows, units), lambda n: (0, 0))
    weight = pl.BlockSpec((wide, units), lambda n: (n, 0))
    return pl.pallas_call(
        expert_rows_kernel,
        grid=(width // wide,),
        in_specs=[whole, whole, weight, weight],
        out_specs=pl.BlockSpec((rows, wide), lambda n: (0, n)),
        out_shape=jax.ShapeDtypeStruct((rows, width), BF),
        compiler_params=pltpu.CompilerParams(dimension_semantics=("arbitrary",), vmem_limit_bytes=56 * 2**20),
        cost_estimate=LONG,
        name="expert_rows",
    )(gate_grads, up_grads, gate_w, up_w)


def times_kernel(a_ref, b_ref, o_ref):
    o_ref[...] = dot_nt(a_ref[...], b_ref[...]).astype(o_ref.dtype)


def times_transpose(a, b):
    (rows, depth), columns = a.shape, b.shape[0]
    wide = min(512, columns)
    return pl.pallas_call(
        times_kernel,
        grid=(columns // wide,),
        in_specs=[pl.BlockSpec((rows, depth), lambda n: (0, 0)), pl.BlockSpec((wide, depth), lambda n: (n, 0))],
        out_specs=pl.BlockSpec((rows, wide), lambda n: (0, n)),
        out_shape=jax.ShapeDtypeStruct((rows, columns), BF),
        compiler_params=pltpu.CompilerParams(dimension_semantics=("arbitrary",), vmem_limit_bytes=56 * 2**20),
        cost_estimate=LONG,
        name="times_transpose",
    )(a, b)


def sum_kernel(*refs):
    *pair_refs, o_ref = refs
    count = len(pair_refs) // 2
    total = dot_tn(pair_refs[0][...], pair_refs[count][...])
    for index in range(1, count):
        total = total + dot_tn(pair_refs[index][...], pair_refs[count + index][...])
    o_ref[...] = total.astype(o_ref.dtype)


def sum_of_outer(lefts, rights):
    rows, columns = lefts[0].shape[1], rights[0].shape[1]
    tall, wide = min(512, rows), columns if len(lefts) <= 2 else min(1024, columns)
    return pl.pallas_call(
        sum_kernel,
        grid=(columns // wide, rows // tall),
        in_specs=[pl.BlockSpec((left.shape[0], tall), lambda n, m: (0, m)) for left in lefts]
        + [pl.BlockSpec((right.shape[0], wide), lambda n, m: (0, n)) for right in rights],
        out_specs=pl.BlockSpec((tall, wide), lambda n, m: (m, n)),
        out_shape=jax.ShapeDtypeStruct((rows, columns), BF),
        compiler_params=pltpu.CompilerParams(
            dimension_semantics=("arbitrary", "arbitrary"), vmem_limit_bytes=56 * 2**20
        ),
        cost_estimate=LONG,
        name="sum_of_outer",
    )(*lefts, *rights)


NN, NT = ((1,), (0,)), ((1,), (1,))


def pairs_kernel(b_ref, *refs, contract, kinds, parts):
    *block_refs, o_ref, rows_ref = refs
    kind = pl.program_id(1)

    @pl.when((pl.program_id(0) == 0) & (kind == 0))
    def _():
        stack_blocks(block_refs, rows_ref)

    product = dot(rows_ref[...], b_ref[...], contract).astype(BF)
    rows, head_dim = o_ref.shape[2:]
    per = o_ref.shape[1] // kinds
    for pair in range(2 * parts):
        head, part = divmod(pair, parts)
        piece = product[part * rows : (part + 1) * rows, head * head_dim : (head + 1) * head_dim]
        o_ref[pair // per, pair % per * kinds + kind] = piece


def matmul_to_pairs(blocks, b, contract, kinds, per, head_dim, cost):
    parts, (rows, depth) = len(blocks), blocks[0].shape
    heads = b.shape[1 - contract[1][0]] // head_dim // kinds
    if contract[1][0] == 0:
        right = pl.BlockSpec((depth, 2 * head_dim), lambda h, k: (0, k * (heads // 2) + h))
    else:
        right = pl.BlockSpec((2 * head_dim, depth), lambda h, k: (k * (heads // 2) + h, 0))
    return pl.pallas_call(
        functools.partial(pairs_kernel, contract=contract, kinds=kinds, parts=parts),
        grid=(heads // 2, kinds),
        in_specs=[right] + [pl.BlockSpec((rows, depth), lambda h, k: (0, 0))] * parts,
        out_specs=pl.BlockSpec((2 * parts // per, per * kinds, rows, head_dim), lambda h, k: (h, 0, 0, 0)),
        out_shape=jax.ShapeDtypeStruct((heads * parts // per, per * kinds, rows, head_dim), BF),
        scratch_shapes=[pltpu.VMEM((parts * rows, depth), BF)],
        compiler_params=pltpu.CompilerParams(
            dimension_semantics=("arbitrary", "arbitrary"), vmem_limit_bytes=32 * 2**20
        ),
        cost_estimate=cost,
        name="matmul_to_pairs",
    )(b, *blocks)


def own_pairs_kernel(table_ref, *refs, parts, kinds, places):
    *piece_refs, o_ref, columns_ref, rows_ref = refs
    block_refs, piece_refs = piece_refs[:parts], piece_refs[parts:]
    head_step, kind = pl.program_id(0), pl.program_id(1)

    @pl.when((head_step == 0) & (kind == 0))
    def _():
        stack_blocks(block_refs, rows_ref)
        place_kernel(table_ref, *piece_refs, columns_ref, slabs=parts, places=places)

    rows, head_dim = o_ref.shape[2:]
    per = o_ref.shape[1] // kinds
    wide = 2 * head_dim
    at = (kind * pl.num_programs(0) + head_step) * wide
    product = dot(rows_ref[...], columns_ref[:, pl.ds(pl.multiple_of(at, wide), wide)]).astype(BF)
    for pair in range(2 * parts):
        head, part = divmod(pair, parts)
        piece = product[part * rows : (part + 1) * rows, head * head_dim : (head + 1) * head_dim]
        o_ref[pair // per, pair % per * kinds + kind] = piece


def own_pairs(table, blocks, pieces, places, kinds, per, head_dim):
    parts, (rows, depth) = len(blocks), blocks[0].shape
    columns = pieces[0].shape[1]
    heads = columns // head_dim // kinds
    whole = [pl.BlockSpec(v.shape, lambda h, k: (0, 0)) for v in (*blocks, *pieces)]
    return pl.pallas_call(
        functools.partial(own_pairs_kernel, parts=parts, kinds=kinds, places=places),
        grid=(heads // 2, kinds),
        in_specs=[pl.BlockSpec(memory_space=pltpu.SMEM)] + whole,
        out_specs=[
            pl.BlockSpec((2 * parts // per, per * kinds, rows, head_dim), lambda h, k: (h, 0, 0, 0)),
            pl.BlockSpec((depth, columns), lambda h, k: (0, 0)),
        ],
        out_shape=[
            jax.ShapeDtypeStruct((heads * parts // per, per * kinds, rows, head_dim), BF),
            jax.ShapeDtypeStruct((depth, columns), BF),
        ],
        scratch_shapes=[pltpu.VMEM((parts * rows, depth), BF)],
        compiler_params=pltpu.CompilerParams(
            dimension_semantics=("arbitrary", "arbitrary"), vmem_limit_bytes=48 * 2**20
        ),
        cost_estimate=SMALL,
        name="own_pairs",
    )(table, *blocks, *pieces)


def small_call(kernel, name, out_shape, *operands, cost=SMALL, scratch=(), **kwargs):
    vmem = pl.BlockSpec(memory_space=pltpu.VMEM)
    return pl.pallas_call(
        functools.partial(kernel, **kwargs),
        in_specs=[pl.BlockSpec(memory_space=pltpu.SMEM)] + [vmem] * (len(operands) - 1),
        out_specs=jax.tree.map(lambda _unused: vmem, out_shape),
        out_shape=out_shape,
        scratch_shapes=list(scratch),
        compiler_params=pltpu.CompilerParams(vmem_limit_bytes=40 * 2**20),
        cost_estimate=cost,
        name=name,
    )(*operands)


def pair_rows(ref, head, parts):
    per = ref.shape[1]
    return [ref[(head * parts + part) // per, (head * parts + part) % per] for part in range(parts)]


def mixed_out_kernel(_unused, m_ref, w_ref, *refs, parts):
    heads = m_ref.shape[0] * m_ref.shape[1] // parts
    pieces = [pair_rows(m_ref, head, parts) for head in range(heads)]
    for part, ref in enumerate(refs):
        ref[...] = dot(jnp.concatenate([p[part] for p in pieces], axis=1), w_ref[...]).astype(ref.dtype)


def mixed_out(table, mixed, w_out, parts):
    shape = (mixed.shape[2], w_out.shape[1])
    out = [jax.ShapeDtypeStruct(shape, kind) for kind in (F32, BF, F32, BF)]
    return small_call(mixed_out_kernel, "mixed_out", out, table, mixed, w_out, cost=MEDIUM, parts=parts)


def out_grads_kernel(table_ref, m_ref, *refs, parts, turn, own_rows):
    *block_refs, o_ref, mixed_ref, turned_ref, grads_ref = refs
    head_dim = m_ref.shape[3]
    for head in range(m_ref.shape[0] * m_ref.shape[1] // parts):
        rows = jnp.concatenate(pair_rows(m_ref, head, parts), axis=0)
        mixed_ref[head * head_dim : (head + 1) * head_dim, :] = rows.astype(F32).T.astype(BF)
    for index in range(mixed_ref.shape[0] // own_rows):
        at = pl.multiple_of(table_ref[turn + index] * own_rows, own_rows)
        turned_ref[index * own_rows : (index + 1) * own_rows, :] = mixed_ref[pl.ds(at, own_rows), :]
    stack_blocks(block_refs, grads_ref)
    o_ref[...] = dot(turned_ref[...], grads_ref[...])


def out_grads(table, mixed, blocks, turn, own_rows):
    parts, (rows, width) = len(blocks), blocks[0].shape
    features = mixed.shape[0] * mixed.shape[1] // parts * mixed.shape[3]
    side = pltpu.VMEM((features, parts * rows), BF)
    out = jax.ShapeDtypeStruct((features, width), F32)
    scratch = [side, side, pltpu.VMEM((parts * rows, width), BF)]
    return small_call(
        out_grads_kernel, "out_grads", out, table, mixed, *blocks, scratch=scratch, parts=parts, turn=turn,
        own_rows=own_rows,
    )


def turned_kernel(table_ref, *refs, turn, own_rows, parts, order):
    *block_refs, o_ref, rows_ref = refs
    rows, width = block_refs[0].shape
    slab = width // parts
    for index, block_ref in enumerate(block_refs):
        rows_ref[:, index * rows : (index + 1) * rows] = block_ref[...].astype(F32).T.astype(BF)
    for index in range(width // own_rows):
        step, first = divmod(index, parts)
        at = first * slab + table_ref[turn + order[step]] * own_rows
        o_ref[index * own_rows : (index + 1) * own_rows, :] = rows_ref[pl.ds(pl.multiple_of(at, own_rows), own_rows), :]


def turned_transpose(table, blocks, turn, own_rows, order):
    parts, (rows, width) = len(blocks), blocks[0].shape
    out = jax.ShapeDtypeStruct((width, parts * rows), BF)
    scratch = [pltpu.VMEM((width, parts * rows), BF)]
    return small_call(
        turned_kernel, "turned_transpose", out, table, *blocks, scratch=scratch, turn=turn, own_rows=own_rows,
        parts=parts, order=order,
    )


def pair_tile(g_ref, kind, kinds, parts):
    per = g_ref.shape[1] // kinds
    heads = []
    for head in range(2):
        pieces = [g_ref[pair // per, pair % per * kinds + kind] for pair in range(head * parts, (head + 1) * parts)]
        heads.append(jnp.concatenate(pieces, axis=0))
    return jnp.concatenate(heads, axis=1)


def pair_weights_kernel(g_ref, n_ref, dw_ref, *, kinds, parts):
    dw_ref[...] = dot(n_ref[...], pair_tile(g_ref, pl.program_id(1), kinds, parts)).astype(BF)


def pair_rows_kernel(g_ref, w_ref, *refs, kinds, parts):
    *out_refs, dn_ref = refs
    kind = pl.program_id(1)

    @pl.when((pl.program_id(0) == 0) & (kind == 0))
    def _():
        dn_ref[...] = jnp.zeros_like(dn_ref)

    dn_ref[...] += dot_nt(pair_tile(g_ref, kind, kinds, parts), w_ref[...])

    @pl.when((pl.program_id(0) == pl.num_programs(0) - 1) & (kind == kinds - 1))
    def _():
        for part, out_ref in enumerate(out_refs):
            rows = out_ref.shape[0]
            out_ref[...] = dn_ref[part * rows : (part + 1) * rows, :].astype(out_ref.dtype)


def pair_specs(grads, kinds, parts):
    places, slots, rows, head_dim = grads.shape
    heads = places * slots // kinds // parts
    per = slots // kinds
    block = pl.BlockSpec((2 * parts // per, slots, rows, head_dim), lambda h, k: (h, 0, 0, 0))
    params = pltpu.CompilerParams(dimension_semantics=("arbitrary", "arbitrary"), vmem_limit_bytes=48 * 2**20)
    return block, heads, 2 * head_dim, params


def pair_weights(grads, normed_t, kinds, parts, half):
    width, total = normed_t.shape
    block, heads, wide, params = pair_specs(grads, kinds, parts)
    return pl.pallas_call(
        functools.partial(pair_weights_kernel, kinds=kinds, parts=parts),
        grid=(heads // 2, kinds),
        in_specs=[block, pl.BlockSpec((width // 2, total), lambda h, k: (half, 0))],
        out_specs=pl.BlockSpec((width // 2, wide), lambda h, k: (0, k * (heads // 2) + h)),
        out_shape=jax.ShapeDtypeStruct((width // 2, kinds * heads * wide // 2), BF),
        compiler_params=params,
        cost_estimate=LONG,
        name="pair_weights",
    )(grads, normed_t)


def pair_normed(grads, columns, kinds, parts):
    rows, width = grads.shape[2], columns.shape[0]
    block, heads, wide, params = pair_specs(grads, kinds, parts)
    return pl.pallas_call(
        functools.partial(pair_rows_kernel, kinds=kinds, parts=parts),
        grid=(heads // 2, kinds),
        in_specs=[block, pl.BlockSpec((width, wide), lambda h, k: (0, k * (heads // 2) + h))],
        out_specs=[pl.BlockSpec((rows, width), lambda h, k: (0, 0))] * parts,
        out_shape=[jax.ShapeDtypeStruct((rows, width), kind) for kind in (F32, BF, F32, BF)],
        scratch_shapes=[pltpu.VMEM((parts * rows, width), F32)],
        compiler_params=params,
        cost_estimate=LONG,
        name="pair_normed",
    )(grads, columns)


def part_kernel(_unused, *refs, count):
    weights, outs = refs[:-count], refs[-count:]
    wide = weights[0].shape[1]
    per = len(weights) // count
    for index, weight in enumerate(weights):
        outs[index // per][:, index % per * wide : (index % per + 1) * wide] = weight[...]


def take_parts(table, weights, shape, places, cost):
    def spec(row, column):
        return pl.BlockSpec(shape, lambda i, t: (0 if row is None else t[row], t[column]))

    out = (shape[0], shape[1] * len(weights))
    return pl.pallas_call(
        functools.partial(part_kernel, count=len(places)),
        grid_spec=pltpu.PrefetchScalarGridSpec(
            num_scalar_prefetch=1,
            grid=(1,),
            in_specs=[spec(*where) for where in places for _unused in weights],
            out_specs=[pl.BlockSpec(out, lambda i, t: (0, 0))] * len(places),
        ),
        out_shape=[jax.ShapeDtypeStruct(out, weights[0].dtype)] * len(places),
        compiler_params=pltpu.CompilerParams(vmem_limit_bytes=32 * 2**20),
        cost_estimate=cost,
        name="take_parts",
    )(table, *[w for _unused in places for w in weights])


def stack_kernel(_unused, *refs):
    stack_blocks(refs[:-1], refs[-1])


def stack_rows(table, *pieces):
    rows = sum(piece.shape[0] for piece in pieces)
    out = jax.ShapeDtypeStruct((rows, pieces[0].shape[1]), pieces[0].dtype)
    return small_call(stack_kernel, "stack_rows", out, table, *pieces)


def place_kernel(table_ref, *refs, slabs, places):
    *pieces, out = refs
    slab = out.shape[0] // slabs
    for piece, (where, then) in zip(pieces, places):
        half = piece.shape[0] // len(where)
        for index, slot in enumerate(where):
            at = table_ref[slot] * slab
            if then is not None:
                at = at + table_ref[then] * half
            out[pl.ds(pl.multiple_of(at, half), half), :] = piece[index * half : (index + 1) * half, :]


def place_rows(table, pieces, slabs, places):
    rows = sum(piece.shape[0] for piece in pieces)
    out = jax.ShapeDtypeStruct((rows, pieces[0].shape[1]), pieces[0].dtype)
    return small_call(place_kernel, "place_rows", out, table, *pieces, slabs=slabs, places=places)


def total_kernel(table_ref, term_ref, right_ref, left_ref, *refs, slots):
    own_rows = refs[0].shape[0]
    for slot, ref in zip(slots, refs):
        slab = table_ref[slot]
        here = pl.ds(pl.multiple_of(slab * own_rows, own_rows), own_rows)
        ref[...] = (term_ref[here, :].astype(F32) + right_ref[here, :].astype(F32) + left_ref[here, :].astype(F32)).astype(BF)


def total_parts(table, term, right, left, slots):
    out = [jax.ShapeDtypeStruct((term.shape[0] // len(slots), term.shape[1]), BF)] * len(slots)
    return small_call(total_kernel, "total_parts", out, table, term, right, left, slots=slots)


def join_kernel(table_ref, below_ref, last_ref, *refs, slots, kinds):
    *pieces, out = refs
    own_rows, wide = pieces[0].shape[0], pieces[0].shape[1] // kinds
    for slot, piece in zip(slots, pieces):
        here = pl.ds(pl.multiple_of(table_ref[slot] * wide, wide), wide)
        for kind in range(kinds):
            out[kind * own_rows : (kind + 1) * own_rows, here] = piece[:, kind * wide : (kind + 1) * wide]
    out[kinds * own_rows : (kinds + 1) * own_rows, :] = below_ref[...].astype(BF)
    out[(kinds + 1) * own_rows :, :] = last_ref[...]


def join_columns(table, pieces, below, last, slots, kinds):
    rows, columns = pieces[0].shape
    height = rows * (kinds + 1) + last.shape[0]
    out = jax.ShapeDtypeStruct((height, columns // kinds * len(pieces)), pieces[0].dtype)
    return small_call(join_kernel, "join_columns", out, table, below, last, *pieces, slots=slots, kinds=kinds)


def pack_kernel(table_ref, early_ref, late_ref, o_ref, *, slot, experts):
    slab = o_ref.shape[1] // 4
    here = pl.ds(pl.multiple_of(table_ref[slot] * slab, slab), slab)
    o_ref[...] = jnp.zeros_like(o_ref)
    for index in range(experts):
        row = early_ref[index : index + 1, here].astype(BF)
        o_ref[index // 4 : index // 4 + 1, index % 4 * slab : (index % 4 + 1) * slab] = row
    o_ref[experts // 4 : experts // 4 + 1, :] = early_ref[experts : experts + 1, :].astype(BF)
    o_ref[experts // 4 + 1 : experts // 4 + 3, :] = late_ref[...].astype(BF)


def pack_gains(table, early, late, slot, experts):
    height = -(-(experts // 4 + 3) // 16) * 16
    out = jax.ShapeDtypeStruct((height, early.shape[1]), BF)
    return small_call(pack_kernel, "pack_gains", out, table, early, late, slot=slot, experts=experts)


def unpack_kernel(table_ref, *refs, back, experts):
    *pieces, router_ref, gains_ref, all_ref = refs
    height = all_ref.shape[1]
    for index, piece in enumerate(pieces):
        all_ref[index] = piece[piece.shape[0] - height :, :].astype(F32)
    total = all_ref[table_ref[back]]
    for place in range(1, len(pieces)):
        total = total + all_ref[table_ref[back + place]]
    slab = total.shape[1] // 4
    rows = [total[i // 4 : i // 4 + 1, i % 4 * slab : (i % 4 + 1) * slab] for i in range(experts)]
    router_ref[...] = jnp.concatenate(rows, axis=0).T
    gains_ref[...] = total[experts // 4 : experts // 4 + 3, :]


def unpack_gains(table, pieces, back, experts, height):
    width = pieces[0].shape[1]
    out = [jax.ShapeDtypeStruct((width // 4, experts), F32), jax.ShapeDtypeStruct((3, width), F32)]
    scratch = [pltpu.VMEM((len(pieces), height, width), F32)]
    return small_call(
        unpack_kernel, "unpack_gains", out, table, *pieces, scratch=scratch, back=back, experts=experts
    )


def spread_kernel(table_ref, *refs, slots, count, fresh):
    pieces = refs[: len(slots)]
    outs = refs[len(slots) + (0 if fresh else count) :][:count]
    wide_ref, sems = refs[-2:]
    own_rows = wide_ref.shape[1]
    copies = []
    for index, (slot, piece) in enumerate(zip(slots, pieces)):
        here = pl.ds(pl.multiple_of(table_ref[slot] * own_rows, own_rows), own_rows)
        for kind in range(count):
            at = index * count + kind
            wide_ref[at] = piece[kind * own_rows : (kind + 1) * own_rows, :].astype(F32)
            copies.append(pltpu.make_async_copy(wide_ref.at[at], outs[kind].at[here, :], sems.at[at]))
            copies[-1].start()
    for copy in copies:
        copy.wait()


def spread_rows(table, pieces, slots, shape, places, count, before):
    vmem, anywhere = pl.BlockSpec(memory_space=pltpu.VMEM), pl.BlockSpec(memory_space=pl.ANY)
    number = len(pieces) * count
    fresh = before is None
    own_rows = shape[0] // places
    return pl.pallas_call(
        functools.partial(spread_kernel, slots=slots, count=count, fresh=fresh),
        in_specs=[pl.BlockSpec(memory_space=pltpu.SMEM)] + [vmem] * len(pieces) + [anywhere] * (0 if fresh else count),
        out_specs=[anywhere] * count,
        out_shape=[jax.ShapeDtypeStruct(shape, F32)] * count,
        input_output_aliases={} if fresh else {1 + len(pieces) + kind: kind for kind in range(count)},
        scratch_shapes=[pltpu.VMEM((number, own_rows, shape[1]), F32), pltpu.SemaphoreType.DMA((number,))],
        compiler_params=pltpu.CompilerParams(vmem_limit_bytes=24 * 2**20),
        cost_estimate=SMALL,
        name="spread_rows",
    )(table, *pieces, *([] if fresh else before))


def merge_kernel(w_ref, o_ref):
    units = w_ref.shape[2]
    for index in range(w_ref.shape[1]):
        o_ref[:, index * units : (index + 1) * units] = w_ref[:, index, :]


def merge_experts(weight):
    rows, count, units = weight.shape
    at_once = 128
    return pl.pallas_call(
        merge_kernel,
        grid=(rows // at_once,),
        in_specs=[pl.BlockSpec((at_once, count, units), lambda m: (m, 0, 0))],
        out_specs=pl.BlockSpec((at_once, count * units), lambda m: (m, 0)),
        out_shape=jax.ShapeDtypeStruct((rows, count * units), weight.dtype),
        cost_estimate=MEDIUM,
        name="merge_experts",
    )(weight)


def split_kernel(w_ref, o_ref):
    units = o_ref.shape[2]
    for index in range(o_ref.shape[1]):
        o_ref[:, index, :] = w_ref[:, index * units : (index + 1) * units].astype(F32)


def split_experts(grad, count):
    rows, columns = grad.shape
    at_once = 128
    return pl.pallas_call(
        split_kernel,
        grid=(rows // at_once,),
        in_specs=[pl.BlockSpec((at_once, columns), lambda m: (m, 0))],
        out_specs=pl.BlockSpec((at_once, count, columns // count), lambda m: (m, 0, 0)),
        out_shape=jax.ShapeDtypeStruct((rows, count, columns // count), F32),
        cost_estimate=SMALL,
        name="split_experts",
    )(grad)


def swap(v, mask):
    size = lax.axis_size("fsdp")
    return lax.ppermute(v, "fsdp", [(i, i ^ mask) for i in range(size)])


def ring_order(size):
    if size == 8:
        return [0, 2, 4, 6, 7, 5, 3, 1]
    return list(range(size))


def ring_send(v, direction):
    order = ring_order(lax.axis_size("ctx"))
    size = len(order)
    return lax.ppermute(v, "ctx", [(order[i], order[(i + direction) % size]) for i in range(size)])


class Ring:
    def __init__(self, steps):
        self.steps = steps
        self.value = None
        self.flying = False
        self.advance()

    def advance(self):
        try:
            next(self.steps)
            self.flying = not self.flying
        except StopIteration as end:
            self.value = end.value

    def land(self):
        if self.value is None and self.flying:
            self.advance()

    def step(self):
        self.land()
        if self.value is None:
            self.advance()

    def finish(self):
        while self.value is None:
            self.step()
        return self.value


def ring_gather(v, in_order, found):
    size = lax.axis_size("ctx")
    far, half = size // 2, v.shape[0] // 2
    found[0] = v
    right, left = v, v
    for step in range(1, far):
        right, left = ring_send(right, 1), ring_send(left, -1)
        yield
        right, left = in_order(right, left)
        found[size - step], found[step] = right, left
        yield
    right, left = ring_send(right[:half], 1), ring_send(left[half:], -1)
    yield
    found[far] = jnp.concatenate(in_order(right, left))
    yield
    return found


def ring_scatter(term, in_order, last=None):
    size = lax.axis_size("ctx")
    far = size // 2
    first = term(far)
    half = first.shape[0] // 2
    right, left = ring_send(first[:half].astype(BF), 1), ring_send(first[half:].astype(BF), -1)
    for offset in range(far - 1, 0, -1):
        yield
        right, left = in_order(right, left)
        yield
        ahead, behind = term(offset), term(size - offset)
        if offset == far - 1:
            ahead = jnp.concatenate([ahead[:half].astype(F32) + right.astype(F32), ahead[half:].astype(F32)])
            behind = jnp.concatenate([behind[:half].astype(F32), behind[half:].astype(F32) + left.astype(F32)])
        else:
            ahead, behind = ahead.astype(F32) + right.astype(F32), behind.astype(F32) + left.astype(F32)
        right, left = ring_send(ahead.astype(BF), 1), ring_send(behind.astype(BF), -1)
    yield
    right, left = in_order(right, left)
    yield
    if last is not None:
        return last(term(0), right, left)
    return term(0).astype(F32) + right.astype(F32) + left.astype(F32)


def after(v, *others):
    return lax.optimization_barrier((v, *others))[0]


class Order:
    def __init__(self, first):
        self.last = first

    def __call__(self, *values):
        self.last, *values = lax.optimization_barrier((self.last, *values))
        return values[0] if len(values) == 1 else values


def sum_fsdp(v, in_order):
    size = lax.axis_size("fsdp")
    mask = 1
    while mask < size:
        other = swap(v, mask)
        yield
        v = v + in_order(other)
        yield
        mask *= 2
    return v


def body(
    tokens, attn_gain, w_query, w_key, w_value, query_gain, key_gain, w_out,
    ffn_gain, w_router, w_gate, w_up, w_down, routes, cotangent,
):
    ctx_size = lax.axis_size("ctx")
    parts = lax.axis_size("fsdp")
    rows = tokens.shape[1]
    width = tokens.shape[2]
    slab = w_query.shape[0]
    head_dim = query_gain.shape[0]
    own_heads = width // head_dim // parts
    own_width = own_heads * head_dim
    own_rows = slab // ctx_size
    own_experts = w_gate.shape[1]
    hidden_units = w_gate.shape[2]
    experts = own_experts * ctx_size
    seq_length = rows * ctx_size
    in_order = Order(jnp.zeros((), F32))

    order = ring_order(ctx_size)
    offsets = [0] + [o for step in range(1, ctx_size // 2) for o in (step, ctx_size - step)] + [ctx_size // 2]
    at_ring, at_place, at_slab = 0, 1, [2 + mask for mask in range(parts)]
    at_from = 2 + parts
    at_blocks = {offset: at_from + ctx_size + index for index, offset in enumerate(offsets)}
    at_turn = at_from + 2 * ctx_size
    at_back = at_from + 3 * ctx_size
    lines = []
    for place in range(ctx_size):
        ring_place = order.index(place)
        for mine in range(parts):
            line = [ring_place, place] + [mine ^ mask for mask in range(parts)]
            line += [order[(ring_place + offset) % ctx_size] for offset in offsets]
            line += [(ring_place + offset) % ctx_size for offset in offsets]
            line += [(ring_place + index) % ctx_size for index in range(ctx_size)]
            line += [offsets.index((order.index(other) - ring_place) % ctx_size) for other in range(ctx_size)]
            lines.append(line)
    device = lax.axis_index("ctx").astype(jnp.uint32) * parts + lax.axis_index("fsdp").astype(jnp.uint32)
    table = lax.dynamic_slice(jnp.asarray(np.array(lines, np.int32)), (device, jnp.uint32(0)), (1, len(lines[0])))
    table = table.reshape(-1)

    pairs = own_heads * parts
    per = max(1, pairs // ctx_size)
    repeats = max(1, ctx_size // pairs)

    def spread_pairs(v):
        if repeats > 1:
            v = jnp.repeat(v, repeats, axis=0)
        return lax.all_to_all(v, "ctx", split_axis=0, concat_axis=0, tiled=True)

    def collect_pairs(v):
        v = lax.all_to_all(v, "ctx", split_axis=0, concat_axis=0, tiled=True)
        return v[::repeats] if repeats > 1 else v

    projections = (w_query, w_key, w_value)
    ring_row = table[at_ring].astype(jnp.uint32) * own_rows

    def fetched_part(slot):
        column = table[slot].astype(jnp.uint32) * own_width
        parts_of = [lax.dynamic_slice(w, (ring_row, column), (own_rows, own_width)) for w in projections]
        return jnp.concatenate(parts_of, axis=1)

    fetched = in_order(fetched_part(at_slab[2]), fetched_part(at_slab[3]))
    fetched = swap(fetched[0], 2), swap(fetched[1], 3)
    source = tokens[0].astype(F32)
    factor_one = lax.rsqrt(jnp.mean(source * source, axis=-1, keepdims=True) + EPSILON)
    normed = (source * factor_one * attn_gain).astype(BF)
    projections = after(projections, in_order.last)
    near, own = in_order(
        *take_parts(table, projections, (slab, own_width), [(None, at_slab[1]), (None, at_slab[0])], MEDIUM)
    )
    fetched = in_order(*fetched)
    column_blocks = {}
    ring = Ring(ring_gather(stack_rows(table, *fetched), in_order, column_blocks))
    normed, near = after((normed, near), fetched)
    across, beside, near = swap(normed, 2), swap(normed, 1), swap(near, 1)
    w_router = after(w_router, in_order.last)
    router = [w_router, swap(w_router, 1), swap(w_router, 2), swap(w_router, 3)]
    routes = after(routes, in_order.last)
    routes_all = lax.all_to_all(
        jnp.broadcast_to(routes, (ctx_size, *routes.shape[1:])), "ctx", split_axis=0, concat_axis=0, tiled=True
    )
    w_down = in_order(merge_experts(after(w_down, in_order.last)))
    ring.step()
    down_w = lax.all_gather(w_down, "fsdp", axis=0, tiled=True)
    across = after(across, in_order.last)
    diagonal = swap(across, 1)
    w_gate = in_order(merge_experts(after(w_gate, in_order.last)))
    ring.step()
    gate_w = lax.all_gather(w_gate, "fsdp", axis=0, tiled=True)
    normed = in_order(normed, beside, across, diagonal)
    w_up = in_order(merge_experts(after(w_up, in_order.last)))
    ring.step()
    up_w = lax.all_gather(w_up, "fsdp", axis=0, tiled=True)

    half = head_dim // 2
    frequency = ROPE_BASE ** (-jnp.arange(half, dtype=F32) * 2.0 / head_dim)
    angles = jnp.arange(seq_length, dtype=jnp.int32).astype(F32)[:, None] * frequency[None, :]
    cosine, sine = jnp.cos(angles), jnp.sin(angles)
    cosine = jnp.concatenate([cosine, cosine], axis=1)
    sine = jnp.concatenate([-sine, sine], axis=1)
    q_gain, k_gain = query_gain[None, :], key_gain[None, :]

    ring.finish()
    routes_all = in_order(routes_all)
    qkv, own_columns = own_pairs(
        table,
        normed,
        [own, near] + [column_blocks[offset] for offset in offsets],
        [((at_slab[0],), None), ((at_slab[1],), None)]
        + [((at_slab[2], at_slab[3]), at_blocks[offset]) for offset in offsets],
        3,
        per,
        head_dim,
    )
    qkv = spread_pairs(in_order(qkv))
    router = after(router, in_order.last)
    router_w = in_order(place_rows(table, router, parts, [((slot,), None) for slot in at_slab]))
    qkv = in_order(qkv)
    down_w = in_order(down_w)
    cot_blocks = {}
    ring = Ring(ring_gather(after(cotangent[0], qkv), in_order, cot_blocks))
    mixed = in_order(attend(qkv, q_gain, k_gain, cosine, sine))
    ring.step()
    mixed = in_order(collect_pairs(mixed))
    ring.step()
    hidden, near, across, far = in_order(*mixed_out(table, mixed, w_out, parts))
    far, near = swap(far, 1), swap(near, 1)
    far = in_order((across + in_order(far).astype(F32)).astype(BF))
    far = swap(far, 2)
    hidden = in_order(source + hidden + in_order(near).astype(F32))
    ring.step()
    hidden = hidden + in_order(far).astype(F32)
    factor_two = lax.rsqrt(jnp.mean(hidden * hidden, axis=-1, keepdims=True) + EPSILON)
    ffn_in = in_order((hidden * factor_two * ffn_gain).astype(BF))

    ffn_blocks = {}
    ffn_ring = Ring(ring_gather(ffn_in, in_order, ffn_blocks))
    gate_w = in_order(gate_w)
    ring.finish()
    ffn_ring.step()
    grad_act, cots = in_order(
        *grouped(lambda _unused, blocks: stacked_matmul(blocks, down_w), [cot_blocks[o] for o in offsets])
    )
    ffn_ring.step()

    size = 4
    groups = [offsets[first : first + size] for first in range(0, ctx_size, size)]

    def group_units(group):
        if group > 0:
            ffn_ring.finish()
        return in_order(
            *expert_units(
                table, at_place, at_from + group * size, group, [ffn_blocks[o] for o in groups[group]], routes_all,
                router_w, gate_w, up_w, grad_act, own_experts,
            )
        )

    up_w = in_order(up_w)
    units = [group_units(0)]
    order_of_rows = [ctx_size // 2] + [o for step in range(ctx_size // 2 - 1, 0, -1) for o in (step, ctx_size - step)]
    order_of_rows += [0]
    ffn_ring.step()
    normed_t = in_order(turned_transpose(table, after(normed, in_order.last), at_turn, own_rows, order_of_rows))
    for group in range(1, len(groups)):
        units.append(group_units(group))
    acts, gate_grads, up_grads, d_gates, inputs = zip(*units)

    def term_of(terms):
        def term(offset):
            group, index = divmod(offsets.index(offset), size)
            return terms[group][index * rows : (index + 1) * rows]

        return term

    def weight_grad(lefts, rights):
        lefts, rights = after((lefts, rights), in_order.last)
        return in_order(sum_of_outer(lefts, rights))

    def share(grad):
        return lax.psum_scatter(after(grad, in_order.last), "fsdp", scatter_dimension=0, tiled=True)

    grad_rows, weighted = {}, {}

    def make_rows(group):
        some = after((gate_grads[group], up_grads[group]), in_order.last)
        grad_rows[group] = in_order(expert_rows(*some, gate_w, up_w))

    for group in range(len(groups) - 1, 0, -1):
        make_rows(group)
    row_ring = Ring(ring_scatter(term_of(grad_rows), in_order))
    make_rows(0)
    row_ring.step()
    for group in range(len(groups) - 1, -1, -1):
        weighted[group] = in_order(times_transpose(after(acts[group], in_order.last), down_w))
    row_ring.step()
    d_gates = jnp.concatenate(after(d_gates, in_order.last), axis=1).reshape(own_experts, ctx_size, rows)
    d_gates = d_gates.at[:, table[at_back : at_back + ctx_size], :].get(mode="promise_in_bounds").transpose(1, 0, 2)
    d_gates = lax.all_to_all(d_gates, "ctx", split_axis=0, concat_axis=0, tiled=True)
    row_ring.step()
    d_gates = in_order(d_gates).reshape(experts, rows).T
    gates = routed_gates(dot(ffn_in, router_w), routes[0])
    grad_logits = gates * (d_gates - jnp.sum(gates * d_gates, axis=-1, keepdims=True))
    routed = dot(grad_logits, router_w.astype(F32), ((1,), (1,)), precision=lax.Precision.HIGHEST)
    routed = in_order(routed)
    grad_ffn_in = row_ring.finish() + routed

    inner = grad_ffn_in * ffn_gain
    grad_hidden = (
        cotangent[0].astype(F32)
        + factor_two * inner
        - hidden * (factor_two * factor_two * factor_two) * jnp.mean(inner * hidden, axis=-1, keepdims=True)
    )
    grad_proj, grad_hidden, grad_ffn_in = in_order(grad_hidden.astype(BF), grad_hidden, grad_ffn_in)

    across, beside = swap(grad_proj, 2), swap(grad_proj, 1)
    ring = Ring(ring_scatter(term_of(weighted), in_order))
    d_gate = weight_grad(inputs, gate_grads)
    ring.land()
    across = in_order(across)
    d_gate = share(d_gate)
    grad_proj = in_order(grad_proj, beside, across, swap(across, 1))
    ring.step()
    grad_mixed = in_order(matmul_to_pairs(grad_proj, w_out, NT, 1, per, head_dim, LONG))
    grad_mixed = spread_pairs(grad_mixed)
    d_up = weight_grad(inputs, up_grads)
    mixed, grad_ffn_in, *grad_proj = after((mixed, grad_ffn_in, *grad_proj), in_order.last)
    d_out = in_order(out_grads(table, mixed, grad_proj, at_turn, own_rows))
    d_ffn_gain = jnp.sum(grad_ffn_in * hidden * factor_two, axis=0, keepdims=True)
    d_router = dot(grad_logits, ffn_in.astype(F32), ((0,), (0,)), precision=lax.Precision.HIGHEST)
    early = in_order(jnp.concatenate([d_router, d_ffn_gain]))
    ring.land()
    grad_mixed = in_order(grad_mixed)
    d_up = share(d_up)
    early = Ring(sum_fsdp(early, in_order))
    ring.step()
    grads, head_gains = in_order(*attend_back(qkv, grad_mixed, q_gain, k_gain, cosine, sine))
    if repeats > 1:
        head_gains = jnp.where(lax.axis_index("ctx") % repeats == 0, head_gains, 0.0)
    early.step()
    ring.step()
    grads = collect_pairs(grads)
    d_down = weight_grad([cots[i * size * rows : (i + 1) * size * rows] for i in range(len(groups))], acts)
    ring.land()
    early = early.finish()
    output = in_order((hidden + ring.finish()).astype(BF))
    ring = Ring(ring_scatter(lambda offset: d_out[offset * own_rows : (offset + 1) * own_rows], in_order))
    grads = in_order(grads)
    d_down = share(d_down)
    ring.step()

    chunk = parts * own_rows
    all_grads = {0: in_order(pair_weights(grads, normed_t, 3, parts, 0))}

    def total_term(offset):
        half, index = divmod(order_of_rows.index(offset), ctx_size // 2)
        return all_grads[half][index * chunk : (index + 1) * chunk]

    total_ring = Ring(
        ring_scatter(
            total_term, in_order, lambda term, right, left: total_parts(table, term, right, left, at_slab)
        )
    )
    grads = after(grads, in_order.last)
    all_grads[1] = in_order(pair_weights(grads, normed_t, 3, parts, 1))
    ring.step()
    total_ring.step()
    grads = after(grads, in_order.last)
    own, near, across, far = in_order(*pair_normed(grads, own_columns, 3, parts))
    far, near = swap(far, 1), swap(near, 1)
    far = swap(in_order((across + in_order(far).astype(F32)).astype(BF)), 2)
    d_out = ring.finish()
    total_ring.step()
    grad_normed = own + near.astype(F32) + in_order(far).astype(F32)
    d_attn_gain = jnp.sum(grad_normed * source * factor_one, axis=0)
    inner = grad_normed * attn_gain
    d_tokens = (
        grad_hidden
        + factor_one * inner
        - source * (factor_one * factor_one * factor_one) * jnp.mean(inner * source, axis=-1, keepdims=True)
    )
    d_tokens, d_attn_gain = in_order(d_tokens, d_attn_gain)
    late = jnp.concatenate([d_attn_gain, head_gains[0], head_gains[1], jnp.zeros((width - 2 * head_dim,), F32)])
    late = Ring(sum_fsdp(late.reshape(2, width), in_order))
    total_ring.step()
    late.step()
    total = in_order(*total_ring.finish())
    total = [total[0]] + [swap(total[mask], mask) for mask in range(1, parts)]
    packed = pack_gains(table, early, late.finish(), at_slab[0], experts)
    d_out, packed, *total = in_order(d_out, packed, *total)

    pieces, seen, whole = {}, set(), None
    ring = Ring(ring_gather(join_columns(table, total, d_out, packed, at_slab, 3), in_order, pieces))
    d_down, d_gate, d_up = after((d_down, d_gate, d_up), in_order.last)
    expert_grads = [d_down, d_gate, d_up]
    while True:
        new = [offset for offset in pieces if offset not in seen]
        seen.update(new)
        whole = in_order(
            *spread_rows(
                table, [pieces[offset] for offset in new], [at_blocks[offset] for offset in new], (slab, width),
                ctx_size, 4, whole,
            )
        )
        if len(seen) == ctx_size:
            break
        if len(seen) < 6:
            index = len(seen) // 2
            expert_grads[index] = in_order(split_experts(expert_grads[index], own_experts))
        ring.step()
    d_query, d_key, d_value, d_out = whole
    d_down, d_gate, d_up = expert_grads
    d_router, gains = unpack_gains(table, [pieces[o] for o in offsets], at_back, experts, packed.shape[0])
    d_ffn_gain, d_attn_gain, head_gains = gains + in_order.last
    return (
        output[None],
        d_tokens[None],
        d_attn_gain,
        d_query,
        d_key,
        d_value,
        head_gains[:head_dim],
        head_gains[head_dim : 2 * head_dim],
        d_out,
        d_ffn_gain,
        d_router,
        d_gate,
        d_up,
        d_down,
    )


def solution(mesh):
    token_split = P("fsdp", "ctx", None)
    row_split = P("fsdp", None)
    return jax.shard_map(
        body,
        mesh=mesh,
        in_specs=(
            token_split, P(), row_split, row_split, row_split, P(), P(), row_split,
            P(), row_split, token_split, token_split, token_split, token_split, token_split,
        ),
        out_specs=(
            token_split, token_split, P(), row_split, row_split, row_split, P(), P(),
            row_split, P(), row_split, token_split, token_split, token_split,
        ),
        check_vma=False,
    )
```

time: 892 us -> 791 us (0.89)
  Pallas kernels: 24.4 us -> 256 us
  matrix products: 172 us -> 4.02 us
  local copies, waits for them, and re-layouts: 114 us -> 49.4 us
  starting transfers between devices: 143 us -> 112 us
  waiting for transfers between devices: 316 us -> 286 us
  between operations: 38.3 us -> 17.9 us
  other arithmetic: 72 us -> 54.9 us
    pallas_call x0 -> x36, Pallas kernels: none -> 230 us  [the longest x3 41.5 us: sum_of_outer(): pl.pallas_call(sum_kernel, grid=(columns // wide, rows // tall), in_specs...]
    dot_general x28 -> x3, matrix products: 172 us -> 4.02 us  [dot(): lax.dot_general(a, b, (contract, ((), ())), precision=precision, preferre...]
    ppermute x24 -> x25, waiting for transfers between devices: 104 us -> 45.1 us  [swap(): return lax.ppermute(v, 'fsdp', [(i, i ^ mask) for i in range(size)])]
    ppermute x64, waiting for transfers between devices: 201 us -> 150 us  [ring_send(): lax.ppermute(v, 'ctx', [(order[i], order[(i + direction) % size]) for i i...]
    all_to_all x4, waiting for transfers between devices: 3.3 us -> 51.4 us  [the longest x2 33 us: collect_pairs(): v = lax.all_to_all(v, 'ctx', split_axis=0, concat_axis=0, tiled=True)]
    reshape x10 -> x2, local copies, waits for them, and re-layouts: 39.5 us -> 0.71 us  [the longest x1 0.7 us: body(): table = table.reshape(-1)]
    all_gather x3, waiting for transfers between devices: 0.02 us -> 27.9 us  [the longest x1 27.9 us: body(): up_w = lax.all_gather(w_up, 'fsdp', axis=0, tiled=True)]
    dynamic_update_slice x23 -> x0, other arithmetic: 21.3 us -> none  [the longest x18 20.3 us: gather_rows(): wholes[index] = lax.dynamic_update_slice_in_dim(wholes[index], part, at, 0)]
  transfers between devices with their start and end apart: 110 -> 101, of which waited for: 46 -> 51; matrix products, arithmetic and copies ran while one was open for 29% -> 9% of each run, Pallas kernels for 3% -> 26%
where the time goes in v2:
time: 791 us; the launch traced here: 780 us
  waiting for transfers between devices  286 us (36%)
  Pallas kernels  256 us (32%)
  starting transfers between devices  112 us (14%)
  other arithmetic  54.9 us (7%)
  local copies, waits for them, and re-layouts  49.4 us (6%)
  between operations  17.9 us (2%)
    ppermute x64, waiting for transfers between devices, ring_send(): lax.ppermute(v, 'ctx', [(order[i], order[(i + direction) % size]) for i i...  150 us
    ppermute x64, starting transfers between devices, ring_send(): lax.ppermute(v, 'ctx', [(order[i], order[(i + direction) % size]) for i i...  69.3 us
    ppermute x25, waiting for transfers between devices, swap(): return lax.ppermute(v, 'fsdp', [(i, i ^ mask) for i in range(size)])  45.1 us
    pallas_call x3, Pallas kernels, sum_of_outer(): pl.pallas_call(sum_kernel, grid=(columns // wide, rows // tall), in_specs...  41.5 us
    pallas_call x2, Pallas kernels, expert_units(): pl.pallas_call(functools.partial(expert_kernel, per=per, place=place, at=...  37.9 us
    all_to_all x2, waiting for transfers between devices, collect_pairs(): v = lax.all_to_all(v, 'ctx', split_axis=0, concat_axis=0, tiled=True)  33 us
    all_gather x1, waiting for transfers between devices, body(): up_w = lax.all_gather(w_up, 'fsdp', axis=0, tiled=True)  27.9 us
    pallas_call x2, Pallas kernels, expert_rows(): pl.pallas_call(expert_rows_kernel, grid=(width // wide,), in_specs=[whole...  27.7 us
  transfers between devices with their start and end apart: 101, of which 51 were waited for; matrix products, arithmetic and copies ran while one was open for 9% of the time, Pallas kernels for 26%

profile of v2, /device:TPU:0, one launch (start us, length us, event | category | flops | bytes accessed | tf_op | source)
XLA Modules:
  0.0 779.9 jit_solution(1149788723963169790)
XLA Ops:
  12.4 3.0 collective-permute-start
  23.8 6.6 merge_experts.3
  36.8 9.2 %collective-permute-done.2.refs_8_ = bf16[128,1536]{1,0:T(8,128)(2,1)S(1)} collective-permute-done((bf16[128,1536]{1,0:T(8,128)(2,1)S(1)}, bf16[128,1536]{1,0:T(8,128)(2,1)S(1)}, u32[]{:S(2)}, u32[]{:S(2)}) %collective-permute-start.2) | collective-permute-done | bytes 393248 | tf_op jit(solution)/shard_map/ppermute | solution.py:835
  50.4 6.6 merge_experts.4
  61.5 6.6 merge_experts.5
  74.6 4.5 all-to-all-start
  79.5 6.4 all-to-all-done
  88.9 9.5 %own_pairs.1 = (bf16[8,6,128,128]{3,2,1,0:T(8,128)(2,1)}, bf16[2048,1536]{1,0:T(8,128)(2,1)}) custom-call(s32[38]{0:T(128)S(1)} %get-tuple-element.886._unused.table_ref, bf16[128,2048]{1,0:T(8,128)(2,1)S(1)} %fusion.2.refs_0_, bf16[128,2048]{1,0:T(8,128)(2,1)S(1)} %collective-permute-done.6.refs_1_, bf16[128,2048]{1,0:T(8,128)(2,1)S(1)} %collective-permute-done.7.refs_2_, ...), custom_call_target="tpu_custom_call" | custom-call | flops 1 | bytes 1 | tf_op jit(solution)/shard_map/own_pairs/pallas_call | solution.py:449
  98.4 4.4 all-to-all-start.1
  102.9 3.2 fusion.9
  110.7 4.7 collective-permute-done.15.refs_2_
  115.4 5.3 collective-permute-done.16.refs_3_
  123.1 14.9 %all-to-all-done.1.q_ref.k_ref.v_ref = bf16[8,6,128,128]{3,2,1,0:T(8,128)(2,1)} async-done(((bf16[8,6,128,128]{3,2,1,0:T(8,128)(2,1)}), bf16[8,6,128,128]{3,2,1,0:T(8,128)(2,1)}, u32[]{:S(2)}, u32[]{:S(2)}) %all-to-all-start.1) | async-done | bytes 1572896 | tf_op jit(solution)/shard_map/all_to_all | solution.py:982
  140.0 9.1 %attend.1 = bf16[8,2,128,128]{3,2,1,0:T(8,128)(2,1)S(1)} custom-call(bf16[8,6,128,128]{3,2,1,0:T(8,128)(2,1)} %all-to-all-done.1.q_ref.k_ref.v_ref, bf16[8,6,128,128]{3,2,1,0:T(8,128)(2,1)} %all-to-all-done.1.q_ref.k_ref.v_ref, bf16[8,6,128,128]{3,2,1,0:T(8,128)(2,1)} %all-to-all-done.1.q_ref.k_ref.v_ref, f32[1,128]{1,0:T(1,128)S(1)} %bitcast.61, ...), custom_call_target="tpu_custom_call" | custom-call | flops 20000000000 | bytes 50000000 | tf_op jit(solution)/shard_map/attend/pallas_call | solution.py:152
  149.8 3.6 all-to-all-start.2
  155.8 13.5 %all-to-all-done.2.m_ref = bf16[8,2,128,128]{3,2,1,0:T(8,128)(2,1)S(1)} async-done(((bf16[8,2,128,128]{3,2,1,0:T(8,128)(2,1)}), bf16[8,2,128,128]{3,2,1,0:T(8,128)(2,1)S(1)}, u32[]{:S(2)}, u32[]{:S(2)}) %all-to-all-start.2) | async-done | bytes 524320 | tf_op jit(solution)/shard_map/all_to_all | solution.py:985
  169.3 3.7 collective-permute-done.19.refs_4_
  179.6 4.0 collective-permute-start.23
  186.1 9.2 %collective-permute-done.23.refs_6_ = bf16[128,2048]{1,0:T(8,128)(2,1)S(1)} collective-permute-done((bf16[128,2048]{1,0:T(8,128)(2,1)}, bf16[128,2048]{1,0:T(8,128)(2,1)S(1)}, u32[]{:S(2)}, u32[]{:S(2)}) %collective-permute-start.23) | collective-permute-done | bytes 524320 | tf_op jit(solution)/shard_map/ppermute | solution.py:835
  209.5 6.4 collective-permute-done.28.refs_2_
  219.3 14.0 %stacked_matmul.1 = (f32[1024,2048]{1,0:T(8,128)}, bf16[1024,2048]{1,0:T(8,128)(2,1)}) custom-call(bf16[2048,2048]{1,0:T(8,128)(2,1)} %all-gather.4.cloned.1.call-done.w_ref.b_ref, bf16[128,2048]{1,0:T(8,128)(2,1)} %bitcast.68, bf16[128,2048]{1,0:T(8,128)(2,1)} %collective-permute-done.18.refs_1_, bf16[128,2048]{1,0:T(8,128)(2,1)} %collective-permute-done.17.refs_2_, ...), custom_call_target="tpu_custom_call" | custom-call | flops 999999995904 | bytes 1000000000 | tf_op jit(solution)/shard_map/stacked_matmul/pallas_call | solution.py:209
  235.9 27.9 %all-gather.8.cloned.1.call-done.up_w_ref = bf16[2048,2048]{1,0:T(8,128)(2,1)} async-done(((bf16[512,2048]{1,0:T(8,128)(2,1)}), bf16[2048,2048]{1,0:T(8,128)(2,1)}) %all-gather.8.cloned.1.call-update) | async-done | bytes 8388624 | tf_op jit(solution)/shard_map/all_gather | solution.py:1027
  265.8 19.0 %expert_units.2 = (bf16[512,2048]{1,0:T(8,128)(2,1)}, bf16[512,2048]{1,0:T(8,128)(2,1)}, bf16[512,2048]{1,0:T(8,128)(2,1)}, f32[2,512,1]{2,1,0:T(8,128)}, bf16[512,2048]{1,0:T(8,128)(2,1)}) custom-call(s32[38]{0:T(128)} %copy-done.22, bf16[2048,16]{1,0:T(8,128)(2,1)} %copy-done.1, s32[8,128,8]{2,1,0:T(8,128)} %copy.64.routes_ref, ...), custom_call_target="tpu_custom_call" | custom-call | flops 999999995904 | bytes 1000000000 | tf_op jit(solution)/shard_map/expert_units/pallas_call | solution.py:273
  289.3 4.8 fusion.27
  297.5 18.9 %expert_units.3 = (bf16[512,2048]{1,0:T(8,128)(2,1)}, bf16[512,2048]{1,0:T(8,128)(2,1)}, bf16[512,2048]{1,0:T(8,128)(2,1)}, f32[2,512,1]{2,1,0:T(8,128)}, bf16[512,2048]{1,0:T(8,128)(2,1)}) custom-call(s32[38]{0:T(128)} %copy-done.22, bf16[2048,16]{1,0:T(8,128)(2,1)} %copy-done.1, s32[8,128,8]{2,1,0:T(8,128)} %copy.64.routes_ref, ...), custom_call_target="tpu_custom_call" | custom-call | flops 999999995904 | bytes 1000000000 | tf_op jit(solution)/shard_map/expert_units/pallas_call | solution.py:273
  316.4 13.9 %expert_rows.2 = bf16[512,2048]{1,0:T(8,128)(2,1)} custom-call(bf16[512,2048]{1,0:T(8,128)(2,1)} %get-tuple-element.580.gate_ref.refs_3_, bf16[512,2048]{1,0:T(8,128)(2,1)} %get-tuple-element.596.up_ref.refs_3_, bf16[2048,2048]{1,0:T(8,128)(2,1)} %all-gather.6.cloned.1.call-done.gate_w_ref, bf16[2048,2048]{1,0:T(8,128)(2,1)} %all-gather.8.cloned.1.call-done.up_w_ref), custom_call_target="tpu_custom_call" | custom-call | flops 999999995904 | bytes 1000000000 | tf_op jit(solution)/shard_map/expert_rows/pallas_call | solution.py:323
  334.5 13.9 %expert_rows.3 = bf16[512,2048]{1,0:T(8,128)(2,1)} custom-call(bf16[512,2048]{1,0:T(8,128)(2,1)} %get-tuple-element.579.gate_ref.refs_2_, bf16[512,2048]{1,0:T(8,128)(2,1)} %get-tuple-element.595.up_ref.refs_2_, bf16[2048,2048]{1,0:T(8,128)(2,1)} %all-gather.6.cloned.1.call-done.gate_w_ref, bf16[2048,2048]{1,0:T(8,128)(2,1)} %all-gather.8.cloned.1.call-done.up_w_ref), custom_call_target="tpu_custom_call" | custom-call | flops 999999995904 | bytes 1000000000 | tf_op jit(solution)/shard_map/expert_rows/pallas_call | solution.py:323
  348.3 8.8 %times_transpose.2 = bf16[512,2048]{1,0:T(8,128)(2,1)} custom-call(bf16[512,2048]{1,0:T(8,128)(2,1)} %get-tuple-element.626.a_ref.refs_3_, bf16[2048,2048]{1,0:T(8,128)(2,1)} %all-gather.4.cloned.1.call-done.w_ref.b_ref), custom_call_target="tpu_custom_call" | custom-call | flops 999999995904 | bytes 1000000000 | tf_op jit(solution)/shard_map/times_transpose/pallas_call | solution.py:342
  362.3 8.8 %times_transpose.3 = bf16[512,2048]{1,0:T(8,128)(2,1)} custom-call(bf16[512,2048]{1,0:T(8,128)(2,1)} %get-tuple-element.625.a_ref.refs_2_, bf16[2048,2048]{1,0:T(8,128)(2,1)} %all-gather.4.cloned.1.call-done.w_ref.b_ref), custom_call_target="tpu_custom_call" | custom-call | flops 999999995904 | bytes 1000000000 | tf_op jit(solution)/shard_map/times_transpose/pallas_call | solution.py:342
  384.2 4.6 all-to-all-start.3
  392.2 3.3 all-to-all-done.3
  402.1 5.6 collective-permute-done.42
  413.2 13.5 %sum_of_outer.3 = bf16[2048,2048]{1,0:T(8,128)(2,1)} custom-call(bf16[512,2048]{1,0:T(8,128)(2,1)} %get-tuple-element.593.refs_0_, bf16[512,2048]{1,0:T(8,128)(2,1)} %get-tuple-element.594.refs_1_, bf16[512,2048]{1,0:T(8,128)(2,1)} %get-tuple-element.579.gate_ref.refs_2_, bf16[512,2048]{1,0:T(8,128)(2,1)} %get-tuple-element.580.gate_ref.refs_3_), custom_call_target="tpu_custom_call" | custom-call | flops 999999995904 | bytes 1000000000 | tf_op jit(solution)/shard_map/sum_of_outer/pallas_call | solution.py:366
  433.9 3.7 matmul_to_pairs.1
  437.6 14.6 %sum_of_outer.4 = bf16[2048,2048]{1,0:T(8,128)(2,1)} custom-call(bf16[512,2048]{1,0:T(8,128)(2,1)} %get-tuple-element.593.refs_0_, bf16[512,2048]{1,0:T(8,128)(2,1)} %get-tuple-element.594.refs_1_, bf16[512,2048]{1,0:T(8,128)(2,1)} %get-tuple-element.595.up_ref.refs_2_, bf16[512,2048]{1,0:T(8,128)(2,1)} %get-tuple-element.596.up_ref.refs_3_), custom_call_target="tpu_custom_call" | custom-call | flops 999999995904 | bytes 1000000000 | tf_op jit(solution)/shard_map/sum_of_outer/pallas_call | solution.py:366
  452.2 2.9 out_grads.1
  458.8 3.5 all-to-all-start.4
  468.7 2.7 convert.43
  474.4 3.5 all-to-all-done.4.m_ref
  478.0 16.2 %attend_back.1 = (bf16[8,6,128,128]{3,2,1,0:T(8,128)(2,1)}, f32[8,128]{1,0:T(8,128)S(1)}) custom-call(bf16[8,6,128,128]{3,2,1,0:T(8,128)(2,1)} %all-to-all-done.1.q_ref.k_ref.v_ref, bf16[8,6,128,128]{3,2,1,0:T(8,128)(2,1)} %all-to-all-done.1.q_ref.k_ref.v_ref, bf16[8,6,128,128]{3,2,1,0:T(8,128)(2,1)} %all-to-all-done.1.q_ref.k_ref.v_ref, ...), custom_call_target="tpu_custom_call" | custom-call | flops 999999995904 | bytes 1000000000 | tf_op jit(solution)/shard_map/attend_back/pallas_call | solution.py:169
  494.2 2.6 add_convert_fusion.6
  498.8 4.3 all-to-all-start.5
  503.1 13.5 %sum_of_outer.5 = bf16[2048,2048]{1,0:T(8,128)(2,1)} custom-call(bf16[512,2048]{1,0:T(8,128)(2,1)} %get-tuple-element.623.refs_0_, bf16[512,2048]{1,0:T(8,128)(2,1)} %get-tuple-element.624.refs_1_, bf16[512,2048]{1,0:T(8,128)(2,1)} %get-tuple-element.625.a_ref.refs_2_, bf16[512,2048]{1,0:T(8,128)(2,1)} %get-tuple-element.626.a_ref.refs_3_), custom_call_target="tpu_custom_call" | custom-call | flops 999999995904 | bytes 1000000000 | tf_op jit(solution)/shard_map/sum_of_outer/pallas_call | solution.py:366
  519.1 2.9 add_convert_fusion.5
  523.4 19.5 %all-to-all-done.5.g_ref = bf16[8,6,128,128]{3,2,1,0:T(8,128)(2,1)} async-done(((bf16[8,6,128,128]{3,2,1,0:T(8,128)(2,1)}), bf16[8,6,128,128]{3,2,1,0:T(8,128)(2,1)}, u32[]{:S(2)}, u32[]{:S(2)}) %all-to-all-start.5) | async-done | bytes 1572896 | tf_op jit(solution)/shard_map/all_to_all | solution.py:985
  542.8 6.1 pair_weights.2
  549.0 6.1 pair_weights.3
  569.8 3.9 collective-permute-done.61
  573.8 8.2 %pair_normed.1 = (f32[128,2048]{1,0:T(8,128)S(1)}, bf16[128,2048]{1,0:T(8,128)(2,1)S(1)}, f32[128,2048]{1,0:T(8,128)S(1)}, bf16[128,2048]{1,0:T(8,128)(2,1)S(1)}) custom-call(bf16[8,6,128,128]{3,2,1,0:T(8,128)(2,1)} %all-to-all-done.5.g_ref, bf16[2048,1536]{1,0:T(8,128)(2,1)} %get-tuple-element.652.w_ref), custom_call_target="tpu_custom_call" | custom-call | flops 999999995904 | bytes 1000000000 | tf_op jit(solution)/shard_map/pair_normed/pallas_call | solution.py:606
  589.7 19.7 %collective-permute-done.66 = bf16[64,2048]{1,0:T(8,128)(2,1)S(1)} collective-permute-done((bf16[64,2048]{1,0:T(8,128)(2,1)S(1)}, bf16[64,2048]{1,0:T(8,128)(2,1)S(1)}, u32[]{:S(2)}, u32[]{:S(2)}) %collective-permute-start.66) | collective-permute-done | bytes 262176 | tf_op jit(solution)/shard_map/ppermute | solution.py:835
  613.1 15.0 %collective-permute-done.70 = bf16[128,2048]{1,0:T(8,128)(2,1)S(1)} collective-permute-done((bf16[128,2048]{1,0:T(8,128)(2,1)S(1)}, bf16[128,2048]{1,0:T(8,128)(2,1)S(1)}, u32[]{:S(2)}, u32[]{:S(2)}) %collective-permute-start.70) | collective-permute-done | bytes 524320 | tf_op jit(solution)/shard_map/ppermute | solution.py:823
  638.8 10.8 %collective-permute-done.75.right_ref = bf16[256,1536]{1,0:T(8,128)(2,1)S(1)} collective-permute-done((bf16[256,1536]{1,0:T(8,128)(2,1)}, bf16[256,1536]{1,0:T(8,128)(2,1)S(1)}, u32[]{:S(2)}, u32[]{:S(2)}) %collective-permute-start.75) | collective-permute-done | bytes 786464 | tf_op jit(solution)/shard_map/ppermute | solution.py:835
  655.5 8.4 %collective-permute-done.79.refs_2_ = bf16[64,1536]{1,0:T(8,128)(2,1)S(1)} collective-permute-done((bf16[64,1536]{1,0:T(8,128)(2,1)S(1)}, bf16[64,1536]{1,0:T(8,128)(2,1)S(1)}, u32[]{:S(2)}, u32[]{:S(2)}) %collective-permute-start.79) | collective-permute-done | bytes 196640 | tf_op jit(solution)/shard_map/ppermute | solution.py:823
  663.9 7.7 collective-permute-done.80.refs_3_
  678.3 4.5 split_experts.3
  682.7 16.8 %collective-permute-done.81.refs_0_.refs_2_ = bf16[272,2048]{1,0:T(8,128)(2,1)S(1)} collective-permute-done((bf16[272,2048]{1,0:T(8,128)(2,1)S(1)}, bf16[272,2048]{1,0:T(8,128)(2,1)S(1)}, u32[]{:S(2)}, u32[]{:S(2)}) %collective-permute-start.81) | collective-permute-done | bytes 1114144 | tf_op jit(solution)/shard_map/ppermute | solution.py:835
  702.2 4.5 split_experts.4
  706.7 2.6 spread_rows.6
  709.4 17.1 %collective-permute-done.83.refs_0_.refs_4_ = bf16[272,2048]{1,0:T(8,128)(2,1)} collective-permute-done((bf16[272,2048]{1,0:T(8,128)(2,1)S(1)}, bf16[272,2048]{1,0:T(8,128)(2,1)}, u32[]{:S(2)}, u32[]{:S(2)}) %collective-permute-start.83) | collective-permute-done | bytes 1114144 | tf_op jit(solution)/shard_map/ppermute | solution.py:835
  728.7 4.5 split_experts.5
  733.2 3.7 spread_rows.7
  736.9 15.2 %collective-permute-done.85.refs_0_.refs_6_ = bf16[272,2048]{1,0:T(8,128)(2,1)S(1)} collective-permute-done((bf16[272,2048]{1,0:T(8,128)(2,1)}, bf16[272,2048]{1,0:T(8,128)(2,1)S(1)}, u32[]{:S(2)}, u32[]{:S(2)}) %collective-permute-start.85) | collective-permute-done | bytes 1114144 | tf_op jit(solution)/shard_map/ppermute | solution.py:835
  755.3 2.6 spread_rows.8
  758.0 7.0 collective-permute-done.87
  (474 shorter events, 216.7 us)
Async XLA Ops:
  7.2 142.7 %all-gather.4.cloned.1.call-start = ((), (), s32[]{:S(2)}) async-start(), calls=%async_computation.9 | async-start | bytes 10485760 | tf_op jit(solution)/shard_map/all_gather | solution.py:1018
  30.4 176.3 %all-gather.6.cloned.1.call-start = ((), (), s32[]{:S(2)}) async-start(), calls=%async_computation.10 | async-start | bytes 10485760 | tf_op jit(solution)/shard_map/all_gather | solution.py:1023
  32.3 18.0 %collective-permute-start.7 = (bf16[128,2048]{1,0:T(8,128)(2,1)S(1)}, bf16[128,2048]{1,0:T(8,128)(2,1)S(1)}, u32[]{:S(2)}, u32[]{:S(2)}) collective-permute-start(bf16[128,2048]{1,0:T(8,128)(2,1)S(1)} %fusion.2.refs_0_), channel_id=1, source_target_pairs={{0,2},{1,3},{2,0},{3,1},{4,6},{5,7},{6,4},{7,5},{8,10},{9,11},{10,... | collective-permute-start | bytes 1572872 | tf_op jit(solution)/shard_map/ppermute | solution.py:823
  36.3 25.2 %collective-permute-start.6 = (bf16[128,2048]{1,0:T(8,128)(2,1)S(1)}, bf16[128,2048]{1,0:T(8,128)(2,1)S(1)}, u32[]{:S(2)}, u32[]{:S(2)}) collective-permute-start(bf16[128,2048]{1,0:T(8,128)(2,1)S(1)} %fusion.2.refs_0_), channel_id=1, source_target_pairs={{0,1},{1,0},{2,3},{3,2},{4,5},{5,4},{6,7},{7,6},{8,9},{9,8},{10,11... | collective-permute-start | bytes 1572872 | tf_op jit(solution)/shard_map/ppermute | solution.py:823
  36.5 50.4 %collective-permute-start.13 = (bf16[512,1536]{1,0:T(8,128)(2,1)}, bf16[512,1536]{1,0:T(8,128)(2,1)}, u32[]{:S(2)}, u32[]{:S(2)}) collective-permute-start(bf16[512,1536]{1,0:T(8,128)(2,1)} %copy-done.31), channel_id=1, source_target_pairs={{0,1},{1,0},{2,3},{3,2},{4,5},{5,4},{6,7},{7,6},{8,9},{9,8},{10,11... | collective-permute-start | bytes 4718600 | tf_op jit(solution)/shard_map/ppermute | solution.py:823
  98.4 39.5 %all-to-all-start.1 = ((bf16[8,6,128,128]{3,2,1,0:T(8,128)(2,1)}), bf16[8,6,128,128]{3,2,1,0:T(8,128)(2,1)}, u32[]{:S(2)}, u32[]{:S(2)}) async-start(bf16[8,6,128,128]{3,2,1,0:T(8,128)(2,1)} %get-tuple-element.451), calls=%async_computation.1 | async-start | bytes 3145728 | tf_op jit(solution)/shard_map/all_to_all | solution.py:982
  137.9 15.6 %collective-permute-start.17 = (bf16[128,2048]{1,0:T(8,128)(2,1)}, bf16[128,2048]{1,0:T(8,128)(2,1)}, u32[]{:S(2)}, u32[]{:S(2)}) collective-permute-start(bf16[128,2048]{1,0:T(8,128)(2,1)} %bitcast.66), channel_id=1, source_target_pairs={{0,8},{8,16},{16,24},{24,28},{28,20},{20,12},{12,4},{4,0},{1,9},{9... | collective-permute-start | bytes 1572872 | tf_op jit(solution)/shard_map/ppermute | solution.py:835
  137.9 15.6 %collective-permute-start.18 = (bf16[128,2048]{1,0:T(8,128)(2,1)}, bf16[128,2048]{1,0:T(8,128)(2,1)}, u32[]{:S(2)}, u32[]{:S(2)}) collective-permute-start(bf16[128,2048]{1,0:T(8,128)(2,1)} %bitcast.67), channel_id=1, source_target_pairs={{0,4},{8,0},{16,8},{24,16},{28,24},{20,28},{12,20},{4,12},{1,5},{9... | collective-permute-start | bytes 1572872 | tf_op jit(solution)/shard_map/ppermute | solution.py:835
  149.8 19.5 %all-to-all-start.2 = ((bf16[8,2,128,128]{3,2,1,0:T(8,128)(2,1)}), bf16[8,2,128,128]{3,2,1,0:T(8,128)(2,1)S(1)}, u32[]{:S(2)}, u32[]{:S(2)}) async-start(bf16[8,2,128,128]{3,2,1,0:T(8,128)(2,1)} %copy-done.14), calls=%async_computation.2 | async-start | bytes 1048576 | tf_op jit(solution)/shard_map/all_to_all | solution.py:985
  153.5 110.3 %all-gather.8.cloned.1.call-start = ((), (), s32[]{:S(2)}) async-start(), calls=%async_computation.11 | async-start | bytes 10485760 | tf_op jit(solution)/shard_map/all_gather | solution.py:1027
  153.5 19.5 %collective-permute-start.19 = (bf16[128,2048]{1,0:T(8,128)(2,1)}, bf16[128,2048]{1,0:T(8,128)(2,1)}, u32[]{:S(2)}, u32[]{:S(2)}) collective-permute-start(bf16[128,2048]{1,0:T(8,128)(2,1)} %collective-permute-done.17.refs_2_), channel_id=1, source_target_pairs={{0,8},{8,16},{16,24},{24,28},{28,20},{20,12},{12,4},{4,0},{1,9},{9... | collective-permute-start | bytes 1572872 | tf_op jit(solution)/shard_map/ppermute | solution.py:835
  155.5 20.0 %collective-permute-start.20 = (bf16[128,2048]{1,0:T(8,128)(2,1)}, bf16[128,2048]{1,0:T(8,128)(2,1)}, u32[]{:S(2)}, u32[]{:S(2)}) collective-permute-start(bf16[128,2048]{1,0:T(8,128)(2,1)} %collective-permute-done.18.refs_1_), channel_id=1, source_target_pairs={{0,4},{8,0},{16,8},{24,16},{28,24},{20,28},{12,20},{4,12},{1,5},{9... | collective-permute-start | bytes 1572872 | tf_op jit(solution)/shard_map/ppermute | solution.py:835
  179.6 15.7 %collective-permute-start.23 = (bf16[128,2048]{1,0:T(8,128)(2,1)}, bf16[128,2048]{1,0:T(8,128)(2,1)S(1)}, u32[]{:S(2)}, u32[]{:S(2)}) collective-permute-start(bf16[128,2048]{1,0:T(8,128)(2,1)} %collective-permute-done.19.refs_4_), channel_id=1, source_target_pairs={{0,8},{8,16},{16,24},{24,28},{28,20},{20,12},{12,4},{4,0},{1,9},{9... | collective-permute-start | bytes 1572872 | tf_op jit(solution)/shard_map/ppermute | solution.py:835
  183.6 13.8 %collective-permute-start.24 = (bf16[128,2048]{1,0:T(8,128)(2,1)}, bf16[128,2048]{1,0:T(8,128)(2,1)S(1)}, u32[]{:S(2)}, u32[]{:S(2)}) collective-permute-start(bf16[128,2048]{1,0:T(8,128)(2,1)} %collective-permute-done.20.refs_3_), channel_id=1, source_target_pairs={{0,4},{8,0},{16,8},{24,16},{28,24},{20,28},{12,20},{4,12},{1,5},{9... | collective-permute-start | bytes 1572872 | tf_op jit(solution)/shard_map/ppermute | solution.py:835
  183.7 16.5 %collective-permute-start.25 = (bf16[128,2048]{1,0:T(8,128)(2,1)S(1)}, bf16[128,2048]{1,0:T(8,128)(2,1)S(1)}, u32[]{:S(2)}, u32[]{:S(2)}) collective-permute-start(bf16[128,2048]{1,0:T(8,128)(2,1)S(1)} %add_convert_fusion.14), channel_id=1, source_target_pairs={{0,2},{1,3},{2,0},{3,1},{4,6},{5,7},{6,4},{7,5},{8,10},{9,11},{10,... | collective-permute-start | bytes 1572872 | tf_op jit(solution)/shard_map/ppermute | solution.py:823
  202.4 13.6 %collective-permute-start.28 = (bf16[128,2048]{1,0:T(8,128)(2,1)}, bf16[128,2048]{1,0:T(8,128)(2,1)}, u32[]{:S(2)}, u32[]{:S(2)}) collective-permute-start(bf16[128,2048]{1,0:T(8,128)(2,1)} %multiply_convert_fusion.refs_0_), channel_id=1, source_target_pairs={{0,8},{8,16},{16,24},{24,28},{28,20},{20,12},{12,4},{4,0},{1,9},{9... | collective-permute-start | bytes 1572872 | tf_op jit(solution)/shard_map/ppermute | solution.py:835
  202.7 14.5 %collective-permute-start.29 = (bf16[128,2048]{1,0:T(8,128)(2,1)}, bf16[128,2048]{1,0:T(8,128)(2,1)}, u32[]{:S(2)}, u32[]{:S(2)}) collective-permute-start(bf16[128,2048]{1,0:T(8,128)(2,1)} %multiply_convert_fusion.refs_0_), channel_id=1, source_target_pairs={{0,4},{8,0},{16,8},{24,16},{28,24},{20,28},{12,20},{4,12},{1,5},{9... | collective-permute-start | bytes 1572872 | tf_op jit(solution)/shard_map/ppermute | solution.py:835
  217.2 18.7 %collective-permute-start.30 = (bf16[128,2048]{1,0:T(8,128)(2,1)}, bf16[128,2048]{1,0:T(8,128)(2,1)}, u32[]{:S(2)}, u32[]{:S(2)}) collective-permute-start(bf16[128,2048]{1,0:T(8,128)(2,1)} %collective-permute-done.28.refs_2_), channel_id=1, source_target_pairs={{0,8},{8,16},{16,24},{24,28},{28,20},{20,12},{12,4},{4,0},{1,9},{9... | collective-permute-start | bytes 1572872 | tf_op jit(solution)/shard_map/ppermute | solution.py:835
  217.7 18.2 %collective-permute-start.31 = (bf16[128,2048]{1,0:T(8,128)(2,1)}, bf16[128,2048]{1,0:T(8,128)(2,1)}, u32[]{:S(2)}, u32[]{:S(2)}) collective-permute-start(bf16[128,2048]{1,0:T(8,128)(2,1)} %collective-permute-done.29.refs_1_), channel_id=1, source_target_pairs={{0,4},{8,0},{16,8},{24,16},{28,24},{20,28},{12,20},{4,12},{1,5},{9... | collective-permute-start | bytes 1572872 | tf_op jit(solution)/shard_map/ppermute | solution.py:835
  263.8 21.0 %collective-permute-start.32 = (bf16[128,2048]{1,0:T(8,128)(2,1)}, bf16[128,2048]{1,0:T(8,128)(2,1)}, u32[]{:S(2)}, u32[]{:S(2)}) collective-permute-start(bf16[128,2048]{1,0:T(8,128)(2,1)} %collective-permute-done.30.refs_0_), channel_id=1, source_target_pairs={{0,8},{8,16},{16,24},{24,28},{28,20},{20,12},{12,4},{4,0},{1,9},{9... | collective-permute-start | bytes 1572872 | tf_op jit(solution)/shard_map/ppermute | solution.py:835
  265.3 19.5 %collective-permute-start.33 = (bf16[128,2048]{1,0:T(8,128)(2,1)}, bf16[128,2048]{1,0:T(8,128)(2,1)}, u32[]{:S(2)}, u32[]{:S(2)}) collective-permute-start(bf16[128,2048]{1,0:T(8,128)(2,1)} %collective-permute-done.31.refs_3_), channel_id=1, source_target_pairs={{0,4},{8,0},{16,8},{24,16},{28,24},{20,28},{12,20},{4,12},{1,5},{9... | collective-permute-start | bytes 1572872 | tf_op jit(solution)/shard_map/ppermute | solution.py:835
  332.4 15.9 %collective-permute-start.36 = (bf16[64,2048]{1,0:T(8,128)(2,1)}, bf16[64,2048]{1,0:T(8,128)(2,1)}, u32[]{:S(2)}, u32[]{:S(2)}) collective-permute-start(bf16[64,2048]{1,0:T(8,128)(2,1)} %get-tuple-element.873), channel_id=1, source_target_pairs={{0,8},{8,16},{16,24},{24,28},{28,20},{20,12},{12,4},{4,0},{1,9},{9... | collective-permute-start | bytes 786440 | tf_op jit(solution)/shard_map/ppermute | solution.py:835
  333.9 14.4 %collective-permute-start.37 = (bf16[64,2048]{1,0:T(8,128)(2,1)}, bf16[64,2048]{1,0:T(8,128)(2,1)}, u32[]{:S(2)}, u32[]{:S(2)}) collective-permute-start(bf16[64,2048]{1,0:T(8,128)(2,1)} %get-tuple-element.872), channel_id=1, source_target_pairs={{0,4},{8,0},{16,8},{24,16},{28,24},{20,28},{12,20},{4,12},{1,5},{9... | collective-permute-start | bytes 786440 | tf_op jit(solution)/shard_map/ppermute | solution.py:835
  376.3 15.9 %collective-permute-start.40 = (bf16[128,2048]{1,0:T(8,128)(2,1)}, bf16[128,2048]{1,0:T(8,128)(2,1)}, u32[]{:S(2)}, u32[]{:S(2)}) collective-permute-start(bf16[128,2048]{1,0:T(8,128)(2,1)} %add_convert_fusion.13), channel_id=1, source_target_pairs={{0,8},{8,16},{16,24},{24,28},{28,20},{20,12},{12,4},{4,0},{1,9},{9... | collective-permute-start | bytes 1572872 | tf_op jit(solution)/shard_map/ppermute | solution.py:835
  388.8 287.4 %reduce-scatter.6.cloned.1.call-start = ((), (), s32[]{:S(2)}) async-start(), calls=%async_computation.13 | async-start | bytes 10485760 | tf_op jit(solution)/shard_map/reduce_scatter | solution.py:1115
  389.9 36.8 %collective-permute-start.44 = (bf16[64,2048]{1,0:T(8,128)(2,1)}, bf16[64,2048]{1,0:T(8,128)(2,1)}, u32[]{:S(2)}, u32[]{:S(2)}) collective-permute-start(bf16[64,2048]{1,0:T(8,128)(2,1)} %get-tuple-element.865), channel_id=1, source_target_pairs={{0,8},{8,16},{16,24},{24,28},{28,20},{20,12},{12,4},{4,0},{1,9},{9... | collective-permute-start | bytes 786440 | tf_op jit(solution)/shard_map/ppermute | solution.py:835
  391.9 34.8 %collective-permute-start.45 = (bf16[64,2048]{1,0:T(8,128)(2,1)}, bf16[64,2048]{1,0:T(8,128)(2,1)}, u32[]{:S(2)}, u32[]{:S(2)}) collective-permute-start(bf16[64,2048]{1,0:T(8,128)(2,1)} %get-tuple-element.864), channel_id=1, source_target_pairs={{0,4},{8,0},{16,8},{24,16},{28,24},{20,28},{12,20},{4,12},{1,5},{9... | collective-permute-start | bytes 786440 | tf_op jit(solution)/shard_map/ppermute | solution.py:835
  412.6 14.1 %collective-permute-start.46 = (bf16[128,2048]{1,0:T(8,128)(2,1)}, bf16[128,2048]{1,0:T(8,128)(2,1)}, u32[]{:S(2)}, u32[]{:S(2)}) collective-permute-start(bf16[128,2048]{1,0:T(8,128)(2,1)} %get-tuple-element.600.refs_0_), channel_id=1, source_target_pairs={{0,2},{1,3},{2,0},{3,1},{4,6},{5,7},{6,4},{7,5},{8,10},{9,11},{10,... | collective-permute-start | bytes 1572872 | tf_op jit(solution)/shard_map/ppermute | solution.py:823
  413.2 19.1 %collective-permute-start.47 = (bf16[128,2048]{1,0:T(8,128)(2,1)}, bf16[128,2048]{1,0:T(8,128)(2,1)}, u32[]{:S(2)}, u32[]{:S(2)}) collective-permute-start(bf16[128,2048]{1,0:T(8,128)(2,1)} %get-tuple-element.600.refs_0_), channel_id=1, source_target_pairs={{0,1},{1,0},{2,3},{3,2},{4,5},{5,4},{6,7},{7,6},{8,9},{9,8},{10,11... | collective-permute-start | bytes 1572872 | tf_op jit(solution)/shard_map/ppermute | solution.py:823
  429.4 29.4 %collective-permute-start.49 = (bf16[128,2048]{1,0:T(8,128)(2,1)}, bf16[128,2048]{1,0:T(8,128)(2,1)}, u32[]{:S(2)}, u32[]{:S(2)}) collective-permute-start(bf16[128,2048]{1,0:T(8,128)(2,1)} %pad_maximum_fusion.8), channel_id=1, source_target_pairs={{0,8},{8,16},{16,24},{24,28},{28,20},{20,12},{12,4},{4,0},{1,9},{9... | collective-permute-start | bytes 1572872 | tf_op jit(solution)/shard_map/ppermute | solution.py:835
  430.9 27.9 %collective-permute-start.50 = (bf16[128,2048]{1,0:T(8,128)(2,1)}, bf16[128,2048]{1,0:T(8,128)(2,1)}, u32[]{:S(2)}, u32[]{:S(2)}) collective-permute-start(bf16[128,2048]{1,0:T(8,128)(2,1)} %pad_maximum_fusion.9), channel_id=1, source_target_pairs={{0,4},{8,0},{16,8},{24,16},{28,24},{20,28},{12,20},{4,12},{1,5},{9... | collective-permute-start | bytes 1572872 | tf_op jit(solution)/shard_map/ppermute | solution.py:835
  458.8 19.1 %all-to-all-start.4 = ((bf16[8,2,128,128]{3,2,1,0:T(8,128)(2,1)}), bf16[8,2,128,128]{3,2,1,0:T(8,128)(2,1)S(1)}, u32[]{:S(2)}, u32[]{:S(2)}) async-start(bf16[8,2,128,128]{3,2,1,0:T(8,128)(2,1)} %matmul_to_pairs.1), calls=%async_computation.4 | async-start | bytes 1048576 | tf_op jit(solution)/shard_map/all_to_all | solution.py:982
  462.3 31.8 %collective-permute-start.51 = (f32[17,2048]{1,0:T(8,128)}, f32[17,2048]{1,0:T(8,128)}, u32[]{:S(2)}, u32[]{:S(2)}) collective-permute-start(f32[17,2048]{1,0:T(8,128)} %pad_maximum_fusion.15), channel_id=1, source_target_pairs={{0,1},{1,0},{2,3},{3,2},{4,5},{5,4},{6,7},{7,6},{8,9},{9,8},{10,11... | collective-permute-start | bytes 417800 | tf_op jit(solution)/shard_map/ppermute | solution.py:823
  464.5 29.6 %collective-permute-start.52 = (bf16[128,2048]{1,0:T(8,128)(2,1)}, bf16[128,2048]{1,0:T(8,128)(2,1)}, u32[]{:S(2)}, u32[]{:S(2)}) collective-permute-start(bf16[128,2048]{1,0:T(8,128)(2,1)} %add_convert_fusion.9), channel_id=1, source_target_pairs={{0,8},{8,16},{16,24},{24,28},{28,20},{20,12},{12,4},{4,0},{1,9},{9... | collective-permute-start | bytes 1572872 | tf_op jit(solution)/shard_map/ppermute | solution.py:835
  468.6 25.6 %collective-permute-start.53 = (bf16[128,2048]{1,0:T(8,128)(2,1)}, bf16[128,2048]{1,0:T(8,128)(2,1)}, u32[]{:S(2)}, u32[]{:S(2)}) collective-permute-start(bf16[128,2048]{1,0:T(8,128)(2,1)} %add_convert_fusion.8), channel_id=1, source_target_pairs={{0,4},{8,0},{16,8},{24,16},{28,24},{20,28},{12,20},{4,12},{1,5},{9... | collective-permute-start | bytes 1572872 | tf_op jit(solution)/shard_map/ppermute | solution.py:835
  472.2 70.6 %collective-permute-start.57 = (bf16[32,2048]{1,0:T(8,128)(2,1)}, bf16[32,2048]{1,0:T(8,128)(2,1)}, u32[]{:S(2)}, u32[]{:S(2)}) collective-permute-start(bf16[32,2048]{1,0:T(8,128)(2,1)} %get-tuple-element.859), channel_id=1, source_target_pairs={{0,8},{8,16},{16,24},{24,28},{28,20},{20,12},{12,4},{4,0},{1,9},{9... | collective-permute-start | bytes 393224 | tf_op jit(solution)/shard_map/ppermute | solution.py:835
  474.0 68.9 %collective-permute-start.58 = (bf16[32,2048]{1,0:T(8,128)(2,1)}, bf16[32,2048]{1,0:T(8,128)(2,1)}, u32[]{:S(2)}, u32[]{:S(2)}) collective-permute-start(bf16[32,2048]{1,0:T(8,128)(2,1)} %get-tuple-element.858), channel_id=1, source_target_pairs={{0,4},{8,0},{16,8},{24,16},{28,24},{20,28},{12,20},{4,12},{1,5},{9... | collective-permute-start | bytes 393224 | tf_op jit(solution)/shard_map/ppermute | solution.py:835
  496.7 22.3 %collective-permute-start.54 = (bf16[128,2048]{1,0:T(8,128)(2,1)}, bf16[128,2048]{1,0:T(8,128)(2,1)}, u32[]{:S(2)}, u32[]{:S(2)}) collective-permute-start(bf16[128,2048]{1,0:T(8,128)(2,1)} %get-tuple-element.861), channel_id=1, source_target_pairs={{0,8},{8,16},{16,24},{24,28},{28,20},{20,12},{12,4},{4,0},{1,9},{9... | collective-permute-start | bytes 1572872 | tf_op jit(solution)/shard_map/ppermute | solution.py:835
  496.7 22.3 %collective-permute-start.55 = (bf16[128,2048]{1,0:T(8,128)(2,1)}, bf16[128,2048]{1,0:T(8,128)(2,1)}, u32[]{:S(2)}, u32[]{:S(2)}) collective-permute-start(bf16[128,2048]{1,0:T(8,128)(2,1)} %get-tuple-element.860), channel_id=1, source_target_pairs={{0,4},{8,0},{16,8},{24,16},{28,24},{20,28},{12,20},{4,12},{1,5},{9... | collective-permute-start | bytes 1572872 | tf_op jit(solution)/shard_map/ppermute | solution.py:835
  498.8 44.1 %all-to-all-start.5 = ((bf16[8,6,128,128]{3,2,1,0:T(8,128)(2,1)}), bf16[8,6,128,128]{3,2,1,0:T(8,128)(2,1)}, u32[]{:S(2)}, u32[]{:S(2)}) async-start(bf16[8,6,128,128]{3,2,1,0:T(8,128)(2,1)} %get-tuple-element.637), calls=%async_computation.5 | async-start | bytes 3145728 | tf_op jit(solution)/shard_map/all_to_all | solution.py:985
  503.1 173.2 %reduce-scatter.8.cloned.1.call-start = ((), (), s32[]{:S(2)}) async-start(), calls=%async_computation.14 | async-start | bytes 10485760 | tf_op jit(solution)/shard_map/reduce_scatter | solution.py:1115
  519.0 159.3 %reduce-scatter.4.cloned.1.call-start = ((), (), s32[]{:S(2)}) async-start(), calls=%async_computation.12 | async-start | bytes 10485760 | tf_op jit(solution)/shard_map/reduce_scatter | solution.py:1115
  560.8 12.8 %collective-permute-start.61 = (bf16[128,1536]{1,0:T(8,128)(2,1)S(1)}, bf16[128,1536]{1,0:T(8,128)(2,1)S(1)}, u32[]{:S(2)}, u32[]{:S(2)}) collective-permute-start(bf16[128,1536]{1,0:T(8,128)(2,1)S(1)} %get-tuple-element.853), channel_id=1, source_target_pairs={{0,8},{8,16},{16,24},{24,28},{28,20},{20,12},{12,4},{4,0},{1,9},{9... | collective-permute-start | bytes 1179656 | tf_op jit(solution)/shard_map/ppermute | solution.py:835
  561.0 12.8 %collective-permute-start.62 = (bf16[128,1536]{1,0:T(8,128)(2,1)S(1)}, bf16[128,1536]{1,0:T(8,128)(2,1)S(1)}, u32[]{:S(2)}, u32[]{:S(2)}) collective-permute-start(bf16[128,1536]{1,0:T(8,128)(2,1)S(1)} %get-tuple-element.852), channel_id=1, source_target_pairs={{0,4},{8,0},{16,8},{24,16},{28,24},{20,28},{12,20},{4,12},{1,5},{9... | collective-permute-start | bytes 1179656 | tf_op jit(solution)/shard_map/ppermute | solution.py:835
  567.5 18.4 %collective-permute-start.64 = (bf16[64,2048]{1,0:T(8,128)(2,1)}, bf16[64,2048]{1,0:T(8,128)(2,1)}, u32[]{:S(2)}, u32[]{:S(2)}) collective-permute-start(bf16[64,2048]{1,0:T(8,128)(2,1)} %get-tuple-element.843), channel_id=1, source_target_pairs={{0,8},{8,16},{16,24},{24,28},{28,20},{20,12},{12,4},{4,0},{1,9},{9... | collective-permute-start | bytes 786440 | tf_op jit(solution)/shard_map/ppermute | solution.py:835
  567.7 18.2 %collective-permute-start.65 = (bf16[64,2048]{1,0:T(8,128)(2,1)}, bf16[64,2048]{1,0:T(8,128)(2,1)}, u32[]{:S(2)}, u32[]{:S(2)}) collective-permute-start(bf16[64,2048]{1,0:T(8,128)(2,1)} %get-tuple-element.842), channel_id=1, source_target_pairs={{0,4},{8,0},{16,8},{24,16},{28,24},{20,28},{12,20},{4,12},{1,5},{9... | collective-permute-start | bytes 786440 | tf_op jit(solution)/shard_map/ppermute | solution.py:835
  583.5 27.0 %collective-permute-start.68 = (bf16[256,1536]{1,0:T(8,128)(2,1)S(1)}, bf16[256,1536]{1,0:T(8,128)(2,1)S(1)}, u32[]{:S(2)}, u32[]{:S(2)}) collective-permute-start(bf16[256,1536]{1,0:T(8,128)(2,1)S(1)} %pad_maximum_fusion), channel_id=1, source_target_pairs={{0,8},{8,16},{16,24},{24,28},{28,20},{20,12},{12,4},{4,0},{1,9},{9... | collective-permute-start | bytes 2359304 | tf_op jit(solution)/shard_map/ppermute | solution.py:835
  583.7 26.8 %collective-permute-start.69 = (bf16[256,1536]{1,0:T(8,128)(2,1)S(1)}, bf16[256,1536]{1,0:T(8,128)(2,1)S(1)}, u32[]{:S(2)}, u32[]{:S(2)}) collective-permute-start(bf16[256,1536]{1,0:T(8,128)(2,1)S(1)} %pad_maximum_fusion.1), channel_id=1, source_target_pairs={{0,4},{8,0},{16,8},{24,16},{28,24},{20,28},{12,20},{4,12},{1,5},{9... | collective-permute-start | bytes 2359304 | tf_op jit(solution)/shard_map/ppermute | solution.py:835
  587.6 21.9 %collective-permute-start.66 = (bf16[64,2048]{1,0:T(8,128)(2,1)S(1)}, bf16[64,2048]{1,0:T(8,128)(2,1)S(1)}, u32[]{:S(2)}, u32[]{:S(2)}) collective-permute-start(bf16[64,2048]{1,0:T(8,128)(2,1)S(1)} %get-tuple-element.841), channel_id=1, source_target_pairs={{0,8},{8,16},{16,24},{24,28},{28,20},{20,12},{12,4},{4,0},{1,9},{9... | collective-permute-start | bytes 786440 | tf_op jit(solution)/shard_map/ppermute | solution.py:835
  588.0 22.5 %collective-permute-start.67 = (bf16[64,2048]{1,0:T(8,128)(2,1)S(1)}, bf16[64,2048]{1,0:T(8,128)(2,1)S(1)}, u32[]{:S(2)}, u32[]{:S(2)}) collective-permute-start(bf16[64,2048]{1,0:T(8,128)(2,1)S(1)} %get-tuple-element.840), channel_id=1, source_target_pairs={{0,4},{8,0},{16,8},{24,16},{28,24},{20,28},{12,20},{4,12},{1,5},{9... | collective-permute-start | bytes 786440 | tf_op jit(solution)/shard_map/ppermute | solution.py:835
  589.7 38.3 %collective-permute-start.71 = (bf16[128,2048]{1,0:T(8,128)(2,1)S(1)}, bf16[128,2048]{1,0:T(8,128)(2,1)S(1)}, u32[]{:S(2)}, u32[]{:S(2)}) collective-permute-start(bf16[128,2048]{1,0:T(8,128)(2,1)S(1)} %get-tuple-element.676), channel_id=1, source_target_pairs={{0,1},{1,0},{2,3},{3,2},{4,5},{5,4},{6,7},{7,6},{8,9},{9,8},{10,11... | collective-permute-start | bytes 1572872 | tf_op jit(solution)/shard_map/ppermute | solution.py:823
  609.4 18.6 %collective-permute-start.70 = (bf16[128,2048]{1,0:T(8,128)(2,1)S(1)}, bf16[128,2048]{1,0:T(8,128)(2,1)S(1)}, u32[]{:S(2)}, u32[]{:S(2)}) collective-permute-start(bf16[128,2048]{1,0:T(8,128)(2,1)S(1)} %add_convert_fusion.4), channel_id=1, source_target_pairs={{0,2},{1,3},{2,0},{3,1},{4,6},{5,7},{6,4},{7,5},{8,10},{9,11},{10,... | collective-permute-start | bytes 1572872 | tf_op jit(solution)/shard_map/ppermute | solution.py:823
  610.8 19.2 %collective-permute-start.72 = (bf16[256,1536]{1,0:T(8,128)(2,1)S(1)}, bf16[256,1536]{1,0:T(8,128)(2,1)S(1)}, u32[]{:S(2)}, u32[]{:S(2)}) collective-permute-start(bf16[256,1536]{1,0:T(8,128)(2,1)S(1)} %add_convert_fusion.3), channel_id=1, source_target_pairs={{0,8},{8,16},{16,24},{24,28},{28,20},{20,12},{12,4},{4,0},{1,9},{9... | collective-permute-start | bytes 2359304 | tf_op jit(solution)/shard_map/ppermute | solution.py:835
  611.8 18.6 %collective-permute-start.73 = (bf16[256,1536]{1,0:T(8,128)(2,1)S(1)}, bf16[256,1536]{1,0:T(8,128)(2,1)S(1)}, u32[]{:S(2)}, u32[]{:S(2)}) collective-permute-start(bf16[256,1536]{1,0:T(8,128)(2,1)S(1)} %add_convert_fusion.2), channel_id=1, source_target_pairs={{0,4},{8,0},{16,8},{24,16},{28,24},{20,28},{12,20},{4,12},{1,5},{9... | collective-permute-start | bytes 2359304 | tf_op jit(solution)/shard_map/ppermute | solution.py:835
  631.7 17.9 %collective-permute-start.75 = (bf16[256,1536]{1,0:T(8,128)(2,1)}, bf16[256,1536]{1,0:T(8,128)(2,1)S(1)}, u32[]{:S(2)}, u32[]{:S(2)}) collective-permute-start(bf16[256,1536]{1,0:T(8,128)(2,1)} %get-tuple-element.849), channel_id=1, source_target_pairs={{0,8},{8,16},{16,24},{24,28},{28,20},{20,12},{12,4},{4,0},{1,9},{9... | collective-permute-start | bytes 2359304 | tf_op jit(solution)/shard_map/ppermute | solution.py:835
  633.2 17.7 %collective-permute-start.76 = (bf16[256,1536]{1,0:T(8,128)(2,1)S(1)}, bf16[256,1536]{1,0:T(8,128)(2,1)S(1)}, u32[]{:S(2)}, u32[]{:S(2)}) collective-permute-start(bf16[256,1536]{1,0:T(8,128)(2,1)S(1)} %get-tuple-element.848), channel_id=1, source_target_pairs={{0,4},{8,0},{16,8},{24,16},{28,24},{20,28},{12,20},{4,12},{1,5},{9... | collective-permute-start | bytes 2359304 | tf_op jit(solution)/shard_map/ppermute | solution.py:835
  635.2 16.5 %collective-permute-start.77 = (f32[2,2048]{1,0:T(2,128)S(1)}, f32[2,2048]{1,0:T(2,128)S(1)}, u32[]{:S(2)}, u32[]{:S(2)}) collective-permute-start(f32[2,2048]{1,0:T(2,128)S(1)} %add.226), channel_id=1, source_target_pairs={{0,2},{1,3},{2,0},{3,1},{4,6},{5,7},{6,4},{7,5},{8,10},{9,11},{10,... | collective-permute-start | bytes 49160 | tf_op jit(solution)/shard_map/ppermute | solution.py:823
  652.6 19.0 %collective-permute-start.80 = (bf16[64,1536]{1,0:T(8,128)(2,1)S(1)}, bf16[64,1536]{1,0:T(8,128)(2,1)S(1)}, u32[]{:S(2)}, u32[]{:S(2)}) collective-permute-start(bf16[64,1536]{1,0:T(8,128)(2,1)S(1)} %get-tuple-element.706), channel_id=1, source_target_pairs={{0,3},{1,2},{2,1},{3,0},{4,7},{5,6},{6,5},{7,4},{8,11},{9,10},{10,... | collective-permute-start | bytes 589832 | tf_op jit(solution)/shard_map/ppermute | solution.py:823
  672.2 27.3 %collective-permute-start.81 = (bf16[272,2048]{1,0:T(8,128)(2,1)S(1)}, bf16[272,2048]{1,0:T(8,128)(2,1)S(1)}, u32[]{:S(2)}, u32[]{:S(2)}) collective-permute-start(bf16[272,2048]{1,0:T(8,128)(2,1)S(1)} %join_columns.1.refs_0_), channel_id=1, source_target_pairs={{0,8},{8,16},{16,24},{24,28},{28,20},{20,12},{12,4},{4,0},{1,9},{9... | collective-permute-start | bytes 3342344 | tf_op jit(solution)/shard_map/ppermute | solution.py:835
  673.3 26.9 %collective-permute-start.82 = (bf16[272,2048]{1,0:T(8,128)(2,1)S(1)}, bf16[272,2048]{1,0:T(8,128)(2,1)S(1)}, u32[]{:S(2)}, u32[]{:S(2)}) collective-permute-start(bf16[272,2048]{1,0:T(8,128)(2,1)S(1)} %join_columns.1.refs_0_), channel_id=1, source_target_pairs={{0,4},{8,0},{16,8},{24,16},{28,24},{20,28},{12,20},{4,12},{1,5},{9... | collective-permute-start | bytes 3342344 | tf_op jit(solution)/shard_map/ppermute | solution.py:835
  700.2 26.2 %collective-permute-start.83 = (bf16[272,2048]{1,0:T(8,128)(2,1)S(1)}, bf16[272,2048]{1,0:T(8,128)(2,1)}, u32[]{:S(2)}, u32[]{:S(2)}) collective-permute-start(bf16[272,2048]{1,0:T(8,128)(2,1)S(1)} %collective-permute-done.81.refs_0_.refs_2_), channel_id=1, source_target_pairs={{0,8},{8,16},{16,24},{24,28},{28,20},{20,12},{12,4},{4,0},{1,9},{9... | collective-permute-start | bytes 3342344 | tf_op jit(solution)/shard_map/ppermute | solution.py:835
  700.5 26.2 %collective-permute-start.84 = (bf16[272,2048]{1,0:T(8,128)(2,1)S(1)}, bf16[272,2048]{1,0:T(8,128)(2,1)}, u32[]{:S(2)}, u32[]{:S(2)}) collective-permute-start(bf16[272,2048]{1,0:T(8,128)(2,1)S(1)} %collective-permute-done.82.refs_1_), channel_id=1, source_target_pairs={{0,4},{8,0},{16,8},{24,16},{28,24},{20,28},{12,20},{4,12},{1,5},{9... | collective-permute-start | bytes 3342344 | tf_op jit(solution)/shard_map/ppermute | solution.py:835
  726.7 25.4 %collective-permute-start.85 = (bf16[272,2048]{1,0:T(8,128)(2,1)}, bf16[272,2048]{1,0:T(8,128)(2,1)S(1)}, u32[]{:S(2)}, u32[]{:S(2)}) collective-permute-start(bf16[272,2048]{1,0:T(8,128)(2,1)} %collective-permute-done.83.refs_0_.refs_4_), channel_id=1, source_target_pairs={{0,8},{8,16},{16,24},{24,28},{28,20},{20,12},{12,4},{4,0},{1,9},{9... | collective-permute-start | bytes 3342344 | tf_op jit(solution)/shard_map/ppermute | solution.py:835
  728.2 24.9 %collective-permute-start.86 = (bf16[272,2048]{1,0:T(8,128)(2,1)}, bf16[272,2048]{1,0:T(8,128)(2,1)S(1)}, u32[]{:S(2)}, u32[]{:S(2)}) collective-permute-start(bf16[272,2048]{1,0:T(8,128)(2,1)} %collective-permute-done.84.refs_1_.refs_3_), channel_id=1, source_target_pairs={{0,4},{8,0},{16,8},{24,16},{28,24},{20,28},{12,20},{4,12},{1,5},{9... | collective-permute-start | bytes 3342344 | tf_op jit(solution)/shard_map/ppermute | solution.py:835
  (133 other events, 1657.6 us)
Sparse Core Ops, SparseCore 0:
  30.5 62.9 all-gather.3
  95.6 65.3 all-gather.5
  205.8 57.9 all-gather.7
  432.4 70.2 reduce-scatter.5
  519.1 72.2 reduce-scatter.7
  593.8 84.4 reduce-scatter.3

commit v3 on v2

v3 whole, which is shorter than its diff:
```python
import functools

import jax
import jax.numpy as jnp
import numpy as np
from jax import lax
from jax.experimental import pallas as pl
from jax.experimental.pallas import tpu as pltpu
from jax.sharding import PartitionSpec as P

EPSILON = 1e-06
ROPE_BASE = 10000.0
BF = jnp.bfloat16
F32 = jnp.float32
LONG = pl.CostEstimate(flops=10**12, bytes_accessed=10**9, transcendentals=0)
MEDIUM = pl.CostEstimate(flops=2 * 10**10, bytes_accessed=5 * 10**7, transcendentals=0)
SMALL = pl.CostEstimate(flops=1, bytes_accessed=1, transcendentals=0)


def dot(a, b, contract=((1,), (0,)), precision=None):
    return lax.dot_general(a, b, (contract, ((), ())), precision=precision, preferred_element_type=F32)


def dot_nt(a, b):
    return dot(a, b, ((1,), (1,)))


def dot_tn(a, b):
    return dot(a, b, ((0,), (0,)))


def head_norm(v, gain):
    factor = lax.rsqrt(jnp.mean(v * v, axis=-1, keepdims=True) + EPSILON)
    return v * factor * gain, factor


def turn(v, cosine, sine):
    return v * cosine + pltpu.roll(v, v.shape[-1] // 2, 1) * sine


def head_back(grad, v, gain, cosine, sine):
    grad = turn(grad, cosine, -sine)
    factor = lax.rsqrt(jnp.mean(v * v, axis=-1, keepdims=True) + EPSILON)
    gain_grad = jnp.sum(grad * v * factor, axis=0, keepdims=True)
    inner = grad * gain
    return factor * inner - v * (factor * factor * factor) * jnp.mean(inner * v, axis=-1, keepdims=True), gain_grad


def rows_of(ref):
    block = ref[...]
    return block.reshape(-1, block.shape[-1])


def attend_kernel(q_ref, k_ref, v_ref, qg_ref, kg_ref, cos_ref, sin_ref, o_ref, keys, values_t):
    step = pl.program_id(1)

    @pl.when(step == 0)
    def _():
        normed, _unused = head_norm(rows_of(k_ref).astype(F32), kg_ref[...])
        keys[...] = turn(normed, cos_ref[...], sin_ref[...]).astype(BF)
        values_t[...] = rows_of(v_ref).astype(F32).T.astype(BF)

    queries = rows_of(q_ref).astype(F32)
    number, head_dim = queries.shape
    here = pl.ds(pl.multiple_of(step * number, number), number)
    normed, _unused = head_norm(queries, qg_ref[...])
    queries = turn(normed, cos_ref[here, :], sin_ref[here, :]).astype(BF)
    weights = jnp.exp(dot_nt(keys[...], queries) * (head_dim**-0.5))
    total = jnp.sum(weights, axis=0, keepdims=True)
    mixed = dot(values_t[...], weights.astype(BF)) / total
    o_ref[...] = mixed.T.astype(BF).reshape(o_ref.shape)


def attend_back_kernel(
    q_ref, k_ref, v_ref, m_ref, qg_ref, kg_ref, cos_ref, sin_ref,
    g_ref, gain_ref, keys, keys_t, key_acc, value_acc,
):
    pair = pl.program_id(0)
    step = pl.program_id(1)
    last = pl.num_programs(1) - 1

    @pl.when((pair == 0) & (step == 0))
    def _():
        gain_ref[...] = jnp.zeros_like(gain_ref)

    @pl.when(step == 0)
    def _():
        normed, _unused = head_norm(rows_of(k_ref).astype(F32), kg_ref[...])
        turned = turn(normed, cos_ref[...], sin_ref[...])
        keys[...] = turned.astype(BF)
        keys_t[...] = turned.T.astype(BF)
        key_acc[...] = jnp.zeros_like(key_acc)
        value_acc[...] = jnp.zeros_like(value_acc)

    query_pre = rows_of(q_ref).astype(F32)
    grad_mixed = rows_of(m_ref)
    number, head_dim = query_pre.shape
    scale = head_dim**-0.5
    here = pl.ds(pl.multiple_of(step * number, number), number)
    cosine, sine = cos_ref[here, :], sin_ref[here, :]
    normed, _unused = head_norm(query_pre, qg_ref[...])
    queries = turn(normed, cosine, sine).astype(BF)
    weights = jnp.exp(dot_nt(keys[...], queries) * scale)
    probs = weights * (1.0 / jnp.sum(weights, axis=0, keepdims=True))
    value_acc[...] += dot(probs.astype(BF), grad_mixed)
    weighted = probs * dot_nt(rows_of(v_ref), grad_mixed)
    delta = jnp.sum(weighted, axis=0, keepdims=True)
    grad_scores = (weighted - probs * delta).astype(BF)
    key_acc[...] += dot(grad_scores, queries)
    grad_query = dot(keys_t[...], grad_scores).T * scale
    grad_query, gain_grad = head_back(grad_query, query_pre, qg_ref[...], cosine, sine)
    rows = g_ref.shape[2]
    blocks = number // rows
    g_ref[pl.ds(step * blocks, blocks), 0] = grad_query.astype(BF).reshape(blocks, rows, head_dim)
    gain_ref[0:1, :] += gain_grad

    @pl.when(step == last)
    def _():
        grad_key, gain_grad = head_back(
            key_acc[...] * scale, rows_of(k_ref).astype(F32), kg_ref[...], cos_ref[...], sin_ref[...]
        )
        g_ref[:, 1] = grad_key.astype(BF).reshape(-1, rows, head_dim)
        g_ref[:, 2] = value_acc[...].astype(BF).reshape(-1, rows, head_dim)
        gain_ref[1:2, :] += gain_grad


def attention_specs(shape):
    blocks, pairs, rows, head_dim = shape
    at_once = max(1, 256 // rows)
    while blocks % at_once:
        at_once -= 1
    pairs //= 3
    part = pl.BlockSpec((at_once, 1, rows, head_dim), lambda p, i: (i, p, 0, 0))
    three = [
        pl.BlockSpec((at_once, 1, rows, head_dim), lambda p, i: (i, 3 * p, 0, 0)),
        pl.BlockSpec((blocks, 1, rows, head_dim), lambda p, i: (0, 3 * p + 1, 0, 0)),
        pl.BlockSpec((blocks, 1, rows, head_dim), lambda p, i: (0, 3 * p + 2, 0, 0)),
    ]
    gain = pl.BlockSpec((1, head_dim), lambda p, i: (0, 0))
    table = pl.BlockSpec((blocks * rows, head_dim), lambda p, i: (0, 0))
    params = pltpu.CompilerParams(
        dimension_semantics=("arbitrary", "arbitrary"),
        vmem_limit_bytes=(24 if blocks * rows <= 1024 else 56) * 2**20,
    )
    return part, three, gain, table, (pairs, blocks // at_once), params


def attend(qkv, query_gain, key_gain, cosine, sine):
    part, three, gain, table, grid, params = attention_specs(qkv.shape)
    blocks, _unused, rows, head_dim = qkv.shape
    length = blocks * rows
    return pl.pallas_call(
        attend_kernel,
        grid=grid,
        in_specs=[*three, gain, gain, table, table],
        out_specs=part,
        out_shape=jax.ShapeDtypeStruct((blocks, grid[0], rows, head_dim), BF),
        scratch_shapes=[pltpu.VMEM((length, head_dim), BF), pltpu.VMEM((head_dim, length), BF)],
        compiler_params=params,
        cost_estimate=MEDIUM,
        name="attend",
    )(qkv, qkv, qkv, query_gain, key_gain, cosine, sine)


def attend_back(qkv, grad_mixed, query_gain, key_gain, cosine, sine):
    part, three, gain, table, grid, params = attention_specs(qkv.shape)
    blocks, _unused, rows, head_dim = qkv.shape
    length = blocks * rows
    return pl.pallas_call(
        attend_back_kernel,
        grid=grid,
        in_specs=[*three, part, gain, gain, table, table],
        out_specs=[
            pl.BlockSpec((blocks, 3, rows, head_dim), lambda p, i: (0, p, 0, 0)),
            pl.BlockSpec((8, head_dim), lambda p, i: (0, 0)),
        ],
        out_shape=[jax.ShapeDtypeStruct(qkv.shape, BF), jax.ShapeDtypeStruct((8, head_dim), F32)],
        scratch_shapes=[
            pltpu.VMEM((length, head_dim), BF),
            pltpu.VMEM((head_dim, length), BF),
            pltpu.VMEM((length, head_dim), F32),
            pltpu.VMEM((length, head_dim), F32),
        ],
        compiler_params=params,
        cost_estimate=LONG,
        name="attend_back",
    )(qkv, qkv, qkv, grad_mixed, query_gain, key_gain, cosine, sine)


def stack_blocks(block_refs, out_ref):
    rows = block_refs[0].shape[0]
    for index, block_ref in enumerate(block_refs):
        out_ref[index * rows : (index + 1) * rows, :] = block_ref[...]


def stacked_kernel(w_ref, *refs):
    *block_refs, o_ref, rows_ref = refs

    @pl.when(pl.program_id(0) == 0)
    def _():
        stack_blocks(block_refs, rows_ref)

    o_ref[...] = dot(rows_ref[...], w_ref[...])


def stacked_matmul(blocks, weight):
    rows, depth = len(blocks) * blocks[0].shape[0], weight.shape[0]
    wide = min(512, weight.shape[1])
    return pl.pallas_call(
        stacked_kernel,
        grid=(weight.shape[1] // wide,),
        in_specs=[pl.BlockSpec((depth, wide), lambda n: (0, n))]
        + [pl.BlockSpec(block.shape, lambda n: (0, 0)) for block in blocks],
        out_specs=[pl.BlockSpec((rows, wide), lambda n: (0, n)), pl.BlockSpec((rows, depth), lambda n: (0, 0))],
        out_shape=[jax.ShapeDtypeStruct((rows, weight.shape[1]), F32), jax.ShapeDtypeStruct((rows, depth), BF)],
        compiler_params=pltpu.CompilerParams(dimension_semantics=("arbitrary",), vmem_limit_bytes=56 * 2**20),
        cost_estimate=LONG,
        name="stacked_matmul",
    )(weight, *blocks)


def routed_gates(logits, routes):
    columns = lax.broadcasted_iota(jnp.int32, logits.shape, 1)
    chosen = columns == routes[:, 0:1]
    for index in range(1, routes.shape[1]):
        chosen = chosen | (columns == routes[:, index : index + 1])
    high = jnp.max(jnp.where(chosen, logits, -1e30), axis=-1, keepdims=True)
    weights = jnp.where(chosen, jnp.exp(jnp.where(chosen, logits - high, 0.0)), 0.0)
    return weights / jnp.sum(weights, axis=-1, keepdims=True)


def expert_kernel(table_ref, router_ref, routes_ref, gate_w_ref, up_w_ref, grad_ref, *refs, per, place, at):
    *block_refs, act_ref, gate_ref, up_ref, d_gates_ref, x_ref, gates_ref = refs
    step = pl.program_id(0)

    @pl.when(step == 0)
    def _():
        stack_blocks(block_refs, x_ref)
        routes = jnp.concatenate([routes_ref[table_ref[at + index]] for index in range(len(block_refs))], axis=0)
        gates = routed_gates(dot(x_ref[...], router_ref[...]), routes)
        columns = lax.broadcasted_iota(jnp.int32, gates.shape, 1)
        count = gates_ref.shape[0]
        for index in range(count):
            here = columns == table_ref[place] * count + index
            gates_ref[index] = jnp.sum(jnp.where(here, gates, 0.0), axis=1, keepdims=True)

    @pl.when(step % per == 0)
    def _():
        d_gates_ref[...] = jnp.zeros_like(d_gates_ref)

    gate_pre = dot(x_ref[...], gate_w_ref[...])
    up_pre = dot(x_ref[...], up_w_ref[...])
    grad_act = grad_ref[...]
    gates = gates_ref[step // per]
    sigmoid = 1.0 / (1.0 + jnp.exp(-gate_pre))
    silu = gate_pre * sigmoid
    act = (silu * up_pre).astype(BF).astype(F32)
    d_gates_ref[0] += jnp.sum(act * grad_act, axis=1, keepdims=True)
    grad_act = grad_act * gates
    act_ref[...] = (act * gates).astype(BF)
    up_ref[...] = (grad_act * silu).astype(BF)
    gate_ref[...] = (grad_act * up_pre * (sigmoid * (1.0 + gate_pre * (1.0 - sigmoid)))).astype(BF)


def expert_units(table, place, at, blocks, routes, router_w, gate_w, up_w, grad_act, count):
    rows, width = len(blocks) * blocks[0].shape[0], blocks[0].shape[1]
    units = gate_w.shape[1]
    wide = min(512, units // count)
    per = units // wide // count
    weight = pl.BlockSpec((width, wide), lambda n: (0, n))
    tile = pl.BlockSpec((rows, wide), lambda n: (0, n))
    out = jax.ShapeDtypeStruct((rows, units), BF)
    return pl.pallas_call(
        functools.partial(expert_kernel, per=per, place=place, at=at),
        grid=(units // wide,),
        in_specs=[
            pl.BlockSpec(memory_space=pltpu.SMEM),
            pl.BlockSpec(router_w.shape, lambda n: (0, 0)),
            pl.BlockSpec(routes.shape, lambda n: (0, 0, 0)),
            weight,
            weight,
            tile,
        ]
        + [pl.BlockSpec(block.shape, lambda n: (0, 0)) for block in blocks],
        out_specs=[
            tile,
            tile,
            tile,
            pl.BlockSpec((1, rows, 1), lambda n: (n // per, 0, 0)),
            pl.BlockSpec((rows, width), lambda n: (0, 0)),
        ],
        out_shape=[
            out, out, out, jax.ShapeDtypeStruct((count, rows, 1), F32), jax.ShapeDtypeStruct((rows, width), BF),
        ],
        scratch_shapes=[pltpu.VMEM((count, rows, 1), F32)],
        compiler_params=pltpu.CompilerParams(dimension_semantics=("arbitrary",), vmem_limit_bytes=58 * 2**20),
        cost_estimate=LONG,
        name="expert_units",
    )(table, router_w, routes, gate_w, up_w, grad_act, *blocks)


def expert_rows_kernel(gate_ref, up_ref, gate_w_ref, up_w_ref, o_ref):
    o_ref[...] = (dot_nt(gate_ref[...], gate_w_ref[...]) + dot_nt(up_ref[...], up_w_ref[...])).astype(BF)


def expert_rows(gate_grads, up_grads, gate_w, up_w):
    rows, units = gate_grads.shape
    width = gate_w.shape[0]
    wide = min(512, width)
    whole = pl.BlockSpec((rows, units), lambda n: (0, 0))
    weight = pl.BlockSpec((wide, units), lambda n: (n, 0))
    return pl.pallas_call(
        expert_rows_kernel,
        grid=(width // wide,),
        in_specs=[whole, whole, weight, weight],
        out_specs=pl.BlockSpec((rows, wide), lambda n: (0, n)),
        out_shape=jax.ShapeDtypeStruct((rows, width), BF),
        compiler_params=pltpu.CompilerParams(dimension_semantics=("arbitrary",), vmem_limit_bytes=56 * 2**20),
        cost_estimate=LONG,
        name="expert_rows",
    )(gate_grads, up_grads, gate_w, up_w)


def times_kernel(b_ref, *refs):
    count = len(refs) // 2
    for a_ref, o_ref in zip(refs[:count], refs[count:]):
        o_ref[...] = dot_nt(a_ref[...], b_ref[...]).astype(o_ref.dtype)


def times_transpose(lefts, b):
    columns, depth = b.shape
    wide = min(512, columns)
    return pl.pallas_call(
        times_kernel,
        grid=(columns // wide,),
        in_specs=[pl.BlockSpec((wide, depth), lambda n: (n, 0))]
        + [pl.BlockSpec(left.shape, lambda n: (0, 0)) for left in lefts],
        out_specs=[pl.BlockSpec((left.shape[0], wide), lambda n: (0, n)) for left in lefts],
        out_shape=[jax.ShapeDtypeStruct((left.shape[0], columns), BF) for left in lefts],
        compiler_params=pltpu.CompilerParams(dimension_semantics=("arbitrary",), vmem_limit_bytes=58 * 2**20),
        cost_estimate=LONG,
        name="times_transpose",
    )(b, *lefts)


def sum_kernel(*refs):
    *pair_refs, o_ref = refs
    count = len(pair_refs) // 2
    total = dot_tn(pair_refs[0][...], pair_refs[count][...])
    for index in range(1, count):
        total = total + dot_tn(pair_refs[index][...], pair_refs[count + index][...])
    o_ref[...] = total.astype(o_ref.dtype)


def sum_of_outer(lefts, rights):
    whole = not isinstance(lefts, (list, tuple))
    count, depth = len(rights), rights[0].shape[0]
    rows, columns = (lefts if whole else lefts[0]).shape[1], rights[0].shape[1]
    tall, wide = min(512, rows), columns if count <= 2 else min(1024, columns)

    def left_spec(index):
        at = index if whole else 0
        return pl.BlockSpec((depth, tall), lambda n, m: (at, m))

    return pl.pallas_call(
        sum_kernel,
        grid=(columns // wide, rows // tall),
        in_specs=[left_spec(index) for index in range(count)]
        + [pl.BlockSpec((depth, wide), lambda n, m: (0, n)) for _unused in rights],
        out_specs=pl.BlockSpec((tall, wide), lambda n, m: (m, n)),
        out_shape=jax.ShapeDtypeStruct((rows, columns), BF),
        compiler_params=pltpu.CompilerParams(
            dimension_semantics=("arbitrary", "arbitrary"), vmem_limit_bytes=56 * 2**20
        ),
        cost_estimate=LONG,
        name="sum_of_outer",
    )(*([lefts] * count if whole else lefts), *rights)


NN, NT = ((1,), (0,)), ((1,), (1,))


def small_call(kernel, name, out_shape, *operands, cost=SMALL, scratch=(), **kwargs):
    vmem = pl.BlockSpec(memory_space=pltpu.VMEM)
    return pl.pallas_call(
        functools.partial(kernel, **kwargs),
        in_specs=[pl.BlockSpec(memory_space=pltpu.SMEM)] + [vmem] * (len(operands) - 1),
        out_specs=jax.tree.map(lambda _unused: vmem, out_shape),
        out_shape=out_shape,
        scratch_shapes=list(scratch),
        compiler_params=pltpu.CompilerParams(vmem_limit_bytes=48 * 2**20),
        cost_estimate=cost,
        name=name,
    )(*operands)


def payload_kernel(_unused, a_ref, b_ref, o_ref):
    rows, width = b_ref.shape[0], o_ref.shape[1]
    columns = b_ref.shape[1]
    rest = columns - width
    o_ref[:rows, :] = a_ref[:, :width]
    o_ref[rows : 2 * rows, :] = b_ref[:, :width]
    o_ref[2 * rows : 3 * rows, :rest] = a_ref[:, width:columns]
    o_ref[2 * rows : 3 * rows, rest:] = b_ref[:, width:]
    o_ref[3 * rows :, :] = a_ref[:, columns:]


def fetched_payload(table, from_beyond, from_across, width):
    out = jax.ShapeDtypeStruct((4 * from_across.shape[0], width), BF)
    return small_call(payload_kernel, "fetched_payload", out, table, from_beyond, from_across)


def own_pairs_kernel(table_ref, *refs, blocks, kinds, slabs, ring_slots):
    block_refs, refs = refs[:blocks], refs[blocks:]
    own_ref, near_ref, *piece_refs = refs[:-5]
    o_ref, columns_out, columns_ref, rows_ref, sems = refs[-5:]
    head_step, kind = pl.program_id(0), pl.program_id(1)
    slab, columns = own_ref.shape
    width = piece_refs[0].shape[1]
    part = piece_refs[0].shape[0] // 4
    rest = columns - width
    back = pltpu.make_async_copy(columns_ref, columns_out, sems.at[2 + 4 * len(piece_refs)])

    @pl.when((head_step == 0) & (kind == 0))
    def _():
        def at(slot, ring_slot=None):
            start = table_ref[slot] * slab
            if ring_slot is None:
                return pl.ds(pl.multiple_of(start, slab), slab)
            return pl.ds(pl.multiple_of(start + table_ref[ring_slot] * part, part), part)

        pairs = [(own_ref, columns_ref.at[at(slabs[0]), :]), (near_ref, columns_ref.at[at(slabs[1]), :])]
        for ring_slot, piece in zip(ring_slots, piece_refs):
            for index in range(2):
                to = at(slabs[2 + index], ring_slot)
                pairs.append((piece.at[index * part : (index + 1) * part, :], columns_ref.at[to, :width]))
                some = piece.at[2 * part : 3 * part, index * rest : (index + 1) * rest]
                pairs.append((some, columns_ref.at[to, width:]))
        copies = [pltpu.make_async_copy(*pair, sems.at[index]) for index, pair in enumerate(pairs)]
        for copy in copies:
            copy.start()
        stack_blocks(block_refs, rows_ref)
        for copy in copies:
            copy.wait()
        back.start()

    rows, head_dim = o_ref.shape[2:]
    wide = o_ref.shape[0] * head_dim
    at_column = (kind * pl.num_programs(0) + head_step) * wide
    product = dot(rows_ref[...], columns_ref[:, pl.ds(pl.multiple_of(at_column, wide), wide)]).astype(BF)
    for head in range(o_ref.shape[0]):
        for block in range(blocks):
            piece = product[block * rows : (block + 1) * rows, head * head_dim : (head + 1) * head_dim]
            o_ref[head, block * kinds + kind] = piece

    @pl.when((head_step == pl.num_programs(0) - 1) & (kind == kinds - 1))
    def _():
        back.wait()


def own_pairs(table, blocks, own, near, pieces, kinds, head_dim, slabs, ring_slots):
    rows, depth = blocks[0].shape
    columns = own.shape[1]
    heads = columns // head_dim // kinds
    at_once = 2
    anywhere = pl.BlockSpec(memory_space=pl.ANY)
    return pl.pallas_call(
        functools.partial(
            own_pairs_kernel, blocks=len(blocks), kinds=kinds, slabs=slabs, ring_slots=ring_slots
        ),
        grid=(heads // at_once, kinds),
        in_specs=[pl.BlockSpec(memory_space=pltpu.SMEM)]
        + [pl.BlockSpec(block.shape, lambda h, k: (0, 0)) for block in blocks]
        + [anywhere] * (2 + len(pieces)),
        out_specs=[
            pl.BlockSpec((at_once, len(blocks) * kinds, rows, head_dim), lambda h, k: (h, 0, 0, 0)),
            anywhere,
        ],
        out_shape=[
            jax.ShapeDtypeStruct((heads, len(blocks) * kinds, rows, head_dim), BF),
            jax.ShapeDtypeStruct((depth, columns), BF),
        ],
        scratch_shapes=[
            pltpu.VMEM((depth, columns), BF),
            pltpu.VMEM((len(blocks) * rows, depth), BF),
            pltpu.SemaphoreType.DMA((3 + 4 * len(pieces),)),
        ],
        compiler_params=pltpu.CompilerParams(
            dimension_semantics=("arbitrary", "arbitrary"), vmem_limit_bytes=40 * 2**20
        ),
        cost_estimate=SMALL,
        name="own_pairs",
    )(table, *blocks, own, near, *pieces)


def far_rows_kernel(table_ref, *refs, ring_slots):
    *pieces, o_ref = refs
    part = pieces[0].shape[0] // 4
    for slot, piece in zip(ring_slots, pieces):
        o_ref[pl.ds(pl.multiple_of(table_ref[slot] * part, part), part), :] = piece[3 * part :, :]


def far_rows(table, pieces, ring_slots):
    rows, width = pieces[0].shape
    out = jax.ShapeDtypeStruct((rows // 4 * len(pieces), width), BF)
    return small_call(far_rows_kernel, "far_rows", out, table, *pieces, ring_slots=ring_slots)


def heads_of(ref, side, sequence, count):
    return [ref[side * count + head, sequence] for head in range(count)]


def mixed_out_kernel(table_ref, m_ref, w_ref, far_ref, *refs, side):
    count = m_ref.shape[0] // 2
    for sequence, ref in enumerate(refs):
        own = jnp.concatenate(heads_of(m_ref, table_ref[side], sequence, count), axis=1)
        far = jnp.concatenate(heads_of(m_ref, 1 - table_ref[side], sequence, count), axis=1)
        ref[...] = (dot(own, w_ref[...]) + dot(far, far_ref[...])).astype(ref.dtype)


def mixed_out(table, mixed, w_out, w_far, side):
    shape = (mixed.shape[2], w_out.shape[1])
    out = [jax.ShapeDtypeStruct(shape, kind) for kind in (F32, BF)]
    return small_call(mixed_out_kernel, "mixed_out", out, table, mixed, w_out, w_far, cost=MEDIUM, side=side)


def grad_pairs_kernel(table_ref, own_ref, beside_ref, w_ref, far_ref, o_ref, *, side):
    rows, head_dim = o_ref.shape[2:]
    count = o_ref.shape[0] // 2
    grads = jnp.concatenate([own_ref[...], beside_ref[...]], axis=0)
    for slab_ref, at in ((w_ref, table_ref[side]), (far_ref, 1 - table_ref[side])):
        product = dot_nt(grads, slab_ref[...]).astype(BF)
        for head in range(count):
            for sequence in range(2):
                piece = product[sequence * rows : (sequence + 1) * rows, head * head_dim : (head + 1) * head_dim]
                o_ref[at * count + head, sequence] = piece


def grad_pairs(table, own, beside, w_out, w_far, side, head_dim):
    out = jax.ShapeDtypeStruct((2 * w_out.shape[0] // head_dim, 2, own.shape[0], head_dim), BF)
    return small_call(
        grad_pairs_kernel, "grad_pairs", out, table, own, beside, w_out, w_far, cost=LONG, side=side
    )


def out_grads_kernel(table_ref, m_ref, other_ref, *refs, turn, own_rows, side):
    *block_refs, o_ref, mixed_ref, turned_ref, grads_ref = refs
    head_dim = m_ref.shape[3]
    count = m_ref.shape[0] // 2
    for head in range(count):
        rows = [m_ref[table_ref[side] * count + head, sequence] for sequence in range(2)]
        rows += [other_ref[head, sequence] for sequence in range(2)]
        rows = jnp.concatenate(rows, axis=0)
        mixed_ref[head * head_dim : (head + 1) * head_dim, :] = rows.astype(F32).T.astype(BF)
    for index in range(mixed_ref.shape[0] // own_rows):
        at = pl.multiple_of(table_ref[turn + index] * own_rows, own_rows)
        turned_ref[index * own_rows : (index + 1) * own_rows, :] = mixed_ref[pl.ds(at, own_rows), :]
    stack_blocks(block_refs, grads_ref)
    o_ref[...] = dot(turned_ref[...], grads_ref[...])


def out_grads(table, mixed, other, blocks, turn, own_rows, side):
    rows, width = blocks[0].shape
    features = mixed.shape[0] // 2 * mixed.shape[3]
    turned = pltpu.VMEM((features, len(blocks) * rows), BF)
    out = jax.ShapeDtypeStruct((features, width), F32)
    scratch = [turned, turned, pltpu.VMEM((len(blocks) * rows, width), BF)]
    return small_call(
        out_grads_kernel, "out_grads", out, table, mixed, other, *blocks, scratch=scratch, turn=turn,
        own_rows=own_rows, side=side,
    )


def transposed_kernel(table_ref, *refs, slots):
    *block_refs, o_ref = refs
    rows, width = block_refs[0].shape
    slab = width // len(slots)
    for index, block_ref in enumerate(block_refs):
        for number, slot in enumerate(slots):
            here = pl.ds(pl.multiple_of(table_ref[slot] * slab, slab), slab)
            some = block_ref[:, here].astype(F32).T.astype(BF)
            o_ref[number * slab : (number + 1) * slab, index * rows : (index + 1) * rows] = some


def transposed(table, blocks, slots):
    rows, width = blocks[0].shape
    out = jax.ShapeDtypeStruct((width, len(blocks) * rows), BF)
    return small_call(transposed_kernel, "transposed", out, table, *blocks, cost=LONG, slots=slots)


def head_weights_kernel(table_ref, g_ref, own_ref, beside_ref, o_ref, grads_ref, *, kinds, places):
    rows, head_dim = g_ref.shape[2:]

    @pl.when(pl.program_id(0) == 0)
    def _():
        for index in range(g_ref.shape[0]):
            for sequence in range(2):
                for kind in range(kinds):
                    piece = g_ref[table_ref[places + index], sequence * kinds + kind]
                    here = slice(kind * head_dim, (kind + 1) * head_dim)
                    grads_ref[sequence, index * rows : (index + 1) * rows, here] = piece

    o_ref[...] = (dot(own_ref[...], grads_ref[0]) + dot(beside_ref[...], grads_ref[1])).astype(BF)


def head_weights(table, grads, own, beside, kinds, places):
    blocks, _unused, rows, head_dim = grads.shape
    width, total = own.shape
    tall = width // 4
    row = pl.BlockSpec((tall, total), lambda m: (m, 0))
    return pl.pallas_call(
        functools.partial(head_weights_kernel, kinds=kinds, places=places),
        grid=(4,),
        in_specs=[pl.BlockSpec(memory_space=pltpu.SMEM), pl.BlockSpec(grads.shape, lambda m: (0, 0, 0, 0)), row, row],
        out_specs=pl.BlockSpec((tall, kinds * head_dim), lambda m: (m, 0)),
        out_shape=jax.ShapeDtypeStruct((width, kinds * head_dim), BF),
        scratch_shapes=[pltpu.VMEM((2, total, kinds * head_dim), BF)],
        compiler_params=pltpu.CompilerParams(dimension_semantics=("arbitrary",), vmem_limit_bytes=48 * 2**20),
        cost_estimate=LONG,
        name="head_weights",
    )(table, grads, own, beside)


def chip_total_kernel(table_ref, own_ref, other_ref, keep_ref, send_ref, *, core):
    slab = keep_ref.shape[0]
    for ref, at in ((keep_ref, table_ref[core]), (send_ref, 1 - table_ref[core])):
        here = pl.ds(pl.multiple_of(at * slab, slab), slab)
        ref[...] = (own_ref[here, :].astype(F32) + other_ref[here, :].astype(F32)).astype(BF)


def chip_total(table, own, other, core):
    out = [jax.ShapeDtypeStruct((other.shape[0] // 2, own.shape[1]), BF)] * 2
    return small_call(chip_total_kernel, "chip_total", out, table, own, other, core=core)


def beside_kernel(_unused, left_ref, right_ref, o_ref):
    columns = left_ref.shape[1]
    o_ref[:, :columns] = left_ref[...].astype(BF)
    o_ref[:, columns:] = right_ref[...].astype(BF)


def side_by_side(table, left, right):
    out = jax.ShapeDtypeStruct((left.shape[0], left.shape[1] + right.shape[1]), BF)
    return small_call(beside_kernel, "side_by_side", out, table, left, right)


def pair_rows_kernel(g_ref, w_ref, own_ref, beside_ref, dn_ref, *, kinds):
    kind = pl.program_id(1)

    @pl.when((pl.program_id(0) == 0) & (kind == 0))
    def _():
        dn_ref[...] = jnp.zeros_like(dn_ref)

    heads = []
    for head in range(g_ref.shape[0]):
        heads.append(jnp.concatenate([g_ref[head, sequence * kinds + kind] for sequence in range(2)], axis=0))
    dn_ref[...] += dot_nt(jnp.concatenate(heads, axis=1), w_ref[...])

    @pl.when((pl.program_id(0) == pl.num_programs(0) - 1) & (kind == kinds - 1))
    def _():
        rows = own_ref.shape[0]
        own_ref[...] = dn_ref[:rows, :]
        beside_ref[...] = dn_ref[rows:, :].astype(BF)


def pair_normed(grads, columns, kinds):
    heads, _unused, rows, head_dim = grads.shape
    width, at_once = columns.shape[0], 2
    whole = pl.BlockSpec((rows, width), lambda h, k: (0, 0))
    return pl.pallas_call(
        functools.partial(pair_rows_kernel, kinds=kinds),
        grid=(heads // at_once, kinds),
        in_specs=[
            pl.BlockSpec((at_once, 2 * kinds, rows, head_dim), lambda h, k: (h, 0, 0, 0)),
            pl.BlockSpec((width, at_once * head_dim), lambda h, k: (0, k * (heads // at_once) + h)),
        ],
        out_specs=[whole, whole],
        out_shape=[jax.ShapeDtypeStruct((rows, width), kind) for kind in (F32, BF)],
        scratch_shapes=[pltpu.VMEM((2 * rows, width), F32)],
        compiler_params=pltpu.CompilerParams(
            dimension_semantics=("arbitrary", "arbitrary"), vmem_limit_bytes=40 * 2**20
        ),
        cost_estimate=LONG,
        name="pair_normed",
    )(grads, columns)


def take_kernel(table_ref, *refs, count, sides):
    weights, outs, sems = refs[:count], refs[count : count + len(sides)], refs[-1]
    copies = []
    for out, (row, rows, pieces) in zip(outs, sides):
        at = 0
        if row is None:
            here = slice(None)
        else:
            here = pl.ds(pl.multiple_of(table_ref[row] * rows, rows), rows)
        for number, slot, wide in pieces:
            there = slice(None)
            if slot is not None:
                there = pl.ds(pl.multiple_of(table_ref[slot] * wide, wide), wide)
            copies.append(
                pltpu.make_async_copy(
                    weights[number].at[here, there], out.at[:, at : at + wide], sems.at[len(copies)]
                )
            )
            at += wide
    for copy in copies:
        copy.start()
    for copy in copies:
        copy.wait()


def take_parts(table, weights, sides, cost):
    outs = []
    for row, rows, pieces in sides:
        outs.append(jax.ShapeDtypeStruct((rows, sum(wide for _unused, _unused2, wide in pieces)), BF))
    number = sum(len(pieces) for _unused, _unused2, pieces in sides)
    return pl.pallas_call(
        functools.partial(take_kernel, count=len(weights), sides=sides),
        in_specs=[pl.BlockSpec(memory_space=pltpu.SMEM)] + [pl.BlockSpec(memory_space=pl.ANY)] * len(weights),
        out_specs=[pl.BlockSpec(memory_space=pltpu.VMEM)] * len(sides),
        out_shape=outs,
        scratch_shapes=[pltpu.SemaphoreType.DMA((number,))],
        compiler_params=pltpu.CompilerParams(vmem_limit_bytes=40 * 2**20),
        cost_estimate=cost,
        name="take_parts",
    )(table, *weights)


def place_kernel(table_ref, *refs, slots):
    *pieces, out = refs
    for piece, slot in zip(pieces, slots):
        rows = piece.shape[0]
        out[pl.ds(pl.multiple_of(table_ref[slot] * rows, rows), rows), :] = piece[...]


def place_rows(table, pieces, slots):
    rows = sum(piece.shape[0] for piece in pieces)
    out = jax.ShapeDtypeStruct((rows, pieces[0].shape[1]), pieces[0].dtype)
    return small_call(place_kernel, "place_rows", out, table, *pieces, slots=slots)


def pack_kernel(table_ref, below_ref, early_ref, late_ref, o_ref, *, slot, experts):
    slab = o_ref.shape[1] // 4
    first = below_ref.shape[0]
    here = pl.ds(pl.multiple_of(table_ref[slot] * slab, slab), slab)
    o_ref[...] = jnp.zeros_like(o_ref)
    o_ref[:first, :] = below_ref[...].astype(BF)
    for index in range(experts):
        at = first + index // 4
        o_ref[at : at + 1, index % 4 * slab : (index % 4 + 1) * slab] = early_ref[index : index + 1, here].astype(BF)
    at = first + experts // 4
    o_ref[at : at + 1, :] = early_ref[experts : experts + 1, :].astype(BF)
    o_ref[at + 1 : at + 3, :] = late_ref[...].astype(BF)


def pack_gains(table, below, early, late, slot, experts):
    height = below.shape[0] + -(-(experts // 4 + 3) // 16) * 16
    out = jax.ShapeDtypeStruct((height, early.shape[1]), BF)
    return small_call(pack_kernel, "pack_gains", out, table, below, early, late, slot=slot, experts=experts)


def unpack_kernel(table_ref, *refs, back, experts):
    *pieces, router_ref, gains_ref, all_ref = refs
    height = all_ref.shape[1]
    for index, piece in enumerate(pieces):
        all_ref[index] = piece[piece.shape[0] - height :, :].astype(F32)
    total = all_ref[table_ref[back]]
    for place in range(1, len(pieces)):
        total = total + all_ref[table_ref[back + place]]
    slab = total.shape[1] // 4
    rows = [total[i // 4 : i // 4 + 1, i % 4 * slab : (i % 4 + 1) * slab] for i in range(experts)]
    router_ref[...] = jnp.concatenate(rows, axis=0).T
    gains_ref[...] = total[experts // 4 : experts // 4 + 3, :]


def unpack_gains(table, pieces, back, experts, height):
    width = pieces[0].shape[1]
    out = [jax.ShapeDtypeStruct((width // 4, experts), F32), jax.ShapeDtypeStruct((3, width), F32)]
    scratch = [pltpu.VMEM((len(pieces), height, width), F32)]
    return small_call(
        unpack_kernel, "unpack_gains", out, table, *pieces, scratch=scratch, back=back, experts=experts
    )


def spread_kernel(table_ref, *refs, count, outs, cuts):
    pieces = refs[:count]
    out_refs = refs[-2 - outs : -2]
    wide_ref, sems = refs[-2:]
    copies = []
    for index, (number, rows, columns, out, slot, by_rows) in enumerate(cuts):
        wide_ref[index] = pieces[number][rows[0] : rows[1], columns[0] : columns[1]].astype(F32)
        size = rows[1] - rows[0] if by_rows else columns[1] - columns[0]
        here = pl.ds(pl.multiple_of(table_ref[slot] * size, size), size)
        to = out_refs[out].at[here, :] if by_rows else out_refs[out].at[:, here]
        copies.append(pltpu.make_async_copy(wide_ref.at[index], to, sems.at[index]))
        copies[-1].start()
    for copy in copies:
        copy.wait()


def spread(table, pieces, cuts, shape, outs, before):
    vmem, anywhere = pl.BlockSpec(memory_space=pltpu.VMEM), pl.BlockSpec(memory_space=pl.ANY)
    old = [] if before is None else list(before)
    _unused, rows, columns, *_rest = cuts[0]
    return pl.pallas_call(
        functools.partial(spread_kernel, count=len(pieces), outs=outs, cuts=cuts),
        in_specs=[pl.BlockSpec(memory_space=pltpu.SMEM)] + [vmem] * len(pieces) + [anywhere] * len(old),
        out_specs=[anywhere] * outs,
        out_shape=[jax.ShapeDtypeStruct(shape, F32)] * outs,
        input_output_aliases={1 + len(pieces) + index: index for index in range(len(old))},
        scratch_shapes=[
            pltpu.VMEM((len(cuts), rows[1] - rows[0], columns[1] - columns[0]), F32),
            pltpu.SemaphoreType.DMA((len(cuts),)),
        ],
        compiler_params=pltpu.CompilerParams(vmem_limit_bytes=24 * 2**20),
        cost_estimate=SMALL,
        name="spread",
    )(table, *pieces, *old)


def merge_kernel(w_ref, o_ref):
    units = w_ref.shape[2]
    for index in range(w_ref.shape[1]):
        o_ref[:, index * units : (index + 1) * units] = w_ref[:, index, :]


def merge_experts(weight):
    rows, count, units = weight.shape
    at_once = 128
    return pl.pallas_call(
        merge_kernel,
        grid=(rows // at_once,),
        in_specs=[pl.BlockSpec((at_once, count, units), lambda m: (m, 0, 0))],
        out_specs=pl.BlockSpec((at_once, count * units), lambda m: (m, 0)),
        out_shape=jax.ShapeDtypeStruct((rows, count * units), weight.dtype),
        cost_estimate=MEDIUM,
        name="merge_experts",
    )(weight)


def split_kernel(w_ref, o_ref):
    units = o_ref.shape[2]
    for index in range(o_ref.shape[1]):
        o_ref[:, index, :] = w_ref[:, index * units : (index + 1) * units].astype(F32)


def split_experts(grad, count):
    rows, columns = grad.shape
    at_once = 128
    return pl.pallas_call(
        split_kernel,
        grid=(rows // at_once,),
        in_specs=[pl.BlockSpec((at_once, columns), lambda m: (m, 0))],
        out_specs=pl.BlockSpec((at_once, count, columns // count), lambda m: (m, 0, 0)),
        out_shape=jax.ShapeDtypeStruct((rows, count, columns // count), F32),
        cost_estimate=SMALL,
        name="split_experts",
    )(grad)


def swap(v, mask):
    size = lax.axis_size("fsdp")
    return lax.ppermute(v, "fsdp", [(i, i ^ mask) for i in range(size)])


def ring_order(size):
    if size == 8:
        return [0, 2, 4, 6, 7, 5, 3, 1]
    return list(range(size))


def ring_send(v, direction):
    order = ring_order(lax.axis_size("ctx"))
    size = len(order)
    return lax.ppermute(v, "ctx", [(order[i], order[(i + direction) % size]) for i in range(size)])


class Ring:
    def __init__(self, steps):
        self.steps = steps
        self.value = None
        self.flying = False
        self.advance()

    def advance(self):
        try:
            next(self.steps)
            self.flying = not self.flying
        except StopIteration as end:
            self.value = end.value

    def land(self):
        if self.value is None and self.flying:
            self.advance()

    def step(self):
        self.land()
        if self.value is None:
            self.advance()

    def finish(self):
        while self.value is None:
            self.step()
        return self.value


def ring_gather(v, in_order, found):
    size = lax.axis_size("ctx")
    far, half = size // 2, v.shape[0] // 2
    found[0] = v
    right, left = v, v
    for step in range(1, far):
        right, left = ring_send(right, 1), ring_send(left, -1)
        yield
        right, left = in_order(right, left)
        found[size - step], found[step] = right, left
        yield
    right, left = ring_send(right[:half], 1), ring_send(left[half:], -1)
    yield
    found[far] = jnp.concatenate(in_order(right, left))
    yield
    return found


def ring_scatter(term, in_order):
    size = lax.axis_size("ctx")
    far = size // 2
    first = term(far)
    half = first.shape[0] // 2
    right, left = ring_send(first[:half].astype(BF), 1), ring_send(first[half:].astype(BF), -1)
    for offset in range(far - 1, 0, -1):
        yield
        right, left = in_order(right, left)
        yield
        ahead, behind = term(offset), term(size - offset)
        if offset == far - 1:
            ahead = jnp.concatenate([ahead[:half].astype(F32) + right.astype(F32), ahead[half:].astype(F32)])
            behind = jnp.concatenate([behind[:half].astype(F32), behind[half:].astype(F32) + left.astype(F32)])
        else:
            ahead, behind = ahead.astype(F32) + right.astype(F32), behind.astype(F32) + left.astype(F32)
        right, left = ring_send(ahead.astype(BF), 1), ring_send(behind.astype(BF), -1)
    yield
    right, left = in_order(right, left)
    yield
    return term(0).astype(F32) + right.astype(F32) + left.astype(F32)


def after(v, *others):
    return lax.optimization_barrier((v, *others))[0]


class Order:
    def __init__(self, first):
        self.last = first

    def __call__(self, *values):
        self.last, *values = lax.optimization_barrier((self.last, *values))
        return values[0] if len(values) == 1 else values


def sum_fsdp(v, in_order):
    size = lax.axis_size("fsdp")
    mask = 1
    while mask < size:
        other = swap(v, mask)
        yield
        v = v + in_order(other)
        yield
        mask *= 2
    return v


def body(
    tokens, attn_gain, w_query, w_key, w_value, query_gain, key_gain, w_out,
    ffn_gain, w_router, w_gate, w_up, w_down, routes, cotangent,
):
    ctx_size = lax.axis_size("ctx")
    parts = lax.axis_size("fsdp")
    rows = tokens.shape[1]
    width = tokens.shape[2]
    slab = w_query.shape[0]
    head_dim = query_gain.shape[0]
    own_heads = width // head_dim // parts
    own_width = own_heads * head_dim
    own_rows = slab // ctx_size
    own_experts = w_gate.shape[1]
    hidden_units = w_gate.shape[2]
    experts = own_experts * ctx_size
    seq_length = rows * ctx_size
    in_order = Order(jnp.zeros((), F32))

    heads = 2 * own_heads
    repeats = ctx_size // heads
    order = ring_order(ctx_size)
    offsets = [0] + [o for step in range(1, ctx_size // 2) for o in (step, ctx_size - step)] + [ctx_size // 2]
    at_ring, at_place, at_core, at_side = 0, 1, 2, 3
    at_slab = [4 + mask for mask in range(parts)]
    at_groups, at_beside, at_chip = (8, 9), (10, 11), (12, 13, 14, 15)
    at_from = 16
    at_blocks = [at_from + ctx_size + index for index in range(ctx_size)]
    at_heads = [(at_from + 2 * ctx_size + index, at_from + 3 * ctx_size + index) for index in range(ctx_size)]
    at_turn = at_from + 4 * ctx_size
    at_back = at_from + 5 * ctx_size
    lines = []
    for place in range(ctx_size):
        ring_place = order.index(place)
        for mine in range(parts):
            side, core = divmod(mine, 2)
            line = [ring_place, place, core, side] + [mine ^ mask for mask in range(parts)]
            line += [core, core + 2, 1 - core, 3 - core, 2 * side, 2 * side + 1, 2 - 2 * side, 3 - 2 * side]
            places = [order[(ring_place + offset) % ctx_size] for offset in offsets]
            line += places
            line += [(ring_place + offset) % ctx_size for offset in offsets]
            for first in (core, 1 - core):
                line += [first * own_heads + other // repeats + other // repeats // own_heads * own_heads for other in places]
            line += [(ring_place + index) % ctx_size for index in range(ctx_size)]
            line += [offsets.index((order.index(other) - ring_place) % ctx_size) for other in range(ctx_size)]
            lines.append(line)
    device = lax.axis_index("ctx").astype(jnp.uint32) * parts + lax.axis_index("fsdp").astype(jnp.uint32)
    table = lax.dynamic_slice(jnp.asarray(np.array(lines, np.int32)), (device, jnp.uint32(0)), (1, len(lines[0])))
    table = table.reshape(-1)

    def spread_pairs(v):
        if repeats > 1:
            v = jnp.repeat(v, repeats, axis=0)
        return lax.all_to_all(v, "ctx", split_axis=0, concat_axis=0, tiled=True)

    def collect_pairs(v):
        v = lax.all_to_all(v, "ctx", split_axis=0, concat_axis=0, tiled=True)
        return v[::repeats] if repeats > 1 else v

    projections = (w_query, w_key, w_value)

    def side_of(row, rows, slots):
        return row, rows, [(number, slot, own_width) for number in range(3) for slot in slots]

    row, rows_of, some = side_of(at_ring, own_rows, at_groups)
    fetched = in_order(
        *take_parts(
            table, (*projections, w_out), [(row, rows_of, some + [(3, None, width)]), side_of(row, rows_of, at_beside)], SMALL
        )
    )
    fetched = swap(fetched[0], 2), swap(fetched[1], 3)
    cot_blocks = {}
    cot_ring = Ring(ring_gather(after(cotangent[0], in_order.last), in_order, cot_blocks))
    source = tokens[0].astype(F32)
    factor_one = lax.rsqrt(jnp.mean(source * source, axis=-1, keepdims=True) + EPSILON)
    normed = (source * factor_one * attn_gain).astype(BF)
    projections, w_down, w_gate, w_up = after((projections, w_down, w_gate, w_up), in_order.last)
    near, own = in_order(
        *take_parts(
            table, projections, [side_of(None, slab, at_beside), side_of(None, slab, at_groups)], MEDIUM
        )
    )
    cot_ring.step()
    beside, near = swap(normed, 1), swap(near, 1)
    w_down = in_order(merge_experts(after(w_down, in_order.last)))
    cot_ring.land()
    fetched = in_order(*fetched)
    column_blocks = {}
    ring = Ring(ring_gather(fetched_payload(table, *fetched, width), in_order, column_blocks))
    down_w = lax.all_gather(after(w_down, in_order.last), "fsdp", axis=0, tiled=True)
    w_gate = in_order(merge_experts(after(w_gate, in_order.last)))
    ring.step()
    gate_w = lax.all_gather(after(w_gate, in_order.last), "fsdp", axis=0, tiled=True)
    w_router, routes = after((w_router, routes), in_order.last)
    router = [w_router, swap(w_router, 1), swap(w_router, 2), swap(w_router, 3)]
    routes_all = lax.all_to_all(
        jnp.broadcast_to(routes, (ctx_size, *routes.shape[1:])), "ctx", split_axis=0, concat_axis=0, tiled=True
    )
    normed, near, beside = in_order(normed, near, beside)
    w_up = in_order(merge_experts(after(w_up, in_order.last)))
    ring.step()
    up_w = lax.all_gather(after(w_up, in_order.last), "fsdp", axis=0, tiled=True)
    routes_all, *router = in_order(routes_all, *router)
    ring.step()

    half = head_dim // 2
    frequency = ROPE_BASE ** (-jnp.arange(half, dtype=F32) * 2.0 / head_dim)
    angles = jnp.arange(seq_length, dtype=jnp.int32).astype(F32)[:, None] * frequency[None, :]
    cosine, sine = jnp.cos(angles), jnp.sin(angles)
    cosine = jnp.concatenate([cosine, cosine], axis=1)
    sine = jnp.concatenate([-sine, sine], axis=1)
    q_gain, k_gain = query_gain[None, :], key_gain[None, :]

    ring.finish()
    qkv, own_columns = own_pairs(
        table,
        (normed, beside),
        own,
        near,
        [column_blocks[offset] for offset in offsets],
        3,
        head_dim,
        at_slab,
        at_blocks,
    )
    qkv = spread_pairs(in_order(qkv))
    router_w = in_order(place_rows(table, after(router, in_order.last), at_slab))
    w_far = in_order(far_rows(table, [column_blocks[offset] for offset in offsets], at_blocks))
    qkv = in_order(qkv)
    down_w, gate_w = in_order(down_w, gate_w)
    mixed = in_order(attend(qkv, q_gain, k_gain, cosine, sine))
    mixed = in_order(collect_pairs(mixed))
    hidden, far = in_order(*mixed_out(table, mixed, w_out, w_far, at_side))
    far = swap(far, 1)
    hidden = in_order(source + hidden)
    hidden = hidden + in_order(far).astype(F32)
    up_w = in_order(up_w)
    factor_two = lax.rsqrt(jnp.mean(hidden * hidden, axis=-1, keepdims=True) + EPSILON)
    ffn_in = in_order((hidden * factor_two * ffn_gain).astype(BF))

    ffn_blocks = {}
    ffn_ring = Ring(ring_gather(ffn_in, in_order, ffn_blocks))
    ffn_ring.step()

    size = 4
    groups = [offsets[first : first + size] for first in range(0, ctx_size, size)]

    def group_cots(group):
        return in_order(*stacked_matmul([cot_blocks[o] for o in groups[group]], down_w))

    def group_units(group, grad_act):
        return in_order(
            *expert_units(
                table, at_place, at_from + group * size, [ffn_blocks[o] for o in groups[group]], routes_all, router_w,
                gate_w, up_w, grad_act, own_experts,
            )
        )

    cots = [group_cots(0)]
    ffn_ring.step()
    cot_ring.step()
    units = [group_units(0, cots[0][0])]
    ffn_ring.step()
    cot_ring.step()
    other_side = (1 - table[at_side]).astype(jnp.uint32) * own_heads
    zero = jnp.uint32(0)
    other_mixed = lax.dynamic_slice(
        after(mixed, in_order.last), (other_side, zero, zero, zero), (own_heads, *mixed.shape[1:])
    )
    other_mixed = swap(other_mixed, 2)
    cot_ring.finish()
    ffn_ring.finish()
    normed_blocks = {}
    normed_ring = Ring(ring_gather(after(normed, in_order.last), in_order, normed_blocks))
    for group in range(1, len(groups)):
        cots.append(group_cots(group))
        if group == 1:
            normed_ring.step()
        units.append(group_units(group, cots[group][0]))
    cots = [part for _unused, part in cots]
    acts, gate_grads, up_grads, d_gates, inputs = zip(*units)

    def term_of(terms):
        def term(offset):
            group, index = divmod(offsets.index(offset), size)
            return terms[group][index * rows : (index + 1) * rows]

        return term

    def weight_grad(lefts, rights):
        lefts, rights = after((lefts, rights), in_order.last)
        return in_order(sum_of_outer(lefts, rights))

    def share(grad):
        return lax.psum_scatter(after(grad, in_order.last), "fsdp", scatter_dimension=0, tiled=True)

    grad_rows = {}

    def make_rows(group):
        some = after((gate_grads[group], up_grads[group]), in_order.last)
        grad_rows[group] = in_order(expert_rows(*some, gate_w, up_w))

    other_mixed = in_order(other_mixed)
    normed_ring.step()
    for group in range(len(groups) - 1, 0, -1):
        make_rows(group)
    normed_ring.step()
    row_ring = Ring(ring_scatter(term_of(grad_rows), in_order))
    d_gate = weight_grad(inputs, gate_grads)
    row_ring.step()
    d_gate = share(d_gate)
    normed_ring.finish()
    make_rows(0)
    row_ring.step()
    weighted = in_order(*times_transpose(after(acts, in_order.last), down_w))
    row_ring.step()
    ring = Ring(ring_scatter(term_of(weighted), in_order))
    d_gates = jnp.concatenate(after(d_gates, in_order.last), axis=1).reshape(own_experts, ctx_size, rows)
    d_gates = d_gates.at[:, table[at_back : at_back + ctx_size], :].get(mode="promise_in_bounds").transpose(1, 0, 2)
    d_gates = lax.all_to_all(d_gates, "ctx", split_axis=0, concat_axis=0, tiled=True)
    normed_t = in_order(transposed(table, [normed_blocks[offset] for offset in offsets], at_chip))
    row_ring.land()
    d_gates = in_order(d_gates).reshape(experts, rows).T
    beside_t = swap(normed_t, 1)
    gates = routed_gates(dot(ffn_in, router_w), routes[0])
    grad_logits = gates * (d_gates - jnp.sum(gates * d_gates, axis=-1, keepdims=True))
    routed = dot(grad_logits, router_w.astype(F32), ((1,), (1,)), precision=lax.Precision.HIGHEST)
    routed = in_order(routed)
    grad_ffn_in = row_ring.finish() + routed

    inner = grad_ffn_in * ffn_gain
    grad_hidden = (
        cotangent[0].astype(F32)
        + factor_two * inner
        - hidden * (factor_two * factor_two * factor_two) * jnp.mean(inner * hidden, axis=-1, keepdims=True)
    )
    grad_proj, grad_hidden, grad_ffn_in = in_order(grad_hidden.astype(BF), grad_hidden, grad_ffn_in)

    beside = swap(grad_proj, 1)
    grad_proj, beside, beside_t = in_order(grad_proj, beside, beside_t)
    grad_mixed = in_order(grad_pairs(table, grad_proj, beside, w_out, w_far, at_side, head_dim))
    across = swap(after(grad_proj, in_order.last), 2)
    ring.step()
    grad_mixed = spread_pairs(grad_mixed)
    d_up = weight_grad(inputs, up_grads)
    grad_mixed = in_order(grad_mixed)
    d_up = share(d_up)
    across = in_order(across)
    diagonal = in_order(swap(across, 1))
    mixed = after(mixed, in_order.last)
    d_out = in_order(
        out_grads(table, mixed, other_mixed, [grad_proj, beside, across, diagonal], at_turn, own_rows, at_side)
    )
    ring.step()
    out_ring = Ring(ring_scatter(lambda offset: d_out[offset * own_rows : (offset + 1) * own_rows], in_order))
    grads, head_gains = in_order(*attend_back(qkv, grad_mixed, q_gain, k_gain, cosine, sine))
    if repeats > 1:
        head_gains = jnp.where(lax.axis_index("ctx") % repeats == 0, head_gains, 0.0)
    ring.step()
    out_ring.step()

    half_grads = in_order(head_weights(table, grads, normed_t, beside_t, 3, at_from))
    other_half = swap(half_grads[width // 2 :], 2)
    grads = collect_pairs(grads)
    d_down = weight_grad(cots, acts)
    other_half = in_order(other_half)
    d_down = share(d_down)
    keep, send = in_order(*chip_total(table, half_grads, other_half, at_core))
    send = in_order(swap(send, 1))
    pieces = {}
    total_ring = Ring(ring_gather(side_by_side(table, keep, send), in_order, pieces))
    output = in_order((hidden + ring.finish()).astype(BF))
    out_ring.step()
    d_ffn_gain = jnp.sum(grad_ffn_in * hidden * factor_two, axis=0, keepdims=True)
    d_router = dot(grad_logits, ffn_in.astype(F32), ((0,), (0,)), precision=lax.Precision.HIGHEST)
    early = in_order(jnp.concatenate([d_router, d_ffn_gain]))
    early = Ring(sum_fsdp(early, in_order))
    grads = in_order(grads)
    own, far = in_order(*pair_normed(grads, own_columns, 3))
    far = swap(far, 1)
    early.step()
    total_ring.step()
    out_ring.step()

    whole = None
    seen = set()

    def take_whole(arrays):
        new = [index for index, offset in enumerate(offsets) if offset in pieces and index not in seen]
        seen.update(new)
        high = pieces[offsets[0]].shape[0]
        for first in range(0, len(new), 4):
            some = new[first : first + 4]
            cuts = []
            for number, index in enumerate(some):
                for where in range(2):
                    for kind in range(3):
                        at = (where * 3 + kind) * head_dim
                        cuts.append((number, (0, high), (at, at + head_dim), kind, at_heads[index][where], False))
            found = [pieces[offsets[index]] for index in some]
            arrays = in_order(*spread(table, found, cuts, (slab, width), 3, arrays))
        return arrays

    whole = take_whole(whole)
    early.finish()
    grad_normed = own + in_order(far).astype(F32)
    d_attn_gain = jnp.sum(grad_normed * source * factor_one, axis=0)
    inner = grad_normed * attn_gain
    d_tokens = (
        grad_hidden
        + factor_one * inner
        - source * (factor_one * factor_one * factor_one) * jnp.mean(inner * source, axis=-1, keepdims=True)
    )
    d_tokens, d_attn_gain = in_order(d_tokens, d_attn_gain)
    late = jnp.concatenate([d_attn_gain, head_gains[0], head_gains[1], jnp.zeros((width - 2 * head_dim,), F32)])
    late = Ring(sum_fsdp(late.reshape(2, width), in_order))
    d_gate = in_order(split_experts(after(d_gate, in_order.last), own_experts))
    total_ring.step()
    d_out = out_ring.finish()
    late.step()
    whole = take_whole(whole)
    packed = in_order(pack_gains(table, d_out, early.value, late.finish(), at_slab[0], experts))
    packed_pieces = {}
    packed_ring = Ring(ring_gather(packed, in_order, packed_pieces))
    d_up = in_order(split_experts(after(d_up, in_order.last), own_experts))
    total_ring.step()
    whole = take_whole(whole)
    packed_ring.step()
    total_ring.finish()
    whole = take_whole(whole)
    d_query, d_key, d_value = whole
    packed_ring.step()
    d_down = in_order(split_experts(after(d_down, in_order.last), own_experts))
    packed_ring.finish()
    packed_blocks = [packed_pieces[offset] for offset in offsets]
    cuts = [(index, (0, own_rows), (0, width), 0, at_blocks[index], True) for index in range(ctx_size)]
    (d_out,) = spread(table, packed_blocks, cuts, (slab, width), 1, None)
    height = packed.shape[0] - own_rows
    d_router, gains = unpack_gains(table, packed_blocks, at_back, experts, height)
    d_ffn_gain, d_attn_gain, head_gains = gains + in_order.last
    return (
        output[None],
        d_tokens[None],
        d_attn_gain,
        d_query,
        d_key,
        d_value,
        head_gains[:head_dim],
        head_gains[head_dim : 2 * head_dim],
        d_out,
        d_ffn_gain,
        d_router,
        d_gate,
        d_up,
        d_down,
    )


def solution(mesh):
    token_split = P("fsdp", "ctx", None)
    row_split = P("fsdp", None)
    return jax.shard_map(
        body,
        mesh=mesh,
        in_specs=(
            token_split, P(), row_split, row_split, row_split, P(), P(), row_split,
            P(), row_split, token_split, token_split, token_split, token_split, token_split,
        ),
        out_specs=(
            token_split, token_split, P(), row_split, row_split, row_split, P(), P(),
            row_split, P(), row_split, token_split, token_split, token_split,
        ),
        check_vma=False,
    )
```

time: 791 us -> 710 us (0.90)
  waiting for transfers between devices: 286 us -> 175 us
  blocking collectives: 0 us -> 18.1 us
  starting transfers between devices: 112 us -> 125 us
  Pallas kernels: 256 us -> 268 us
    all_to_all x2 -> x1, waiting for transfers between devices: 33 us -> 0.01 us  [collect_pairs(): v = lax.all_to_all(v, 'ctx', split_axis=0, concat_axis=0, tiled=True)]
    ppermute x64 -> x72, waiting for transfers between devices: 150 us -> 119 us  [ring_send(): lax.ppermute(v, 'ctx', [(order[i], order[(i + direction) % size]) for i i...]
    all_gather x3, waiting for transfers between devices: 27.9 us -> 0.01 us  [the longest x1 0.01 us: body(): lax.all_gather(after(w_down, in_order.last), 'fsdp', axis=0, tiled=True)]
    ppermute x25 -> x20, waiting for transfers between devices: 45.1 us -> 19.4 us  [swap(): return lax.ppermute(v, 'fsdp', [(i, i ^ mask) for i in range(size)])]
    ppermute x64 -> x72, starting transfers between devices: 69.3 us -> 91.7 us  [ring_send(): lax.ppermute(v, 'ctx', [(order[i], order[(i + direction) % size]) for i i...]
    all_to_all x0 -> x1, blocking collectives: none -> 18.1 us  [collect_pairs(): v = lax.all_to_all(v, 'ctx', split_axis=0, concat_axis=0, tiled=True)]
    pallas_call x9 -> x11, Pallas kernels: 11.1 us -> 26.1 us  [small_call(): pl.pallas_call(functools.partial(kernel, **kwargs), in_specs=[pl.BlockSpe...]
    ppermute x25 -> x20, starting transfers between devices: 17.4 us -> 11.7 us  [swap(): return lax.ppermute(v, 'fsdp', [(i, i ^ mask) for i in range(size)])]
  transfers between devices with their start and end apart: 101 -> 103, of which waited for: 51 -> 46; matrix products, arithmetic and copies ran while one was open for 9% -> 9% of each run, Pallas kernels for 26% -> 38%
where the time goes in v3:
time: 710 us; the launch traced here: 701 us
  Pallas kernels  268 us (38%)
  waiting for transfers between devices  175 us (25%)
  starting transfers between devices  125 us (18%)
  other arithmetic  50.9 us (7%)
  local copies, waits for them, and re-layouts  45.3 us (6%)
  blocking collectives  18.1 us (3%)
  between operations  16.5 us (2%)
    ppermute x72, waiting for transfers between devices, ring_send(): lax.ppermute(v, 'ctx', [(order[i], order[(i + direction) % size]) for i i...  119 us
    ppermute x72, starting transfers between devices, ring_send(): lax.ppermute(v, 'ctx', [(order[i], order[(i + direction) % size]) for i i...  91.7 us
    pallas_call x3, Pallas kernels, sum_of_outer(): pl.pallas_call(sum_kernel, grid=(columns // wide, rows // tall), in_specs...  40.3 us
    pallas_call x2, Pallas kernels, expert_units(): pl.pallas_call(functools.partial(expert_kernel, per=per, place=place, at=...  37.8 us
    pallas_call x2, Pallas kernels, expert_rows(): pl.pallas_call(expert_rows_kernel, grid=(width // wide,), in_specs=[whole...  27.6 us
    pallas_call x11, Pallas kernels, small_call(): pl.pallas_call(functools.partial(kernel, **kwargs), in_specs=[pl.BlockSpe...  26.1 us
    unnamed x175, local copies, waits for them, and re-layouts  24.9 us
    all_to_all x2, waiting for transfers between devices, spread_pairs(): return lax.all_to_all(v, 'ctx', split_axis=0, concat_axis=0, tiled=True)  24.8 us
  transfers between devices with their start and end apart: 103, of which 46 were waited for; matrix products, arithmetic and copies ran while one was open for 9% of the time, Pallas kernels for 38%

profile of v3, /device:TPU:0, one launch (start us, length us, event | category | flops | bytes accessed | tf_op | source)
XLA Modules:
  0.0 701.0 jit_solution(9177544589167751891)
XLA Ops:
  15.8 3.0 collective-permute-start
  25.8 4.9 collective-permute-done.refs_2_
  34.4 6.6 merge_experts.3
  41.0 4.0 collective-permute-done.2.refs_0_
  49.2 6.7 merge_experts.4
  55.9 13.8 %collective-permute-done.6.refs_6_.refs_2_ = bf16[256,2048]{1,0:T(8,128)(2,1)S(1)} collective-permute-done((bf16[256,2048]{1,0:T(8,128)(2,1)S(1)}, bf16[256,2048]{1,0:T(8,128)(2,1)S(1)}, u32[]{:S(2)}, u32[]{:S(2)}) %collective-permute-start.6) | collective-permute-done | bytes 1048608 | tf_op jit(solution)/shard_map/ppermute | solution.py:876
  78.9 6.6 merge_experts.5
  85.5 15.3 %collective-permute-done.10.refs_8_.refs_4_ = bf16[256,2048]{1,0:T(8,128)(2,1)} collective-permute-done((bf16[256,2048]{1,0:T(8,128)(2,1)S(1)}, bf16[256,2048]{1,0:T(8,128)(2,1)}, u32[]{:S(2)}, u32[]{:S(2)}) %collective-permute-start.10) | collective-permute-done | bytes 1048608 | tf_op jit(solution)/shard_map/ppermute | solution.py:876
  104.9 4.0 all-to-all-start
  111.5 4.6 collective-permute-done.13.refs_2_
  116.1 3.6 collective-permute-done.14.refs_3_
  119.7 10.0 %all-to-all-done = s32[8,128,8]{1,2,0:T(8,128)} async-done(((s32[8,128,8]{1,2,0:T(8,128)}), s32[8,128,8]{1,2,0:T(8,128)}, u32[]{:S(2)}, u32[]{:S(2)}) %all-to-all-start) | async-done | bytes 32800 | tf_op jit(solution)/shard_map/all_to_all | solution.py:1069
  131.9 9.5 %collective-permute-done.17 = bf16[128,2048]{1,0:T(8,128)(2,1)S(1)} collective-permute-done((bf16[128,2048]{1,0:T(8,128)(2,1)S(1)}, bf16[128,2048]{1,0:T(8,128)(2,1)S(1)}, u32[]{:S(2)}, u32[]{:S(2)}) %collective-permute-start.17) | collective-permute-done | bytes 524320 | tf_op jit(solution)/shard_map/ppermute | solution.py:876
  144.0 10.3 %own_pairs.1 = (bf16[8,6,128,128]{3,2,1,0:T(8,128)(2,1)S(1)}, bf16[2048,3072]{1,0:T(8,128)(2,1)}) custom-call(s32[64]{0:T(128)S(1)} %get-tuple-element.833.table_ref._unused, bf16[128,2048]{1,0:T(8,128)(2,1)} %fusion.2.refs_0_, bf16[128,2048]{1,0:T(8,128)(2,1)S(1)} %copy-done.33, bf16[512,3072]{1,0:T(8,128)(2,1)S(1)} %copy-done.17, ...), custom_call_target="tpu_custom_call" | custom-call | flops 1 | bytes 1 | tf_op jit(solution)/shard_map/own_pairs/pallas_call | solution.py:467
  155.5 3.9 all-to-all-start.1
  162.4 4.0 far_rows.1.far_ref
  168.8 24.8 %all-to-all-done.1.q_ref.k_ref.v_ref = bf16[8,6,128,128]{3,2,1,0:T(8,128)(2,1)S(1)} async-done(((bf16[8,6,128,128]{3,2,1,0:T(8,128)(2,1)}), bf16[8,6,128,128]{3,2,1,0:T(8,128)(2,1)S(1)}, u32[]{:S(2)}, u32[]{:S(2)}) %all-to-all-start.1) | async-done | bytes 1572896 | tf_op jit(solution)/shard_map/all_to_all | solution.py:1027
  197.2 7.8 %attend.1 = bf16[8,2,128,128]{3,2,1,0:T(8,128)(2,1)S(1)} custom-call(bf16[8,6,128,128]{3,2,1,0:T(8,128)(2,1)S(1)} %copy-done.26, bf16[8,6,128,128]{3,2,1,0:T(8,128)(2,1)S(1)} %copy-done.26, bf16[8,6,128,128]{3,2,1,0:T(8,128)(2,1)S(1)} %copy-done.26, f32[1,128]{1,0:T(1,128)S(1)} %bitcast.59, f32[1,128]{1,0:T(1,128)S(1)} %bitcast.61, ...), custom_call_target="tpu_custom_call" | custom-call | flops 20000000000 | bytes 50000000 | tf_op jit(solution)/shard_map/attend/pallas_call | solution.py:152
  205.8 18.1 %all_to_all.30.m_ref = bf16[8,2,128,128]{3,2,1,0:T(8,128)(2,1)S(1)} all-to-all(bf16[8,2,128,128]{3,2,1,0:T(8,128)(2,1)} %copy-done.34), channel_id=1, replica_groups=mesh['ctx'=8,'fsdp'=4] {'ctx'}, dimensions={0} | all-to-all | bytes 1048576 | tf_op jit(solution)/shard_map/all_to_all | solution.py:1030
  223.9 3.1 mixed_out.1
  236.2 9.1 %collective-permute-done.20.refs_2_ = bf16[128,2048]{1,0:T(8,128)(2,1)} collective-permute-done((bf16[128,2048]{1,0:T(8,128)(2,1)S(1)}, bf16[128,2048]{1,0:T(8,128)(2,1)}, u32[]{:S(2)}, u32[]{:S(2)}) %collective-permute-start.20) | collective-permute-done | bytes 524320 | tf_op jit(solution)/shard_map/ppermute | solution.py:876
  248.4 9.2 %stacked_matmul.2 = (f32[512,2048]{1,0:T(8,128)}, bf16[512,2048]{1,0:T(8,128)(2,1)}) custom-call(bf16[2048,2048]{1,0:T(8,128)(2,1)} %all-gather.4.cloned.1.call-done.w_ref.b_ref, bf16[128,2048]{1,0:T(8,128)(2,1)} %bitcast.64, bf16[128,2048]{1,0:T(8,128)(2,1)} %collective-permute-done.1.refs_1_, bf16[128,2048]{1,0:T(8,128)(2,1)} %copy-done.85, ...), custom_call_target="tpu_custom_call" | custom-call | flops 999999995904 | bytes 1000000000 | tf_op jit(solution)/shard_map/stacked_matmul/pallas_call | solution.py:209
  257.6 9.3 %collective-permute-done.22.refs_0_ = bf16[128,2048]{1,0:T(8,128)(2,1)} collective-permute-done((bf16[128,2048]{1,0:T(8,128)(2,1)}, bf16[128,2048]{1,0:T(8,128)(2,1)}, u32[]{:S(2)}, u32[]{:S(2)}) %collective-permute-start.22) | collective-permute-done | bytes 524320 | tf_op jit(solution)/shard_map/ppermute | solution.py:876
  269.8 18.9 %expert_units.2 = (bf16[512,2048]{1,0:T(8,128)(2,1)}, bf16[512,2048]{1,0:T(8,128)(2,1)}, bf16[512,2048]{1,0:T(8,128)(2,1)}, f32[2,512,1]{2,1,0:T(8,128)}, bf16[512,2048]{1,0:T(8,128)(2,1)}) custom-call(s32[64]{0:T(128)} %copy-done.35, bf16[2048,16]{1,0:T(8,128)(2,1)} %copy-done.3, s32[8,128,8]{2,1,0:T(8,128)} %copy.57.routes_ref, ...), custom_call_target="tpu_custom_call" | custom-call | flops 999999995904 | bytes 1000000000 | tf_op jit(solution)/shard_map/expert_units/pallas_call | solution.py:273
  307.0 9.3 %stacked_matmul.3 = (f32[512,2048]{1,0:T(8,128)}, bf16[512,2048]{1,0:T(8,128)(2,1)}) custom-call(bf16[2048,2048]{1,0:T(8,128)(2,1)} %all-gather.4.cloned.1.call-done.w_ref.b_ref, bf16[128,2048]{1,0:T(8,128)(2,1)} %collective-permute-done.2.refs_0_, bf16[128,2048]{1,0:T(8,128)(2,1)} %collective-permute-done.27.refs_1_, ...), custom_call_target="tpu_custom_call" | custom-call | flops 999999995904 | bytes 1000000000 | tf_op jit(solution)/shard_map/stacked_matmul/pallas_call | solution.py:209
  319.1 18.9 %expert_units.3 = (bf16[512,2048]{1,0:T(8,128)(2,1)}, bf16[512,2048]{1,0:T(8,128)(2,1)}, bf16[512,2048]{1,0:T(8,128)(2,1)}, f32[2,512,1]{2,1,0:T(8,128)}, bf16[512,2048]{1,0:T(8,128)(2,1)}) custom-call(s32[64]{0:T(128)} %copy-done.35, bf16[2048,16]{1,0:T(8,128)(2,1)} %copy-done.3, s32[8,128,8]{2,1,0:T(8,128)} %copy.57.routes_ref, ...), custom_call_target="tpu_custom_call" | custom-call | flops 999999995904 | bytes 1000000000 | tf_op jit(solution)/shard_map/expert_units/pallas_call | solution.py:273
  340.1 13.8 %expert_rows.2 = bf16[512,2048]{1,0:T(8,128)(2,1)} custom-call(bf16[512,2048]{1,0:T(8,128)(2,1)} %get-tuple-element.535.gate_ref.refs_3_, bf16[512,2048]{1,0:T(8,128)(2,1)} %get-tuple-element.588.up_ref.refs_3_, bf16[2048,2048]{1,0:T(8,128)(2,1)} %all-gather.6.cloned.1.call-done.gate_w_ref, bf16[2048,2048]{1,0:T(8,128)(2,1)} %all-gather.8.cloned.1.call-done.up_w_ref), custom_call_target="tpu_custom_call" | custom-call | flops 999999995904 | bytes 1000000000 | tf_op jit(solution)/shard_map/expert_rows/pallas_call | solution.py:312
  358.2 13.5 %sum_of_outer.3 = bf16[2048,2048]{1,0:T(8,128)(2,1)} custom-call(bf16[512,2048]{1,0:T(8,128)(2,1)} %get-tuple-element.585.refs_0_, bf16[512,2048]{1,0:T(8,128)(2,1)} %get-tuple-element.586.refs_1_, bf16[512,2048]{1,0:T(8,128)(2,1)} %get-tuple-element.543.refs_2_.gate_ref, bf16[512,2048]{1,0:T(8,128)(2,1)} %get-tuple-element.535.gate_ref.refs_3_), custom_call_target="tpu_custom_call" | custom-call | flops 999999995904 | bytes 1000000000 | tf_op jit(solution)/shard_map/sum_of_outer/pallas_call | solution.py:365
  381.9 2.5 collective-permute-done.42
  384.5 5.3 transposed.1.own_ref
  389.7 13.8 %expert_rows.3 = bf16[512,2048]{1,0:T(8,128)(2,1)} custom-call(bf16[512,2048]{1,0:T(8,128)(2,1)} %get-tuple-element.543.refs_2_.gate_ref, bf16[512,2048]{1,0:T(8,128)(2,1)} %get-tuple-element.587.up_ref.refs_2_, bf16[2048,2048]{1,0:T(8,128)(2,1)} %all-gather.6.cloned.1.call-done.gate_w_ref, bf16[2048,2048]{1,0:T(8,128)(2,1)} %all-gather.8.cloned.1.call-done.up_w_ref), custom_call_target="tpu_custom_call" | custom-call | flops 999999995904 | bytes 1000000000 | tf_op jit(solution)/shard_map/expert_rows/pallas_call | solution.py:312
  409.9 13.4 %times_transpose.1 = (bf16[512,2048]{1,0:T(8,128)(2,1)}, bf16[512,2048]{1,0:T(8,128)(2,1)}) custom-call(bf16[2048,2048]{1,0:T(8,128)(2,1)} %all-gather.4.cloned.1.call-done.w_ref.b_ref, bf16[512,2048]{1,0:T(8,128)(2,1)} %get-tuple-element.620.refs_0_.refs_2_, bf16[512,2048]{1,0:T(8,128)(2,1)} %get-tuple-element.621.refs_1_.refs_3_), custom_call_target="tpu_custom_call" | custom-call | flops 999999995904 | bytes 1000000000 | tf_op jit(solution)/shard_map/times_transpose/pallas_call | solution.py:333
  423.5 2.7 add_convert_fusion.5
  430.1 3.7 all-to-all-start.3
  434.4 6.4 collective-permute-done.47
  453.0 3.4 grad_pairs.1
  457.9 4.2 all-to-all-start.4
  463.8 13.4 %sum_of_outer.4 = bf16[2048,2048]{1,0:T(8,128)(2,1)} custom-call(bf16[512,2048]{1,0:T(8,128)(2,1)} %get-tuple-element.585.refs_0_, bf16[512,2048]{1,0:T(8,128)(2,1)} %get-tuple-element.586.refs_1_, bf16[512,2048]{1,0:T(8,128)(2,1)} %get-tuple-element.587.up_ref.refs_2_, bf16[512,2048]{1,0:T(8,128)(2,1)} %get-tuple-element.588.up_ref.refs_3_), custom_call_target="tpu_custom_call" | custom-call | flops 999999995904 | bytes 1000000000 | tf_op jit(solution)/shard_map/sum_of_outer/pallas_call | solution.py:365
  483.5 4.0 collective-permute-done.53.refs_2_
  487.5 15.6 %attend_back.1 = (bf16[8,6,128,128]{3,2,1,0:T(8,128)(2,1)}, f32[8,128]{1,0:T(8,128)S(1)}) custom-call(bf16[8,6,128,128]{3,2,1,0:T(8,128)(2,1)S(1)} %copy-done.27, bf16[8,6,128,128]{3,2,1,0:T(8,128)(2,1)S(1)} %copy-done.27, bf16[8,6,128,128]{3,2,1,0:T(8,128)(2,1)S(1)} %copy-done.27, bf16[8,2,128,128]{3,2,1,0:T(8,128)(2,1)} %all-to-all-done.4.m_ref, ...), custom_call_target="tpu_custom_call" | custom-call | flops 999999995904 | bytes 1000000000 | tf_op jit(solution)/shard_map/attend_back/pallas_call | solution.py:169
  504.2 4.9 out_grads.1
  515.5 2.5 convert.35
  520.8 5.7 all-to-all-start.5
  526.6 8.4 %head_weights.1.own_ref = bf16[2048,384]{1,0:T(8,128)(2,1)S(1)} custom-call(s32[64]{0:T(128)S(1)} %copy-done.38, bf16[8,6,128,128]{3,2,1,0:T(8,128)(2,1)} %get-tuple-element.613.g_ref, bf16[2048,1024]{1,0:T(8,128)(2,1)} %transposed.1.own_ref, bf16[2048,1024]{1,0:T(8,128)(2,1)} %collective-permute-done.50.beside_ref), custom_call_target="tpu_custom_call" | custom-call | flops 999999995904 | bytes 1000000000 | tf_op jit(solution)/shard_map/head_weights/pallas_call | solution.py:611
  537.8 3.2 add_convert_fusion.1
  543.0 13.4 %sum_of_outer.5 = bf16[2048,2048]{1,0:T(8,128)(2,1)} custom-call(bf16[512,2048]{1,0:T(8,128)(2,1)} %get-tuple-element.618.refs_0_, bf16[512,2048]{1,0:T(8,128)(2,1)} %get-tuple-element.619.refs_1_, bf16[512,2048]{1,0:T(8,128)(2,1)} %get-tuple-element.620.refs_0_.refs_2_, bf16[512,2048]{1,0:T(8,128)(2,1)} %get-tuple-element.621.refs_1_.refs_3_), custom_call_target="tpu_custom_call" | custom-call | flops 999999995904 | bytes 1000000000 | tf_op jit(solution)/shard_map/sum_of_outer/pallas_call | solution.py:365
  557.6 4.8 collective-permute-done.61.other_ref
  570.7 2.9 collective-permute-start.69
  573.7 2.6 multiply_reduce_fusion
  579.0 10.2 %collective-permute-start.70 = (bf16[64,2048]{1,0:T(8,128)(2,1)}, bf16[64,2048]{1,0:T(8,128)(2,1)}, u32[]{:S(2)}, u32[]{:S(2)}) collective-permute-start(bf16[64,2048]{1,0:T(8,128)(2,1)} %get-tuple-element.803), channel_id=1, source_target_pairs={{0,8},{8,16},{16,24},{24,28},{28,20},{20,12},{12,4},{4,0},{1,9},{9... | collective-permute-start | bytes 786440 | tf_op jit(solution)/shard_map/ppermute | solution.py:876
  589.3 11.8 %pair_normed.1 = (f32[128,2048]{1,0:T(8,128)S(1)}, bf16[128,2048]{1,0:T(8,128)(2,1)S(1)}) custom-call(bf16[8,6,128,128]{3,2,1,0:T(8,128)(2,1)} %all-to-all-done.5.g_ref, bf16[2048,3072]{1,0:T(8,128)(2,1)} %get-tuple-element.645.w_ref), custom_call_target="tpu_custom_call" | custom-call | flops 999999995904 | bytes 1000000000 | tf_op jit(solution)/shard_map/pair_normed/pallas_call | solution.py:670
  604.2 6.8 collective-permute-start.74
  613.3 5.1 spread.5
  622.8 4.5 split_experts.3
  629.3 2.5 collective-permute-done.75.refs_0_
  634.9 2.5 collective-permute-done.77
  639.2 2.9 spread.6
  644.9 4.5 split_experts.4
  651.7 2.5 collective-permute-done.81.refs_0_
  663.2 3.9 collective-permute-done.84
  667.1 2.5 collective-permute-done.85
  676.7 4.5 split_experts.5
  684.4 3.2 collective-permute-done.90
  690.4 2.6 spread.9
  (453 shorter events, 211.5 us)
Async XLA Ops:
  7.2 198.6 %all-gather.4.cloned.1.call-start = ((), (), s32[]{:S(2)}) async-start(), calls=%async_computation.9 | async-start | bytes 10485760 | tf_op jit(solution)/shard_map/all_gather | solution.py:1063
  15.8 14.9 %collective-permute-start = (bf16[128,2048]{1,0:T(8,128)(2,1)S(1)}, bf16[128,2048]{1,0:T(8,128)(2,1)S(1)}, u32[]{:S(2)}, u32[]{:S(2)}) collective-permute-start(bf16[128,2048]{1,0:T(8,128)(2,1)S(1)} %bitcast.65), channel_id=1, source_target_pairs={{0,8},{8,16},{16,24},{24,28},{28,20},{20,12},{12,4},{4,0},{1,9},{9... | collective-permute-start | bytes 1572872 | tf_op jit(solution)/shard_map/ppermute | solution.py:876
  18.9 27.6 %collective-permute-start.4 = (bf16[64,5120]{1,0:T(8,128)(2,1)S(1)}, bf16[64,5120]{1,0:T(8,128)(2,1)S(1)}, u32[]{:S(2)}, u32[]{:S(2)}) collective-permute-start(bf16[64,5120]{1,0:T(8,128)(2,1)S(1)} %get-tuple-element.398), channel_id=1, source_target_pairs={{0,2},{1,3},{2,0},{3,1},{4,6},{5,7},{6,4},{7,5},{8,10},{9,11},{10,... | collective-permute-start | bytes 1966088 | tf_op jit(solution)/shard_map/ppermute | solution.py:864
  20.8 25.6 %collective-permute-start.5 = (bf16[64,3072]{1,0:T(8,128)(2,1)S(1)}, bf16[64,3072]{1,0:T(8,128)(2,1)S(1)}, u32[]{:S(2)}, u32[]{:S(2)}) collective-permute-start(bf16[64,3072]{1,0:T(8,128)(2,1)S(1)} %get-tuple-element.399), channel_id=1, source_target_pairs={{0,3},{1,2},{2,1},{3,0},{4,7},{5,6},{6,5},{7,4},{8,11},{9,10},{10,... | collective-permute-start | bytes 1179656 | tf_op jit(solution)/shard_map/ppermute | solution.py:864
  46.5 159.3 %all-gather.6.cloned.1.call-start = ((), (), s32[]{:S(2)}) async-start(), calls=%async_computation.10 | async-start | bytes 10485760 | tf_op jit(solution)/shard_map/all_gather | solution.py:1066
  47.1 22.6 %collective-permute-start.6 = (bf16[256,2048]{1,0:T(8,128)(2,1)S(1)}, bf16[256,2048]{1,0:T(8,128)(2,1)S(1)}, u32[]{:S(2)}, u32[]{:S(2)}) collective-permute-start(bf16[256,2048]{1,0:T(8,128)(2,1)S(1)} %fetched_payload.1.refs_4_.refs_0_), channel_id=1, source_target_pairs={{0,8},{8,16},{16,24},{24,28},{28,20},{20,12},{12,4},{4,0},{1,9},{9... | collective-permute-start | bytes 3145736 | tf_op jit(solution)/shard_map/ppermute | solution.py:876
  48.8 22.2 %collective-permute-start.7 = (bf16[256,2048]{1,0:T(8,128)(2,1)S(1)}, bf16[256,2048]{1,0:T(8,128)(2,1)S(1)}, u32[]{:S(2)}, u32[]{:S(2)}) collective-permute-start(bf16[256,2048]{1,0:T(8,128)(2,1)S(1)} %fetched_payload.1.refs_4_.refs_0_), channel_id=1, source_target_pairs={{0,4},{8,0},{16,8},{24,16},{28,24},{20,28},{12,20},{4,12},{1,5},{9... | collective-permute-start | bytes 3145736 | tf_op jit(solution)/shard_map/ppermute | solution.py:876
  71.0 157.9 %all-gather.8.cloned.1.call-start = ((), (), s32[]{:S(2)}) async-start(), calls=%async_computation.11 | async-start | bytes 10485760 | tf_op jit(solution)/shard_map/all_gather | solution.py:1075
  75.4 25.4 %collective-permute-start.10 = (bf16[256,2048]{1,0:T(8,128)(2,1)S(1)}, bf16[256,2048]{1,0:T(8,128)(2,1)}, u32[]{:S(2)}, u32[]{:S(2)}) collective-permute-start(bf16[256,2048]{1,0:T(8,128)(2,1)S(1)} %collective-permute-done.6.refs_6_.refs_2_), channel_id=1, source_target_pairs={{0,8},{8,16},{16,24},{24,28},{28,20},{20,12},{12,4},{4,0},{1,9},{9... | collective-permute-start | bytes 3145736 | tf_op jit(solution)/shard_map/ppermute | solution.py:876
  77.0 25.1 %collective-permute-start.11 = (bf16[256,2048]{1,0:T(8,128)(2,1)S(1)}, bf16[256,2048]{1,0:T(8,128)(2,1)}, u32[]{:S(2)}, u32[]{:S(2)}) collective-permute-start(bf16[256,2048]{1,0:T(8,128)(2,1)S(1)} %collective-permute-done.7.refs_5_.refs_1_), channel_id=1, source_target_pairs={{0,4},{8,0},{16,8},{24,16},{28,24},{20,28},{12,20},{4,12},{1,5},{9... | collective-permute-start | bytes 3145736 | tf_op jit(solution)/shard_map/ppermute | solution.py:876
  102.2 27.5 %collective-permute-start.15 = (bf16[256,2048]{1,0:T(8,128)(2,1)}, bf16[256,2048]{1,0:T(8,128)(2,1)S(1)}, u32[]{:S(2)}, u32[]{:S(2)}) collective-permute-start(bf16[256,2048]{1,0:T(8,128)(2,1)} %collective-permute-done.10.refs_8_.refs_4_), channel_id=1, source_target_pairs={{0,8},{8,16},{16,24},{24,28},{28,20},{20,12},{12,4},{4,0},{1,9},{9... | collective-permute-start | bytes 3145736 | tf_op jit(solution)/shard_map/ppermute | solution.py:876
  103.8 25.9 %collective-permute-start.16 = (bf16[256,2048]{1,0:T(8,128)(2,1)}, bf16[256,2048]{1,0:T(8,128)(2,1)S(1)}, u32[]{:S(2)}, u32[]{:S(2)}) collective-permute-start(bf16[256,2048]{1,0:T(8,128)(2,1)} %collective-permute-done.11.refs_7_.refs_3_), channel_id=1, source_target_pairs={{0,4},{8,0},{16,8},{24,16},{28,24},{20,28},{12,20},{4,12},{1,5},{9... | collective-permute-start | bytes 3145736 | tf_op jit(solution)/shard_map/ppermute | solution.py:876
  104.9 24.8 %all-to-all-start = ((s32[8,128,8]{1,2,0:T(8,128)}), s32[8,128,8]{1,2,0:T(8,128)}, u32[]{:S(2)}, u32[]{:S(2)}) async-start(s32[8,128,8]{1,2,0:T(8,128)} %broadcast_in_dim.48), calls=%async_computation | async-start | bytes 65536 | tf_op jit(solution)/shard_map/all_to_all | solution.py:1069
  155.5 38.1 %all-to-all-start.1 = ((bf16[8,6,128,128]{3,2,1,0:T(8,128)(2,1)}), bf16[8,6,128,128]{3,2,1,0:T(8,128)(2,1)S(1)}, u32[]{:S(2)}, u32[]{:S(2)}) async-start(bf16[8,6,128,128]{3,2,1,0:T(8,128)(2,1)} %copy-done.28), calls=%async_computation.1 | async-start | bytes 3145728 | tf_op jit(solution)/shard_map/all_to_all | solution.py:1027
  230.3 14.9 %collective-permute-start.20 = (bf16[128,2048]{1,0:T(8,128)(2,1)S(1)}, bf16[128,2048]{1,0:T(8,128)(2,1)}, u32[]{:S(2)}, u32[]{:S(2)}) collective-permute-start(bf16[128,2048]{1,0:T(8,128)(2,1)S(1)} %multiply_convert_fusion.refs_0_), channel_id=1, source_target_pairs={{0,8},{8,16},{16,24},{24,28},{28,20},{20,12},{12,4},{4,0},{1,9},{9... | collective-permute-start | bytes 1572872 | tf_op jit(solution)/shard_map/ppermute | solution.py:876
  231.5 14.9 %collective-permute-start.21 = (bf16[128,2048]{1,0:T(8,128)(2,1)S(1)}, bf16[128,2048]{1,0:T(8,128)(2,1)}, u32[]{:S(2)}, u32[]{:S(2)}) collective-permute-start(bf16[128,2048]{1,0:T(8,128)(2,1)S(1)} %multiply_convert_fusion.refs_0_), channel_id=1, source_target_pairs={{0,4},{8,0},{16,8},{24,16},{28,24},{20,28},{12,20},{4,12},{1,5},{9... | collective-permute-start | bytes 1572872 | tf_op jit(solution)/shard_map/ppermute | solution.py:876
  232.4 56.4 %collective-permute-start.26 = (bf16[128,2048]{1,0:T(8,128)(2,1)}, bf16[128,2048]{1,0:T(8,128)(2,1)}, u32[]{:S(2)}, u32[]{:S(2)}) collective-permute-start(bf16[128,2048]{1,0:T(8,128)(2,1)} %collective-permute-done.2.refs_0_), channel_id=1, source_target_pairs={{0,8},{8,16},{16,24},{24,28},{28,20},{20,12},{12,4},{4,0},{1,9},{9... | collective-permute-start | bytes 1572872 | tf_op jit(solution)/shard_map/ppermute | solution.py:876
  233.5 55.3 %collective-permute-start.27 = (bf16[128,2048]{1,0:T(8,128)(2,1)}, bf16[128,2048]{1,0:T(8,128)(2,1)}, u32[]{:S(2)}, u32[]{:S(2)}) collective-permute-start(bf16[128,2048]{1,0:T(8,128)(2,1)} %collective-permute-done.3.refs_3_), channel_id=1, source_target_pairs={{0,4},{8,0},{16,8},{24,16},{28,24},{20,28},{12,20},{4,12},{1,5},{9... | collective-permute-start | bytes 1572872 | tf_op jit(solution)/shard_map/ppermute | solution.py:876
  246.4 20.5 %collective-permute-start.22 = (bf16[128,2048]{1,0:T(8,128)(2,1)}, bf16[128,2048]{1,0:T(8,128)(2,1)}, u32[]{:S(2)}, u32[]{:S(2)}) collective-permute-start(bf16[128,2048]{1,0:T(8,128)(2,1)} %collective-permute-done.20.refs_2_), channel_id=1, source_target_pairs={{0,8},{8,16},{16,24},{24,28},{28,20},{20,12},{12,4},{4,0},{1,9},{9... | collective-permute-start | bytes 1572872 | tf_op jit(solution)/shard_map/ppermute | solution.py:876
  246.9 20.8 %collective-permute-start.23 = (bf16[128,2048]{1,0:T(8,128)(2,1)}, bf16[128,2048]{1,0:T(8,128)(2,1)}, u32[]{:S(2)}, u32[]{:S(2)}) collective-permute-start(bf16[128,2048]{1,0:T(8,128)(2,1)} %collective-permute-done.21.refs_1_), channel_id=1, source_target_pairs={{0,4},{8,0},{16,8},{24,16},{28,24},{20,28},{12,20},{4,12},{1,5},{9... | collective-permute-start | bytes 1572872 | tf_op jit(solution)/shard_map/ppermute | solution.py:876
  267.7 21.0 %collective-permute-start.24 = (bf16[128,2048]{1,0:T(8,128)(2,1)}, bf16[128,2048]{1,0:T(8,128)(2,1)}, u32[]{:S(2)}, u32[]{:S(2)}) collective-permute-start(bf16[128,2048]{1,0:T(8,128)(2,1)} %collective-permute-done.22.refs_0_), channel_id=1, source_target_pairs={{0,8},{8,16},{16,24},{24,28},{28,20},{20,12},{12,4},{4,0},{1,9},{9... | collective-permute-start | bytes 1572872 | tf_op jit(solution)/shard_map/ppermute | solution.py:876
  268.4 20.3 %collective-permute-start.25 = (bf16[128,2048]{1,0:T(8,128)(2,1)}, bf16[128,2048]{1,0:T(8,128)(2,1)}, u32[]{:S(2)}, u32[]{:S(2)}) collective-permute-start(bf16[128,2048]{1,0:T(8,128)(2,1)} %collective-permute-done.23.refs_3_), channel_id=1, source_target_pairs={{0,4},{8,0},{16,8},{24,16},{28,24},{20,28},{12,20},{4,12},{1,5},{9... | collective-permute-start | bytes 1572872 | tf_op jit(solution)/shard_map/ppermute | solution.py:876
  298.9 39.1 %collective-permute-start.34 = (bf16[4,2,128,128]{3,2,1,0:T(8,128)(2,1)}, bf16[4,2,128,128]{3,2,1,0:T(8,128)(2,1)}, u32[]{:S(2)}, u32[]{:S(2)}) collective-permute-start(bf16[4,2,128,128]{3,2,1,0:T(8,128)(2,1)} %constant_dynamic-slice_fusion), channel_id=1, source_target_pairs={{0,2},{1,3},{2,0},{3,1},{4,6},{5,7},{6,4},{7,5},{8,10},{9,11},{10,... | collective-permute-start | bytes 786440 | tf_op jit(solution)/shard_map/ppermute | solution.py:864
  317.1 20.9 %collective-permute-start.35 = (bf16[128,2048]{1,0:T(8,128)(2,1)}, bf16[128,2048]{1,0:T(8,128)(2,1)}, u32[]{:S(2)}, u32[]{:S(2)}) collective-permute-start(bf16[128,2048]{1,0:T(8,128)(2,1)} %collective-permute-done.32.refs_2_), channel_id=1, source_target_pairs={{0,8},{8,16},{16,24},{24,28},{28,20},{20,12},{12,4},{4,0},{1,9},{9... | collective-permute-start | bytes 1572872 | tf_op jit(solution)/shard_map/ppermute | solution.py:876
  318.5 19.5 %collective-permute-start.36 = (bf16[128,2048]{1,0:T(8,128)(2,1)}, bf16[128,2048]{1,0:T(8,128)(2,1)}, u32[]{:S(2)}, u32[]{:S(2)}) collective-permute-start(bf16[128,2048]{1,0:T(8,128)(2,1)} %collective-permute-done.33.refs_1_), channel_id=1, source_target_pairs={{0,4},{8,0},{16,8},{24,16},{28,24},{20,28},{12,20},{4,12},{1,5},{9... | collective-permute-start | bytes 1572872 | tf_op jit(solution)/shard_map/ppermute | solution.py:876
  338.1 20.1 %collective-permute-start.37 = (bf16[128,2048]{1,0:T(8,128)(2,1)}, bf16[128,2048]{1,0:T(8,128)(2,1)}, u32[]{:S(2)}, u32[]{:S(2)}) collective-permute-start(bf16[128,2048]{1,0:T(8,128)(2,1)} %collective-permute-done.35.refs_4_), channel_id=1, source_target_pairs={{0,8},{8,16},{16,24},{24,28},{28,20},{20,12},{12,4},{4,0},{1,9},{9... | collective-permute-start | bytes 1572872 | tf_op jit(solution)/shard_map/ppermute | solution.py:876
  339.5 18.6 %collective-permute-start.38 = (bf16[128,2048]{1,0:T(8,128)(2,1)}, bf16[128,2048]{1,0:T(8,128)(2,1)}, u32[]{:S(2)}, u32[]{:S(2)}) collective-permute-start(bf16[128,2048]{1,0:T(8,128)(2,1)} %collective-permute-done.36.refs_3_), channel_id=1, source_target_pairs={{0,4},{8,0},{16,8},{24,16},{28,24},{20,28},{12,20},{4,12},{1,5},{9... | collective-permute-start | bytes 1572872 | tf_op jit(solution)/shard_map/ppermute | solution.py:876
  356.1 15.5 %collective-permute-start.39 = (bf16[64,2048]{1,0:T(8,128)(2,1)}, bf16[64,2048]{1,0:T(8,128)(2,1)}, u32[]{:S(2)}, u32[]{:S(2)}) collective-permute-start(bf16[64,2048]{1,0:T(8,128)(2,1)} %get-tuple-element.823), channel_id=1, source_target_pairs={{0,8},{8,16},{16,24},{24,28},{28,20},{20,12},{12,4},{4,0},{1,9},{9... | collective-permute-start | bytes 786440 | tf_op jit(solution)/shard_map/ppermute | solution.py:876
  378.0 25.6 %collective-permute-start.43 = (bf16[128,2048]{1,0:T(8,128)(2,1)}, bf16[128,2048]{1,0:T(8,128)(2,1)}, u32[]{:S(2)}, u32[]{:S(2)}) collective-permute-start(bf16[128,2048]{1,0:T(8,128)(2,1)} %pad_maximum_fusion.5), channel_id=1, source_target_pairs={{0,8},{8,16},{16,24},{24,28},{28,20},{20,12},{12,4},{4,0},{1,9},{9... | collective-permute-start | bytes 1572872 | tf_op jit(solution)/shard_map/ppermute | solution.py:876
  380.3 23.3 %collective-permute-start.44 = (bf16[128,2048]{1,0:T(8,128)(2,1)}, bf16[128,2048]{1,0:T(8,128)(2,1)}, u32[]{:S(2)}, u32[]{:S(2)}) collective-permute-start(bf16[128,2048]{1,0:T(8,128)(2,1)} %pad_maximum_fusion.6), channel_id=1, source_target_pairs={{0,4},{8,0},{16,8},{24,16},{28,24},{20,28},{12,20},{4,12},{1,5},{9... | collective-permute-start | bytes 1572872 | tf_op jit(solution)/shard_map/ppermute | solution.py:876
  405.8 17.5 %collective-permute-start.45 = (bf16[128,2048]{1,0:T(8,128)(2,1)}, bf16[128,2048]{1,0:T(8,128)(2,1)}, u32[]{:S(2)}, u32[]{:S(2)}) collective-permute-start(bf16[128,2048]{1,0:T(8,128)(2,1)} %add_convert_fusion.8), channel_id=1, source_target_pairs={{0,8},{8,16},{16,24},{24,28},{28,20},{20,12},{12,4},{4,0},{1,9},{9... | collective-permute-start | bytes 1572872 | tf_op jit(solution)/shard_map/ppermute | solution.py:876
  423.3 29.7 %collective-permute-start.50 = (bf16[2048,1024]{1,0:T(8,128)(2,1)}, bf16[2048,1024]{1,0:T(8,128)(2,1)}, u32[]{:S(2)}, u32[]{:S(2)}) collective-permute-start(bf16[2048,1024]{1,0:T(8,128)(2,1)} %transposed.1.own_ref), channel_id=1, source_target_pairs={{0,1},{1,0},{2,3},{3,2},{4,5},{5,4},{6,7},{7,6},{8,9},{9,8},{10,11... | collective-permute-start | bytes 12582920 | tf_op jit(solution)/shard_map/ppermute | solution.py:864
  426.2 14.6 %collective-permute-start.47 = (bf16[128,2048]{1,0:T(8,128)(2,1)}, bf16[128,2048]{1,0:T(8,128)(2,1)}, u32[]{:S(2)}, u32[]{:S(2)}) collective-permute-start(bf16[128,2048]{1,0:T(8,128)(2,1)} %get-tuple-element.819), channel_id=1, source_target_pairs={{0,8},{8,16},{16,24},{24,28},{28,20},{20,12},{12,4},{4,0},{1,9},{9... | collective-permute-start | bytes 1572872 | tf_op jit(solution)/shard_map/ppermute | solution.py:876
  433.8 189.0 %reduce-scatter.4.cloned.1.call-start = ((), (), s32[]{:S(2)}) async-start(), calls=%async_computation.12 | async-start | bytes 10485760 | tf_op jit(solution)/shard_map/reduce_scatter | solution.py:1168
  457.9 25.6 %all-to-all-start.4 = ((bf16[8,2,128,128]{3,2,1,0:T(8,128)(2,1)}), bf16[8,2,128,128]{3,2,1,0:T(8,128)(2,1)}, u32[]{:S(2)}, u32[]{:S(2)}) async-start(bf16[8,2,128,128]{3,2,1,0:T(8,128)(2,1)} %grad_pairs.1), calls=%async_computation.4 | async-start | bytes 1048576 | tf_op jit(solution)/shard_map/all_to_all | solution.py:1027
  462.1 182.8 %reduce-scatter.6.cloned.1.call-start = ((), (), s32[]{:S(2)}) async-start(), calls=%async_computation.13 | async-start | bytes 10485760 | tf_op jit(solution)/shard_map/reduce_scatter | solution.py:1168
  462.2 25.3 %collective-permute-start.53 = (bf16[128,2048]{1,0:T(8,128)(2,1)}, bf16[128,2048]{1,0:T(8,128)(2,1)}, u32[]{:S(2)}, u32[]{:S(2)}) collective-permute-start(bf16[128,2048]{1,0:T(8,128)(2,1)} %get-tuple-element.592.own_ref.refs_0_), channel_id=1, source_target_pairs={{0,2},{1,3},{2,0},{3,1},{4,6},{5,7},{6,4},{7,5},{8,10},{9,11},{10,... | collective-permute-start | bytes 1572872 | tf_op jit(solution)/shard_map/ppermute | solution.py:864
  480.4 28.7 %collective-permute-start.55 = (bf16[128,2048]{1,0:T(8,128)(2,1)}, bf16[128,2048]{1,0:T(8,128)(2,1)}, u32[]{:S(2)}, u32[]{:S(2)}) collective-permute-start(bf16[128,2048]{1,0:T(8,128)(2,1)} %pad_maximum_fusion.8), channel_id=1, source_target_pairs={{0,8},{8,16},{16,24},{24,28},{28,20},{20,12},{12,4},{4,0},{1,9},{9... | collective-permute-start | bytes 1572872 | tf_op jit(solution)/shard_map/ppermute | solution.py:876
  483.2 25.9 %collective-permute-start.56 = (bf16[128,2048]{1,0:T(8,128)(2,1)}, bf16[128,2048]{1,0:T(8,128)(2,1)}, u32[]{:S(2)}, u32[]{:S(2)}) collective-permute-start(bf16[128,2048]{1,0:T(8,128)(2,1)} %pad_maximum_fusion.9), channel_id=1, source_target_pairs={{0,4},{8,0},{16,8},{24,16},{28,24},{20,28},{12,20},{4,12},{1,5},{9... | collective-permute-start | bytes 1572872 | tf_op jit(solution)/shard_map/ppermute | solution.py:876
  487.5 15.6 %collective-permute-start.54 = (bf16[128,2048]{1,0:T(8,128)(2,1)}, bf16[128,2048]{1,0:T(8,128)(2,1)}, u32[]{:S(2)}, u32[]{:S(2)}) collective-permute-start(bf16[128,2048]{1,0:T(8,128)(2,1)} %collective-permute-done.53.refs_2_), channel_id=1, source_target_pairs={{0,1},{1,0},{2,3},{3,2},{4,5},{5,4},{6,7},{7,6},{8,9},{9,8},{10,11... | collective-permute-start | bytes 1572872 | tf_op jit(solution)/shard_map/ppermute | solution.py:864
  511.3 23.6 %collective-permute-start.57 = (bf16[128,2048]{1,0:T(8,128)(2,1)}, bf16[128,2048]{1,0:T(8,128)(2,1)}, u32[]{:S(2)}, u32[]{:S(2)}) collective-permute-start(bf16[128,2048]{1,0:T(8,128)(2,1)} %add_convert_fusion.4), channel_id=1, source_target_pairs={{0,8},{8,16},{16,24},{24,28},{28,20},{20,12},{12,4},{4,0},{1,9},{9... | collective-permute-start | bytes 1572872 | tf_op jit(solution)/shard_map/ppermute | solution.py:876
  515.2 19.8 %collective-permute-start.58 = (bf16[128,2048]{1,0:T(8,128)(2,1)}, bf16[128,2048]{1,0:T(8,128)(2,1)}, u32[]{:S(2)}, u32[]{:S(2)}) collective-permute-start(bf16[128,2048]{1,0:T(8,128)(2,1)} %add_convert_fusion.3), channel_id=1, source_target_pairs={{0,4},{8,0},{16,8},{24,16},{28,24},{20,28},{12,20},{4,12},{1,5},{9... | collective-permute-start | bytes 1572872 | tf_op jit(solution)/shard_map/ppermute | solution.py:876
  518.7 16.2 %collective-permute-start.59 = (bf16[32,2048]{1,0:T(8,128)(2,1)}, bf16[32,2048]{1,0:T(8,128)(2,1)}, u32[]{:S(2)}, u32[]{:S(2)}) collective-permute-start(bf16[32,2048]{1,0:T(8,128)(2,1)} %get-tuple-element.809), channel_id=1, source_target_pairs={{0,8},{8,16},{16,24},{24,28},{28,20},{20,12},{12,4},{4,0},{1,9},{9... | collective-permute-start | bytes 393224 | tf_op jit(solution)/shard_map/ppermute | solution.py:876
  520.5 14.5 %collective-permute-start.60 = (bf16[32,2048]{1,0:T(8,128)(2,1)}, bf16[32,2048]{1,0:T(8,128)(2,1)}, u32[]{:S(2)}, u32[]{:S(2)}) collective-permute-start(bf16[32,2048]{1,0:T(8,128)(2,1)} %get-tuple-element.808), channel_id=1, source_target_pairs={{0,4},{8,0},{16,8},{24,16},{28,24},{20,28},{12,20},{4,12},{1,5},{9... | collective-permute-start | bytes 393224 | tf_op jit(solution)/shard_map/ppermute | solution.py:876
  520.8 68.5 %all-to-all-start.5 = ((bf16[8,6,128,128]{3,2,1,0:T(8,128)(2,1)}), bf16[8,6,128,128]{3,2,1,0:T(8,128)(2,1)}, u32[]{:S(2)}, u32[]{:S(2)}) async-start(bf16[8,6,128,128]{3,2,1,0:T(8,128)(2,1)} %get-tuple-element.613.g_ref), calls=%async_computation.5 | async-start | bytes 3145728 | tf_op jit(solution)/shard_map/all_to_all | solution.py:1030
  526.5 150.2 %reduce-scatter.8.cloned.1.call-start = ((), (), s32[]{:S(2)}) async-start(), calls=%async_computation.14 | async-start | bytes 10485760 | tf_op jit(solution)/shard_map/reduce_scatter | solution.py:1168
  536.1 26.3 %collective-permute-start.61 = (bf16[1024,384]{1,0:T(8,128)(2,1)}, bf16[1024,384]{1,0:T(8,128)(2,1)}, u32[]{:S(2)}, u32[]{:S(2)}) collective-permute-start(bf16[1024,384]{1,0:T(8,128)(2,1)} %slice.263), channel_id=1, source_target_pairs={{0,2},{1,3},{2,0},{3,1},{4,6},{5,7},{6,4},{7,5},{8,10},{9,11},{10,... | collective-permute-start | bytes 2359304 | tf_op jit(solution)/shard_map/ppermute | solution.py:864
  541.0 29.7 %collective-permute-start.63 = (bf16[128,2048]{1,0:T(8,128)(2,1)}, bf16[128,2048]{1,0:T(8,128)(2,1)}, u32[]{:S(2)}, u32[]{:S(2)}) collective-permute-start(bf16[128,2048]{1,0:T(8,128)(2,1)} %get-tuple-element.811), channel_id=1, source_target_pairs={{0,8},{8,16},{16,24},{24,28},{28,20},{20,12},{12,4},{4,0},{1,9},{9... | collective-permute-start | bytes 1572872 | tf_op jit(solution)/shard_map/ppermute | solution.py:876
  542.8 30.8 %collective-permute-start.64 = (bf16[128,2048]{1,0:T(8,128)(2,1)}, bf16[128,2048]{1,0:T(8,128)(2,1)}, u32[]{:S(2)}, u32[]{:S(2)}) collective-permute-start(bf16[128,2048]{1,0:T(8,128)(2,1)} %get-tuple-element.810), channel_id=1, source_target_pairs={{0,4},{8,0},{16,8},{24,16},{28,24},{20,28},{12,20},{4,12},{1,5},{9... | collective-permute-start | bytes 1572872 | tf_op jit(solution)/shard_map/ppermute | solution.py:876
  569.0 32.4 %collective-permute-start.68 = (bf16[512,768]{1,0:T(8,128)(2,1)}, bf16[512,768]{1,0:T(8,128)(2,1)}, u32[]{:S(2)}, u32[]{:S(2)}) collective-permute-start(bf16[512,768]{1,0:T(8,128)(2,1)} %side_by_side.1.refs_0_), channel_id=1, source_target_pairs={{0,8},{8,16},{16,24},{24,28},{28,20},{20,12},{12,4},{4,0},{1,9},{9... | collective-permute-start | bytes 2359304 | tf_op jit(solution)/shard_map/ppermute | solution.py:876
  570.7 30.7 %collective-permute-start.69 = (bf16[512,768]{1,0:T(8,128)(2,1)}, bf16[512,768]{1,0:T(8,128)(2,1)}, u32[]{:S(2)}, u32[]{:S(2)}) collective-permute-start(bf16[512,768]{1,0:T(8,128)(2,1)} %side_by_side.1.refs_0_), channel_id=1, source_target_pairs={{0,4},{8,0},{16,8},{24,16},{28,24},{20,28},{12,20},{4,12},{1,5},{9... | collective-permute-start | bytes 2359304 | tf_op jit(solution)/shard_map/ppermute | solution.py:876
  576.9 24.2 %collective-permute-start.67 = (f32[17,2048]{1,0:T(8,128)}, f32[17,2048]{1,0:T(8,128)}, u32[]{:S(2)}, u32[]{:S(2)}) collective-permute-start(f32[17,2048]{1,0:T(8,128)} %pad_maximum_fusion.12), channel_id=1, source_target_pairs={{0,1},{1,0},{2,3},{3,2},{4,5},{5,4},{6,7},{7,6},{8,9},{9,8},{10,11... | collective-permute-start | bytes 417800 | tf_op jit(solution)/shard_map/ppermute | solution.py:864
  579.0 22.3 %collective-permute-start.70 = (bf16[64,2048]{1,0:T(8,128)(2,1)}, bf16[64,2048]{1,0:T(8,128)(2,1)}, u32[]{:S(2)}, u32[]{:S(2)}) collective-permute-start(bf16[64,2048]{1,0:T(8,128)(2,1)} %get-tuple-element.803), channel_id=1, source_target_pairs={{0,8},{8,16},{16,24},{24,28},{28,20},{20,12},{12,4},{4,0},{1,9},{9... | collective-permute-start | bytes 786440 | tf_op jit(solution)/shard_map/ppermute | solution.py:876
  601.1 19.9 %collective-permute-start.73 = (bf16[128,2048]{1,0:T(8,128)(2,1)S(1)}, bf16[128,2048]{1,0:T(8,128)(2,1)S(1)}, u32[]{:S(2)}, u32[]{:S(2)}) collective-permute-start(bf16[128,2048]{1,0:T(8,128)(2,1)S(1)} %get-tuple-element.665), channel_id=1, source_target_pairs={{0,1},{1,0},{2,3},{3,2},{4,5},{5,4},{6,7},{7,6},{8,9},{9,8},{10,11... | collective-permute-start | bytes 1572872 | tf_op jit(solution)/shard_map/ppermute | solution.py:864
  602.5 18.2 %collective-permute-start.72 = (f32[17,2048]{1,0:T(8,128)S(1)}, f32[17,2048]{1,0:T(8,128)S(1)}, u32[]{:S(2)}, u32[]{:S(2)}) collective-permute-start(f32[17,2048]{1,0:T(8,128)S(1)} %add.181), channel_id=1, source_target_pairs={{0,2},{1,3},{2,0},{3,1},{4,6},{5,7},{6,4},{7,5},{8,10},{9,11},{10,... | collective-permute-start | bytes 417800 | tf_op jit(solution)/shard_map/ppermute | solution.py:864
  604.2 25.1 %collective-permute-start.74 = (bf16[512,768]{1,0:T(8,128)(2,1)}, bf16[512,768]{1,0:T(8,128)(2,1)S(1)}, u32[]{:S(2)}, u32[]{:S(2)}) collective-permute-start(bf16[512,768]{1,0:T(8,128)(2,1)} %collective-permute-done.68.refs_2_), channel_id=1, source_target_pairs={{0,8},{8,16},{16,24},{24,28},{28,20},{20,12},{12,4},{4,0},{1,9},{9... | collective-permute-start | bytes 2359304 | tf_op jit(solution)/shard_map/ppermute | solution.py:876
  611.0 20.8 %collective-permute-start.75 = (bf16[512,768]{1,0:T(8,128)(2,1)}, bf16[512,768]{1,0:T(8,128)(2,1)}, u32[]{:S(2)}, u32[]{:S(2)}) collective-permute-start(bf16[512,768]{1,0:T(8,128)(2,1)} %collective-permute-done.69.refs_1_), channel_id=1, source_target_pairs={{0,4},{8,0},{16,8},{24,16},{28,24},{20,28},{12,20},{4,12},{1,5},{9... | collective-permute-start | bytes 2359304 | tf_op jit(solution)/shard_map/ppermute | solution.py:876
  618.5 16.5 %collective-permute-start.76 = (bf16[64,2048]{1,0:T(8,128)(2,1)}, bf16[64,2048]{1,0:T(8,128)(2,1)}, u32[]{:S(2)}, u32[]{:S(2)}) collective-permute-start(bf16[64,2048]{1,0:T(8,128)(2,1)} %get-tuple-element.801), channel_id=1, source_target_pairs={{0,8},{8,16},{16,24},{24,28},{28,20},{20,12},{12,4},{4,0},{1,9},{9... | collective-permute-start | bytes 786440 | tf_op jit(solution)/shard_map/ppermute | solution.py:876
  620.7 16.7 %collective-permute-start.77 = (bf16[64,2048]{1,0:T(8,128)(2,1)}, bf16[64,2048]{1,0:T(8,128)(2,1)}, u32[]{:S(2)}, u32[]{:S(2)}) collective-permute-start(bf16[64,2048]{1,0:T(8,128)(2,1)} %get-tuple-element.800), channel_id=1, source_target_pairs={{0,4},{8,0},{16,8},{24,16},{28,24},{20,28},{12,20},{4,12},{1,5},{9... | collective-permute-start | bytes 786440 | tf_op jit(solution)/shard_map/ppermute | solution.py:876
  631.8 19.9 %collective-permute-start.80 = (bf16[512,768]{1,0:T(8,128)(2,1)S(1)}, bf16[512,768]{1,0:T(8,128)(2,1)S(1)}, u32[]{:S(2)}, u32[]{:S(2)}) collective-permute-start(bf16[512,768]{1,0:T(8,128)(2,1)S(1)} %collective-permute-done.74.refs_1_), channel_id=1, source_target_pairs={{0,8},{8,16},{16,24},{24,28},{28,20},{20,12},{12,4},{4,0},{1,9},{9... | collective-permute-start | bytes 2359304 | tf_op jit(solution)/shard_map/ppermute | solution.py:876
  631.8 22.4 %collective-permute-start.81 = (bf16[512,768]{1,0:T(8,128)(2,1)}, bf16[512,768]{1,0:T(8,128)(2,1)S(1)}, u32[]{:S(2)}, u32[]{:S(2)}) collective-permute-start(bf16[512,768]{1,0:T(8,128)(2,1)} %collective-permute-done.75.refs_0_), channel_id=1, source_target_pairs={{0,4},{8,0},{16,8},{24,16},{28,24},{20,28},{12,20},{4,12},{1,5},{9... | collective-permute-start | bytes 2359304 | tf_op jit(solution)/shard_map/ppermute | solution.py:876
  642.8 15.9 %collective-permute-start.82 = (bf16[80,2048]{1,0:T(8,128)(2,1)S(1)}, bf16[80,2048]{1,0:T(8,128)(2,1)S(1)}, u32[]{:S(2)}, u32[]{:S(2)}) collective-permute-start(bf16[80,2048]{1,0:T(8,128)(2,1)S(1)} %pack_gains.1.refs_0_), channel_id=1, source_target_pairs={{0,8},{8,16},{16,24},{24,28},{28,20},{20,12},{12,4},{4,0},{1,9},{9... | collective-permute-start | bytes 983048 | tf_op jit(solution)/shard_map/ppermute | solution.py:876
  643.0 18.2 %collective-permute-start.83 = (bf16[80,2048]{1,0:T(8,128)(2,1)S(1)}, bf16[80,2048]{1,0:T(8,128)(2,1)S(1)}, u32[]{:S(2)}, u32[]{:S(2)}) collective-permute-start(bf16[80,2048]{1,0:T(8,128)(2,1)S(1)} %pack_gains.1.refs_0_), channel_id=1, source_target_pairs={{0,4},{8,0},{16,8},{24,16},{28,24},{20,28},{12,20},{4,12},{1,5},{9... | collective-permute-start | bytes 983048 | tf_op jit(solution)/shard_map/ppermute | solution.py:876
  654.3 15.3 %collective-permute-start.85 = (bf16[256,768]{1,0:T(8,128)(2,1)S(1)}, bf16[256,768]{1,0:T(8,128)(2,1)S(1)}, u32[]{:S(2)}, u32[]{:S(2)}) collective-permute-start(bf16[256,768]{1,0:T(8,128)(2,1)S(1)} %slice.279), channel_id=1, source_target_pairs={{0,4},{8,0},{16,8},{24,16},{28,24},{20,28},{12,20},{4,12},{1,5},{9... | collective-permute-start | bytes 1179656 | tf_op jit(solution)/shard_map/ppermute | solution.py:876
  (125 other events, 1250.6 us)
Sparse Core Ops, SparseCore 0:
  46.6 57.5 all-gather.3
  106.3 58.8 all-gather.5
  167.4 59.5 all-gather.7
  436.9 84.2 reduce-scatter.3
  523.8 77.1 reduce-scatter.5
  603.4 73.2 reduce-scatter.7

commit v4 on v3

--- a/solution.py
+++ b/solution.py
@@ -294,7 +294,7 @@
         ],
         scratch_shapes=[pltpu.VMEM((count, rows, 1), F32)],
         compiler_params=pltpu.CompilerParams(dimension_semantics=("arbitrary",), vmem_limit_bytes=58 * 2**20),
-        cost_estimate=LONG,
+        cost_estimate=MEDIUM,
         name="expert_units",
     )(table, router_w, routes, gate_w, up_w, grad_act, *blocks)
 
@@ -316,7 +316,7 @@
         out_specs=pl.BlockSpec((rows, wide), lambda n: (0, n)),
         out_shape=jax.ShapeDtypeStruct((rows, width), BF),
         compiler_params=pltpu.CompilerParams(dimension_semantics=("arbitrary",), vmem_limit_bytes=56 * 2**20),
-        cost_estimate=LONG,
+        cost_estimate=MEDIUM,
         name="expert_rows",
     )(gate_grads, up_grads, gate_w, up_w)
 
@@ -338,12 +338,12 @@
         out_specs=[pl.BlockSpec((left.shape[0], wide), lambda n: (0, n)) for left in lefts],
         out_shape=[jax.ShapeDtypeStruct((left.shape[0], columns), BF) for left in lefts],
         compiler_params=pltpu.CompilerParams(dimension_semantics=("arbitrary",), vmem_limit_bytes=58 * 2**20),
-        cost_estimate=LONG,
+        cost_estimate=MEDIUM,
         name="times_transpose",
     )(b, *lefts)
 
 
-def sum_kernel(*refs):
+def sum_kernel(_unused, *refs):
     *pair_refs, o_ref = refs
     count = len(pair_refs) // 2
     total = dot_tn(pair_refs[0][...], pair_refs[count][...])
@@ -352,29 +352,57 @@
     o_ref[...] = total.astype(o_ref.dtype)
 
 
-def sum_of_outer(lefts, rights):
+def sum_of_outer(table, lefts, rights, slots=None):
     whole = not isinstance(lefts, (list, tuple))
     count, depth = len(rights), rights[0].shape[0]
     rows, columns = (lefts if whole else lefts[0]).shape[1], rights[0].shape[1]
-    tall, wide = min(512, rows), columns if count <= 2 else min(1024, columns)
+    tall, wide = 512, columns if count <= 2 else min(1024, columns)
 
     def left_spec(index):
         at = index if whole else 0
-        return pl.BlockSpec((depth, tall), lambda n, m: (at, m))
+        if slots is None:
+            return pl.BlockSpec((depth, tall), lambda n, m, t: (at, m))
+        return pl.BlockSpec((depth, tall), lambda n, m, t: (at, t[slots[0] + m]))
 
     return pl.pallas_call(
         sum_kernel,
-        grid=(columns // wide, rows // tall),
-        in_specs=[left_spec(index) for index in range(count)]
-        + [pl.BlockSpec((depth, wide), lambda n, m: (0, n)) for _unused in rights],
-        out_specs=pl.BlockSpec((tall, wide), lambda n, m: (m, n)),
+        grid_spec=pltpu.PrefetchScalarGridSpec(
+            num_scalar_prefetch=1,
+            grid=(columns // wide, rows // tall),
+            in_specs=[left_spec(index) for index in range(count)]
+            + [pl.BlockSpec((depth, wide), lambda n, m, t: (0, n)) for _unused in rights],
+            out_specs=pl.BlockSpec((tall, wide), lambda n, m, t: (m, n)),
+        ),
         out_shape=jax.ShapeDtypeStruct((rows, columns), BF),
         compiler_params=pltpu.CompilerParams(
             dimension_semantics=("arbitrary", "arbitrary"), vmem_limit_bytes=56 * 2**20
         ),
         cost_estimate=LONG,
         name="sum_of_outer",
-    )(*([lefts] * count if whole else lefts), *rights)
+    )(table, *([lefts] * count if whole else lefts), *rights)
+
+
+def add_kernel(_unused, left_ref, right_ref, o_ref):
+    o_ref[...] = (left_ref[...].astype(F32) + right_ref[...].astype(F32)).astype(BF)
+
+
+def add_slabs(table, left, right, first, second):
+    columns = left.shape[1]
+    slab = left.shape[0] // 4
+    tall = slab // 4
+
+    def spec(at):
+        return pl.BlockSpec((tall, columns), lambda m, t: (4 * at + m, 0))
+
+    return pl.pallas_call(
+        add_kernel,
+        grid_spec=pltpu.PrefetchScalarGridSpec(
+            num_scalar_prefetch=1, grid=(4,), in_specs=[spec(first), spec(second)], out_specs=spec(0)
+        ),
+        out_shape=jax.ShapeDtypeStruct((slab, columns), BF),
+        cost_estimate=SMALL,
+        name="add_slabs",
+    )(table, left, right)
 
 
 NN, NT = ((1,), (0,)), ((1,), (1,))
@@ -566,7 +594,7 @@
     out = jax.ShapeDtypeStruct((features, width), F32)
     scratch = [turned, turned, pltpu.VMEM((len(blocks) * rows, width), BF)]
     return small_call(
-        out_grads_kernel, "out_grads", out, table, mixed, other, *blocks, scratch=scratch, turn=turn,
+        out_grads_kernel, "out_grads", out, table, mixed, other, *blocks, cost=LONG, scratch=scratch, turn=turn,
         own_rows=own_rows, side=side,
     )
 
@@ -721,7 +749,7 @@
         out_specs=[pl.BlockSpec(memory_space=pltpu.VMEM)] * len(sides),
         out_shape=outs,
         scratch_shapes=[pltpu.SemaphoreType.DMA((number,))],
-        compiler_params=pltpu.CompilerParams(vmem_limit_bytes=40 * 2**20),
+        compiler_params=pltpu.CompilerParams(vmem_limit_bytes=60 * 2**20),
         cost_estimate=cost,
         name="take_parts",
     )(table, *weights)
@@ -839,24 +867,34 @@
     )(weight)
 
 
-def split_kernel(w_ref, o_ref):
+def split_kernel(*refs):
+    *term_refs, o_ref = refs
     units = o_ref.shape[2]
     for index in range(o_ref.shape[1]):
-        o_ref[:, index, :] = w_ref[:, index * units : (index + 1) * units].astype(F32)
-
-
-def split_experts(grad, count):
-    rows, columns = grad.shape
+        here = slice(index * units, (index + 1) * units)
+        total = term_refs[0][:, here].astype(F32)
+        for term_ref in term_refs[1:]:
+            total = total + term_ref[:, here].astype(F32)
+        o_ref[:, index, :] = total
+
+
+def split_experts(count, rows, *terms):
+    columns = terms[0][0].shape[1]
     at_once = 128
+    steps = rows // at_once
+
+    def spec(at):
+        return pl.BlockSpec((at_once, columns), lambda m: (at * steps + m, 0))
+
     return pl.pallas_call(
         split_kernel,
-        grid=(rows // at_once,),
-        in_specs=[pl.BlockSpec((at_once, columns), lambda m: (m, 0))],
+        grid=(steps,),
+        in_specs=[spec(at) for _unused, at in terms],
         out_specs=pl.BlockSpec((at_once, count, columns // count), lambda m: (m, 0, 0)),
         out_shape=jax.ShapeDtypeStruct((rows, count, columns // count), F32),
         cost_estimate=SMALL,
         name="split_experts",
-    )(grad)
+    )(*[array for array, _unused in terms])
 
 
 def swap(v, mask):
@@ -876,33 +914,47 @@
     return lax.ppermute(v, "ctx", [(order[i], order[(i + direction) % size]) for i in range(size)])
 
 
+class Flight(tuple):
+    def noted(self, note):
+        self.note = note
+        return self
+
+
 class Ring:
-    def __init__(self, steps):
-        self.steps = steps
-        self.value = None
-        self.flying = False
-        self.advance()
-
-    def advance(self):
+    def __init__(self, in_order, steps):
+        self.in_order, self.steps, self.value, self.landed = in_order, steps, None, None
+        self.flying = next(steps)
+
+    def land(self):
+        land(self.in_order, (self,))
+
+    def step(self):
+        if self.flying is None:
+            return
+        self.land()
         try:
-            next(self.steps)
-            self.flying = not self.flying
+            self.flying = self.steps.send(self.landed)
         except StopIteration as end:
-            self.value = end.value
-
-    def land(self):
-        if self.value is None and self.flying:
-            self.advance()
-
-    def step(self):
-        self.land()
-        if self.value is None:
-            self.advance()
+            self.flying, self.value = None, end.value
+        self.landed = None
 
     def finish(self):
-        while self.value is None:
+        while self.flying is not None:
             self.step()
         return self.value
+
+
+def land(in_order, rings, *more):
+    rings = [ring for ring in rings if ring.flying is not None and ring.landed is None]
+    found = [v for ring in rings for v in ring.flying] + list(more)
+    if not found:
+        return more
+    found = in_order(*found) if len(found) > 1 else [in_order(*found)]
+    for ring in rings:
+        ring.landed, found = found[: len(ring.flying)], found[len(ring.flying) :]
+        if isinstance(ring.flying, Flight):
+            ring.flying.note(*ring.landed)
+    return found
 
 
 def ring_gather(v, in_order, found):
@@ -911,38 +963,34 @@
     found[0] = v
     right, left = v, v
     for step in range(1, far):
-        right, left = ring_send(right, 1), ring_send(left, -1)
-        yield
-        right, left = in_order(right, left)
-        found[size - step], found[step] = right, left
-        yield
-    right, left = ring_send(right[:half], 1), ring_send(left[half:], -1)
-    yield
-    found[far] = jnp.concatenate(in_order(right, left))
-    yield
+        right, left = after((right, left), in_order.last)
+
+        def note(right, left, step=step):
+            found[size - step], found[step] = right, left
+
+        right, left = yield Flight((ring_send(right, 1), ring_send(left, -1))).noted(note)
+
+    def note_far(right, left):
+        found[far] = jnp.concatenate([right, left])
+
+    yield Flight((ring_send(right[:half], 1), ring_send(left[half:], -1))).noted(note_far)
     return found
 
 
-def ring_scatter(term, in_order):
+def ring_scatter(term):
     size = lax.axis_size("ctx")
     far = size // 2
     first = term(far)
     half = first.shape[0] // 2
-    right, left = ring_send(first[:half].astype(BF), 1), ring_send(first[half:].astype(BF), -1)
+    right, left = yield (ring_send(first[:half].astype(BF), 1), ring_send(first[half:].astype(BF), -1))
     for offset in range(far - 1, 0, -1):
-        yield
-        right, left = in_order(right, left)
-        yield
         ahead, behind = term(offset), term(size - offset)
         if offset == far - 1:
             ahead = jnp.concatenate([ahead[:half].astype(F32) + right.astype(F32), ahead[half:].astype(F32)])
             behind = jnp.concatenate([behind[:half].astype(F32), behind[half:].astype(F32) + left.astype(F32)])
         else:
             ahead, behind = ahead.astype(F32) + right.astype(F32), behind.astype(F32) + left.astype(F32)
-        right, left = ring_send(ahead.astype(BF), 1), ring_send(behind.astype(BF), -1)
-    yield
-    right, left = in_order(right, left)
-    yield
+        right, left = yield (ring_send(ahead.astype(BF), 1), ring_send(behind.astype(BF), -1))
     return term(0).astype(F32) + right.astype(F32) + left.astype(F32)
 
 
@@ -959,14 +1007,12 @@
         return values[0] if len(values) == 1 else values
 
 
-def sum_fsdp(v, in_order):
+def sum_fsdp(v):
     size = lax.axis_size("fsdp")
     mask = 1
     while mask < size:
-        other = swap(v, mask)
-        yield
-        v = v + in_order(other)
-        yield
+        (other,) = yield (swap(v, mask),)
+        v = v + other
         mask *= 2
     return v
 
@@ -997,7 +1043,8 @@
     at_ring, at_place, at_core, at_side = 0, 1, 2, 3
     at_slab = [4 + mask for mask in range(parts)]
     at_groups, at_beside, at_chip = (8, 9), (10, 11), (12, 13, 14, 15)
-    at_from = 16
+    at_order = (16, 17, 18, 19)
+    at_from = 20
     at_blocks = [at_from + ctx_size + index for index in range(ctx_size)]
     at_heads = [(at_from + 2 * ctx_size + index, at_from + 3 * ctx_size + index) for index in range(ctx_size)]
     at_turn = at_from + 4 * ctx_size
@@ -1009,6 +1056,7 @@
             side, core = divmod(mine, 2)
             line = [ring_place, place, core, side] + [mine ^ mask for mask in range(parts)]
             line += [core, core + 2, 1 - core, 3 - core, 2 * side, 2 * side + 1, 2 - 2 * side, 3 - 2 * side]
+            line += [mine ^ 1, mine ^ 3, mine ^ 2, mine]
             places = [order[(ring_place + offset) % ctx_size] for offset in offsets]
             line += places
             line += [(ring_place + offset) % ctx_size for offset in offsets]
@@ -1043,15 +1091,16 @@
     )
     fetched = swap(fetched[0], 2), swap(fetched[1], 3)
     cot_blocks = {}
-    cot_ring = Ring(ring_gather(after(cotangent[0], in_order.last), in_order, cot_blocks))
+    cot_ring = Ring(in_order, ring_gather(after(cotangent[0], in_order.last), in_order, cot_blocks))
     source = tokens[0].astype(F32)
     factor_one = lax.rsqrt(jnp.mean(source * source, axis=-1, keepdims=True) + EPSILON)
     normed = (source * factor_one * attn_gain).astype(BF)
     projections, w_down, w_gate, w_up = after((projections, w_down, w_gate, w_up), in_order.last)
-    near, own = in_order(
+    near, own, normed = in_order(
         *take_parts(
             table, projections, [side_of(None, slab, at_beside), side_of(None, slab, at_groups)], MEDIUM
-        )
+        ),
+        normed,
     )
     cot_ring.step()
     beside, near = swap(normed, 1), swap(near, 1)
@@ -1059,7 +1108,7 @@
     cot_ring.land()
     fetched = in_order(*fetched)
     column_blocks = {}
-    ring = Ring(ring_gather(fetched_payload(table, *fetched, width), in_order, column_blocks))
+    ring = Ring(in_order, ring_gather(fetched_payload(table, *fetched, width), in_order, column_blocks))
     down_w = lax.all_gather(after(w_down, in_order.last), "fsdp", axis=0, tiled=True)
     w_gate = in_order(merge_experts(after(w_gate, in_order.last)))
     ring.step()
@@ -1112,7 +1161,7 @@
     ffn_in = in_order((hidden * factor_two * ffn_gain).astype(BF))
 
     ffn_blocks = {}
-    ffn_ring = Ring(ring_gather(ffn_in, in_order, ffn_blocks))
+    ffn_ring = Ring(in_order, ring_gather(ffn_in, in_order, ffn_blocks))
     ffn_ring.step()
 
     size = 4
@@ -1144,7 +1193,7 @@
     cot_ring.finish()
     ffn_ring.finish()
     normed_blocks = {}
-    normed_ring = Ring(ring_gather(after(normed, in_order.last), in_order, normed_blocks))
+    normed_ring = Ring(in_order, ring_gather(after(normed, in_order.last), in_order, normed_blocks))
     for group in range(1, len(groups)):
         cots.append(group_cots(group))
         if group == 1:
@@ -1162,7 +1211,7 @@
 
     def weight_grad(lefts, rights):
         lefts, rights = after((lefts, rights), in_order.last)
-        return in_order(sum_of_outer(lefts, rights))
+        return in_order(sum_of_outer(table, lefts, rights))
 
     def share(grad):
         return lax.psum_scatter(after(grad, in_order.last), "fsdp", scatter_dimension=0, tiled=True)
@@ -1178,7 +1227,7 @@
     for group in range(len(groups) - 1, 0, -1):
         make_rows(group)
     normed_ring.step()
-    row_ring = Ring(ring_scatter(term_of(grad_rows), in_order))
+    row_ring = Ring(in_order, ring_scatter(term_of(grad_rows)))
     d_gate = weight_grad(inputs, gate_grads)
     row_ring.step()
     d_gate = share(d_gate)
@@ -1187,12 +1236,13 @@
     row_ring.step()
     weighted = in_order(*times_transpose(after(acts, in_order.last), down_w))
     row_ring.step()
-    ring = Ring(ring_scatter(term_of(weighted), in_order))
+    ring = Ring(in_order, ring_scatter(term_of(weighted)))
     d_gates = jnp.concatenate(after(d_gates, in_order.last), axis=1).reshape(own_experts, ctx_size, rows)
     d_gates = d_gates.at[:, table[at_back : at_back + ctx_size], :].get(mode="promise_in_bounds").transpose(1, 0, 2)
     d_gates = lax.all_to_all(d_gates, "ctx", split_axis=0, concat_axis=0, tiled=True)
-    normed_t = in_order(transposed(table, [normed_blocks[offset] for offset in offsets], at_chip))
-    row_ring.land()
+    some = after(tuple(normed_blocks[offset] for offset in offsets), in_order.last)
+    normed_t = in_order(transposed(table, some, at_chip))
+    land(in_order, (row_ring, ring))
     d_gates = in_order(d_gates).reshape(experts, rows).T
     beside_t = swap(normed_t, 1)
     gates = routed_gates(dot(ffn_in, router_w), routes[0])
@@ -1216,44 +1266,48 @@
     ring.step()
     grad_mixed = spread_pairs(grad_mixed)
     d_up = weight_grad(inputs, up_grads)
-    grad_mixed = in_order(grad_mixed)
+    (grad_mixed,) = land(in_order, (ring,), grad_mixed)
     d_up = share(d_up)
+    ring.step()
+    grads, head_gains = in_order(
+        *attend_back(qkv, after(grad_mixed, in_order.last), q_gain, k_gain, cosine, sine)
+    )
+    if repeats > 1:
+        head_gains = jnp.where(lax.axis_index("ctx") % repeats == 0, head_gains, 0.0)
     across = in_order(across)
-    diagonal = in_order(swap(across, 1))
-    mixed = after(mixed, in_order.last)
+    diagonal = swap(across, 1)
+    ring.land()
+
+    grads = after(grads, in_order.last)
+    ring.step()
+    half_grads = in_order(head_weights(table, grads, normed_t, beside_t, 3, at_from))
+    other_half = swap(half_grads[width // 2 :], 2)
+    grads = collect_pairs(after(grads, in_order.last))
+    mixed, diagonal = after((mixed, diagonal), in_order.last)
     d_out = in_order(
         out_grads(table, mixed, other_mixed, [grad_proj, beside, across, diagonal], at_turn, own_rows, at_side)
     )
-    ring.step()
-    out_ring = Ring(ring_scatter(lambda offset: d_out[offset * own_rows : (offset + 1) * own_rows], in_order))
-    grads, head_gains = in_order(*attend_back(qkv, grad_mixed, q_gain, k_gain, cosine, sine))
-    if repeats > 1:
-        head_gains = jnp.where(lax.axis_index("ctx") % repeats == 0, head_gains, 0.0)
-    ring.step()
-    out_ring.step()
-
-    half_grads = in_order(head_weights(table, grads, normed_t, beside_t, 3, at_from))
-    other_half = swap(half_grads[width // 2 :], 2)
-    grads = collect_pairs(grads)
-    d_down = weight_grad(cots, acts)
     other_half = in_order(other_half)
-    d_down = share(d_down)
     keep, send = in_order(*chip_total(table, half_grads, other_half, at_core))
     send = in_order(swap(send, 1))
     pieces = {}
-    total_ring = Ring(ring_gather(side_by_side(table, keep, send), in_order, pieces))
+    total_ring = Ring(in_order, ring_gather(side_by_side(table, keep, send), in_order, pieces))
+    out_ring = Ring(in_order, ring_scatter(lambda offset: d_out[offset * own_rows : (offset + 1) * own_rows]))
+    d_down = weight_grad(cots, acts)
     output = in_order((hidden + ring.finish()).astype(BF))
+    grads = in_order(grads)
+    total_ring.step()
+    d_down = share(d_down)
     out_ring.step()
+    grads, grad_ffn_in, grad_logits = after((grads, grad_ffn_in, grad_logits), in_order.last)
+    own, far = in_order(*pair_normed(grads, own_columns, 3))
+    far = swap(far, 1)
     d_ffn_gain = jnp.sum(grad_ffn_in * hidden * factor_two, axis=0, keepdims=True)
     d_router = dot(grad_logits, ffn_in.astype(F32), ((0,), (0,)), precision=lax.Precision.HIGHEST)
     early = in_order(jnp.concatenate([d_router, d_ffn_gain]))
-    early = Ring(sum_fsdp(early, in_order))
-    grads = in_order(grads)
-    own, far = in_order(*pair_normed(grads, own_columns, 3))
-    far = swap(far, 1)
-    early.step()
+    early = Ring(in_order, sum_fsdp(early))
+    out_ring.step()
     total_ring.step()
-    out_ring.step()
 
     whole = None
     seen = set()
@@ -1275,7 +1329,7 @@
         return arrays
 
     whole = take_whole(whole)
-    early.finish()
+    early.step()
     grad_normed = own + in_order(far).astype(F32)
     d_attn_gain = jnp.sum(grad_normed * source * factor_one, axis=0)
     inner = grad_normed * attn_gain
@@ -1286,24 +1340,24 @@
     )
     d_tokens, d_attn_gain = in_order(d_tokens, d_attn_gain)
     late = jnp.concatenate([d_attn_gain, head_gains[0], head_gains[1], jnp.zeros((width - 2 * head_dim,), F32)])
-    late = Ring(sum_fsdp(late.reshape(2, width), in_order))
-    d_gate = in_order(split_experts(after(d_gate, in_order.last), own_experts))
+    late = Ring(in_order, sum_fsdp(late.reshape(2, width)))
+    out_ring.step()
+    early.finish()
+    d_gate = in_order(split_experts(own_experts, slab, (after(d_gate, in_order.last), 0)))
+    late.step()
     total_ring.step()
     d_out = out_ring.finish()
-    late.step()
     whole = take_whole(whole)
     packed = in_order(pack_gains(table, d_out, early.value, late.finish(), at_slab[0], experts))
     packed_pieces = {}
-    packed_ring = Ring(ring_gather(packed, in_order, packed_pieces))
-    d_up = in_order(split_experts(after(d_up, in_order.last), own_experts))
-    total_ring.step()
-    whole = take_whole(whole)
-    packed_ring.step()
+    packed_ring = Ring(in_order, ring_gather(packed, in_order, packed_pieces))
+    d_up = in_order(split_experts(own_experts, slab, (after(d_up, in_order.last), 0)))
     total_ring.finish()
     whole = take_whole(whole)
     d_query, d_key, d_value = whole
     packed_ring.step()
-    d_down = in_order(split_experts(after(d_down, in_order.last), own_experts))
+    packed_ring.step()
+    d_down = in_order(split_experts(own_experts, slab, (after(d_down, in_order.last), 0)))
     packed_ring.finish()
     packed_blocks = [packed_pieces[offset] for offset in offsets]
     cuts = [(index, (0, own_rows), (0, width), 0, at_blocks[index], True) for index in range(ctx_size)]

time: 710 us -> 706 us (level)
  waiting for transfers between devices: 175 us -> 191 us
  local copies, waits for them, and re-layouts: 45.3 us -> 33 us
  Pallas kernels: 268 us -> 277 us
  other arithmetic: 50.9 us -> 42.7 us
    unnamed x175 -> x205, local copies, waits for them, and re-layouts: 24.9 us -> 15.4 us
    ppermute x72, waiting for transfers between devices: 119 us -> 129 us  [ring_send(): lax.ppermute(v, 'ctx', [(order[i], order[(i + direction) % size]) for i i...]
  transfers between devices with their start and end apart: 103 -> 103, of which waited for: 46 -> 51; matrix products, arithmetic and copies ran while one was open for 9% -> 8% of each run, Pallas kernels for 38% -> 38%
where the time goes in v4:
time: 706 us; the launch traced here: 697 us
  Pallas kernels  277 us (39%)
  waiting for transfers between devices  191 us (27%)
  starting transfers between devices  118 us (17%)
  other arithmetic  42.7 us (6%)
  local copies, waits for them, and re-layouts  33 us (5%)
  blocking collectives  17.8 us (3%)
  between operations  16.5 us (2%)
    ppermute x72, waiting for transfers between devices, ring_send(): lax.ppermute(v, 'ctx', [(order[i], order[(i + direction) % size]) for i i...  129 us
    ppermute x72, starting transfers between devices, ring_send(): lax.ppermute(v, 'ctx', [(order[i], order[(i + direction) % size]) for i i...  87.3 us
    pallas_call x3, Pallas kernels, sum_of_outer(): pl.pallas_call(sum_kernel, grid_spec=pltpu.PrefetchScalarGridSpec(num_sca...  42.6 us
    pallas_call x2, Pallas kernels, expert_units(): pl.pallas_call(functools.partial(expert_kernel, per=per, place=place, at=...  37.8 us
    pallas_call x2, Pallas kernels, expert_rows(): pl.pallas_call(expert_rows_kernel, grid=(width // wide,), in_specs=[whole...  27.7 us
    pallas_call x11, Pallas kernels, small_call(): pl.pallas_call(functools.partial(kernel, **kwargs), in_specs=[pl.BlockSpe...  26.2 us
    all_to_all x2, waiting for transfers between devices, spread_pairs(): return lax.all_to_all(v, 'ctx', split_axis=0, concat_axis=0, tiled=True)  24.8 us
    ppermute x20, waiting for transfers between devices, swap(): return lax.ppermute(v, 'fsdp', [(i, i ^ mask) for i in range(size)])  24.3 us
  transfers between devices with their start and end apart: 103, of which 51 were waited for; matrix products, arithmetic and copies ran while one was open for 8% of the time, Pallas kernels for 38%

profile of v4, /device:TPU:0, one launch (start us, length us, event | category | flops | bytes accessed | tf_op | source)
XLA Modules:
  0.0 697.0 jit_solution(18173302110191177791)
XLA Ops:
  8.4 3.1 take_parts.2
  11.6 3.1 collective-permute-start
  16.8 6.4 take_parts.3
  30.8 6.6 merge_experts.3
  37.4 3.9 collective-permute-done.2.refs_0_
  45.6 6.7 merge_experts.4
  52.3 13.8 %collective-permute-done.6.refs_6_.refs_2_ = bf16[256,2048]{1,0:T(8,128)(2,1)S(1)} collective-permute-done((bf16[256,2048]{1,0:T(8,128)(2,1)S(1)}, bf16[256,2048]{1,0:T(8,128)(2,1)S(1)}, u32[]{:S(2)}, u32[]{:S(2)}) %collective-permute-start.6) | collective-permute-done | bytes 1048608 | tf_op jit(solution)/shard_map/ppermute | solution.py:914
  70.1 4.1 collective-permute-done.9.refs_1_
  75.0 6.6 merge_experts.5
  81.6 11.7 %collective-permute-done.10.refs_8_.refs_4_ = bf16[256,2048]{1,0:T(8,128)(2,1)} collective-permute-done((bf16[256,2048]{1,0:T(8,128)(2,1)S(1)}, bf16[256,2048]{1,0:T(8,128)(2,1)}, u32[]{:S(2)}, u32[]{:S(2)}) %collective-permute-start.10) | collective-permute-done | bytes 1048608 | tf_op jit(solution)/shard_map/ppermute | solution.py:914
  97.3 4.0 all-to-all-start
  103.9 4.6 collective-permute-done.13.refs_2_
  110.6 10.9 %all-to-all-done = s32[8,128,8]{1,2,0:T(8,128)} async-done(((s32[8,128,8]{1,2,0:T(8,128)}), s32[8,128,8]{1,2,0:T(8,128)}, u32[]{:S(2)}, u32[]{:S(2)}) %all-to-all-start) | async-done | bytes 32800 | tf_op jit(solution)/shard_map/all_to_all | solution.py:1118
  123.7 9.1 %collective-permute-done.17 = bf16[128,2048]{1,0:T(8,128)(2,1)S(1)} collective-permute-done((bf16[128,2048]{1,0:T(8,128)(2,1)S(1)}, bf16[128,2048]{1,0:T(8,128)(2,1)S(1)}, u32[]{:S(2)}, u32[]{:S(2)}) %collective-permute-start.17) | collective-permute-done | bytes 524320 | tf_op jit(solution)/shard_map/ppermute | solution.py:914
  135.2 10.4 %own_pairs.1 = (bf16[8,6,128,128]{3,2,1,0:T(8,128)(2,1)S(1)}, bf16[2048,3072]{1,0:T(8,128)(2,1)}) custom-call(s32[68]{0:T(128)S(1)} %copy-done.28, bf16[128,2048]{1,0:T(8,128)(2,1)} %fusion.2.refs_0_, bf16[128,2048]{1,0:T(8,128)(2,1)S(1)} %copy-done.26, bf16[512,3072]{1,0:T(8,128)(2,1)S(1)} %copy-done.13, bf16[512,3072]{1,0:T(8,128)(2,1)} %collective-permute-done.8.refs_3_, ...), custom_call_target="tpu_custom_call" | custom-call | flops 1 | bytes 1 | tf_op jit(solution)/shard_map/own_pairs/pallas_call | solution.py:495
  146.8 3.8 all-to-all-start.1
  153.7 4.1 far_rows.1.far_ref
  160.0 24.4 %all-to-all-done.1.q_ref.k_ref.v_ref = bf16[8,6,128,128]{3,2,1,0:T(8,128)(2,1)S(1)} async-done(((bf16[8,6,128,128]{3,2,1,0:T(8,128)(2,1)}), bf16[8,6,128,128]{3,2,1,0:T(8,128)(2,1)S(1)}, u32[]{:S(2)}, u32[]{:S(2)}) %all-to-all-start.1) | async-done | bytes 1572896 | tf_op jit(solution)/shard_map/all_to_all | solution.py:1075
  188.1 7.8 %attend.1 = bf16[8,2,128,128]{3,2,1,0:T(8,128)(2,1)S(1)} custom-call(bf16[8,6,128,128]{3,2,1,0:T(8,128)(2,1)S(1)} %copy-done.18, bf16[8,6,128,128]{3,2,1,0:T(8,128)(2,1)S(1)} %copy-done.18, bf16[8,6,128,128]{3,2,1,0:T(8,128)(2,1)S(1)} %copy-done.18, f32[1,128]{1,0:T(1,128)S(1)} %bitcast.61, f32[1,128]{1,0:T(1,128)S(1)} %bitcast.63, ...), custom_call_target="tpu_custom_call" | custom-call | flops 20000000000 | bytes 50000000 | tf_op jit(solution)/shard_map/attend/pallas_call | solution.py:152
  196.7 17.8 %all_to_all.30.m_ref = bf16[8,2,128,128]{3,2,1,0:T(8,128)(2,1)S(1)} all-to-all(bf16[8,2,128,128]{3,2,1,0:T(8,128)(2,1)} %copy-done.27), channel_id=1, replica_groups=mesh['ctx'=8,'fsdp'=4] {'ctx'}, dimensions={0} | all-to-all | bytes 1048576 | tf_op jit(solution)/shard_map/all_to_all | solution.py:1078
  214.5 3.1 mixed_out.1
  225.6 10.4 %collective-permute-done.20.refs_2_ = bf16[128,2048]{1,0:T(8,128)(2,1)} collective-permute-done((bf16[128,2048]{1,0:T(8,128)(2,1)S(1)}, bf16[128,2048]{1,0:T(8,128)(2,1)}, u32[]{:S(2)}, u32[]{:S(2)}) %collective-permute-start.20) | collective-permute-done | bytes 524320 | tf_op jit(solution)/shard_map/ppermute | solution.py:914
  239.1 9.3 %stacked_matmul.2 = (f32[512,2048]{1,0:T(8,128)}, bf16[512,2048]{1,0:T(8,128)(2,1)}) custom-call(bf16[2048,2048]{1,0:T(8,128)(2,1)} %all-gather.4.cloned.1.call-done.w_ref.b_ref, bf16[128,2048]{1,0:T(8,128)(2,1)} %bitcast.66, bf16[128,2048]{1,0:T(8,128)(2,1)} %copy-done.100, bf16[128,2048]{1,0:T(8,128)(2,1)} %copy-done.99, bf16[128,2048]{1,0:T(8,128)(2,1)} %copy-done.97), custom_call_target="tpu_custom_call" | custom-call | flops 999999995904 | bytes 1000000000 | tf_op jit(solution)/shard_map/stacked_matmul/pallas_call | solution.py:209
  255.7 18.9 %expert_units.2 = (bf16[512,2048]{1,0:T(8,128)(2,1)}, bf16[512,2048]{1,0:T(8,128)(2,1)}, bf16[512,2048]{1,0:T(8,128)(2,1)}, f32[2,512,1]{2,1,0:T(8,128)}, bf16[512,2048]{1,0:T(8,128)(2,1)}) custom-call(s32[68]{0:T(128)} %get-tuple-element.925.table_ref._unused, bf16[2048,16]{1,0:T(8,128)(2,1)} %copy-done.3, s32[8,128,8]{2,1,0:T(8,128)} %copy.57.routes_ref, ...), custom_call_target="tpu_custom_call" | custom-call | flops 20000000000 | bytes 50000000 | tf_op jit(solution)/shard_map/expert_units/pallas_call | solution.py:273
  291.3 9.3 %stacked_matmul.3 = (f32[512,2048]{1,0:T(8,128)}, bf16[512,2048]{1,0:T(8,128)(2,1)}) custom-call(bf16[2048,2048]{1,0:T(8,128)(2,1)} %all-gather.4.cloned.1.call-done.w_ref.b_ref, bf16[128,2048]{1,0:T(8,128)(2,1)} %copy-done.95, bf16[128,2048]{1,0:T(8,128)(2,1)} %copy-done.76, bf16[128,2048]{1,0:T(8,128)(2,1)} %copy-done.75, ...), custom_call_target="tpu_custom_call" | custom-call | flops 999999995904 | bytes 1000000000 | tf_op jit(solution)/shard_map/stacked_matmul/pallas_call | solution.py:209
  303.5 18.9 %expert_units.3 = (bf16[512,2048]{1,0:T(8,128)(2,1)}, bf16[512,2048]{1,0:T(8,128)(2,1)}, bf16[512,2048]{1,0:T(8,128)(2,1)}, f32[2,512,1]{2,1,0:T(8,128)}, bf16[512,2048]{1,0:T(8,128)(2,1)}) custom-call(s32[68]{0:T(128)} %get-tuple-element.925.table_ref._unused, bf16[2048,16]{1,0:T(8,128)(2,1)} %copy-done.3, s32[8,128,8]{2,1,0:T(8,128)} %copy.57.routes_ref, ...), custom_call_target="tpu_custom_call" | custom-call | flops 20000000000 | bytes 50000000 | tf_op jit(solution)/shard_map/expert_units/pallas_call | solution.py:273
  324.5 13.8 %expert_rows.2 = bf16[512,2048]{1,0:T(8,128)(2,1)} custom-call(bf16[512,2048]{1,0:T(8,128)(2,1)} %get-tuple-element.608.gate_ref.refs_3_, bf16[512,2048]{1,0:T(8,128)(2,1)} %get-tuple-element.668.up_ref.refs_3_, bf16[2048,2048]{1,0:T(8,128)(2,1)} %all-gather.6.cloned.1.call-done.gate_w_ref, bf16[2048,2048]{1,0:T(8,128)(2,1)} %all-gather.8.cloned.1.call-done.up_w_ref), custom_call_target="tpu_custom_call" | custom-call | flops 20000000000 | bytes 50000000 | tf_op jit(solution)/shard_map/expert_rows/pallas_call | solution.py:312
  342.6 14.2 %sum_of_outer.3 = bf16[2048,2048]{1,0:T(8,128)(2,1)} custom-call(s32[68]{0:T(128)} %get-tuple-element.925.table_ref._unused, bf16[512,2048]{1,0:T(8,128)(2,1)} %get-tuple-element.665.refs_0_, bf16[512,2048]{1,0:T(8,128)(2,1)} %get-tuple-element.666.refs_1_, bf16[512,2048]{1,0:T(8,128)(2,1)} %get-tuple-element.616.refs_2_.gate_ref, ...), custom_call_target="tpu_custom_call" | custom-call | flops 999999995904 | bytes 1000000000 | tf_op jit(solution)/shard_map/sum_of_outer/pallas_call | solution.py:367
  366.6 13.8 %expert_rows.3 = bf16[512,2048]{1,0:T(8,128)(2,1)} custom-call(bf16[512,2048]{1,0:T(8,128)(2,1)} %get-tuple-element.616.refs_2_.gate_ref, bf16[512,2048]{1,0:T(8,128)(2,1)} %get-tuple-element.667.up_ref.refs_2_, bf16[2048,2048]{1,0:T(8,128)(2,1)} %all-gather.6.cloned.1.call-done.gate_w_ref, bf16[2048,2048]{1,0:T(8,128)(2,1)} %all-gather.8.cloned.1.call-done.up_w_ref), custom_call_target="tpu_custom_call" | custom-call | flops 20000000000 | bytes 50000000 | tf_op jit(solution)/shard_map/expert_rows/pallas_call | solution.py:312
  384.4 13.2 %times_transpose.1 = (bf16[512,2048]{1,0:T(8,128)(2,1)}, bf16[512,2048]{1,0:T(8,128)(2,1)}) custom-call(bf16[2048,2048]{1,0:T(8,128)(2,1)} %all-gather.4.cloned.1.call-done.w_ref.b_ref, bf16[512,2048]{1,0:T(8,128)(2,1)} %get-tuple-element.706.refs_0_.refs_2_, bf16[512,2048]{1,0:T(8,128)(2,1)} %get-tuple-element.707.refs_1_.refs_3_), custom_call_target="tpu_custom_call" | custom-call | flops 20000000000 | bytes 50000000 | tf_op jit(solution)/shard_map/times_transpose/pallas_call | solution.py:333
  398.4 5.1 transposed.1.own_ref
  403.6 2.6 add_convert_fusion.5
  414.2 3.3 all-to-all-start.3
  418.1 8.2 %collective-permute-done.49 = bf16[64,2048]{1,0:T(8,128)(2,1)S(1)} collective-permute-done((bf16[64,2048]{1,0:T(8,128)(2,1)}, bf16[64,2048]{1,0:T(8,128)(2,1)S(1)}, u32[]{:S(2)}, u32[]{:S(2)}) %collective-permute-start.49) | collective-permute-done | bytes 262176 | tf_op jit(solution)/shard_map/ppermute | solution.py:914
  439.4 3.3 grad_pairs.1
  442.7 4.2 all-to-all-start.4
  446.9 14.1 %sum_of_outer.4 = bf16[2048,2048]{1,0:T(8,128)(2,1)} custom-call(s32[68]{0:T(128)} %get-tuple-element.925.table_ref._unused, bf16[512,2048]{1,0:T(8,128)(2,1)} %get-tuple-element.665.refs_0_, bf16[512,2048]{1,0:T(8,128)(2,1)} %get-tuple-element.666.refs_1_, bf16[512,2048]{1,0:T(8,128)(2,1)} %get-tuple-element.667.up_ref.refs_2_, ...), custom_call_target="tpu_custom_call" | custom-call | flops 999999995904 | bytes 1000000000 | tf_op jit(solution)/shard_map/sum_of_outer/pallas_call | solution.py:367
  463.7 2.8 collective-permute-start.57
  468.9 15.6 %attend_back.1 = (bf16[8,6,128,128]{3,2,1,0:T(8,128)(2,1)}, f32[8,128]{1,0:T(8,128)S(1)}) custom-call(bf16[8,6,128,128]{3,2,1,0:T(8,128)(2,1)S(1)} %copy-done.19, bf16[8,6,128,128]{3,2,1,0:T(8,128)(2,1)S(1)} %copy-done.19, bf16[8,6,128,128]{3,2,1,0:T(8,128)(2,1)S(1)} %copy-done.19, bf16[8,2,128,128]{3,2,1,0:T(8,128)(2,1)} %all-to-all-done.4.m_ref, ...), custom_call_target="tpu_custom_call" | custom-call | flops 999999995904 | bytes 1000000000 | tf_op jit(solution)/shard_map/attend_back/pallas_call | solution.py:169
  484.5 2.4 collective-permute-done.55.refs_2_
  487.0 7.9 %head_weights.1.own_ref = bf16[2048,384]{1,0:T(8,128)(2,1)S(1)} custom-call(s32[68]{0:T(128)S(1)} %copy-done.30, bf16[8,6,128,128]{3,2,1,0:T(8,128)(2,1)} %get-tuple-element.716.g_ref, bf16[2048,1024]{1,0:T(8,128)(2,1)} %transposed.1.own_ref, bf16[2048,1024]{1,0:T(8,128)(2,1)} %collective-permute-done.52.beside_ref), custom_call_target="tpu_custom_call" | custom-call | flops 999999995904 | bytes 1000000000 | tf_op jit(solution)/shard_map/head_weights/pallas_call | solution.py:639
  497.2 4.9 out_grads.1
  502.1 5.8 all-to-all-start.5
  508.0 2.9 add_convert_fusion.1
  512.9 2.6 convert.35
  515.5 4.9 collective-permute-done.59.other_ref
  527.9 14.2 %sum_of_outer.5 = bf16[2048,2048]{1,0:T(8,128)(2,1)} custom-call(s32[68]{0:T(128)} %get-tuple-element.925.table_ref._unused, bf16[512,2048]{1,0:T(8,128)(2,1)} %get-tuple-element.704.refs_0_, bf16[512,2048]{1,0:T(8,128)(2,1)} %get-tuple-element.705.refs_1_, bf16[512,2048]{1,0:T(8,128)(2,1)} %get-tuple-element.706.refs_0_.refs_2_, ...), custom_call_target="tpu_custom_call" | custom-call | flops 999999995904 | bytes 1000000000 | tf_op jit(solution)/shard_map/sum_of_outer/pallas_call | solution.py:367
  542.1 5.0 collective-permute-done.61
  547.1 2.7 collective-permute-start.66
  552.2 14.0 %collective-permute-done.63.refs_2_ = bf16[512,768]{1,0:T(8,128)(2,1)} collective-permute-done((bf16[512,768]{1,0:T(8,128)(2,1)}, bf16[512,768]{1,0:T(8,128)(2,1)}, u32[]{:S(2)}, u32[]{:S(2)}) %collective-permute-start.63) | collective-permute-done | bytes 786464 | tf_op jit(solution)/shard_map/ppermute | solution.py:914
  566.2 9.8 %collective-permute-start.69 = (bf16[512,768]{1,0:T(8,128)(2,1)}, bf16[512,768]{1,0:T(8,128)(2,1)}, u32[]{:S(2)}, u32[]{:S(2)}) collective-permute-start(bf16[512,768]{1,0:T(8,128)(2,1)} %collective-permute-done.63.refs_2_), channel_id=1, source_target_pairs={{0,8},{8,16},{16,24},{24,28},{28,20},{20,12},{12,4},{4,0},{1,9},{9... | collective-permute-start | bytes 2359304 | tf_op jit(solution)/shard_map/ppermute | solution.py:914
  577.8 2.6 collective-permute-start.68
  581.2 12.2 %pair_normed.1 = (f32[128,2048]{1,0:T(8,128)S(1)}, bf16[128,2048]{1,0:T(8,128)(2,1)S(1)}) custom-call(bf16[8,6,128,128]{3,2,1,0:T(8,128)(2,1)} %all-to-all-done.5.g_ref, bf16[2048,3072]{1,0:T(8,128)(2,1)} %get-tuple-element.728.w_ref), custom_call_target="tpu_custom_call" | custom-call | flops 999999995904 | bytes 1000000000 | tf_op jit(solution)/shard_map/pair_normed/pallas_call | solution.py:698
  594.1 7.7 %collective-permute-done.68 = bf16[64,2048]{1,0:T(8,128)(2,1)} collective-permute-done((bf16[64,2048]{1,0:T(8,128)(2,1)}, bf16[64,2048]{1,0:T(8,128)(2,1)}, u32[]{:S(2)}, u32[]{:S(2)}) %collective-permute-start.68) | collective-permute-done | bytes 262176 | tf_op jit(solution)/shard_map/ppermute | solution.py:914
  605.5 4.8 spread.5
  622.6 4.5 collective-permute-done.75
  627.1 4.5 split_experts.3
  633.4 4.5 collective-permute-done.77.refs_1_
  639.6 2.4 collective-permute-done.79
  652.2 4.5 split_experts.4
  663.4 5.7 collective-permute-done.86.refs_4_
  671.4 4.5 split_experts.5
  680.6 3.2 collective-permute-done.90
  684.6 2.6 spread.9
  (485 shorter events, 192.8 us)
Async XLA Ops:
  7.2 189.5 %all-gather.4.cloned.1.call-start = ((), (), s32[]{:S(2)}) async-start(), calls=%async_computation.9 | async-start | bytes 10485760 | tf_op jit(solution)/shard_map/all_gather | solution.py:1112
  11.6 14.9 %collective-permute-start = (bf16[128,2048]{1,0:T(8,128)(2,1)S(1)}, bf16[128,2048]{1,0:T(8,128)(2,1)S(1)}, u32[]{:S(2)}, u32[]{:S(2)}) collective-permute-start(bf16[128,2048]{1,0:T(8,128)(2,1)S(1)} %bitcast.67), channel_id=1, source_target_pairs={{0,8},{8,16},{16,24},{24,28},{28,20},{20,12},{12,4},{4,0},{1,9},{9... | collective-permute-start | bytes 1572872 | tf_op jit(solution)/shard_map/ppermute | solution.py:914
  14.6 28.2 %collective-permute-start.4 = (bf16[64,5120]{1,0:T(8,128)(2,1)}, bf16[64,5120]{1,0:T(8,128)(2,1)S(1)}, u32[]{:S(2)}, u32[]{:S(2)}) collective-permute-start(bf16[64,5120]{1,0:T(8,128)(2,1)} %get-tuple-element.450), channel_id=1, source_target_pairs={{0,2},{1,3},{2,0},{3,1},{4,6},{5,7},{6,4},{7,5},{8,10},{9,11},{10,... | collective-permute-start | bytes 1966088 | tf_op jit(solution)/shard_map/ppermute | solution.py:902
  16.6 26.2 %collective-permute-start.5 = (bf16[64,3072]{1,0:T(8,128)(2,1)}, bf16[64,3072]{1,0:T(8,128)(2,1)S(1)}, u32[]{:S(2)}, u32[]{:S(2)}) collective-permute-start(bf16[64,3072]{1,0:T(8,128)(2,1)} %get-tuple-element.451), channel_id=1, source_target_pairs={{0,3},{1,2},{2,1},{3,0},{4,7},{5,6},{6,5},{7,4},{8,11},{9,10},{10,... | collective-permute-start | bytes 1179656 | tf_op jit(solution)/shard_map/ppermute | solution.py:902
  42.8 153.8 %all-gather.6.cloned.1.call-start = ((), (), s32[]{:S(2)}) async-start(), calls=%async_computation.10 | async-start | bytes 10485760 | tf_op jit(solution)/shard_map/all_gather | solution.py:1115
  43.6 22.5 %collective-permute-start.6 = (bf16[256,2048]{1,0:T(8,128)(2,1)S(1)}, bf16[256,2048]{1,0:T(8,128)(2,1)S(1)}, u32[]{:S(2)}, u32[]{:S(2)}) collective-permute-start(bf16[256,2048]{1,0:T(8,128)(2,1)S(1)} %fetched_payload.1.refs_4_.refs_0_), channel_id=1, source_target_pairs={{0,8},{8,16},{16,24},{24,28},{28,20},{20,12},{12,4},{4,0},{1,9},{9... | collective-permute-start | bytes 3145736 | tf_op jit(solution)/shard_map/ppermute | solution.py:914
  45.2 22.2 %collective-permute-start.7 = (bf16[256,2048]{1,0:T(8,128)(2,1)S(1)}, bf16[256,2048]{1,0:T(8,128)(2,1)S(1)}, u32[]{:S(2)}, u32[]{:S(2)}) collective-permute-start(bf16[256,2048]{1,0:T(8,128)(2,1)S(1)} %fetched_payload.1.refs_4_.refs_0_), channel_id=1, source_target_pairs={{0,4},{8,0},{16,8},{24,16},{28,24},{20,28},{12,20},{4,12},{1,5},{9... | collective-permute-start | bytes 3145736 | tf_op jit(solution)/shard_map/ppermute | solution.py:914
  67.4 154.1 %all-gather.8.cloned.1.call-start = ((), (), s32[]{:S(2)}) async-start(), calls=%async_computation.11 | async-start | bytes 10485760 | tf_op jit(solution)/shard_map/all_gather | solution.py:1124
  68.1 25.2 %collective-permute-start.10 = (bf16[256,2048]{1,0:T(8,128)(2,1)S(1)}, bf16[256,2048]{1,0:T(8,128)(2,1)}, u32[]{:S(2)}, u32[]{:S(2)}) collective-permute-start(bf16[256,2048]{1,0:T(8,128)(2,1)S(1)} %collective-permute-done.6.refs_6_.refs_2_), channel_id=1, source_target_pairs={{0,8},{8,16},{16,24},{24,28},{28,20},{20,12},{12,4},{4,0},{1,9},{9... | collective-permute-start | bytes 3145736 | tf_op jit(solution)/shard_map/ppermute | solution.py:914
  69.6 25.0 %collective-permute-start.11 = (bf16[256,2048]{1,0:T(8,128)(2,1)S(1)}, bf16[256,2048]{1,0:T(8,128)(2,1)}, u32[]{:S(2)}, u32[]{:S(2)}) collective-permute-start(bf16[256,2048]{1,0:T(8,128)(2,1)S(1)} %collective-permute-done.7.refs_5_.refs_1_), channel_id=1, source_target_pairs={{0,4},{8,0},{16,8},{24,16},{28,24},{20,28},{12,20},{4,12},{1,5},{9... | collective-permute-start | bytes 3145736 | tf_op jit(solution)/shard_map/ppermute | solution.py:914
  94.6 26.9 %collective-permute-start.15 = (bf16[256,2048]{1,0:T(8,128)(2,1)}, bf16[256,2048]{1,0:T(8,128)(2,1)S(1)}, u32[]{:S(2)}, u32[]{:S(2)}) collective-permute-start(bf16[256,2048]{1,0:T(8,128)(2,1)} %collective-permute-done.10.refs_8_.refs_4_), channel_id=1, source_target_pairs={{0,8},{8,16},{16,24},{24,28},{28,20},{20,12},{12,4},{4,0},{1,9},{9... | collective-permute-start | bytes 3145736 | tf_op jit(solution)/shard_map/ppermute | solution.py:914
  95.7 25.7 %collective-permute-start.16 = (bf16[256,2048]{1,0:T(8,128)(2,1)}, bf16[256,2048]{1,0:T(8,128)(2,1)S(1)}, u32[]{:S(2)}, u32[]{:S(2)}) collective-permute-start(bf16[256,2048]{1,0:T(8,128)(2,1)} %collective-permute-done.11.refs_7_.refs_3_), channel_id=1, source_target_pairs={{0,4},{8,0},{16,8},{24,16},{28,24},{20,28},{12,20},{4,12},{1,5},{9... | collective-permute-start | bytes 3145736 | tf_op jit(solution)/shard_map/ppermute | solution.py:914
  97.3 24.1 %all-to-all-start = ((s32[8,128,8]{1,2,0:T(8,128)}), s32[8,128,8]{1,2,0:T(8,128)}, u32[]{:S(2)}, u32[]{:S(2)}) async-start(s32[8,128,8]{1,2,0:T(8,128)} %broadcast_in_dim.48), calls=%async_computation | async-start | bytes 65536 | tf_op jit(solution)/shard_map/all_to_all | solution.py:1118
  146.8 37.6 %all-to-all-start.1 = ((bf16[8,6,128,128]{3,2,1,0:T(8,128)(2,1)}), bf16[8,6,128,128]{3,2,1,0:T(8,128)(2,1)S(1)}, u32[]{:S(2)}, u32[]{:S(2)}) async-start(bf16[8,6,128,128]{3,2,1,0:T(8,128)(2,1)} %copy-done.20), calls=%async_computation.1 | async-start | bytes 3145728 | tf_op jit(solution)/shard_map/all_to_all | solution.py:1075
  221.7 14.2 %collective-permute-start.20 = (bf16[128,2048]{1,0:T(8,128)(2,1)S(1)}, bf16[128,2048]{1,0:T(8,128)(2,1)}, u32[]{:S(2)}, u32[]{:S(2)}) collective-permute-start(bf16[128,2048]{1,0:T(8,128)(2,1)S(1)} %multiply_convert_fusion.refs_0_), channel_id=1, source_target_pairs={{0,8},{8,16},{16,24},{24,28},{28,20},{20,12},{12,4},{4,0},{1,9},{9... | collective-permute-start | bytes 1572872 | tf_op jit(solution)/shard_map/ppermute | solution.py:914
  223.2 13.9 %collective-permute-start.21 = (bf16[128,2048]{1,0:T(8,128)(2,1)S(1)}, bf16[128,2048]{1,0:T(8,128)(2,1)}, u32[]{:S(2)}, u32[]{:S(2)}) collective-permute-start(bf16[128,2048]{1,0:T(8,128)(2,1)S(1)} %multiply_convert_fusion.refs_0_), channel_id=1, source_target_pairs={{0,4},{8,0},{16,8},{24,16},{28,24},{20,28},{12,20},{4,12},{1,5},{9... | collective-permute-start | bytes 1572872 | tf_op jit(solution)/shard_map/ppermute | solution.py:914
  251.6 24.2 %collective-permute-start.26 = (bf16[128,2048]{1,0:T(8,128)(2,1)S(1)}, bf16[128,2048]{1,0:T(8,128)(2,1)S(1)}, u32[]{:S(2)}, u32[]{:S(2)}) collective-permute-start(bf16[128,2048]{1,0:T(8,128)(2,1)S(1)} %copy-done.96), channel_id=1, source_target_pairs={{0,8},{8,16},{16,24},{24,28},{28,20},{20,12},{12,4},{4,0},{1,9},{9... | collective-permute-start | bytes 1572872 | tf_op jit(solution)/shard_map/ppermute | solution.py:914
  253.1 22.7 %collective-permute-start.27 = (bf16[128,2048]{1,0:T(8,128)(2,1)S(1)}, bf16[128,2048]{1,0:T(8,128)(2,1)S(1)}, u32[]{:S(2)}, u32[]{:S(2)}) collective-permute-start(bf16[128,2048]{1,0:T(8,128)(2,1)S(1)} %copy-done.98), channel_id=1, source_target_pairs={{0,4},{8,0},{16,8},{24,16},{28,24},{20,28},{12,20},{4,12},{1,5},{9... | collective-permute-start | bytes 1572872 | tf_op jit(solution)/shard_map/ppermute | solution.py:914
  253.6 21.0 %collective-permute-start.24 = (bf16[128,2048]{1,0:T(8,128)(2,1)}, bf16[128,2048]{1,0:T(8,128)(2,1)S(1)}, u32[]{:S(2)}, u32[]{:S(2)}) collective-permute-start(bf16[128,2048]{1,0:T(8,128)(2,1)} %collective-permute-done.22.refs_0_), channel_id=1, source_target_pairs={{0,8},{8,16},{16,24},{24,28},{28,20},{20,12},{12,4},{4,0},{1,9},{9... | collective-permute-start | bytes 1572872 | tf_op jit(solution)/shard_map/ppermute | solution.py:914
  255.1 20.7 %collective-permute-start.25 = (bf16[128,2048]{1,0:T(8,128)(2,1)}, bf16[128,2048]{1,0:T(8,128)(2,1)S(1)}, u32[]{:S(2)}, u32[]{:S(2)}) collective-permute-start(bf16[128,2048]{1,0:T(8,128)(2,1)} %collective-permute-done.23.refs_3_), channel_id=1, source_target_pairs={{0,4},{8,0},{16,8},{24,16},{28,24},{20,28},{12,20},{4,12},{1,5},{9... | collective-permute-start | bytes 1572872 | tf_op jit(solution)/shard_map/ppermute | solution.py:914
  282.8 39.6 %collective-permute-start.34 = (bf16[4,2,128,128]{3,2,1,0:T(8,128)(2,1)}, bf16[4,2,128,128]{3,2,1,0:T(8,128)(2,1)}, u32[]{:S(2)}, u32[]{:S(2)}) collective-permute-start(bf16[4,2,128,128]{3,2,1,0:T(8,128)(2,1)} %constant_dynamic-slice_fusion), channel_id=1, source_target_pairs={{0,2},{1,3},{2,0},{3,1},{4,6},{5,7},{6,4},{7,5},{8,10},{9,11},{10,... | collective-permute-start | bytes 786440 | tf_op jit(solution)/shard_map/ppermute | solution.py:902
  301.4 21.0 %collective-permute-start.35 = (bf16[128,2048]{1,0:T(8,128)(2,1)}, bf16[128,2048]{1,0:T(8,128)(2,1)S(1)}, u32[]{:S(2)}, u32[]{:S(2)}) collective-permute-start(bf16[128,2048]{1,0:T(8,128)(2,1)} %collective-permute-done.32.refs_2_), channel_id=1, source_target_pairs={{0,8},{8,16},{16,24},{24,28},{28,20},{20,12},{12,4},{4,0},{1,9},{9... | collective-permute-start | bytes 1572872 | tf_op jit(solution)/shard_map/ppermute | solution.py:914
  302.5 19.9 %collective-permute-start.36 = (bf16[128,2048]{1,0:T(8,128)(2,1)}, bf16[128,2048]{1,0:T(8,128)(2,1)S(1)}, u32[]{:S(2)}, u32[]{:S(2)}) collective-permute-start(bf16[128,2048]{1,0:T(8,128)(2,1)} %collective-permute-done.33.refs_1_), channel_id=1, source_target_pairs={{0,4},{8,0},{16,8},{24,16},{28,24},{20,28},{12,20},{4,12},{1,5},{9... | collective-permute-start | bytes 1572872 | tf_op jit(solution)/shard_map/ppermute | solution.py:914
  322.4 20.2 %collective-permute-start.37 = (bf16[128,2048]{1,0:T(8,128)(2,1)S(1)}, bf16[128,2048]{1,0:T(8,128)(2,1)}, u32[]{:S(2)}, u32[]{:S(2)}) collective-permute-start(bf16[128,2048]{1,0:T(8,128)(2,1)S(1)} %collective-permute-done.35.refs_4_), channel_id=1, source_target_pairs={{0,8},{8,16},{16,24},{24,28},{28,20},{20,12},{12,4},{4,0},{1,9},{9... | collective-permute-start | bytes 1572872 | tf_op jit(solution)/shard_map/ppermute | solution.py:914
  323.5 19.1 %collective-permute-start.38 = (bf16[128,2048]{1,0:T(8,128)(2,1)S(1)}, bf16[128,2048]{1,0:T(8,128)(2,1)}, u32[]{:S(2)}, u32[]{:S(2)}) collective-permute-start(bf16[128,2048]{1,0:T(8,128)(2,1)S(1)} %collective-permute-done.36.refs_3_), channel_id=1, source_target_pairs={{0,4},{8,0},{16,8},{24,16},{28,24},{20,28},{12,20},{4,12},{1,5},{9... | collective-permute-start | bytes 1572872 | tf_op jit(solution)/shard_map/ppermute | solution.py:914
  340.6 16.3 %collective-permute-start.39 = (bf16[64,2048]{1,0:T(8,128)(2,1)}, bf16[64,2048]{1,0:T(8,128)(2,1)}, u32[]{:S(2)}, u32[]{:S(2)}) collective-permute-start(bf16[64,2048]{1,0:T(8,128)(2,1)} %get-tuple-element.917), channel_id=1, source_target_pairs={{0,8},{8,16},{16,24},{24,28},{28,20},{20,12},{12,4},{4,0},{1,9},{9... | collective-permute-start | bytes 786440 | tf_op jit(solution)/shard_map/ppermute | solution.py:914
  341.6 15.3 %collective-permute-start.40 = (bf16[64,2048]{1,0:T(8,128)(2,1)}, bf16[64,2048]{1,0:T(8,128)(2,1)}, u32[]{:S(2)}, u32[]{:S(2)}) collective-permute-start(bf16[64,2048]{1,0:T(8,128)(2,1)} %get-tuple-element.916), channel_id=1, source_target_pairs={{0,4},{8,0},{16,8},{24,16},{28,24},{20,28},{12,20},{4,12},{1,5},{9... | collective-permute-start | bytes 786440 | tf_op jit(solution)/shard_map/ppermute | solution.py:914
  362.3 18.2 %collective-permute-start.44 = (bf16[128,2048]{1,0:T(8,128)(2,1)S(1)}, bf16[128,2048]{1,0:T(8,128)(2,1)S(1)}, u32[]{:S(2)}, u32[]{:S(2)}) collective-permute-start(bf16[128,2048]{1,0:T(8,128)(2,1)S(1)} %pad_maximum_fusion.6), channel_id=1, source_target_pairs={{0,4},{8,0},{16,8},{24,16},{28,24},{20,28},{12,20},{4,12},{1,5},{9... | collective-permute-start | bytes 1572872 | tf_op jit(solution)/shard_map/ppermute | solution.py:914
  362.6 17.8 %collective-permute-start.43 = (bf16[128,2048]{1,0:T(8,128)(2,1)S(1)}, bf16[128,2048]{1,0:T(8,128)(2,1)S(1)}, u32[]{:S(2)}, u32[]{:S(2)}) collective-permute-start(bf16[128,2048]{1,0:T(8,128)(2,1)S(1)} %pad_maximum_fusion.5), channel_id=1, source_target_pairs={{0,8},{8,16},{16,24},{24,28},{28,20},{20,12},{12,4},{4,0},{1,9},{9... | collective-permute-start | bytes 1572872 | tf_op jit(solution)/shard_map/ppermute | solution.py:914
  380.6 17.0 %collective-permute-start.46 = (bf16[128,2048]{1,0:T(8,128)(2,1)S(1)}, bf16[128,2048]{1,0:T(8,128)(2,1)S(1)}, u32[]{:S(2)}, u32[]{:S(2)}) collective-permute-start(bf16[128,2048]{1,0:T(8,128)(2,1)S(1)} %add_convert_fusion.7), channel_id=1, source_target_pairs={{0,4},{8,0},{16,8},{24,16},{28,24},{20,28},{12,20},{4,12},{1,5},{9... | collective-permute-start | bytes 1572872 | tf_op jit(solution)/shard_map/ppermute | solution.py:914
  382.7 15.7 %collective-permute-start.45 = (bf16[128,2048]{1,0:T(8,128)(2,1)S(1)}, bf16[128,2048]{1,0:T(8,128)(2,1)}, u32[]{:S(2)}, u32[]{:S(2)}) collective-permute-start(bf16[128,2048]{1,0:T(8,128)(2,1)S(1)} %add_convert_fusion.8), channel_id=1, source_target_pairs={{0,8},{8,16},{16,24},{24,28},{28,20},{20,12},{12,4},{4,0},{1,9},{9... | collective-permute-start | bytes 1572872 | tf_op jit(solution)/shard_map/ppermute | solution.py:914
  403.5 35.8 %collective-permute-start.52 = (bf16[2048,1024]{1,0:T(8,128)(2,1)}, bf16[2048,1024]{1,0:T(8,128)(2,1)}, u32[]{:S(2)}, u32[]{:S(2)}) collective-permute-start(bf16[2048,1024]{1,0:T(8,128)(2,1)} %transposed.1.own_ref), channel_id=1, source_target_pairs={{0,1},{1,0},{2,3},{3,2},{4,5},{5,4},{6,7},{7,6},{8,9},{9,8},{10,11... | collective-permute-start | bytes 12582920 | tf_op jit(solution)/shard_map/ppermute | solution.py:902
  406.2 21.0 %collective-permute-start.47 = (bf16[128,2048]{1,0:T(8,128)(2,1)}, bf16[128,2048]{1,0:T(8,128)(2,1)}, u32[]{:S(2)}, u32[]{:S(2)}) collective-permute-start(bf16[128,2048]{1,0:T(8,128)(2,1)} %get-tuple-element.913), channel_id=1, source_target_pairs={{0,8},{8,16},{16,24},{24,28},{28,20},{20,12},{12,4},{4,0},{1,9},{9... | collective-permute-start | bytes 1572872 | tf_op jit(solution)/shard_map/ppermute | solution.py:914
  407.2 20.0 %collective-permute-start.48 = (bf16[128,2048]{1,0:T(8,128)(2,1)}, bf16[128,2048]{1,0:T(8,128)(2,1)}, u32[]{:S(2)}, u32[]{:S(2)}) collective-permute-start(bf16[128,2048]{1,0:T(8,128)(2,1)} %get-tuple-element.912), channel_id=1, source_target_pairs={{0,4},{8,0},{16,8},{24,16},{28,24},{20,28},{12,20},{4,12},{1,5},{9... | collective-permute-start | bytes 1572872 | tf_op jit(solution)/shard_map/ppermute | solution.py:914
  409.1 17.2 %collective-permute-start.49 = (bf16[64,2048]{1,0:T(8,128)(2,1)}, bf16[64,2048]{1,0:T(8,128)(2,1)S(1)}, u32[]{:S(2)}, u32[]{:S(2)}) collective-permute-start(bf16[64,2048]{1,0:T(8,128)(2,1)} %get-tuple-element.909), channel_id=1, source_target_pairs={{0,8},{8,16},{16,24},{24,28},{28,20},{20,12},{12,4},{4,0},{1,9},{9... | collective-permute-start | bytes 786440 | tf_op jit(solution)/shard_map/ppermute | solution.py:914
  410.1 17.0 %collective-permute-start.50 = (bf16[64,2048]{1,0:T(8,128)(2,1)}, bf16[64,2048]{1,0:T(8,128)(2,1)}, u32[]{:S(2)}, u32[]{:S(2)}) collective-permute-start(bf16[64,2048]{1,0:T(8,128)(2,1)} %get-tuple-element.908), channel_id=1, source_target_pairs={{0,4},{8,0},{16,8},{24,16},{28,24},{20,28},{12,20},{4,12},{1,5},{9... | collective-permute-start | bytes 786440 | tf_op jit(solution)/shard_map/ppermute | solution.py:914
  417.6 209.6 %reduce-scatter.4.cloned.1.call-start = ((), (), s32[]{:S(2)}) async-start(), calls=%async_computation.12 | async-start | bytes 10485760 | tf_op jit(solution)/shard_map/reduce_scatter | solution.py:1217
  436.5 24.7 %collective-permute-start.54 = (bf16[128,2048]{1,0:T(8,128)(2,1)}, bf16[128,2048]{1,0:T(8,128)(2,1)}, u32[]{:S(2)}, u32[]{:S(2)}) collective-permute-start(bf16[128,2048]{1,0:T(8,128)(2,1)} %pad_maximum_fusion.9), channel_id=1, source_target_pairs={{0,4},{8,0},{16,8},{24,16},{28,24},{20,28},{12,20},{4,12},{1,5},{9... | collective-permute-start | bytes 1572872 | tf_op jit(solution)/shard_map/ppermute | solution.py:914
  438.6 22.6 %collective-permute-start.53 = (bf16[128,2048]{1,0:T(8,128)(2,1)}, bf16[128,2048]{1,0:T(8,128)(2,1)}, u32[]{:S(2)}, u32[]{:S(2)}) collective-permute-start(bf16[128,2048]{1,0:T(8,128)(2,1)} %pad_maximum_fusion.8), channel_id=1, source_target_pairs={{0,8},{8,16},{16,24},{24,28},{28,20},{20,12},{12,4},{4,0},{1,9},{9... | collective-permute-start | bytes 1572872 | tf_op jit(solution)/shard_map/ppermute | solution.py:914
  442.7 18.9 %all-to-all-start.4 = ((bf16[8,2,128,128]{3,2,1,0:T(8,128)(2,1)}), bf16[8,2,128,128]{3,2,1,0:T(8,128)(2,1)}, u32[]{:S(2)}, u32[]{:S(2)}) async-start(bf16[8,2,128,128]{3,2,1,0:T(8,128)(2,1)} %grad_pairs.1), calls=%async_computation.4 | async-start | bytes 1048576 | tf_op jit(solution)/shard_map/all_to_all | solution.py:1075
  446.9 205.3 %reduce-scatter.6.cloned.1.call-start = ((), (), s32[]{:S(2)}) async-start(), calls=%async_computation.13 | async-start | bytes 10485760 | tf_op jit(solution)/shard_map/reduce_scatter | solution.py:1217
  461.1 25.8 %collective-permute-start.55 = (bf16[128,2048]{1,0:T(8,128)(2,1)}, bf16[128,2048]{1,0:T(8,128)(2,1)}, u32[]{:S(2)}, u32[]{:S(2)}) collective-permute-start(bf16[128,2048]{1,0:T(8,128)(2,1)} %get-tuple-element.679.own_ref.refs_0_), channel_id=1, source_target_pairs={{0,2},{1,3},{2,0},{3,1},{4,6},{5,7},{6,4},{7,5},{8,10},{9,11},{10,... | collective-permute-start | bytes 1572872 | tf_op jit(solution)/shard_map/ppermute | solution.py:902
  463.7 23.2 %collective-permute-start.57 = (bf16[128,2048]{1,0:T(8,128)(2,1)}, bf16[128,2048]{1,0:T(8,128)(2,1)}, u32[]{:S(2)}, u32[]{:S(2)}) collective-permute-start(bf16[128,2048]{1,0:T(8,128)(2,1)} %add_convert_fusion.3), channel_id=1, source_target_pairs={{0,4},{8,0},{16,8},{24,16},{28,24},{20,28},{12,20},{4,12},{1,5},{9... | collective-permute-start | bytes 1572872 | tf_op jit(solution)/shard_map/ppermute | solution.py:914
  468.7 18.2 %collective-permute-start.56 = (bf16[128,2048]{1,0:T(8,128)(2,1)}, bf16[128,2048]{1,0:T(8,128)(2,1)}, u32[]{:S(2)}, u32[]{:S(2)}) collective-permute-start(bf16[128,2048]{1,0:T(8,128)(2,1)} %add_convert_fusion.4), channel_id=1, source_target_pairs={{0,8},{8,16},{16,24},{24,28},{28,20},{20,12},{12,4},{4,0},{1,9},{9... | collective-permute-start | bytes 1572872 | tf_op jit(solution)/shard_map/ppermute | solution.py:914
  497.0 23.3 %collective-permute-start.59 = (bf16[1024,384]{1,0:T(8,128)(2,1)}, bf16[1024,384]{1,0:T(8,128)(2,1)}, u32[]{:S(2)}, u32[]{:S(2)}) collective-permute-start(bf16[1024,384]{1,0:T(8,128)(2,1)} %slice.261), channel_id=1, source_target_pairs={{0,2},{1,3},{2,0},{3,1},{4,6},{5,7},{6,4},{7,5},{8,10},{9,11},{10,... | collective-permute-start | bytes 2359304 | tf_op jit(solution)/shard_map/ppermute | solution.py:902
  502.1 50.0 %all-to-all-start.5 = ((bf16[8,6,128,128]{3,2,1,0:T(8,128)(2,1)}), bf16[8,6,128,128]{3,2,1,0:T(8,128)(2,1)}, u32[]{:S(2)}, u32[]{:S(2)}) async-start(bf16[8,6,128,128]{3,2,1,0:T(8,128)(2,1)} %get-tuple-element.716.g_ref), calls=%async_computation.5 | async-start | bytes 3145728 | tf_op jit(solution)/shard_map/all_to_all | solution.py:1078
  507.9 163.5 %reduce-scatter.8.cloned.1.call-start = ((), (), s32[]{:S(2)}) async-start(), calls=%async_computation.14 | async-start | bytes 10485760 | tf_op jit(solution)/shard_map/reduce_scatter | solution.py:1217
  510.8 36.2 %collective-permute-start.61 = (bf16[128,2048]{1,0:T(8,128)(2,1)}, bf16[128,2048]{1,0:T(8,128)(2,1)}, u32[]{:S(2)}, u32[]{:S(2)}) collective-permute-start(bf16[128,2048]{1,0:T(8,128)(2,1)} %get-tuple-element.905), channel_id=1, source_target_pairs={{0,8},{8,16},{16,24},{24,28},{28,20},{20,12},{12,4},{4,0},{1,9},{9... | collective-permute-start | bytes 1572872 | tf_op jit(solution)/shard_map/ppermute | solution.py:914
  512.8 36.9 %collective-permute-start.62 = (bf16[128,2048]{1,0:T(8,128)(2,1)}, bf16[128,2048]{1,0:T(8,128)(2,1)}, u32[]{:S(2)}, u32[]{:S(2)}) collective-permute-start(bf16[128,2048]{1,0:T(8,128)(2,1)} %get-tuple-element.904), channel_id=1, source_target_pairs={{0,4},{8,0},{16,8},{24,16},{28,24},{20,28},{12,20},{4,12},{1,5},{9... | collective-permute-start | bytes 1572872 | tf_op jit(solution)/shard_map/ppermute | solution.py:914
  522.8 53.2 %collective-permute-start.65 = (bf16[32,2048]{1,0:T(8,128)(2,1)}, bf16[32,2048]{1,0:T(8,128)(2,1)}, u32[]{:S(2)}, u32[]{:S(2)}) collective-permute-start(bf16[32,2048]{1,0:T(8,128)(2,1)} %get-tuple-element.903), channel_id=1, source_target_pairs={{0,8},{8,16},{16,24},{24,28},{28,20},{20,12},{12,4},{4,0},{1,9},{9... | collective-permute-start | bytes 393224 | tf_op jit(solution)/shard_map/ppermute | solution.py:914
  525.8 40.3 %collective-permute-start.63 = (bf16[512,768]{1,0:T(8,128)(2,1)}, bf16[512,768]{1,0:T(8,128)(2,1)}, u32[]{:S(2)}, u32[]{:S(2)}) collective-permute-start(bf16[512,768]{1,0:T(8,128)(2,1)} %side_by_side.1.refs_0_), channel_id=1, source_target_pairs={{0,8},{8,16},{16,24},{24,28},{28,20},{20,12},{12,4},{4,0},{1,9},{9... | collective-permute-start | bytes 2359304 | tf_op jit(solution)/shard_map/ppermute | solution.py:914
  527.3 38.8 %collective-permute-start.64 = (bf16[512,768]{1,0:T(8,128)(2,1)}, bf16[512,768]{1,0:T(8,128)(2,1)}, u32[]{:S(2)}, u32[]{:S(2)}) collective-permute-start(bf16[512,768]{1,0:T(8,128)(2,1)} %side_by_side.1.refs_0_), channel_id=1, source_target_pairs={{0,4},{8,0},{16,8},{24,16},{28,24},{20,28},{12,20},{4,12},{1,5},{9... | collective-permute-start | bytes 2359304 | tf_op jit(solution)/shard_map/ppermute | solution.py:914
  547.1 28.9 %collective-permute-start.66 = (bf16[32,2048]{1,0:T(8,128)(2,1)S(1)}, bf16[32,2048]{1,0:T(8,128)(2,1)S(1)}, u32[]{:S(2)}, u32[]{:S(2)}) collective-permute-start(bf16[32,2048]{1,0:T(8,128)(2,1)S(1)} %copy-done.77), channel_id=1, source_target_pairs={{0,4},{8,0},{16,8},{24,16},{28,24},{20,28},{12,20},{4,12},{1,5},{9... | collective-permute-start | bytes 393224 | tf_op jit(solution)/shard_map/ppermute | solution.py:914
  566.2 38.9 %collective-permute-start.69 = (bf16[512,768]{1,0:T(8,128)(2,1)}, bf16[512,768]{1,0:T(8,128)(2,1)}, u32[]{:S(2)}, u32[]{:S(2)}) collective-permute-start(bf16[512,768]{1,0:T(8,128)(2,1)} %collective-permute-done.63.refs_2_), channel_id=1, source_target_pairs={{0,8},{8,16},{16,24},{24,28},{28,20},{20,12},{12,4},{4,0},{1,9},{9... | collective-permute-start | bytes 2359304 | tf_op jit(solution)/shard_map/ppermute | solution.py:914
  575.9 29.6 %collective-permute-start.70 = (bf16[512,768]{1,0:T(8,128)(2,1)}, bf16[512,768]{1,0:T(8,128)(2,1)}, u32[]{:S(2)}, u32[]{:S(2)}) collective-permute-start(bf16[512,768]{1,0:T(8,128)(2,1)} %collective-permute-done.64.refs_1_), channel_id=1, source_target_pairs={{0,4},{8,0},{16,8},{24,16},{28,24},{20,28},{12,20},{4,12},{1,5},{9... | collective-permute-start | bytes 2359304 | tf_op jit(solution)/shard_map/ppermute | solution.py:914
  577.8 24.0 %collective-permute-start.68 = (bf16[64,2048]{1,0:T(8,128)(2,1)}, bf16[64,2048]{1,0:T(8,128)(2,1)}, u32[]{:S(2)}, u32[]{:S(2)}) collective-permute-start(bf16[64,2048]{1,0:T(8,128)(2,1)} %pad_maximum_fusion.11), channel_id=1, source_target_pairs={{0,4},{8,0},{16,8},{24,16},{28,24},{20,28},{12,20},{4,12},{1,5},{9... | collective-permute-start | bytes 786440 | tf_op jit(solution)/shard_map/ppermute | solution.py:914
  581.1 20.7 %collective-permute-start.67 = (bf16[64,2048]{1,0:T(8,128)(2,1)}, bf16[64,2048]{1,0:T(8,128)(2,1)}, u32[]{:S(2)}, u32[]{:S(2)}) collective-permute-start(bf16[64,2048]{1,0:T(8,128)(2,1)} %pad_maximum_fusion.10), channel_id=1, source_target_pairs={{0,8},{8,16},{16,24},{24,28},{28,20},{20,12},{12,4},{4,0},{1,9},{9... | collective-permute-start | bytes 786440 | tf_op jit(solution)/shard_map/ppermute | solution.py:914
  594.0 18.8 %collective-permute-start.72 = (bf16[128,2048]{1,0:T(8,128)(2,1)S(1)}, bf16[128,2048]{1,0:T(8,128)(2,1)S(1)}, u32[]{:S(2)}, u32[]{:S(2)}) collective-permute-start(bf16[128,2048]{1,0:T(8,128)(2,1)S(1)} %get-tuple-element.758), channel_id=1, source_target_pairs={{0,1},{1,0},{2,3},{3,2},{4,5},{5,4},{6,7},{7,6},{8,9},{9,8},{10,11... | collective-permute-start | bytes 1572872 | tf_op jit(solution)/shard_map/ppermute | solution.py:902
  603.2 13.9 %collective-permute-start.73 = (bf16[64,2048]{1,0:T(8,128)(2,1)S(1)}, bf16[64,2048]{1,0:T(8,128)(2,1)S(1)}, u32[]{:S(2)}, u32[]{:S(2)}) collective-permute-start(bf16[64,2048]{1,0:T(8,128)(2,1)S(1)} %get-tuple-element.897), channel_id=1, source_target_pairs={{0,8},{8,16},{16,24},{24,28},{28,20},{20,12},{12,4},{4,0},{1,9},{9... | collective-permute-start | bytes 786440 | tf_op jit(solution)/shard_map/ppermute | solution.py:914
  617.2 20.7 %collective-permute-start.77 = (bf16[512,768]{1,0:T(8,128)(2,1)}, bf16[512,768]{1,0:T(8,128)(2,1)S(1)}, u32[]{:S(2)}, u32[]{:S(2)}) collective-permute-start(bf16[512,768]{1,0:T(8,128)(2,1)} %collective-permute-done.69.refs_0_), channel_id=1, source_target_pairs={{0,8},{8,16},{16,24},{24,28},{28,20},{20,12},{12,4},{4,0},{1,9},{9... | collective-permute-start | bytes 2359304 | tf_op jit(solution)/shard_map/ppermute | solution.py:914
  618.9 20.7 %collective-permute-start.78 = (bf16[512,768]{1,0:T(8,128)(2,1)}, bf16[512,768]{1,0:T(8,128)(2,1)S(1)}, u32[]{:S(2)}, u32[]{:S(2)}) collective-permute-start(bf16[512,768]{1,0:T(8,128)(2,1)} %collective-permute-done.70.refs_3_), channel_id=1, source_target_pairs={{0,4},{8,0},{16,8},{24,16},{28,24},{20,28},{12,20},{4,12},{1,5},{9... | collective-permute-start | bytes 2359304 | tf_op jit(solution)/shard_map/ppermute | solution.py:914
  620.5 21.6 %collective-permute-start.79 = (bf16[64,2048]{1,0:T(8,128)(2,1)S(1)}, bf16[64,2048]{1,0:T(8,128)(2,1)S(1)}, u32[]{:S(2)}, u32[]{:S(2)}) collective-permute-start(bf16[64,2048]{1,0:T(8,128)(2,1)S(1)} %get-tuple-element.895), channel_id=1, source_target_pairs={{0,8},{8,16},{16,24},{24,28},{28,20},{20,12},{12,4},{4,0},{1,9},{9... | collective-permute-start | bytes 786440 | tf_op jit(solution)/shard_map/ppermute | solution.py:914
  622.3 21.4 %collective-permute-start.80 = (bf16[64,2048]{1,0:T(8,128)(2,1)S(1)}, bf16[64,2048]{1,0:T(8,128)(2,1)}, u32[]{:S(2)}, u32[]{:S(2)}) collective-permute-start(bf16[64,2048]{1,0:T(8,128)(2,1)S(1)} %get-tuple-element.894), channel_id=1, source_target_pairs={{0,4},{8,0},{16,8},{24,16},{28,24},{20,28},{12,20},{4,12},{1,5},{9... | collective-permute-start | bytes 786440 | tf_op jit(solution)/shard_map/ppermute | solution.py:914
  631.6 17.8 %collective-permute-start.81 = (f32[2,2048]{1,0:T(2,128)S(1)}, f32[2,2048]{1,0:T(2,128)S(1)}, u32[]{:S(2)}, u32[]{:S(2)}) collective-permute-start(f32[2,2048]{1,0:T(2,128)S(1)} %add.186), channel_id=1, source_target_pairs={{0,2},{1,3},{2,0},{3,1},{4,6},{5,7},{6,4},{7,5},{8,10},{9,11},{10,... | collective-permute-start | bytes 49160 | tf_op jit(solution)/shard_map/ppermute | solution.py:902
  (140 other events, 1316.7 us)
Sparse Core Ops, SparseCore 0:
  43.0 57.5 all-gather.3
  102.7 58.2 all-gather.5
  163.2 58.3 all-gather.7
  420.7 87.2 reduce-scatter.3
  510.5 72.0 reduce-scatter.5
  585.1 77.1 reduce-scatter.7

commit v5 on v4

--- a/solution.py
+++ b/solution.py
@@ -1274,14 +1274,14 @@
     )
     if repeats > 1:
         head_gains = jnp.where(lax.axis_index("ctx") % repeats == 0, head_gains, 0.0)
-    across = in_order(across)
-    diagonal = swap(across, 1)
     ring.land()
 
     grads = after(grads, in_order.last)
     ring.step()
     half_grads = in_order(head_weights(table, grads, normed_t, beside_t, 3, at_from))
     other_half = swap(half_grads[width // 2 :], 2)
+    across = in_order(across)
+    diagonal = swap(across, 1)
     grads = collect_pairs(after(grads, in_order.last))
     mixed, diagonal = after((mixed, diagonal), in_order.last)
     d_out = in_order(
@@ -1294,20 +1294,34 @@
     total_ring = Ring(in_order, ring_gather(side_by_side(table, keep, send), in_order, pieces))
     out_ring = Ring(in_order, ring_scatter(lambda offset: d_out[offset * own_rows : (offset + 1) * own_rows]))
     d_down = weight_grad(cots, acts)
-    output = in_order((hidden + ring.finish()).astype(BF))
-    grads = in_order(grads)
+    (grads,) = land(in_order, (total_ring, out_ring, ring), grads)
     total_ring.step()
+    out_ring.step()
     d_down = share(d_down)
-    out_ring.step()
-    grads, grad_ffn_in, grad_logits = after((grads, grad_ffn_in, grad_logits), in_order.last)
-    own, far = in_order(*pair_normed(grads, own_columns, 3))
+    own, far = in_order(*pair_normed(after(grads, in_order.last), own_columns, 3))
+    land(in_order, (total_ring, out_ring))
     far = swap(far, 1)
+    total_ring.step()
+    grad_ffn_in, grad_logits = after((grad_ffn_in, grad_logits), in_order.last)
     d_ffn_gain = jnp.sum(grad_ffn_in * hidden * factor_two, axis=0, keepdims=True)
     d_router = dot(grad_logits, ffn_in.astype(F32), ((0,), (0,)), precision=lax.Precision.HIGHEST)
-    early = in_order(jnp.concatenate([d_router, d_ffn_gain]))
-    early = Ring(in_order, sum_fsdp(early))
+    early = Ring(in_order, sum_fsdp(in_order(jnp.concatenate([d_router, d_ffn_gain]))))
     out_ring.step()
-    total_ring.step()
+    early.step()
+    grad_normed = own + in_order(far).astype(F32)
+    d_attn_gain = jnp.sum(grad_normed * source * factor_one, axis=0)
+    inner = grad_normed * attn_gain
+    d_tokens = (
+        grad_hidden
+        + factor_one * inner
+        - source * (factor_one * factor_one * factor_one) * jnp.mean(inner * source, axis=-1, keepdims=True)
+    )
+    late = jnp.concatenate([d_attn_gain, head_gains[0], head_gains[1], jnp.zeros((width - 2 * head_dim,), F32)])
+    d_tokens, late = in_order(d_tokens, late.reshape(2, width))
+    late = Ring(in_order, sum_fsdp(late))
+    late.step()
+    early.finish()
+    out_ring.step()
 
     whole = None
     seen = set()
@@ -1329,33 +1343,21 @@
         return arrays
 
     whole = take_whole(whole)
-    early.step()
-    grad_normed = own + in_order(far).astype(F32)
-    d_attn_gain = jnp.sum(grad_normed * source * factor_one, axis=0)
-    inner = grad_normed * attn_gain
-    d_tokens = (
-        grad_hidden
-        + factor_one * inner
-        - source * (factor_one * factor_one * factor_one) * jnp.mean(inner * source, axis=-1, keepdims=True)
-    )
-    d_tokens, d_attn_gain = in_order(d_tokens, d_attn_gain)
-    late = jnp.concatenate([d_attn_gain, head_gains[0], head_gains[1], jnp.zeros((width - 2 * head_dim,), F32)])
-    late = Ring(in_order, sum_fsdp(late.reshape(2, width)))
-    out_ring.step()
-    early.finish()
-    d_gate = in_order(split_experts(own_experts, slab, (after(d_gate, in_order.last), 0)))
-    late.step()
-    total_ring.step()
+    late.finish()
+    output = in_order((hidden + ring.finish()).astype(BF))
     d_out = out_ring.finish()
-    whole = take_whole(whole)
-    packed = in_order(pack_gains(table, d_out, early.value, late.finish(), at_slab[0], experts))
+    packed = in_order(pack_gains(table, d_out, early.value, late.value, at_slab[0], experts))
     packed_pieces = {}
     packed_ring = Ring(in_order, ring_gather(packed, in_order, packed_pieces))
-    d_up = in_order(split_experts(own_experts, slab, (after(d_up, in_order.last), 0)))
+    total_ring.step()
+    d_gate = in_order(split_experts(own_experts, slab, (after(d_gate, in_order.last), 0)))
+    whole = take_whole(whole)
+    packed_ring.step()
     total_ring.finish()
     whole = take_whole(whole)
     d_query, d_key, d_value = whole
     packed_ring.step()
+    d_up = in_order(split_experts(own_experts, slab, (after(d_up, in_order.last), 0)))
     packed_ring.step()
     d_down = in_order(split_experts(own_experts, slab, (after(d_down, in_order.last), 0)))
     packed_ring.finish()

time: 706 us -> 693 us (0.982)
    ppermute x72, waiting for transfers between devices: 129 us -> 121 us  [ring_send(): lax.ppermute(v, 'ctx', [(order[i], order[(i + direction) % size]) for i i...]
    unnamed x205 -> x199, local copies, waits for them, and re-layouts: 15.4 us -> 13.2 us
  transfers between devices with their start and end apart: 103 -> 103, of which waited for: 51 -> 49; matrix products, arithmetic and copies ran while one was open for 8% -> 8% of each run, Pallas kernels for 38% -> 39%
where the time goes in v5:
time: 693 us; the launch traced here: 684 us
  Pallas kernels  276 us (40%)
  waiting for transfers between devices  187 us (27%)
  starting transfers between devices  112 us (16%)
  other arithmetic  42.4 us (6%)
  local copies, waits for them, and re-layouts  31.2 us (5%)
  blocking collectives  17.8 us (3%)
  between operations  16.5 us (2%)
    ppermute x72, waiting for transfers between devices, ring_send(): lax.ppermute(v, 'ctx', [(order[i], order[(i + direction) % size]) for i i...  121 us
    ppermute x72, starting transfers between devices, ring_send(): lax.ppermute(v, 'ctx', [(order[i], order[(i + direction) % size]) for i i...  83.6 us
    pallas_call x3, Pallas kernels, sum_of_outer(): pl.pallas_call(sum_kernel, grid_spec=pltpu.PrefetchScalarGridSpec(num_sca...  43 us
    pallas_call x2, Pallas kernels, expert_units(): pl.pallas_call(functools.partial(expert_kernel, per=per, place=place, at=...  37.9 us
    pallas_call x2, Pallas kernels, expert_rows(): pl.pallas_call(expert_rows_kernel, grid=(width // wide,), in_specs=[whole...  27.6 us
    all_to_all x2, waiting for transfers between devices, spread_pairs(): return lax.all_to_all(v, 'ctx', split_axis=0, concat_axis=0, tiled=True)  27 us
    pallas_call x11, Pallas kernels, small_call(): pl.pallas_call(functools.partial(kernel, **kwargs), in_specs=[pl.BlockSpe...  25.9 us
    ppermute x20, waiting for transfers between devices, swap(): return lax.ppermute(v, 'fsdp', [(i, i ^ mask) for i in range(size)])  24.4 us
  transfers between devices with their start and end apart: 103, of which 49 were waited for; matrix products, arithmetic and copies ran while one was open for 8% of the time, Pallas kernels for 39%

profile of v5, /device:TPU:0, one launch (start us, length us, event | category | flops | bytes accessed | tf_op | source)
XLA Modules:
  0.0 683.9 jit_solution(1548075449716481129)
XLA Ops:
  8.4 3.1 take_parts.2
  11.6 3.1 collective-permute-start
  16.8 6.4 take_parts.3
  30.8 6.6 merge_experts.3
  37.4 3.9 collective-permute-done.2.refs_0_
  45.6 6.7 merge_experts.4
  52.3 13.8 %collective-permute-done.6.refs_6_.refs_2_ = bf16[256,2048]{1,0:T(8,128)(2,1)S(1)} collective-permute-done((bf16[256,2048]{1,0:T(8,128)(2,1)S(1)}, bf16[256,2048]{1,0:T(8,128)(2,1)S(1)}, u32[]{:S(2)}, u32[]{:S(2)}) %collective-permute-start.6) | collective-permute-done | bytes 1048608 | tf_op jit(solution)/shard_map/ppermute | solution.py:914
  70.1 4.1 collective-permute-done.9.refs_1_
  75.0 6.6 merge_experts.5
  81.6 11.7 %collective-permute-done.10.refs_8_.refs_4_ = bf16[256,2048]{1,0:T(8,128)(2,1)} collective-permute-done((bf16[256,2048]{1,0:T(8,128)(2,1)S(1)}, bf16[256,2048]{1,0:T(8,128)(2,1)}, u32[]{:S(2)}, u32[]{:S(2)}) %collective-permute-start.10) | collective-permute-done | bytes 1048608 | tf_op jit(solution)/shard_map/ppermute | solution.py:914
  97.3 4.0 all-to-all-start
  103.9 4.6 collective-permute-done.13.refs_2_
  110.6 10.8 %all-to-all-done = s32[8,128,8]{1,2,0:T(8,128)} async-done(((s32[8,128,8]{1,2,0:T(8,128)}), s32[8,128,8]{1,2,0:T(8,128)}, u32[]{:S(2)}, u32[]{:S(2)}) %all-to-all-start) | async-done | bytes 32800 | tf_op jit(solution)/shard_map/all_to_all | solution.py:1118
  123.7 9.0 %collective-permute-done.17 = bf16[128,2048]{1,0:T(8,128)(2,1)S(1)} collective-permute-done((bf16[128,2048]{1,0:T(8,128)(2,1)S(1)}, bf16[128,2048]{1,0:T(8,128)(2,1)S(1)}, u32[]{:S(2)}, u32[]{:S(2)}) %collective-permute-start.17) | collective-permute-done | bytes 524320 | tf_op jit(solution)/shard_map/ppermute | solution.py:914
  135.2 10.4 %own_pairs.1 = (bf16[8,6,128,128]{3,2,1,0:T(8,128)(2,1)S(1)}, bf16[2048,3072]{1,0:T(8,128)(2,1)}) custom-call(s32[68]{0:T(128)S(1)} %copy-done.26, bf16[128,2048]{1,0:T(8,128)(2,1)} %fusion.2.refs_0_, bf16[128,2048]{1,0:T(8,128)(2,1)S(1)} %copy-done.24, bf16[512,3072]{1,0:T(8,128)(2,1)S(1)} %copy-done.11, bf16[512,3072]{1,0:T(8,128)(2,1)} %collective-permute-done.8.refs_3_, ...), custom_call_target="tpu_custom_call" | custom-call | flops 1 | bytes 1 | tf_op jit(solution)/shard_map/own_pairs/pallas_call | solution.py:495
  146.8 3.8 all-to-all-start.1
  153.7 4.1 far_rows.1.far_ref
  160.1 24.4 %all-to-all-done.1.q_ref.k_ref.v_ref = bf16[8,6,128,128]{3,2,1,0:T(8,128)(2,1)S(1)} async-done(((bf16[8,6,128,128]{3,2,1,0:T(8,128)(2,1)}), bf16[8,6,128,128]{3,2,1,0:T(8,128)(2,1)S(1)}, u32[]{:S(2)}, u32[]{:S(2)}) %all-to-all-start.1) | async-done | bytes 1572896 | tf_op jit(solution)/shard_map/all_to_all | solution.py:1075
  188.1 7.8 %attend.1 = bf16[8,2,128,128]{3,2,1,0:T(8,128)(2,1)S(1)} custom-call(bf16[8,6,128,128]{3,2,1,0:T(8,128)(2,1)S(1)} %copy-done.16, bf16[8,6,128,128]{3,2,1,0:T(8,128)(2,1)S(1)} %copy-done.16, bf16[8,6,128,128]{3,2,1,0:T(8,128)(2,1)S(1)} %copy-done.16, f32[1,128]{1,0:T(1,128)S(1)} %bitcast.61, f32[1,128]{1,0:T(1,128)S(1)} %bitcast.63, ...), custom_call_target="tpu_custom_call" | custom-call | flops 20000000000 | bytes 50000000 | tf_op jit(solution)/shard_map/attend/pallas_call | solution.py:152
  196.7 17.8 %all_to_all.30.m_ref = bf16[8,2,128,128]{3,2,1,0:T(8,128)(2,1)S(1)} all-to-all(bf16[8,2,128,128]{3,2,1,0:T(8,128)(2,1)} %copy-done.25), channel_id=1, replica_groups=mesh['ctx'=8,'fsdp'=4] {'ctx'}, dimensions={0} | all-to-all | bytes 1048576 | tf_op jit(solution)/shard_map/all_to_all | solution.py:1078
  214.6 3.1 mixed_out.1
  226.7 10.4 %collective-permute-done.20.refs_2_ = bf16[128,2048]{1,0:T(8,128)(2,1)} collective-permute-done((bf16[128,2048]{1,0:T(8,128)(2,1)S(1)}, bf16[128,2048]{1,0:T(8,128)(2,1)}, u32[]{:S(2)}, u32[]{:S(2)}) %collective-permute-start.20) | collective-permute-done | bytes 524320 | tf_op jit(solution)/shard_map/ppermute | solution.py:914
  240.4 9.3 %stacked_matmul.2 = (f32[512,2048]{1,0:T(8,128)}, bf16[512,2048]{1,0:T(8,128)(2,1)}) custom-call(bf16[2048,2048]{1,0:T(8,128)(2,1)} %all-gather.4.cloned.1.call-done.w_ref.b_ref, bf16[128,2048]{1,0:T(8,128)(2,1)} %bitcast.66, bf16[128,2048]{1,0:T(8,128)(2,1)} %copy-done.97, bf16[128,2048]{1,0:T(8,128)(2,1)} %copy-done.96, bf16[128,2048]{1,0:T(8,128)(2,1)} %copy-done.94), custom_call_target="tpu_custom_call" | custom-call | flops 999999995904 | bytes 1000000000 | tf_op jit(solution)/shard_map/stacked_matmul/pallas_call | solution.py:209
  256.9 18.9 %expert_units.2 = (bf16[512,2048]{1,0:T(8,128)(2,1)}, bf16[512,2048]{1,0:T(8,128)(2,1)}, bf16[512,2048]{1,0:T(8,128)(2,1)}, f32[2,512,1]{2,1,0:T(8,128)}, bf16[512,2048]{1,0:T(8,128)(2,1)}) custom-call(s32[68]{0:T(128)} %get-tuple-element.919.table_ref._unused, bf16[2048,16]{1,0:T(8,128)(2,1)} %copy-done.3, s32[8,128,8]{2,1,0:T(8,128)} %copy.57.routes_ref, ...), custom_call_target="tpu_custom_call" | custom-call | flops 20000000000 | bytes 50000000 | tf_op jit(solution)/shard_map/expert_units/pallas_call | solution.py:273
  292.7 9.3 %stacked_matmul.3 = (f32[512,2048]{1,0:T(8,128)}, bf16[512,2048]{1,0:T(8,128)(2,1)}) custom-call(bf16[2048,2048]{1,0:T(8,128)(2,1)} %all-gather.4.cloned.1.call-done.w_ref.b_ref, bf16[128,2048]{1,0:T(8,128)(2,1)} %copy-done.92, bf16[128,2048]{1,0:T(8,128)(2,1)} %copy-done.72, bf16[128,2048]{1,0:T(8,128)(2,1)} %copy-done.71, ...), custom_call_target="tpu_custom_call" | custom-call | flops 999999995904 | bytes 1000000000 | tf_op jit(solution)/shard_map/stacked_matmul/pallas_call | solution.py:209
  304.9 19.0 %expert_units.3 = (bf16[512,2048]{1,0:T(8,128)(2,1)}, bf16[512,2048]{1,0:T(8,128)(2,1)}, bf16[512,2048]{1,0:T(8,128)(2,1)}, f32[2,512,1]{2,1,0:T(8,128)}, bf16[512,2048]{1,0:T(8,128)(2,1)}) custom-call(s32[68]{0:T(128)} %get-tuple-element.919.table_ref._unused, bf16[2048,16]{1,0:T(8,128)(2,1)} %copy-done.3, s32[8,128,8]{2,1,0:T(8,128)} %copy.57.routes_ref, ...), custom_call_target="tpu_custom_call" | custom-call | flops 20000000000 | bytes 50000000 | tf_op jit(solution)/shard_map/expert_units/pallas_call | solution.py:273
  326.0 13.8 %expert_rows.2 = bf16[512,2048]{1,0:T(8,128)(2,1)} custom-call(bf16[512,2048]{1,0:T(8,128)(2,1)} %get-tuple-element.604.gate_ref.refs_3_, bf16[512,2048]{1,0:T(8,128)(2,1)} %get-tuple-element.664.up_ref.refs_3_, bf16[2048,2048]{1,0:T(8,128)(2,1)} %all-gather.6.cloned.1.call-done.gate_w_ref, bf16[2048,2048]{1,0:T(8,128)(2,1)} %all-gather.8.cloned.1.call-done.up_w_ref), custom_call_target="tpu_custom_call" | custom-call | flops 20000000000 | bytes 50000000 | tf_op jit(solution)/shard_map/expert_rows/pallas_call | solution.py:312
  339.8 2.2 fusion.23
  344.1 14.2 %sum_of_outer.3 = bf16[2048,2048]{1,0:T(8,128)(2,1)} custom-call(s32[68]{0:T(128)} %get-tuple-element.919.table_ref._unused, bf16[512,2048]{1,0:T(8,128)(2,1)} %get-tuple-element.661.refs_0_, bf16[512,2048]{1,0:T(8,128)(2,1)} %get-tuple-element.662.refs_1_, bf16[512,2048]{1,0:T(8,128)(2,1)} %get-tuple-element.612.refs_2_.gate_ref, ...), custom_call_target="tpu_custom_call" | custom-call | flops 999999995904 | bytes 1000000000 | tf_op jit(solution)/shard_map/sum_of_outer/pallas_call | solution.py:367
  368.0 13.8 %expert_rows.3 = bf16[512,2048]{1,0:T(8,128)(2,1)} custom-call(bf16[512,2048]{1,0:T(8,128)(2,1)} %get-tuple-element.612.refs_2_.gate_ref, bf16[512,2048]{1,0:T(8,128)(2,1)} %get-tuple-element.663.up_ref.refs_2_, bf16[2048,2048]{1,0:T(8,128)(2,1)} %all-gather.6.cloned.1.call-done.gate_w_ref, bf16[2048,2048]{1,0:T(8,128)(2,1)} %all-gather.8.cloned.1.call-done.up_w_ref), custom_call_target="tpu_custom_call" | custom-call | flops 20000000000 | bytes 50000000 | tf_op jit(solution)/shard_map/expert_rows/pallas_call | solution.py:312
  385.8 13.2 %times_transpose.1 = (bf16[512,2048]{1,0:T(8,128)(2,1)}, bf16[512,2048]{1,0:T(8,128)(2,1)}) custom-call(bf16[2048,2048]{1,0:T(8,128)(2,1)} %all-gather.4.cloned.1.call-done.w_ref.b_ref, bf16[512,2048]{1,0:T(8,128)(2,1)} %get-tuple-element.702.refs_0_.refs_2_, bf16[512,2048]{1,0:T(8,128)(2,1)} %get-tuple-element.703.refs_1_.refs_3_), custom_call_target="tpu_custom_call" | custom-call | flops 20000000000 | bytes 50000000 | tf_op jit(solution)/shard_map/times_transpose/pallas_call | solution.py:333
  399.8 5.1 transposed.1.own_ref
  405.0 2.5 add_convert_fusion.5
  415.5 3.3 all-to-all-start.3
  419.5 8.2 %collective-permute-done.49 = bf16[64,2048]{1,0:T(8,128)(2,1)S(1)} collective-permute-done((bf16[64,2048]{1,0:T(8,128)(2,1)}, bf16[64,2048]{1,0:T(8,128)(2,1)S(1)}, u32[]{:S(2)}, u32[]{:S(2)}) %collective-permute-start.49) | collective-permute-done | bytes 262176 | tf_op jit(solution)/shard_map/ppermute | solution.py:914
  429.9 2.3 multiply_reduce_fusion.1
  440.2 3.3 grad_pairs.1
  443.5 4.2 all-to-all-start.4
  447.7 14.1 %sum_of_outer.4 = bf16[2048,2048]{1,0:T(8,128)(2,1)} custom-call(s32[68]{0:T(128)} %get-tuple-element.919.table_ref._unused, bf16[512,2048]{1,0:T(8,128)(2,1)} %get-tuple-element.661.refs_0_, bf16[512,2048]{1,0:T(8,128)(2,1)} %get-tuple-element.662.refs_1_, bf16[512,2048]{1,0:T(8,128)(2,1)} %get-tuple-element.663.up_ref.refs_2_, ...), custom_call_target="tpu_custom_call" | custom-call | flops 999999995904 | bytes 1000000000 | tf_op jit(solution)/shard_map/sum_of_outer/pallas_call | solution.py:367
  462.2 2.5 all-to-all-done.4.m_ref
  469.0 2.3 collective-permute-start.56
  471.3 15.5 %attend_back.1 = (bf16[8,6,128,128]{3,2,1,0:T(8,128)(2,1)}, f32[8,128]{1,0:T(8,128)S(1)}) custom-call(bf16[8,6,128,128]{3,2,1,0:T(8,128)(2,1)S(1)} %copy-done.17, bf16[8,6,128,128]{3,2,1,0:T(8,128)(2,1)S(1)} %copy-done.17, bf16[8,6,128,128]{3,2,1,0:T(8,128)(2,1)S(1)} %copy-done.17, bf16[8,2,128,128]{3,2,1,0:T(8,128)(2,1)} %all-to-all-done.4.m_ref, ...), custom_call_target="tpu_custom_call" | custom-call | flops 999999995904 | bytes 1000000000 | tf_op jit(solution)/shard_map/attend_back/pallas_call | solution.py:169
  486.8 7.8 %head_weights.1.own_ref = bf16[2048,384]{1,0:T(8,128)(2,1)S(1)} custom-call(s32[68]{0:T(128)S(1)} %copy-done.28, bf16[8,6,128,128]{3,2,1,0:T(8,128)(2,1)} %get-tuple-element.712.g_ref, bf16[2048,1024]{1,0:T(8,128)(2,1)} %transposed.1.own_ref, bf16[2048,1024]{1,0:T(8,128)(2,1)} %collective-permute-done.52.beside_ref), custom_call_target="tpu_custom_call" | custom-call | flops 999999995904 | bytes 1000000000 | tf_op jit(solution)/shard_map/head_weights/pallas_call | solution.py:639
  496.8 2.9 add_convert_fusion.1
  501.7 4.5 all-to-all-start.5
  506.2 4.7 out_grads.1
  510.9 2.5 convert.35
  513.5 8.3 %collective-permute-done.59.other_ref = bf16[1024,384]{1,0:T(8,128)(2,1)} collective-permute-done((bf16[1024,384]{1,0:T(8,128)(2,1)}, bf16[1024,384]{1,0:T(8,128)(2,1)}, u32[]{:S(2)}, u32[]{:S(2)}) %collective-permute-start.59) | collective-permute-done | bytes 786464 | tf_op jit(solution)/shard_map/ppermute | solution.py:902
  529.6 14.7 %sum_of_outer.5 = bf16[2048,2048]{1,0:T(8,128)(2,1)} custom-call(s32[68]{0:T(128)} %get-tuple-element.919.table_ref._unused, bf16[512,2048]{1,0:T(8,128)(2,1)} %get-tuple-element.700.refs_0_, bf16[512,2048]{1,0:T(8,128)(2,1)} %get-tuple-element.701.refs_1_, bf16[512,2048]{1,0:T(8,128)(2,1)} %get-tuple-element.702.refs_0_.refs_2_, ...), custom_call_target="tpu_custom_call" | custom-call | flops 999999995904 | bytes 1000000000 | tf_op jit(solution)/shard_map/sum_of_outer/pallas_call | solution.py:367
  544.3 13.8 %collective-permute-done.61.refs_2_ = bf16[512,768]{1,0:T(8,128)(2,1)} collective-permute-done((bf16[512,768]{1,0:T(8,128)(2,1)}, bf16[512,768]{1,0:T(8,128)(2,1)}, u32[]{:S(2)}, u32[]{:S(2)}) %collective-permute-start.61) | collective-permute-done | bytes 786464 | tf_op jit(solution)/shard_map/ppermute | solution.py:914
  559.7 9.3 %collective-permute-start.67 = (bf16[512,768]{1,0:T(8,128)(2,1)}, bf16[512,768]{1,0:T(8,128)(2,1)}, u32[]{:S(2)}, u32[]{:S(2)}) collective-permute-start(bf16[512,768]{1,0:T(8,128)(2,1)} %collective-permute-done.61.refs_2_), channel_id=1, source_target_pairs={{0,8},{8,16},{16,24},{24,28},{28,20},{20,12},{12,4},{4,0},{1,9},{9... | collective-permute-start | bytes 2359304 | tf_op jit(solution)/shard_map/ppermute | solution.py:914
  573.8 12.0 %pair_normed.1 = (f32[128,2048]{1,0:T(8,128)S(1)}, bf16[128,2048]{1,0:T(8,128)(2,1)S(1)}) custom-call(bf16[8,6,128,128]{3,2,1,0:T(8,128)(2,1)} %all-to-all-done.5.g_ref, bf16[2048,3072]{1,0:T(8,128)(2,1)} %get-tuple-element.716.w_ref), custom_call_target="tpu_custom_call" | custom-call | flops 999999995904 | bytes 1000000000 | tf_op jit(solution)/shard_map/pair_normed/pallas_call | solution.py:698
  585.9 5.1 collective-permute-done.69
  593.6 2.5 add_convert_fusion
  604.3 2.4 collective-permute-done.74
  614.1 4.8 spread.5
  618.9 2.3 spread.6
  625.2 9.9 %collective-permute-done.80.refs_1_ = bf16[512,768]{1,0:T(8,128)(2,1)S(1)} collective-permute-done((bf16[512,768]{1,0:T(8,128)(2,1)}, bf16[512,768]{1,0:T(8,128)(2,1)S(1)}, u32[]{:S(2)}, u32[]{:S(2)}) %collective-permute-start.80) | collective-permute-done | bytes 786464 | tf_op jit(solution)/shard_map/ppermute | solution.py:914
  638.0 2.3 spread.7
  640.4 4.5 split_experts.3
  647.0 3.6 collective-permute-done.84
  658.5 4.5 split_experts.4
  667.0 4.5 split_experts.5
  673.5 2.6 spread.9
  (478 shorter events, 184.6 us)
Async XLA Ops:
  7.2 189.6 %all-gather.4.cloned.1.call-start = ((), (), s32[]{:S(2)}) async-start(), calls=%async_computation.9 | async-start | bytes 10485760 | tf_op jit(solution)/shard_map/all_gather | solution.py:1112
  11.6 14.9 %collective-permute-start = (bf16[128,2048]{1,0:T(8,128)(2,1)S(1)}, bf16[128,2048]{1,0:T(8,128)(2,1)S(1)}, u32[]{:S(2)}, u32[]{:S(2)}) collective-permute-start(bf16[128,2048]{1,0:T(8,128)(2,1)S(1)} %bitcast.67), channel_id=1, source_target_pairs={{0,8},{8,16},{16,24},{24,28},{28,20},{20,12},{12,4},{4,0},{1,9},{9... | collective-permute-start | bytes 1572872 | tf_op jit(solution)/shard_map/ppermute | solution.py:914
  14.6 28.2 %collective-permute-start.4 = (bf16[64,5120]{1,0:T(8,128)(2,1)}, bf16[64,5120]{1,0:T(8,128)(2,1)S(1)}, u32[]{:S(2)}, u32[]{:S(2)}) collective-permute-start(bf16[64,5120]{1,0:T(8,128)(2,1)} %get-tuple-element.446), channel_id=1, source_target_pairs={{0,2},{1,3},{2,0},{3,1},{4,6},{5,7},{6,4},{7,5},{8,10},{9,11},{10,... | collective-permute-start | bytes 1966088 | tf_op jit(solution)/shard_map/ppermute | solution.py:902
  16.6 26.2 %collective-permute-start.5 = (bf16[64,3072]{1,0:T(8,128)(2,1)}, bf16[64,3072]{1,0:T(8,128)(2,1)S(1)}, u32[]{:S(2)}, u32[]{:S(2)}) collective-permute-start(bf16[64,3072]{1,0:T(8,128)(2,1)} %get-tuple-element.447), channel_id=1, source_target_pairs={{0,3},{1,2},{2,1},{3,0},{4,7},{5,6},{6,5},{7,4},{8,11},{9,10},{10,... | collective-permute-start | bytes 1179656 | tf_op jit(solution)/shard_map/ppermute | solution.py:902
  42.8 153.9 %all-gather.6.cloned.1.call-start = ((), (), s32[]{:S(2)}) async-start(), calls=%async_computation.10 | async-start | bytes 10485760 | tf_op jit(solution)/shard_map/all_gather | solution.py:1115
  43.6 22.5 %collective-permute-start.6 = (bf16[256,2048]{1,0:T(8,128)(2,1)S(1)}, bf16[256,2048]{1,0:T(8,128)(2,1)S(1)}, u32[]{:S(2)}, u32[]{:S(2)}) collective-permute-start(bf16[256,2048]{1,0:T(8,128)(2,1)S(1)} %fetched_payload.1.refs_4_.refs_0_), channel_id=1, source_target_pairs={{0,8},{8,16},{16,24},{24,28},{28,20},{20,12},{12,4},{4,0},{1,9},{9... | collective-permute-start | bytes 3145736 | tf_op jit(solution)/shard_map/ppermute | solution.py:914
  45.2 22.2 %collective-permute-start.7 = (bf16[256,2048]{1,0:T(8,128)(2,1)S(1)}, bf16[256,2048]{1,0:T(8,128)(2,1)S(1)}, u32[]{:S(2)}, u32[]{:S(2)}) collective-permute-start(bf16[256,2048]{1,0:T(8,128)(2,1)S(1)} %fetched_payload.1.refs_4_.refs_0_), channel_id=1, source_target_pairs={{0,4},{8,0},{16,8},{24,16},{28,24},{20,28},{12,20},{4,12},{1,5},{9... | collective-permute-start | bytes 3145736 | tf_op jit(solution)/shard_map/ppermute | solution.py:914
  67.5 154.0 %all-gather.8.cloned.1.call-start = ((), (), s32[]{:S(2)}) async-start(), calls=%async_computation.11 | async-start | bytes 10485760 | tf_op jit(solution)/shard_map/all_gather | solution.py:1124
  68.1 25.2 %collective-permute-start.10 = (bf16[256,2048]{1,0:T(8,128)(2,1)S(1)}, bf16[256,2048]{1,0:T(8,128)(2,1)}, u32[]{:S(2)}, u32[]{:S(2)}) collective-permute-start(bf16[256,2048]{1,0:T(8,128)(2,1)S(1)} %collective-permute-done.6.refs_6_.refs_2_), channel_id=1, source_target_pairs={{0,8},{8,16},{16,24},{24,28},{28,20},{20,12},{12,4},{4,0},{1,9},{9... | collective-permute-start | bytes 3145736 | tf_op jit(solution)/shard_map/ppermute | solution.py:914
  69.6 25.0 %collective-permute-start.11 = (bf16[256,2048]{1,0:T(8,128)(2,1)S(1)}, bf16[256,2048]{1,0:T(8,128)(2,1)}, u32[]{:S(2)}, u32[]{:S(2)}) collective-permute-start(bf16[256,2048]{1,0:T(8,128)(2,1)S(1)} %collective-permute-done.7.refs_5_.refs_1_), channel_id=1, source_target_pairs={{0,4},{8,0},{16,8},{24,16},{28,24},{20,28},{12,20},{4,12},{1,5},{9... | collective-permute-start | bytes 3145736 | tf_op jit(solution)/shard_map/ppermute | solution.py:914
  94.6 26.8 %collective-permute-start.15 = (bf16[256,2048]{1,0:T(8,128)(2,1)}, bf16[256,2048]{1,0:T(8,128)(2,1)S(1)}, u32[]{:S(2)}, u32[]{:S(2)}) collective-permute-start(bf16[256,2048]{1,0:T(8,128)(2,1)} %collective-permute-done.10.refs_8_.refs_4_), channel_id=1, source_target_pairs={{0,8},{8,16},{16,24},{24,28},{28,20},{20,12},{12,4},{4,0},{1,9},{9... | collective-permute-start | bytes 3145736 | tf_op jit(solution)/shard_map/ppermute | solution.py:914
  95.7 25.7 %collective-permute-start.16 = (bf16[256,2048]{1,0:T(8,128)(2,1)}, bf16[256,2048]{1,0:T(8,128)(2,1)S(1)}, u32[]{:S(2)}, u32[]{:S(2)}) collective-permute-start(bf16[256,2048]{1,0:T(8,128)(2,1)} %collective-permute-done.11.refs_7_.refs_3_), channel_id=1, source_target_pairs={{0,4},{8,0},{16,8},{24,16},{28,24},{20,28},{12,20},{4,12},{1,5},{9... | collective-permute-start | bytes 3145736 | tf_op jit(solution)/shard_map/ppermute | solution.py:914
  97.3 24.1 %all-to-all-start = ((s32[8,128,8]{1,2,0:T(8,128)}), s32[8,128,8]{1,2,0:T(8,128)}, u32[]{:S(2)}, u32[]{:S(2)}) async-start(s32[8,128,8]{1,2,0:T(8,128)} %broadcast_in_dim.48), calls=%async_computation | async-start | bytes 65536 | tf_op jit(solution)/shard_map/all_to_all | solution.py:1118
  146.8 37.7 %all-to-all-start.1 = ((bf16[8,6,128,128]{3,2,1,0:T(8,128)(2,1)}), bf16[8,6,128,128]{3,2,1,0:T(8,128)(2,1)S(1)}, u32[]{:S(2)}, u32[]{:S(2)}) async-start(bf16[8,6,128,128]{3,2,1,0:T(8,128)(2,1)} %copy-done.18), calls=%async_computation.1 | async-start | bytes 3145728 | tf_op jit(solution)/shard_map/all_to_all | solution.py:1075
  222.9 14.2 %collective-permute-start.20 = (bf16[128,2048]{1,0:T(8,128)(2,1)S(1)}, bf16[128,2048]{1,0:T(8,128)(2,1)}, u32[]{:S(2)}, u32[]{:S(2)}) collective-permute-start(bf16[128,2048]{1,0:T(8,128)(2,1)S(1)} %multiply_convert_fusion.refs_0_), channel_id=1, source_target_pairs={{0,8},{8,16},{16,24},{24,28},{28,20},{20,12},{12,4},{4,0},{1,9},{9... | collective-permute-start | bytes 1572872 | tf_op jit(solution)/shard_map/ppermute | solution.py:914
  224.4 13.9 %collective-permute-start.21 = (bf16[128,2048]{1,0:T(8,128)(2,1)S(1)}, bf16[128,2048]{1,0:T(8,128)(2,1)}, u32[]{:S(2)}, u32[]{:S(2)}) collective-permute-start(bf16[128,2048]{1,0:T(8,128)(2,1)S(1)} %multiply_convert_fusion.refs_0_), channel_id=1, source_target_pairs={{0,4},{8,0},{16,8},{24,16},{28,24},{20,28},{12,20},{4,12},{1,5},{9... | collective-permute-start | bytes 1572872 | tf_op jit(solution)/shard_map/ppermute | solution.py:914
  252.8 23.0 %collective-permute-start.24 = (bf16[128,2048]{1,0:T(8,128)(2,1)}, bf16[128,2048]{1,0:T(8,128)(2,1)S(1)}, u32[]{:S(2)}, u32[]{:S(2)}) collective-permute-start(bf16[128,2048]{1,0:T(8,128)(2,1)} %collective-permute-done.22.refs_0_), channel_id=1, source_target_pairs={{0,8},{8,16},{16,24},{24,28},{28,20},{20,12},{12,4},{4,0},{1,9},{9... | collective-permute-start | bytes 1572872 | tf_op jit(solution)/shard_map/ppermute | solution.py:914
  254.3 21.5 %collective-permute-start.25 = (bf16[128,2048]{1,0:T(8,128)(2,1)}, bf16[128,2048]{1,0:T(8,128)(2,1)S(1)}, u32[]{:S(2)}, u32[]{:S(2)}) collective-permute-start(bf16[128,2048]{1,0:T(8,128)(2,1)} %collective-permute-done.23.refs_3_), channel_id=1, source_target_pairs={{0,4},{8,0},{16,8},{24,16},{28,24},{20,28},{12,20},{4,12},{1,5},{9... | collective-permute-start | bytes 1572872 | tf_op jit(solution)/shard_map/ppermute | solution.py:914
  254.8 21.2 %collective-permute-start.26 = (bf16[128,2048]{1,0:T(8,128)(2,1)S(1)}, bf16[128,2048]{1,0:T(8,128)(2,1)S(1)}, u32[]{:S(2)}, u32[]{:S(2)}) collective-permute-start(bf16[128,2048]{1,0:T(8,128)(2,1)S(1)} %copy-done.93), channel_id=1, source_target_pairs={{0,8},{8,16},{16,24},{24,28},{28,20},{20,12},{12,4},{4,0},{1,9},{9... | collective-permute-start | bytes 1572872 | tf_op jit(solution)/shard_map/ppermute | solution.py:914
  256.3 20.9 %collective-permute-start.27 = (bf16[128,2048]{1,0:T(8,128)(2,1)S(1)}, bf16[128,2048]{1,0:T(8,128)(2,1)S(1)}, u32[]{:S(2)}, u32[]{:S(2)}) collective-permute-start(bf16[128,2048]{1,0:T(8,128)(2,1)S(1)} %copy-done.95), channel_id=1, source_target_pairs={{0,4},{8,0},{16,8},{24,16},{28,24},{20,28},{12,20},{4,12},{1,5},{9... | collective-permute-start | bytes 1572872 | tf_op jit(solution)/shard_map/ppermute | solution.py:914
  284.2 39.7 %collective-permute-start.34 = (bf16[4,2,128,128]{3,2,1,0:T(8,128)(2,1)}, bf16[4,2,128,128]{3,2,1,0:T(8,128)(2,1)}, u32[]{:S(2)}, u32[]{:S(2)}) collective-permute-start(bf16[4,2,128,128]{3,2,1,0:T(8,128)(2,1)} %constant_dynamic-slice_fusion), channel_id=1, source_target_pairs={{0,2},{1,3},{2,0},{3,1},{4,6},{5,7},{6,4},{7,5},{8,10},{9,11},{10,... | collective-permute-start | bytes 786440 | tf_op jit(solution)/shard_map/ppermute | solution.py:902
  302.9 21.0 %collective-permute-start.35 = (bf16[128,2048]{1,0:T(8,128)(2,1)}, bf16[128,2048]{1,0:T(8,128)(2,1)S(1)}, u32[]{:S(2)}, u32[]{:S(2)}) collective-permute-start(bf16[128,2048]{1,0:T(8,128)(2,1)} %collective-permute-done.32.refs_2_), channel_id=1, source_target_pairs={{0,8},{8,16},{16,24},{24,28},{28,20},{20,12},{12,4},{4,0},{1,9},{9... | collective-permute-start | bytes 1572872 | tf_op jit(solution)/shard_map/ppermute | solution.py:914
  303.9 20.0 %collective-permute-start.36 = (bf16[128,2048]{1,0:T(8,128)(2,1)}, bf16[128,2048]{1,0:T(8,128)(2,1)S(1)}, u32[]{:S(2)}, u32[]{:S(2)}) collective-permute-start(bf16[128,2048]{1,0:T(8,128)(2,1)} %collective-permute-done.33.refs_1_), channel_id=1, source_target_pairs={{0,4},{8,0},{16,8},{24,16},{28,24},{20,28},{12,20},{4,12},{1,5},{9... | collective-permute-start | bytes 1572872 | tf_op jit(solution)/shard_map/ppermute | solution.py:914
  323.9 20.1 %collective-permute-start.37 = (bf16[128,2048]{1,0:T(8,128)(2,1)S(1)}, bf16[128,2048]{1,0:T(8,128)(2,1)}, u32[]{:S(2)}, u32[]{:S(2)}) collective-permute-start(bf16[128,2048]{1,0:T(8,128)(2,1)S(1)} %collective-permute-done.35.refs_4_), channel_id=1, source_target_pairs={{0,8},{8,16},{16,24},{24,28},{28,20},{20,12},{12,4},{4,0},{1,9},{9... | collective-permute-start | bytes 1572872 | tf_op jit(solution)/shard_map/ppermute | solution.py:914
  325.0 19.1 %collective-permute-start.38 = (bf16[128,2048]{1,0:T(8,128)(2,1)S(1)}, bf16[128,2048]{1,0:T(8,128)(2,1)}, u32[]{:S(2)}, u32[]{:S(2)}) collective-permute-start(bf16[128,2048]{1,0:T(8,128)(2,1)S(1)} %collective-permute-done.36.refs_3_), channel_id=1, source_target_pairs={{0,4},{8,0},{16,8},{24,16},{28,24},{20,28},{12,20},{4,12},{1,5},{9... | collective-permute-start | bytes 1572872 | tf_op jit(solution)/shard_map/ppermute | solution.py:914
  342.1 16.3 %collective-permute-start.39 = (bf16[64,2048]{1,0:T(8,128)(2,1)}, bf16[64,2048]{1,0:T(8,128)(2,1)}, u32[]{:S(2)}, u32[]{:S(2)}) collective-permute-start(bf16[64,2048]{1,0:T(8,128)(2,1)} %get-tuple-element.909), channel_id=1, source_target_pairs={{0,8},{8,16},{16,24},{24,28},{28,20},{20,12},{12,4},{4,0},{1,9},{9... | collective-permute-start | bytes 786440 | tf_op jit(solution)/shard_map/ppermute | solution.py:914
  343.1 15.3 %collective-permute-start.40 = (bf16[64,2048]{1,0:T(8,128)(2,1)}, bf16[64,2048]{1,0:T(8,128)(2,1)}, u32[]{:S(2)}, u32[]{:S(2)}) collective-permute-start(bf16[64,2048]{1,0:T(8,128)(2,1)} %get-tuple-element.908), channel_id=1, source_target_pairs={{0,4},{8,0},{16,8},{24,16},{28,24},{20,28},{12,20},{4,12},{1,5},{9... | collective-permute-start | bytes 786440 | tf_op jit(solution)/shard_map/ppermute | solution.py:914
  363.7 18.2 %collective-permute-start.43 = (bf16[128,2048]{1,0:T(8,128)(2,1)S(1)}, bf16[128,2048]{1,0:T(8,128)(2,1)S(1)}, u32[]{:S(2)}, u32[]{:S(2)}) collective-permute-start(bf16[128,2048]{1,0:T(8,128)(2,1)S(1)} %pad_maximum_fusion.5), channel_id=1, source_target_pairs={{0,8},{8,16},{16,24},{24,28},{28,20},{20,12},{12,4},{4,0},{1,9},{9... | collective-permute-start | bytes 1572872 | tf_op jit(solution)/shard_map/ppermute | solution.py:914
  364.8 17.1 %collective-permute-start.44 = (bf16[128,2048]{1,0:T(8,128)(2,1)S(1)}, bf16[128,2048]{1,0:T(8,128)(2,1)S(1)}, u32[]{:S(2)}, u32[]{:S(2)}) collective-permute-start(bf16[128,2048]{1,0:T(8,128)(2,1)S(1)} %pad_maximum_fusion.6), channel_id=1, source_target_pairs={{0,4},{8,0},{16,8},{24,16},{28,24},{20,28},{12,20},{4,12},{1,5},{9... | collective-permute-start | bytes 1572872 | tf_op jit(solution)/shard_map/ppermute | solution.py:914
  383.1 15.9 %collective-permute-start.45 = (bf16[128,2048]{1,0:T(8,128)(2,1)S(1)}, bf16[128,2048]{1,0:T(8,128)(2,1)S(1)}, u32[]{:S(2)}, u32[]{:S(2)}) collective-permute-start(bf16[128,2048]{1,0:T(8,128)(2,1)S(1)} %add_convert_fusion.8), channel_id=1, source_target_pairs={{0,8},{8,16},{16,24},{24,28},{28,20},{20,12},{12,4},{4,0},{1,9},{9... | collective-permute-start | bytes 1572872 | tf_op jit(solution)/shard_map/ppermute | solution.py:914
  384.3 15.5 %collective-permute-start.46 = (bf16[128,2048]{1,0:T(8,128)(2,1)S(1)}, bf16[128,2048]{1,0:T(8,128)(2,1)}, u32[]{:S(2)}, u32[]{:S(2)}) collective-permute-start(bf16[128,2048]{1,0:T(8,128)(2,1)S(1)} %add_convert_fusion.7), channel_id=1, source_target_pairs={{0,4},{8,0},{16,8},{24,16},{28,24},{20,28},{12,20},{4,12},{1,5},{9... | collective-permute-start | bytes 1572872 | tf_op jit(solution)/shard_map/ppermute | solution.py:914
  404.9 35.2 %collective-permute-start.52 = (bf16[2048,1024]{1,0:T(8,128)(2,1)}, bf16[2048,1024]{1,0:T(8,128)(2,1)}, u32[]{:S(2)}, u32[]{:S(2)}) collective-permute-start(bf16[2048,1024]{1,0:T(8,128)(2,1)} %transposed.1.own_ref), channel_id=1, source_target_pairs={{0,1},{1,0},{2,3},{3,2},{4,5},{5,4},{6,7},{7,6},{8,9},{9,8},{10,11... | collective-permute-start | bytes 12582920 | tf_op jit(solution)/shard_map/ppermute | solution.py:902
  407.5 21.0 %collective-permute-start.47 = (bf16[128,2048]{1,0:T(8,128)(2,1)}, bf16[128,2048]{1,0:T(8,128)(2,1)}, u32[]{:S(2)}, u32[]{:S(2)}) collective-permute-start(bf16[128,2048]{1,0:T(8,128)(2,1)} %get-tuple-element.905), channel_id=1, source_target_pairs={{0,8},{8,16},{16,24},{24,28},{28,20},{20,12},{12,4},{4,0},{1,9},{9... | collective-permute-start | bytes 1572872 | tf_op jit(solution)/shard_map/ppermute | solution.py:914
  408.6 20.0 %collective-permute-start.48 = (bf16[128,2048]{1,0:T(8,128)(2,1)}, bf16[128,2048]{1,0:T(8,128)(2,1)}, u32[]{:S(2)}, u32[]{:S(2)}) collective-permute-start(bf16[128,2048]{1,0:T(8,128)(2,1)} %get-tuple-element.904), channel_id=1, source_target_pairs={{0,4},{8,0},{16,8},{24,16},{28,24},{20,28},{12,20},{4,12},{1,5},{9... | collective-permute-start | bytes 1572872 | tf_op jit(solution)/shard_map/ppermute | solution.py:914
  410.5 17.2 %collective-permute-start.49 = (bf16[64,2048]{1,0:T(8,128)(2,1)}, bf16[64,2048]{1,0:T(8,128)(2,1)S(1)}, u32[]{:S(2)}, u32[]{:S(2)}) collective-permute-start(bf16[64,2048]{1,0:T(8,128)(2,1)} %get-tuple-element.901), channel_id=1, source_target_pairs={{0,8},{8,16},{16,24},{24,28},{28,20},{20,12},{12,4},{4,0},{1,9},{9... | collective-permute-start | bytes 786440 | tf_op jit(solution)/shard_map/ppermute | solution.py:914
  411.5 17.1 %collective-permute-start.50 = (bf16[64,2048]{1,0:T(8,128)(2,1)}, bf16[64,2048]{1,0:T(8,128)(2,1)}, u32[]{:S(2)}, u32[]{:S(2)}) collective-permute-start(bf16[64,2048]{1,0:T(8,128)(2,1)} %get-tuple-element.900), channel_id=1, source_target_pairs={{0,4},{8,0},{16,8},{24,16},{28,24},{20,28},{12,20},{4,12},{1,5},{9... | collective-permute-start | bytes 786440 | tf_op jit(solution)/shard_map/ppermute | solution.py:914
  418.9 221.5 %reduce-scatter.4.cloned.1.call-start = ((), (), s32[]{:S(2)}) async-start(), calls=%async_computation.12 | async-start | bytes 10485760 | tf_op jit(solution)/shard_map/reduce_scatter | solution.py:1217
  437.3 24.9 %collective-permute-start.53 = (bf16[128,2048]{1,0:T(8,128)(2,1)}, bf16[128,2048]{1,0:T(8,128)(2,1)}, u32[]{:S(2)}, u32[]{:S(2)}) collective-permute-start(bf16[128,2048]{1,0:T(8,128)(2,1)} %pad_maximum_fusion.8), channel_id=1, source_target_pairs={{0,8},{8,16},{16,24},{24,28},{28,20},{20,12},{12,4},{4,0},{1,9},{9... | collective-permute-start | bytes 1572872 | tf_op jit(solution)/shard_map/ppermute | solution.py:914
  438.7 23.6 %collective-permute-start.54 = (bf16[128,2048]{1,0:T(8,128)(2,1)}, bf16[128,2048]{1,0:T(8,128)(2,1)}, u32[]{:S(2)}, u32[]{:S(2)}) collective-permute-start(bf16[128,2048]{1,0:T(8,128)(2,1)} %pad_maximum_fusion.9), channel_id=1, source_target_pairs={{0,4},{8,0},{16,8},{24,16},{28,24},{20,28},{12,20},{4,12},{1,5},{9... | collective-permute-start | bytes 1572872 | tf_op jit(solution)/shard_map/ppermute | solution.py:914
  443.5 21.2 %all-to-all-start.4 = ((bf16[8,2,128,128]{3,2,1,0:T(8,128)(2,1)}), bf16[8,2,128,128]{3,2,1,0:T(8,128)(2,1)}, u32[]{:S(2)}, u32[]{:S(2)}) async-start(bf16[8,2,128,128]{3,2,1,0:T(8,128)(2,1)} %grad_pairs.1), calls=%async_computation.4 | async-start | bytes 1048576 | tf_op jit(solution)/shard_map/all_to_all | solution.py:1075
  447.7 210.8 %reduce-scatter.6.cloned.1.call-start = ((), (), s32[]{:S(2)}) async-start(), calls=%async_computation.13 | async-start | bytes 10485760 | tf_op jit(solution)/shard_map/reduce_scatter | solution.py:1217
  461.9 32.7 %collective-permute-start.57 = (bf16[128,2048]{1,0:T(8,128)(2,1)}, bf16[128,2048]{1,0:T(8,128)(2,1)}, u32[]{:S(2)}, u32[]{:S(2)}) collective-permute-start(bf16[128,2048]{1,0:T(8,128)(2,1)} %get-tuple-element.683.own_ref.refs_0_), channel_id=1, source_target_pairs={{0,2},{1,3},{2,0},{3,1},{4,6},{5,7},{6,4},{7,5},{8,10},{9,11},{10,... | collective-permute-start | bytes 1572872 | tf_op jit(solution)/shard_map/ppermute | solution.py:902
  466.9 19.9 %collective-permute-start.55 = (bf16[128,2048]{1,0:T(8,128)(2,1)}, bf16[128,2048]{1,0:T(8,128)(2,1)}, u32[]{:S(2)}, u32[]{:S(2)}) collective-permute-start(bf16[128,2048]{1,0:T(8,128)(2,1)} %add_convert_fusion.4), channel_id=1, source_target_pairs={{0,8},{8,16},{16,24},{24,28},{28,20},{20,12},{12,4},{4,0},{1,9},{9... | collective-permute-start | bytes 1572872 | tf_op jit(solution)/shard_map/ppermute | solution.py:914
  469.0 17.8 %collective-permute-start.56 = (bf16[128,2048]{1,0:T(8,128)(2,1)}, bf16[128,2048]{1,0:T(8,128)(2,1)}, u32[]{:S(2)}, u32[]{:S(2)}) collective-permute-start(bf16[128,2048]{1,0:T(8,128)(2,1)} %add_convert_fusion.3), channel_id=1, source_target_pairs={{0,4},{8,0},{16,8},{24,16},{28,24},{20,28},{12,20},{4,12},{1,5},{9... | collective-permute-start | bytes 1572872 | tf_op jit(solution)/shard_map/ppermute | solution.py:914
  496.2 25.6 %collective-permute-start.59 = (bf16[1024,384]{1,0:T(8,128)(2,1)}, bf16[1024,384]{1,0:T(8,128)(2,1)}, u32[]{:S(2)}, u32[]{:S(2)}) collective-permute-start(bf16[1024,384]{1,0:T(8,128)(2,1)} %slice.261), channel_id=1, source_target_pairs={{0,2},{1,3},{2,0},{3,1},{4,6},{5,7},{6,4},{7,5},{8,10},{9,11},{10,... | collective-permute-start | bytes 2359304 | tf_op jit(solution)/shard_map/ppermute | solution.py:902
  499.6 29.5 %collective-permute-start.65 = (bf16[128,2048]{1,0:T(8,128)(2,1)}, bf16[128,2048]{1,0:T(8,128)(2,1)}, u32[]{:S(2)}, u32[]{:S(2)}) collective-permute-start(bf16[128,2048]{1,0:T(8,128)(2,1)} %get-tuple-element.897), channel_id=1, source_target_pairs={{0,8},{8,16},{16,24},{24,28},{28,20},{20,12},{12,4},{4,0},{1,9},{9... | collective-permute-start | bytes 1572872 | tf_op jit(solution)/shard_map/ppermute | solution.py:914
  500.0 44.3 %collective-permute-start.66 = (bf16[128,2048]{1,0:T(8,128)(2,1)}, bf16[128,2048]{1,0:T(8,128)(2,1)}, u32[]{:S(2)}, u32[]{:S(2)}) collective-permute-start(bf16[128,2048]{1,0:T(8,128)(2,1)} %get-tuple-element.896), channel_id=1, source_target_pairs={{0,4},{8,0},{16,8},{24,16},{28,24},{20,28},{12,20},{4,12},{1,5},{9... | collective-permute-start | bytes 1572872 | tf_op jit(solution)/shard_map/ppermute | solution.py:914
  501.7 58.1 %all-to-all-start.5 = ((bf16[8,6,128,128]{3,2,1,0:T(8,128)(2,1)}), bf16[8,6,128,128]{3,2,1,0:T(8,128)(2,1)}, u32[]{:S(2)}, u32[]{:S(2)}) async-start(bf16[8,6,128,128]{3,2,1,0:T(8,128)(2,1)} %get-tuple-element.712.g_ref), calls=%async_computation.5 | async-start | bytes 3145728 | tf_op jit(solution)/shard_map/all_to_all | solution.py:1078
  506.1 160.9 %reduce-scatter.8.cloned.1.call-start = ((), (), s32[]{:S(2)}) async-start(), calls=%async_computation.14 | async-start | bytes 10485760 | tf_op jit(solution)/shard_map/reduce_scatter | solution.py:1217
  524.0 20.2 %collective-permute-start.63 = (bf16[32,2048]{1,0:T(8,128)(2,1)}, bf16[32,2048]{1,0:T(8,128)(2,1)}, u32[]{:S(2)}, u32[]{:S(2)}) collective-permute-start(bf16[32,2048]{1,0:T(8,128)(2,1)} %get-tuple-element.895), channel_id=1, source_target_pairs={{0,8},{8,16},{16,24},{24,28},{28,20},{20,12},{12,4},{4,0},{1,9},{9... | collective-permute-start | bytes 393224 | tf_op jit(solution)/shard_map/ppermute | solution.py:914
  525.5 18.7 %collective-permute-start.64 = (bf16[32,2048]{1,0:T(8,128)(2,1)}, bf16[32,2048]{1,0:T(8,128)(2,1)}, u32[]{:S(2)}, u32[]{:S(2)}) collective-permute-start(bf16[32,2048]{1,0:T(8,128)(2,1)} %get-tuple-element.894), channel_id=1, source_target_pairs={{0,4},{8,0},{16,8},{24,16},{28,24},{20,28},{12,20},{4,12},{1,5},{9... | collective-permute-start | bytes 393224 | tf_op jit(solution)/shard_map/ppermute | solution.py:914
  527.6 30.6 %collective-permute-start.61 = (bf16[512,768]{1,0:T(8,128)(2,1)}, bf16[512,768]{1,0:T(8,128)(2,1)}, u32[]{:S(2)}, u32[]{:S(2)}) collective-permute-start(bf16[512,768]{1,0:T(8,128)(2,1)} %side_by_side.1.refs_0_), channel_id=1, source_target_pairs={{0,8},{8,16},{16,24},{24,28},{28,20},{20,12},{12,4},{4,0},{1,9},{9... | collective-permute-start | bytes 2359304 | tf_op jit(solution)/shard_map/ppermute | solution.py:914
  529.1 30.6 %collective-permute-start.62 = (bf16[512,768]{1,0:T(8,128)(2,1)}, bf16[512,768]{1,0:T(8,128)(2,1)}, u32[]{:S(2)}, u32[]{:S(2)}) collective-permute-start(bf16[512,768]{1,0:T(8,128)(2,1)} %side_by_side.1.refs_0_), channel_id=1, source_target_pairs={{0,4},{8,0},{16,8},{24,16},{28,24},{20,28},{12,20},{4,12},{1,5},{9... | collective-permute-start | bytes 2359304 | tf_op jit(solution)/shard_map/ppermute | solution.py:914
  559.7 33.5 %collective-permute-start.67 = (bf16[512,768]{1,0:T(8,128)(2,1)}, bf16[512,768]{1,0:T(8,128)(2,1)}, u32[]{:S(2)}, u32[]{:S(2)}) collective-permute-start(bf16[512,768]{1,0:T(8,128)(2,1)} %collective-permute-done.61.refs_2_), channel_id=1, source_target_pairs={{0,8},{8,16},{16,24},{24,28},{28,20},{20,12},{12,4},{4,0},{1,9},{9... | collective-permute-start | bytes 2359304 | tf_op jit(solution)/shard_map/ppermute | solution.py:914
  569.0 24.2 %collective-permute-start.68 = (bf16[512,768]{1,0:T(8,128)(2,1)}, bf16[512,768]{1,0:T(8,128)(2,1)}, u32[]{:S(2)}, u32[]{:S(2)}) collective-permute-start(bf16[512,768]{1,0:T(8,128)(2,1)} %collective-permute-done.62.refs_1_), channel_id=1, source_target_pairs={{0,4},{8,0},{16,8},{24,16},{28,24},{20,28},{12,20},{4,12},{1,5},{9... | collective-permute-start | bytes 2359304 | tf_op jit(solution)/shard_map/ppermute | solution.py:914
  571.0 20.1 %collective-permute-start.69 = (bf16[64,2048]{1,0:T(8,128)(2,1)}, bf16[64,2048]{1,0:T(8,128)(2,1)}, u32[]{:S(2)}, u32[]{:S(2)}) collective-permute-start(bf16[64,2048]{1,0:T(8,128)(2,1)} %pad_maximum_fusion.10), channel_id=1, source_target_pairs={{0,8},{8,16},{16,24},{24,28},{28,20},{20,12},{12,4},{4,0},{1,9},{9... | collective-permute-start | bytes 786440 | tf_op jit(solution)/shard_map/ppermute | solution.py:914
  573.7 19.5 %collective-permute-start.70 = (bf16[64,2048]{1,0:T(8,128)(2,1)}, bf16[64,2048]{1,0:T(8,128)(2,1)}, u32[]{:S(2)}, u32[]{:S(2)}) collective-permute-start(bf16[64,2048]{1,0:T(8,128)(2,1)} %pad_maximum_fusion.11), channel_id=1, source_target_pairs={{0,4},{8,0},{16,8},{24,16},{28,24},{20,28},{12,20},{4,12},{1,5},{9... | collective-permute-start | bytes 786440 | tf_op jit(solution)/shard_map/ppermute | solution.py:914
  585.8 14.1 %collective-permute-start.72 = (bf16[128,2048]{1,0:T(8,128)(2,1)S(1)}, bf16[128,2048]{1,0:T(8,128)(2,1)S(1)}, u32[]{:S(2)}, u32[]{:S(2)}) collective-permute-start(bf16[128,2048]{1,0:T(8,128)(2,1)S(1)} %get-tuple-element.733), channel_id=1, source_target_pairs={{0,1},{1,0},{2,3},{3,2},{4,5},{5,4},{6,7},{7,6},{8,9},{9,8},{10,11... | collective-permute-start | bytes 1572872 | tf_op jit(solution)/shard_map/ppermute | solution.py:902
  611.0 24.1 %collective-permute-start.80 = (bf16[512,768]{1,0:T(8,128)(2,1)}, bf16[512,768]{1,0:T(8,128)(2,1)S(1)}, u32[]{:S(2)}, u32[]{:S(2)}) collective-permute-start(bf16[512,768]{1,0:T(8,128)(2,1)} %collective-permute-done.67.refs_0_), channel_id=1, source_target_pairs={{0,8},{8,16},{16,24},{24,28},{28,20},{20,12},{12,4},{4,0},{1,9},{9... | collective-permute-start | bytes 2359304 | tf_op jit(solution)/shard_map/ppermute | solution.py:914
  612.0 23.8 %collective-permute-start.81 = (bf16[512,768]{1,0:T(8,128)(2,1)}, bf16[512,768]{1,0:T(8,128)(2,1)S(1)}, u32[]{:S(2)}, u32[]{:S(2)}) collective-permute-start(bf16[512,768]{1,0:T(8,128)(2,1)} %collective-permute-done.68.refs_3_), channel_id=1, source_target_pairs={{0,4},{8,0},{16,8},{24,16},{28,24},{20,28},{12,20},{4,12},{1,5},{9... | collective-permute-start | bytes 2359304 | tf_op jit(solution)/shard_map/ppermute | solution.py:914
  623.1 21.8 %collective-permute-start.82 = (bf16[80,2048]{1,0:T(8,128)(2,1)S(1)}, bf16[80,2048]{1,0:T(8,128)(2,1)S(1)}, u32[]{:S(2)}, u32[]{:S(2)}) collective-permute-start(bf16[80,2048]{1,0:T(8,128)(2,1)S(1)} %pack_gains.1.refs_0_), channel_id=1, source_target_pairs={{0,8},{8,16},{16,24},{24,28},{28,20},{20,12},{12,4},{4,0},{1,9},{9... | collective-permute-start | bytes 983048 | tf_op jit(solution)/shard_map/ppermute | solution.py:914
  624.3 20.6 %collective-permute-start.83 = (bf16[80,2048]{1,0:T(8,128)(2,1)S(1)}, bf16[80,2048]{1,0:T(8,128)(2,1)S(1)}, u32[]{:S(2)}, u32[]{:S(2)}) collective-permute-start(bf16[80,2048]{1,0:T(8,128)(2,1)S(1)} %pack_gains.1.refs_0_), channel_id=1, source_target_pairs={{0,4},{8,0},{16,8},{24,16},{28,24},{20,28},{12,20},{4,12},{1,5},{9... | collective-permute-start | bytes 983048 | tf_op jit(solution)/shard_map/ppermute | solution.py:914
  635.9 14.6 %collective-permute-start.84 = (bf16[256,768]{1,0:T(8,128)(2,1)S(1)}, bf16[256,768]{1,0:T(8,128)(2,1)S(1)}, u32[]{:S(2)}, u32[]{:S(2)}) collective-permute-start(bf16[256,768]{1,0:T(8,128)(2,1)S(1)} %slice.278), channel_id=1, source_target_pairs={{0,8},{8,16},{16,24},{24,28},{28,20},{20,12},{12,4},{4,0},{1,9},{9... | collective-permute-start | bytes 1179656 | tf_op jit(solution)/shard_map/ppermute | solution.py:914
  636.5 14.9 %collective-permute-start.85 = (bf16[256,768]{1,0:T(8,128)(2,1)S(1)}, bf16[256,768]{1,0:T(8,128)(2,1)}, u32[]{:S(2)}, u32[]{:S(2)}) collective-permute-start(bf16[256,768]{1,0:T(8,128)(2,1)S(1)} %slice.279), channel_id=1, source_target_pairs={{0,4},{8,0},{16,8},{24,16},{28,24},{20,28},{12,20},{4,12},{1,5},{9... | collective-permute-start | bytes 1179656 | tf_op jit(solution)/shard_map/ppermute | solution.py:914
  (137 other events, 1313.8 us)
Sparse Core Ops, SparseCore 0:
  43.0 57.5 all-gather.3
  102.7 58.2 all-gather.5
  163.2 58.2 all-gather.7
  422.0 89.5 reduce-scatter.3
  514.2 73.6 reduce-scatter.5
  590.4 71.8 reduce-scatter.7

commit v6 on v5

--- a/solution.py
+++ b/solution.py
@@ -768,24 +768,28 @@
     return small_call(place_kernel, "place_rows", out, table, *pieces, slots=slots)
 
 
-def pack_kernel(table_ref, below_ref, early_ref, late_ref, o_ref, *, slot, experts):
+def pack_kernel(table_ref, below_ref, early_ref, late_ref, o_ref, rows_ref, *, slot, experts):
     slab = o_ref.shape[1] // 4
     first = below_ref.shape[0]
     here = pl.ds(pl.multiple_of(table_ref[slot] * slab, slab), slab)
-    o_ref[...] = jnp.zeros_like(o_ref)
+    rows_ref[...] = jnp.zeros_like(rows_ref)
+    for index in range(experts):
+        at = index // 4
+        rows_ref[at : at + 1, index % 4 * slab : (index % 4 + 1) * slab] = early_ref[index : index + 1, here]
+    at = experts // 4
+    rows_ref[at : at + 1, :] = early_ref[experts : experts + 1, :]
+    rows_ref[at + 1 : at + 3, :] = late_ref[...]
     o_ref[:first, :] = below_ref[...].astype(BF)
-    for index in range(experts):
-        at = first + index // 4
-        o_ref[at : at + 1, index % 4 * slab : (index % 4 + 1) * slab] = early_ref[index : index + 1, here].astype(BF)
-    at = first + experts // 4
-    o_ref[at : at + 1, :] = early_ref[experts : experts + 1, :].astype(BF)
-    o_ref[at + 1 : at + 3, :] = late_ref[...].astype(BF)
+    o_ref[first:, :] = rows_ref[...].astype(BF)
 
 
 def pack_gains(table, below, early, late, slot, experts):
-    height = below.shape[0] + -(-(experts // 4 + 3) // 16) * 16
-    out = jax.ShapeDtypeStruct((height, early.shape[1]), BF)
-    return small_call(pack_kernel, "pack_gains", out, table, below, early, late, slot=slot, experts=experts)
+    height = -(-(experts // 4 + 3) // 16) * 16
+    out = jax.ShapeDtypeStruct((below.shape[0] + height, early.shape[1]), BF)
+    scratch = [pltpu.VMEM((height, early.shape[1]), F32)]
+    return small_call(
+        pack_kernel, "pack_gains", out, table, below, early, late, scratch=scratch, slot=slot, experts=experts
+    )
 
 
 def unpack_kernel(table_ref, *refs, back, experts):

time: 693 us -> 693 us (level)
  no operation moved by 1% of the time
where the time goes in v6:
time: 693 us; the launch traced here: 684 us
  Pallas kernels  276 us (40%)
  waiting for transfers between devices  187 us (27%)
  starting transfers between devices  112 us (16%)
  other arithmetic  42.4 us (6%)
  local copies, waits for them, and re-layouts  31.2 us (5%)
  blocking collectives  17.8 us (3%)
  between operations  16.5 us (2%)
    ppermute x72, waiting for transfers between devices, ring_send(): lax.ppermute(v, 'ctx', [(order[i], order[(i + direction) % size]) for i i...  121 us
    ppermute x72, starting transfers between devices, ring_send(): lax.ppermute(v, 'ctx', [(order[i], order[(i + direction) % size]) for i i...  83.6 us
    pallas_call x3, Pallas kernels, sum_of_outer(): pl.pallas_call(sum_kernel, grid_spec=pltpu.PrefetchScalarGridSpec(num_sca...  43 us
    pallas_call x2, Pallas kernels, expert_units(): pl.pallas_call(functools.partial(expert_kernel, per=per, place=place, at=...  37.9 us
    pallas_call x2, Pallas kernels, expert_rows(): pl.pallas_call(expert_rows_kernel, grid=(width // wide,), in_specs=[whole...  27.6 us
    all_to_all x2, waiting for transfers between devices, spread_pairs(): return lax.all_to_all(v, 'ctx', split_axis=0, concat_axis=0, tiled=True)  27 us
    pallas_call x11, Pallas kernels, small_call(): pl.pallas_call(functools.partial(kernel, **kwargs), in_specs=[pl.BlockSpe...  25.8 us
    ppermute x20, waiting for transfers between devices, swap(): return lax.ppermute(v, 'fsdp', [(i, i ^ mask) for i in range(size)])  24.4 us
  transfers between devices with their start and end apart: 103, of which 49 were waited for; matrix products, arithmetic and copies ran while one was open for 8% of the time, Pallas kernels for 39%

profile of v6, /device:TPU:0, one launch (start us, length us, event | category | flops | bytes accessed | tf_op | source)
XLA Modules:
  0.0 683.9 jit_solution(1828818480551416617)
XLA Ops:
  8.4 3.1 take_parts.2
  11.6 3.1 collective-permute-start
  16.8 6.4 take_parts.3
  30.8 6.6 merge_experts.3
  37.4 3.9 collective-permute-done.2.refs_0_
  45.6 6.7 merge_experts.4
  52.3 13.8 %collective-permute-done.6.refs_6_.refs_2_ = bf16[256,2048]{1,0:T(8,128)(2,1)S(1)} collective-permute-done((bf16[256,2048]{1,0:T(8,128)(2,1)S(1)}, bf16[256,2048]{1,0:T(8,128)(2,1)S(1)}, u32[]{:S(2)}, u32[]{:S(2)}) %collective-permute-start.6) | collective-permute-done | bytes 1048608 | tf_op jit(solution)/shard_map/ppermute | solution.py:918
  70.1 4.1 collective-permute-done.9.refs_1_
  75.0 6.6 merge_experts.5
  81.6 11.7 %collective-permute-done.10.refs_8_.refs_4_ = bf16[256,2048]{1,0:T(8,128)(2,1)} collective-permute-done((bf16[256,2048]{1,0:T(8,128)(2,1)S(1)}, bf16[256,2048]{1,0:T(8,128)(2,1)}, u32[]{:S(2)}, u32[]{:S(2)}) %collective-permute-start.10) | collective-permute-done | bytes 1048608 | tf_op jit(solution)/shard_map/ppermute | solution.py:918
  97.3 4.0 all-to-all-start
  103.9 4.6 collective-permute-done.13.refs_2_
  110.6 10.8 %all-to-all-done = s32[8,128,8]{1,2,0:T(8,128)} async-done(((s32[8,128,8]{1,2,0:T(8,128)}), s32[8,128,8]{1,2,0:T(8,128)}, u32[]{:S(2)}, u32[]{:S(2)}) %all-to-all-start) | async-done | bytes 32800 | tf_op jit(solution)/shard_map/all_to_all | solution.py:1122
  123.7 9.0 %collective-permute-done.17 = bf16[128,2048]{1,0:T(8,128)(2,1)S(1)} collective-permute-done((bf16[128,2048]{1,0:T(8,128)(2,1)S(1)}, bf16[128,2048]{1,0:T(8,128)(2,1)S(1)}, u32[]{:S(2)}, u32[]{:S(2)}) %collective-permute-start.17) | collective-permute-done | bytes 524320 | tf_op jit(solution)/shard_map/ppermute | solution.py:918
  135.2 10.4 %own_pairs.1 = (bf16[8,6,128,128]{3,2,1,0:T(8,128)(2,1)S(1)}, bf16[2048,3072]{1,0:T(8,128)(2,1)}) custom-call(s32[68]{0:T(128)S(1)} %copy-done.26, bf16[128,2048]{1,0:T(8,128)(2,1)} %fusion.2.refs_0_, bf16[128,2048]{1,0:T(8,128)(2,1)S(1)} %copy-done.24, bf16[512,3072]{1,0:T(8,128)(2,1)S(1)} %copy-done.11, bf16[512,3072]{1,0:T(8,128)(2,1)} %collective-permute-done.8.refs_3_, ...), custom_call_target="tpu_custom_call" | custom-call | flops 1 | bytes 1 | tf_op jit(solution)/shard_map/own_pairs/pallas_call | solution.py:495
  146.8 3.8 all-to-all-start.1
  153.7 4.1 far_rows.1.far_ref
  160.1 24.4 %all-to-all-done.1.q_ref.k_ref.v_ref = bf16[8,6,128,128]{3,2,1,0:T(8,128)(2,1)S(1)} async-done(((bf16[8,6,128,128]{3,2,1,0:T(8,128)(2,1)}), bf16[8,6,128,128]{3,2,1,0:T(8,128)(2,1)S(1)}, u32[]{:S(2)}, u32[]{:S(2)}) %all-to-all-start.1) | async-done | bytes 1572896 | tf_op jit(solution)/shard_map/all_to_all | solution.py:1079
  188.1 7.8 %attend.1 = bf16[8,2,128,128]{3,2,1,0:T(8,128)(2,1)S(1)} custom-call(bf16[8,6,128,128]{3,2,1,0:T(8,128)(2,1)S(1)} %copy-done.16, bf16[8,6,128,128]{3,2,1,0:T(8,128)(2,1)S(1)} %copy-done.16, bf16[8,6,128,128]{3,2,1,0:T(8,128)(2,1)S(1)} %copy-done.16, f32[1,128]{1,0:T(1,128)S(1)} %bitcast.61, f32[1,128]{1,0:T(1,128)S(1)} %bitcast.63, ...), custom_call_target="tpu_custom_call" | custom-call | flops 20000000000 | bytes 50000000 | tf_op jit(solution)/shard_map/attend/pallas_call | solution.py:152
  196.7 17.8 %all_to_all.30.m_ref = bf16[8,2,128,128]{3,2,1,0:T(8,128)(2,1)S(1)} all-to-all(bf16[8,2,128,128]{3,2,1,0:T(8,128)(2,1)} %copy-done.25), channel_id=1, replica_groups=mesh['ctx'=8,'fsdp'=4] {'ctx'}, dimensions={0} | all-to-all | bytes 1048576 | tf_op jit(solution)/shard_map/all_to_all | solution.py:1082
  214.6 3.1 mixed_out.1
  226.7 10.4 %collective-permute-done.20.refs_2_ = bf16[128,2048]{1,0:T(8,128)(2,1)} collective-permute-done((bf16[128,2048]{1,0:T(8,128)(2,1)S(1)}, bf16[128,2048]{1,0:T(8,128)(2,1)}, u32[]{:S(2)}, u32[]{:S(2)}) %collective-permute-start.20) | collective-permute-done | bytes 524320 | tf_op jit(solution)/shard_map/ppermute | solution.py:918
  240.4 9.3 %stacked_matmul.2 = (f32[512,2048]{1,0:T(8,128)}, bf16[512,2048]{1,0:T(8,128)(2,1)}) custom-call(bf16[2048,2048]{1,0:T(8,128)(2,1)} %all-gather.4.cloned.1.call-done.w_ref.b_ref, bf16[128,2048]{1,0:T(8,128)(2,1)} %bitcast.66, bf16[128,2048]{1,0:T(8,128)(2,1)} %copy-done.97, bf16[128,2048]{1,0:T(8,128)(2,1)} %copy-done.96, bf16[128,2048]{1,0:T(8,128)(2,1)} %copy-done.94), custom_call_target="tpu_custom_call" | custom-call | flops 999999995904 | bytes 1000000000 | tf_op jit(solution)/shard_map/stacked_matmul/pallas_call | solution.py:209
  256.9 18.9 %expert_units.2 = (bf16[512,2048]{1,0:T(8,128)(2,1)}, bf16[512,2048]{1,0:T(8,128)(2,1)}, bf16[512,2048]{1,0:T(8,128)(2,1)}, f32[2,512,1]{2,1,0:T(8,128)}, bf16[512,2048]{1,0:T(8,128)(2,1)}) custom-call(s32[68]{0:T(128)} %get-tuple-element.919.table_ref._unused, bf16[2048,16]{1,0:T(8,128)(2,1)} %copy-done.3, s32[8,128,8]{2,1,0:T(8,128)} %copy.57.routes_ref, ...), custom_call_target="tpu_custom_call" | custom-call | flops 20000000000 | bytes 50000000 | tf_op jit(solution)/shard_map/expert_units/pallas_call | solution.py:273
  292.7 9.3 %stacked_matmul.3 = (f32[512,2048]{1,0:T(8,128)}, bf16[512,2048]{1,0:T(8,128)(2,1)}) custom-call(bf16[2048,2048]{1,0:T(8,128)(2,1)} %all-gather.4.cloned.1.call-done.w_ref.b_ref, bf16[128,2048]{1,0:T(8,128)(2,1)} %copy-done.92, bf16[128,2048]{1,0:T(8,128)(2,1)} %copy-done.72, bf16[128,2048]{1,0:T(8,128)(2,1)} %copy-done.71, ...), custom_call_target="tpu_custom_call" | custom-call | flops 999999995904 | bytes 1000000000 | tf_op jit(solution)/shard_map/stacked_matmul/pallas_call | solution.py:209
  304.9 19.0 %expert_units.3 = (bf16[512,2048]{1,0:T(8,128)(2,1)}, bf16[512,2048]{1,0:T(8,128)(2,1)}, bf16[512,2048]{1,0:T(8,128)(2,1)}, f32[2,512,1]{2,1,0:T(8,128)}, bf16[512,2048]{1,0:T(8,128)(2,1)}) custom-call(s32[68]{0:T(128)} %get-tuple-element.919.table_ref._unused, bf16[2048,16]{1,0:T(8,128)(2,1)} %copy-done.3, s32[8,128,8]{2,1,0:T(8,128)} %copy.57.routes_ref, ...), custom_call_target="tpu_custom_call" | custom-call | flops 20000000000 | bytes 50000000 | tf_op jit(solution)/shard_map/expert_units/pallas_call | solution.py:273
  326.0 13.8 %expert_rows.2 = bf16[512,2048]{1,0:T(8,128)(2,1)} custom-call(bf16[512,2048]{1,0:T(8,128)(2,1)} %get-tuple-element.604.gate_ref.refs_3_, bf16[512,2048]{1,0:T(8,128)(2,1)} %get-tuple-element.664.up_ref.refs_3_, bf16[2048,2048]{1,0:T(8,128)(2,1)} %all-gather.6.cloned.1.call-done.gate_w_ref, bf16[2048,2048]{1,0:T(8,128)(2,1)} %all-gather.8.cloned.1.call-done.up_w_ref), custom_call_target="tpu_custom_call" | custom-call | flops 20000000000 | bytes 50000000 | tf_op jit(solution)/shard_map/expert_rows/pallas_call | solution.py:312
  339.8 2.2 fusion.23
  344.1 14.2 %sum_of_outer.3 = bf16[2048,2048]{1,0:T(8,128)(2,1)} custom-call(s32[68]{0:T(128)} %get-tuple-element.919.table_ref._unused, bf16[512,2048]{1,0:T(8,128)(2,1)} %get-tuple-element.661.refs_0_, bf16[512,2048]{1,0:T(8,128)(2,1)} %get-tuple-element.662.refs_1_, bf16[512,2048]{1,0:T(8,128)(2,1)} %get-tuple-element.612.refs_2_.gate_ref, ...), custom_call_target="tpu_custom_call" | custom-call | flops 999999995904 | bytes 1000000000 | tf_op jit(solution)/shard_map/sum_of_outer/pallas_call | solution.py:367
  368.0 13.8 %expert_rows.3 = bf16[512,2048]{1,0:T(8,128)(2,1)} custom-call(bf16[512,2048]{1,0:T(8,128)(2,1)} %get-tuple-element.612.refs_2_.gate_ref, bf16[512,2048]{1,0:T(8,128)(2,1)} %get-tuple-element.663.up_ref.refs_2_, bf16[2048,2048]{1,0:T(8,128)(2,1)} %all-gather.6.cloned.1.call-done.gate_w_ref, bf16[2048,2048]{1,0:T(8,128)(2,1)} %all-gather.8.cloned.1.call-done.up_w_ref), custom_call_target="tpu_custom_call" | custom-call | flops 20000000000 | bytes 50000000 | tf_op jit(solution)/shard_map/expert_rows/pallas_call | solution.py:312
  385.8 13.2 %times_transpose.1 = (bf16[512,2048]{1,0:T(8,128)(2,1)}, bf16[512,2048]{1,0:T(8,128)(2,1)}) custom-call(bf16[2048,2048]{1,0:T(8,128)(2,1)} %all-gather.4.cloned.1.call-done.w_ref.b_ref, bf16[512,2048]{1,0:T(8,128)(2,1)} %get-tuple-element.702.refs_0_.refs_2_, bf16[512,2048]{1,0:T(8,128)(2,1)} %get-tuple-element.703.refs_1_.refs_3_), custom_call_target="tpu_custom_call" | custom-call | flops 20000000000 | bytes 50000000 | tf_op jit(solution)/shard_map/times_transpose/pallas_call | solution.py:333
  399.8 5.1 transposed.1.own_ref
  405.0 2.5 add_convert_fusion.5
  415.5 3.3 all-to-all-start.3
  419.5 8.2 %collective-permute-done.49 = bf16[64,2048]{1,0:T(8,128)(2,1)S(1)} collective-permute-done((bf16[64,2048]{1,0:T(8,128)(2,1)}, bf16[64,2048]{1,0:T(8,128)(2,1)S(1)}, u32[]{:S(2)}, u32[]{:S(2)}) %collective-permute-start.49) | collective-permute-done | bytes 262176 | tf_op jit(solution)/shard_map/ppermute | solution.py:918
  429.9 2.3 multiply_reduce_fusion.1
  440.2 3.3 grad_pairs.1
  443.5 4.2 all-to-all-start.4
  447.7 14.1 %sum_of_outer.4 = bf16[2048,2048]{1,0:T(8,128)(2,1)} custom-call(s32[68]{0:T(128)} %get-tuple-element.919.table_ref._unused, bf16[512,2048]{1,0:T(8,128)(2,1)} %get-tuple-element.661.refs_0_, bf16[512,2048]{1,0:T(8,128)(2,1)} %get-tuple-element.662.refs_1_, bf16[512,2048]{1,0:T(8,128)(2,1)} %get-tuple-element.663.up_ref.refs_2_, ...), custom_call_target="tpu_custom_call" | custom-call | flops 999999995904 | bytes 1000000000 | tf_op jit(solution)/shard_map/sum_of_outer/pallas_call | solution.py:367
  462.2 2.5 all-to-all-done.4.m_ref
  469.0 2.3 collective-permute-start.56
  471.3 15.5 %attend_back.1 = (bf16[8,6,128,128]{3,2,1,0:T(8,128)(2,1)}, f32[8,128]{1,0:T(8,128)S(1)}) custom-call(bf16[8,6,128,128]{3,2,1,0:T(8,128)(2,1)S(1)} %copy-done.17, bf16[8,6,128,128]{3,2,1,0:T(8,128)(2,1)S(1)} %copy-done.17, bf16[8,6,128,128]{3,2,1,0:T(8,128)(2,1)S(1)} %copy-done.17, bf16[8,2,128,128]{3,2,1,0:T(8,128)(2,1)} %all-to-all-done.4.m_ref, ...), custom_call_target="tpu_custom_call" | custom-call | flops 999999995904 | bytes 1000000000 | tf_op jit(solution)/shard_map/attend_back/pallas_call | solution.py:169
  486.8 7.8 %head_weights.1.own_ref = bf16[2048,384]{1,0:T(8,128)(2,1)S(1)} custom-call(s32[68]{0:T(128)S(1)} %copy-done.28, bf16[8,6,128,128]{3,2,1,0:T(8,128)(2,1)} %get-tuple-element.712.g_ref, bf16[2048,1024]{1,0:T(8,128)(2,1)} %transposed.1.own_ref, bf16[2048,1024]{1,0:T(8,128)(2,1)} %collective-permute-done.52.beside_ref), custom_call_target="tpu_custom_call" | custom-call | flops 999999995904 | bytes 1000000000 | tf_op jit(solution)/shard_map/head_weights/pallas_call | solution.py:639
  496.8 2.9 add_convert_fusion.1
  501.7 4.5 all-to-all-start.5
  506.2 4.7 out_grads.1
  510.9 2.5 convert.35
  513.5 8.3 %collective-permute-done.59.other_ref = bf16[1024,384]{1,0:T(8,128)(2,1)} collective-permute-done((bf16[1024,384]{1,0:T(8,128)(2,1)}, bf16[1024,384]{1,0:T(8,128)(2,1)}, u32[]{:S(2)}, u32[]{:S(2)}) %collective-permute-start.59) | collective-permute-done | bytes 786464 | tf_op jit(solution)/shard_map/ppermute | solution.py:906
  529.6 14.7 %sum_of_outer.5 = bf16[2048,2048]{1,0:T(8,128)(2,1)} custom-call(s32[68]{0:T(128)} %get-tuple-element.919.table_ref._unused, bf16[512,2048]{1,0:T(8,128)(2,1)} %get-tuple-element.700.refs_0_, bf16[512,2048]{1,0:T(8,128)(2,1)} %get-tuple-element.701.refs_1_, bf16[512,2048]{1,0:T(8,128)(2,1)} %get-tuple-element.702.refs_0_.refs_2_, ...), custom_call_target="tpu_custom_call" | custom-call | flops 999999995904 | bytes 1000000000 | tf_op jit(solution)/shard_map/sum_of_outer/pallas_call | solution.py:367
  544.3 13.8 %collective-permute-done.61.refs_2_ = bf16[512,768]{1,0:T(8,128)(2,1)} collective-permute-done((bf16[512,768]{1,0:T(8,128)(2,1)}, bf16[512,768]{1,0:T(8,128)(2,1)}, u32[]{:S(2)}, u32[]{:S(2)}) %collective-permute-start.61) | collective-permute-done | bytes 786464 | tf_op jit(solution)/shard_map/ppermute | solution.py:918
  559.7 9.3 %collective-permute-start.67 = (bf16[512,768]{1,0:T(8,128)(2,1)}, bf16[512,768]{1,0:T(8,128)(2,1)}, u32[]{:S(2)}, u32[]{:S(2)}) collective-permute-start(bf16[512,768]{1,0:T(8,128)(2,1)} %collective-permute-done.61.refs_2_), channel_id=1, source_target_pairs={{0,8},{8,16},{16,24},{24,28},{28,20},{20,12},{12,4},{4,0},{1,9},{9... | collective-permute-start | bytes 2359304 | tf_op jit(solution)/shard_map/ppermute | solution.py:918
  573.8 12.0 %pair_normed.1 = (f32[128,2048]{1,0:T(8,128)S(1)}, bf16[128,2048]{1,0:T(8,128)(2,1)S(1)}) custom-call(bf16[8,6,128,128]{3,2,1,0:T(8,128)(2,1)} %all-to-all-done.5.g_ref, bf16[2048,3072]{1,0:T(8,128)(2,1)} %get-tuple-element.716.w_ref), custom_call_target="tpu_custom_call" | custom-call | flops 999999995904 | bytes 1000000000 | tf_op jit(solution)/shard_map/pair_normed/pallas_call | solution.py:698
  585.9 5.1 collective-permute-done.69
  593.6 2.5 add_convert_fusion
  604.3 2.4 collective-permute-done.74
  614.1 4.8 spread.5
  618.9 2.3 spread.6
  625.2 9.9 %collective-permute-done.80.refs_1_ = bf16[512,768]{1,0:T(8,128)(2,1)S(1)} collective-permute-done((bf16[512,768]{1,0:T(8,128)(2,1)}, bf16[512,768]{1,0:T(8,128)(2,1)S(1)}, u32[]{:S(2)}, u32[]{:S(2)}) %collective-permute-start.80) | collective-permute-done | bytes 786464 | tf_op jit(solution)/shard_map/ppermute | solution.py:918
  638.0 2.3 spread.7
  640.4 4.5 split_experts.3
  647.0 3.6 collective-permute-done.84
  658.5 4.5 split_experts.4
  667.0 4.5 split_experts.5
  673.5 2.6 spread.9
  (478 shorter events, 184.6 us)
Async XLA Ops:
  7.2 189.6 %all-gather.4.cloned.1.call-start = ((), (), s32[]{:S(2)}) async-start(), calls=%async_computation.9 | async-start | bytes 10485760 | tf_op jit(solution)/shard_map/all_gather | solution.py:1116
  11.6 14.9 %collective-permute-start = (bf16[128,2048]{1,0:T(8,128)(2,1)S(1)}, bf16[128,2048]{1,0:T(8,128)(2,1)S(1)}, u32[]{:S(2)}, u32[]{:S(2)}) collective-permute-start(bf16[128,2048]{1,0:T(8,128)(2,1)S(1)} %bitcast.67), channel_id=1, source_target_pairs={{0,8},{8,16},{16,24},{24,28},{28,20},{20,12},{12,4},{4,0},{1,9},{9... | collective-permute-start | bytes 1572872 | tf_op jit(solution)/shard_map/ppermute | solution.py:918
  14.6 28.2 %collective-permute-start.4 = (bf16[64,5120]{1,0:T(8,128)(2,1)}, bf16[64,5120]{1,0:T(8,128)(2,1)S(1)}, u32[]{:S(2)}, u32[]{:S(2)}) collective-permute-start(bf16[64,5120]{1,0:T(8,128)(2,1)} %get-tuple-element.446), channel_id=1, source_target_pairs={{0,2},{1,3},{2,0},{3,1},{4,6},{5,7},{6,4},{7,5},{8,10},{9,11},{10,... | collective-permute-start | bytes 1966088 | tf_op jit(solution)/shard_map/ppermute | solution.py:906
  16.6 26.2 %collective-permute-start.5 = (bf16[64,3072]{1,0:T(8,128)(2,1)}, bf16[64,3072]{1,0:T(8,128)(2,1)S(1)}, u32[]{:S(2)}, u32[]{:S(2)}) collective-permute-start(bf16[64,3072]{1,0:T(8,128)(2,1)} %get-tuple-element.447), channel_id=1, source_target_pairs={{0,3},{1,2},{2,1},{3,0},{4,7},{5,6},{6,5},{7,4},{8,11},{9,10},{10,... | collective-permute-start | bytes 1179656 | tf_op jit(solution)/shard_map/ppermute | solution.py:906
  42.8 153.9 %all-gather.6.cloned.1.call-start = ((), (), s32[]{:S(2)}) async-start(), calls=%async_computation.10 | async-start | bytes 10485760 | tf_op jit(solution)/shard_map/all_gather | solution.py:1119
  43.6 22.5 %collective-permute-start.6 = (bf16[256,2048]{1,0:T(8,128)(2,1)S(1)}, bf16[256,2048]{1,0:T(8,128)(2,1)S(1)}, u32[]{:S(2)}, u32[]{:S(2)}) collective-permute-start(bf16[256,2048]{1,0:T(8,128)(2,1)S(1)} %fetched_payload.1.refs_4_.refs_0_), channel_id=1, source_target_pairs={{0,8},{8,16},{16,24},{24,28},{28,20},{20,12},{12,4},{4,0},{1,9},{9... | collective-permute-start | bytes 3145736 | tf_op jit(solution)/shard_map/ppermute | solution.py:918
  45.2 22.2 %collective-permute-start.7 = (bf16[256,2048]{1,0:T(8,128)(2,1)S(1)}, bf16[256,2048]{1,0:T(8,128)(2,1)S(1)}, u32[]{:S(2)}, u32[]{:S(2)}) collective-permute-start(bf16[256,2048]{1,0:T(8,128)(2,1)S(1)} %fetched_payload.1.refs_4_.refs_0_), channel_id=1, source_target_pairs={{0,4},{8,0},{16,8},{24,16},{28,24},{20,28},{12,20},{4,12},{1,5},{9... | collective-permute-start | bytes 3145736 | tf_op jit(solution)/shard_map/ppermute | solution.py:918
  67.5 154.0 %all-gather.8.cloned.1.call-start = ((), (), s32[]{:S(2)}) async-start(), calls=%async_computation.11 | async-start | bytes 10485760 | tf_op jit(solution)/shard_map/all_gather | solution.py:1128
  68.1 25.2 %collective-permute-start.10 = (bf16[256,2048]{1,0:T(8,128)(2,1)S(1)}, bf16[256,2048]{1,0:T(8,128)(2,1)}, u32[]{:S(2)}, u32[]{:S(2)}) collective-permute-start(bf16[256,2048]{1,0:T(8,128)(2,1)S(1)} %collective-permute-done.6.refs_6_.refs_2_), channel_id=1, source_target_pairs={{0,8},{8,16},{16,24},{24,28},{28,20},{20,12},{12,4},{4,0},{1,9},{9... | collective-permute-start | bytes 3145736 | tf_op jit(solution)/shard_map/ppermute | solution.py:918
  69.6 25.0 %collective-permute-start.11 = (bf16[256,2048]{1,0:T(8,128)(2,1)S(1)}, bf16[256,2048]{1,0:T(8,128)(2,1)}, u32[]{:S(2)}, u32[]{:S(2)}) collective-permute-start(bf16[256,2048]{1,0:T(8,128)(2,1)S(1)} %collective-permute-done.7.refs_5_.refs_1_), channel_id=1, source_target_pairs={{0,4},{8,0},{16,8},{24,16},{28,24},{20,28},{12,20},{4,12},{1,5},{9... | collective-permute-start | bytes 3145736 | tf_op jit(solution)/shard_map/ppermute | solution.py:918
  94.6 26.8 %collective-permute-start.15 = (bf16[256,2048]{1,0:T(8,128)(2,1)}, bf16[256,2048]{1,0:T(8,128)(2,1)S(1)}, u32[]{:S(2)}, u32[]{:S(2)}) collective-permute-start(bf16[256,2048]{1,0:T(8,128)(2,1)} %collective-permute-done.10.refs_8_.refs_4_), channel_id=1, source_target_pairs={{0,8},{8,16},{16,24},{24,28},{28,20},{20,12},{12,4},{4,0},{1,9},{9... | collective-permute-start | bytes 3145736 | tf_op jit(solution)/shard_map/ppermute | solution.py:918
  95.7 25.7 %collective-permute-start.16 = (bf16[256,2048]{1,0:T(8,128)(2,1)}, bf16[256,2048]{1,0:T(8,128)(2,1)S(1)}, u32[]{:S(2)}, u32[]{:S(2)}) collective-permute-start(bf16[256,2048]{1,0:T(8,128)(2,1)} %collective-permute-done.11.refs_7_.refs_3_), channel_id=1, source_target_pairs={{0,4},{8,0},{16,8},{24,16},{28,24},{20,28},{12,20},{4,12},{1,5},{9... | collective-permute-start | bytes 3145736 | tf_op jit(solution)/shard_map/ppermute | solution.py:918
  97.3 24.1 %all-to-all-start = ((s32[8,128,8]{1,2,0:T(8,128)}), s32[8,128,8]{1,2,0:T(8,128)}, u32[]{:S(2)}, u32[]{:S(2)}) async-start(s32[8,128,8]{1,2,0:T(8,128)} %broadcast_in_dim.48), calls=%async_computation | async-start | bytes 65536 | tf_op jit(solution)/shard_map/all_to_all | solution.py:1122
  146.8 37.7 %all-to-all-start.1 = ((bf16[8,6,128,128]{3,2,1,0:T(8,128)(2,1)}), bf16[8,6,128,128]{3,2,1,0:T(8,128)(2,1)S(1)}, u32[]{:S(2)}, u32[]{:S(2)}) async-start(bf16[8,6,128,128]{3,2,1,0:T(8,128)(2,1)} %copy-done.18), calls=%async_computation.1 | async-start | bytes 3145728 | tf_op jit(solution)/shard_map/all_to_all | solution.py:1079
  222.9 14.2 %collective-permute-start.20 = (bf16[128,2048]{1,0:T(8,128)(2,1)S(1)}, bf16[128,2048]{1,0:T(8,128)(2,1)}, u32[]{:S(2)}, u32[]{:S(2)}) collective-permute-start(bf16[128,2048]{1,0:T(8,128)(2,1)S(1)} %multiply_convert_fusion.refs_0_), channel_id=1, source_target_pairs={{0,8},{8,16},{16,24},{24,28},{28,20},{20,12},{12,4},{4,0},{1,9},{9... | collective-permute-start | bytes 1572872 | tf_op jit(solution)/shard_map/ppermute | solution.py:918
  224.4 13.9 %collective-permute-start.21 = (bf16[128,2048]{1,0:T(8,128)(2,1)S(1)}, bf16[128,2048]{1,0:T(8,128)(2,1)}, u32[]{:S(2)}, u32[]{:S(2)}) collective-permute-start(bf16[128,2048]{1,0:T(8,128)(2,1)S(1)} %multiply_convert_fusion.refs_0_), channel_id=1, source_target_pairs={{0,4},{8,0},{16,8},{24,16},{28,24},{20,28},{12,20},{4,12},{1,5},{9... | collective-permute-start | bytes 1572872 | tf_op jit(solution)/shard_map/ppermute | solution.py:918
  252.8 23.0 %collective-permute-start.24 = (bf16[128,2048]{1,0:T(8,128)(2,1)}, bf16[128,2048]{1,0:T(8,128)(2,1)S(1)}, u32[]{:S(2)}, u32[]{:S(2)}) collective-permute-start(bf16[128,2048]{1,0:T(8,128)(2,1)} %collective-permute-done.22.refs_0_), channel_id=1, source_target_pairs={{0,8},{8,16},{16,24},{24,28},{28,20},{20,12},{12,4},{4,0},{1,9},{9... | collective-permute-start | bytes 1572872 | tf_op jit(solution)/shard_map/ppermute | solution.py:918
  254.3 21.5 %collective-permute-start.25 = (bf16[128,2048]{1,0:T(8,128)(2,1)}, bf16[128,2048]{1,0:T(8,128)(2,1)S(1)}, u32[]{:S(2)}, u32[]{:S(2)}) collective-permute-start(bf16[128,2048]{1,0:T(8,128)(2,1)} %collective-permute-done.23.refs_3_), channel_id=1, source_target_pairs={{0,4},{8,0},{16,8},{24,16},{28,24},{20,28},{12,20},{4,12},{1,5},{9... | collective-permute-start | bytes 1572872 | tf_op jit(solution)/shard_map/ppermute | solution.py:918
  254.8 21.2 %collective-permute-start.26 = (bf16[128,2048]{1,0:T(8,128)(2,1)S(1)}, bf16[128,2048]{1,0:T(8,128)(2,1)S(1)}, u32[]{:S(2)}, u32[]{:S(2)}) collective-permute-start(bf16[128,2048]{1,0:T(8,128)(2,1)S(1)} %copy-done.93), channel_id=1, source_target_pairs={{0,8},{8,16},{16,24},{24,28},{28,20},{20,12},{12,4},{4,0},{1,9},{9... | collective-permute-start | bytes 1572872 | tf_op jit(solution)/shard_map/ppermute | solution.py:918
  256.3 20.9 %collective-permute-start.27 = (bf16[128,2048]{1,0:T(8,128)(2,1)S(1)}, bf16[128,2048]{1,0:T(8,128)(2,1)S(1)}, u32[]{:S(2)}, u32[]{:S(2)}) collective-permute-start(bf16[128,2048]{1,0:T(8,128)(2,1)S(1)} %copy-done.95), channel_id=1, source_target_pairs={{0,4},{8,0},{16,8},{24,16},{28,24},{20,28},{12,20},{4,12},{1,5},{9... | collective-permute-start | bytes 1572872 | tf_op jit(solution)/shard_map/ppermute | solution.py:918
  284.2 39.7 %collective-permute-start.34 = (bf16[4,2,128,128]{3,2,1,0:T(8,128)(2,1)}, bf16[4,2,128,128]{3,2,1,0:T(8,128)(2,1)}, u32[]{:S(2)}, u32[]{:S(2)}) collective-permute-start(bf16[4,2,128,128]{3,2,1,0:T(8,128)(2,1)} %constant_dynamic-slice_fusion), channel_id=1, source_target_pairs={{0,2},{1,3},{2,0},{3,1},{4,6},{5,7},{6,4},{7,5},{8,10},{9,11},{10,... | collective-permute-start | bytes 786440 | tf_op jit(solution)/shard_map/ppermute | solution.py:906
  302.9 21.0 %collective-permute-start.35 = (bf16[128,2048]{1,0:T(8,128)(2,1)}, bf16[128,2048]{1,0:T(8,128)(2,1)S(1)}, u32[]{:S(2)}, u32[]{:S(2)}) collective-permute-start(bf16[128,2048]{1,0:T(8,128)(2,1)} %collective-permute-done.32.refs_2_), channel_id=1, source_target_pairs={{0,8},{8,16},{16,24},{24,28},{28,20},{20,12},{12,4},{4,0},{1,9},{9... | collective-permute-start | bytes 1572872 | tf_op jit(solution)/shard_map/ppermute | solution.py:918
  303.9 20.0 %collective-permute-start.36 = (bf16[128,2048]{1,0:T(8,128)(2,1)}, bf16[128,2048]{1,0:T(8,128)(2,1)S(1)}, u32[]{:S(2)}, u32[]{:S(2)}) collective-permute-start(bf16[128,2048]{1,0:T(8,128)(2,1)} %collective-permute-done.33.refs_1_), channel_id=1, source_target_pairs={{0,4},{8,0},{16,8},{24,16},{28,24},{20,28},{12,20},{4,12},{1,5},{9... | collective-permute-start | bytes 1572872 | tf_op jit(solution)/shard_map/ppermute | solution.py:918
  323.9 20.1 %collective-permute-start.37 = (bf16[128,2048]{1,0:T(8,128)(2,1)S(1)}, bf16[128,2048]{1,0:T(8,128)(2,1)}, u32[]{:S(2)}, u32[]{:S(2)}) collective-permute-start(bf16[128,2048]{1,0:T(8,128)(2,1)S(1)} %collective-permute-done.35.refs_4_), channel_id=1, source_target_pairs={{0,8},{8,16},{16,24},{24,28},{28,20},{20,12},{12,4},{4,0},{1,9},{9... | collective-permute-start | bytes 1572872 | tf_op jit(solution)/shard_map/ppermute | solution.py:918
  325.0 19.1 %collective-permute-start.38 = (bf16[128,2048]{1,0:T(8,128)(2,1)S(1)}, bf16[128,2048]{1,0:T(8,128)(2,1)}, u32[]{:S(2)}, u32[]{:S(2)}) collective-permute-start(bf16[128,2048]{1,0:T(8,128)(2,1)S(1)} %collective-permute-done.36.refs_3_), channel_id=1, source_target_pairs={{0,4},{8,0},{16,8},{24,16},{28,24},{20,28},{12,20},{4,12},{1,5},{9... | collective-permute-start | bytes 1572872 | tf_op jit(solution)/shard_map/ppermute | solution.py:918
  342.1 16.3 %collective-permute-start.39 = (bf16[64,2048]{1,0:T(8,128)(2,1)}, bf16[64,2048]{1,0:T(8,128)(2,1)}, u32[]{:S(2)}, u32[]{:S(2)}) collective-permute-start(bf16[64,2048]{1,0:T(8,128)(2,1)} %get-tuple-element.909), channel_id=1, source_target_pairs={{0,8},{8,16},{16,24},{24,28},{28,20},{20,12},{12,4},{4,0},{1,9},{9... | collective-permute-start | bytes 786440 | tf_op jit(solution)/shard_map/ppermute | solution.py:918
  343.1 15.3 %collective-permute-start.40 = (bf16[64,2048]{1,0:T(8,128)(2,1)}, bf16[64,2048]{1,0:T(8,128)(2,1)}, u32[]{:S(2)}, u32[]{:S(2)}) collective-permute-start(bf16[64,2048]{1,0:T(8,128)(2,1)} %get-tuple-element.908), channel_id=1, source_target_pairs={{0,4},{8,0},{16,8},{24,16},{28,24},{20,28},{12,20},{4,12},{1,5},{9... | collective-permute-start | bytes 786440 | tf_op jit(solution)/shard_map/ppermute | solution.py:918
  363.7 18.2 %collective-permute-start.43 = (bf16[128,2048]{1,0:T(8,128)(2,1)S(1)}, bf16[128,2048]{1,0:T(8,128)(2,1)S(1)}, u32[]{:S(2)}, u32[]{:S(2)}) collective-permute-start(bf16[128,2048]{1,0:T(8,128)(2,1)S(1)} %pad_maximum_fusion.5), channel_id=1, source_target_pairs={{0,8},{8,16},{16,24},{24,28},{28,20},{20,12},{12,4},{4,0},{1,9},{9... | collective-permute-start | bytes 1572872 | tf_op jit(solution)/shard_map/ppermute | solution.py:918
  364.8 17.1 %collective-permute-start.44 = (bf16[128,2048]{1,0:T(8,128)(2,1)S(1)}, bf16[128,2048]{1,0:T(8,128)(2,1)S(1)}, u32[]{:S(2)}, u32[]{:S(2)}) collective-permute-start(bf16[128,2048]{1,0:T(8,128)(2,1)S(1)} %pad_maximum_fusion.6), channel_id=1, source_target_pairs={{0,4},{8,0},{16,8},{24,16},{28,24},{20,28},{12,20},{4,12},{1,5},{9... | collective-permute-start | bytes 1572872 | tf_op jit(solution)/shard_map/ppermute | solution.py:918
  383.1 15.9 %collective-permute-start.45 = (bf16[128,2048]{1,0:T(8,128)(2,1)S(1)}, bf16[128,2048]{1,0:T(8,128)(2,1)S(1)}, u32[]{:S(2)}, u32[]{:S(2)}) collective-permute-start(bf16[128,2048]{1,0:T(8,128)(2,1)S(1)} %add_convert_fusion.8), channel_id=1, source_target_pairs={{0,8},{8,16},{16,24},{24,28},{28,20},{20,12},{12,4},{4,0},{1,9},{9... | collective-permute-start | bytes 1572872 | tf_op jit(solution)/shard_map/ppermute | solution.py:918
  384.3 15.5 %collective-permute-start.46 = (bf16[128,2048]{1,0:T(8,128)(2,1)S(1)}, bf16[128,2048]{1,0:T(8,128)(2,1)}, u32[]{:S(2)}, u32[]{:S(2)}) collective-permute-start(bf16[128,2048]{1,0:T(8,128)(2,1)S(1)} %add_convert_fusion.7), channel_id=1, source_target_pairs={{0,4},{8,0},{16,8},{24,16},{28,24},{20,28},{12,20},{4,12},{1,5},{9... | collective-permute-start | bytes 1572872 | tf_op jit(solution)/shard_map/ppermute | solution.py:918
  404.9 35.2 %collective-permute-start.52 = (bf16[2048,1024]{1,0:T(8,128)(2,1)}, bf16[2048,1024]{1,0:T(8,128)(2,1)}, u32[]{:S(2)}, u32[]{:S(2)}) collective-permute-start(bf16[2048,1024]{1,0:T(8,128)(2,1)} %transposed.1.own_ref), channel_id=1, source_target_pairs={{0,1},{1,0},{2,3},{3,2},{4,5},{5,4},{6,7},{7,6},{8,9},{9,8},{10,11... | collective-permute-start | bytes 12582920 | tf_op jit(solution)/shard_map/ppermute | solution.py:906
  407.5 21.0 %collective-permute-start.47 = (bf16[128,2048]{1,0:T(8,128)(2,1)}, bf16[128,2048]{1,0:T(8,128)(2,1)}, u32[]{:S(2)}, u32[]{:S(2)}) collective-permute-start(bf16[128,2048]{1,0:T(8,128)(2,1)} %get-tuple-element.905), channel_id=1, source_target_pairs={{0,8},{8,16},{16,24},{24,28},{28,20},{20,12},{12,4},{4,0},{1,9},{9... | collective-permute-start | bytes 1572872 | tf_op jit(solution)/shard_map/ppermute | solution.py:918
  408.6 20.0 %collective-permute-start.48 = (bf16[128,2048]{1,0:T(8,128)(2,1)}, bf16[128,2048]{1,0:T(8,128)(2,1)}, u32[]{:S(2)}, u32[]{:S(2)}) collective-permute-start(bf16[128,2048]{1,0:T(8,128)(2,1)} %get-tuple-element.904), channel_id=1, source_target_pairs={{0,4},{8,0},{16,8},{24,16},{28,24},{20,28},{12,20},{4,12},{1,5},{9... | collective-permute-start | bytes 1572872 | tf_op jit(solution)/shard_map/ppermute | solution.py:918
  410.5 17.2 %collective-permute-start.49 = (bf16[64,2048]{1,0:T(8,128)(2,1)}, bf16[64,2048]{1,0:T(8,128)(2,1)S(1)}, u32[]{:S(2)}, u32[]{:S(2)}) collective-permute-start(bf16[64,2048]{1,0:T(8,128)(2,1)} %get-tuple-element.901), channel_id=1, source_target_pairs={{0,8},{8,16},{16,24},{24,28},{28,20},{20,12},{12,4},{4,0},{1,9},{9... | collective-permute-start | bytes 786440 | tf_op jit(solution)/shard_map/ppermute | solution.py:918
  411.5 17.1 %collective-permute-start.50 = (bf16[64,2048]{1,0:T(8,128)(2,1)}, bf16[64,2048]{1,0:T(8,128)(2,1)}, u32[]{:S(2)}, u32[]{:S(2)}) collective-permute-start(bf16[64,2048]{1,0:T(8,128)(2,1)} %get-tuple-element.900), channel_id=1, source_target_pairs={{0,4},{8,0},{16,8},{24,16},{28,24},{20,28},{12,20},{4,12},{1,5},{9... | collective-permute-start | bytes 786440 | tf_op jit(solution)/shard_map/ppermute | solution.py:918
  418.9 221.5 %reduce-scatter.4.cloned.1.call-start = ((), (), s32[]{:S(2)}) async-start(), calls=%async_computation.12 | async-start | bytes 10485760 | tf_op jit(solution)/shard_map/reduce_scatter | solution.py:1221
  437.3 24.9 %collective-permute-start.53 = (bf16[128,2048]{1,0:T(8,128)(2,1)}, bf16[128,2048]{1,0:T(8,128)(2,1)}, u32[]{:S(2)}, u32[]{:S(2)}) collective-permute-start(bf16[128,2048]{1,0:T(8,128)(2,1)} %pad_maximum_fusion.8), channel_id=1, source_target_pairs={{0,8},{8,16},{16,24},{24,28},{28,20},{20,12},{12,4},{4,0},{1,9},{9... | collective-permute-start | bytes 1572872 | tf_op jit(solution)/shard_map/ppermute | solution.py:918
  438.7 23.6 %collective-permute-start.54 = (bf16[128,2048]{1,0:T(8,128)(2,1)}, bf16[128,2048]{1,0:T(8,128)(2,1)}, u32[]{:S(2)}, u32[]{:S(2)}) collective-permute-start(bf16[128,2048]{1,0:T(8,128)(2,1)} %pad_maximum_fusion.9), channel_id=1, source_target_pairs={{0,4},{8,0},{16,8},{24,16},{28,24},{20,28},{12,20},{4,12},{1,5},{9... | collective-permute-start | bytes 1572872 | tf_op jit(solution)/shard_map/ppermute | solution.py:918
  443.5 21.2 %all-to-all-start.4 = ((bf16[8,2,128,128]{3,2,1,0:T(8,128)(2,1)}), bf16[8,2,128,128]{3,2,1,0:T(8,128)(2,1)}, u32[]{:S(2)}, u32[]{:S(2)}) async-start(bf16[8,2,128,128]{3,2,1,0:T(8,128)(2,1)} %grad_pairs.1), calls=%async_computation.4 | async-start | bytes 1048576 | tf_op jit(solution)/shard_map/all_to_all | solution.py:1079
  447.7 210.8 %reduce-scatter.6.cloned.1.call-start = ((), (), s32[]{:S(2)}) async-start(), calls=%async_computation.13 | async-start | bytes 10485760 | tf_op jit(solution)/shard_map/reduce_scatter | solution.py:1221
  461.9 32.7 %collective-permute-start.57 = (bf16[128,2048]{1,0:T(8,128)(2,1)}, bf16[128,2048]{1,0:T(8,128)(2,1)}, u32[]{:S(2)}, u32[]{:S(2)}) collective-permute-start(bf16[128,2048]{1,0:T(8,128)(2,1)} %get-tuple-element.683.own_ref.refs_0_), channel_id=1, source_target_pairs={{0,2},{1,3},{2,0},{3,1},{4,6},{5,7},{6,4},{7,5},{8,10},{9,11},{10,... | collective-permute-start | bytes 1572872 | tf_op jit(solution)/shard_map/ppermute | solution.py:906
  466.9 19.9 %collective-permute-start.55 = (bf16[128,2048]{1,0:T(8,128)(2,1)}, bf16[128,2048]{1,0:T(8,128)(2,1)}, u32[]{:S(2)}, u32[]{:S(2)}) collective-permute-start(bf16[128,2048]{1,0:T(8,128)(2,1)} %add_convert_fusion.4), channel_id=1, source_target_pairs={{0,8},{8,16},{16,24},{24,28},{28,20},{20,12},{12,4},{4,0},{1,9},{9... | collective-permute-start | bytes 1572872 | tf_op jit(solution)/shard_map/ppermute | solution.py:918
  469.0 17.8 %collective-permute-start.56 = (bf16[128,2048]{1,0:T(8,128)(2,1)}, bf16[128,2048]{1,0:T(8,128)(2,1)}, u32[]{:S(2)}, u32[]{:S(2)}) collective-permute-start(bf16[128,2048]{1,0:T(8,128)(2,1)} %add_convert_fusion.3), channel_id=1, source_target_pairs={{0,4},{8,0},{16,8},{24,16},{28,24},{20,28},{12,20},{4,12},{1,5},{9... | collective-permute-start | bytes 1572872 | tf_op jit(solution)/shard_map/ppermute | solution.py:918
  496.2 25.6 %collective-permute-start.59 = (bf16[1024,384]{1,0:T(8,128)(2,1)}, bf16[1024,384]{1,0:T(8,128)(2,1)}, u32[]{:S(2)}, u32[]{:S(2)}) collective-permute-start(bf16[1024,384]{1,0:T(8,128)(2,1)} %slice.261), channel_id=1, source_target_pairs={{0,2},{1,3},{2,0},{3,1},{4,6},{5,7},{6,4},{7,5},{8,10},{9,11},{10,... | collective-permute-start | bytes 2359304 | tf_op jit(solution)/shard_map/ppermute | solution.py:906
  499.6 29.5 %collective-permute-start.65 = (bf16[128,2048]{1,0:T(8,128)(2,1)}, bf16[128,2048]{1,0:T(8,128)(2,1)}, u32[]{:S(2)}, u32[]{:S(2)}) collective-permute-start(bf16[128,2048]{1,0:T(8,128)(2,1)} %get-tuple-element.897), channel_id=1, source_target_pairs={{0,8},{8,16},{16,24},{24,28},{28,20},{20,12},{12,4},{4,0},{1,9},{9... | collective-permute-start | bytes 1572872 | tf_op jit(solution)/shard_map/ppermute | solution.py:918
  500.0 44.3 %collective-permute-start.66 = (bf16[128,2048]{1,0:T(8,128)(2,1)}, bf16[128,2048]{1,0:T(8,128)(2,1)}, u32[]{:S(2)}, u32[]{:S(2)}) collective-permute-start(bf16[128,2048]{1,0:T(8,128)(2,1)} %get-tuple-element.896), channel_id=1, source_target_pairs={{0,4},{8,0},{16,8},{24,16},{28,24},{20,28},{12,20},{4,12},{1,5},{9... | collective-permute-start | bytes 1572872 | tf_op jit(solution)/shard_map/ppermute | solution.py:918
  501.7 58.1 %all-to-all-start.5 = ((bf16[8,6,128,128]{3,2,1,0:T(8,128)(2,1)}), bf16[8,6,128,128]{3,2,1,0:T(8,128)(2,1)}, u32[]{:S(2)}, u32[]{:S(2)}) async-start(bf16[8,6,128,128]{3,2,1,0:T(8,128)(2,1)} %get-tuple-element.712.g_ref), calls=%async_computation.5 | async-start | bytes 3145728 | tf_op jit(solution)/shard_map/all_to_all | solution.py:1082
  506.1 160.9 %reduce-scatter.8.cloned.1.call-start = ((), (), s32[]{:S(2)}) async-start(), calls=%async_computation.14 | async-start | bytes 10485760 | tf_op jit(solution)/shard_map/reduce_scatter | solution.py:1221
  524.0 20.2 %collective-permute-start.63 = (bf16[32,2048]{1,0:T(8,128)(2,1)}, bf16[32,2048]{1,0:T(8,128)(2,1)}, u32[]{:S(2)}, u32[]{:S(2)}) collective-permute-start(bf16[32,2048]{1,0:T(8,128)(2,1)} %get-tuple-element.895), channel_id=1, source_target_pairs={{0,8},{8,16},{16,24},{24,28},{28,20},{20,12},{12,4},{4,0},{1,9},{9... | collective-permute-start | bytes 393224 | tf_op jit(solution)/shard_map/ppermute | solution.py:918
  525.5 18.7 %collective-permute-start.64 = (bf16[32,2048]{1,0:T(8,128)(2,1)}, bf16[32,2048]{1,0:T(8,128)(2,1)}, u32[]{:S(2)}, u32[]{:S(2)}) collective-permute-start(bf16[32,2048]{1,0:T(8,128)(2,1)} %get-tuple-element.894), channel_id=1, source_target_pairs={{0,4},{8,0},{16,8},{24,16},{28,24},{20,28},{12,20},{4,12},{1,5},{9... | collective-permute-start | bytes 393224 | tf_op jit(solution)/shard_map/ppermute | solution.py:918
  527.6 30.6 %collective-permute-start.61 = (bf16[512,768]{1,0:T(8,128)(2,1)}, bf16[512,768]{1,0:T(8,128)(2,1)}, u32[]{:S(2)}, u32[]{:S(2)}) collective-permute-start(bf16[512,768]{1,0:T(8,128)(2,1)} %side_by_side.1.refs_0_), channel_id=1, source_target_pairs={{0,8},{8,16},{16,24},{24,28},{28,20},{20,12},{12,4},{4,0},{1,9},{9... | collective-permute-start | bytes 2359304 | tf_op jit(solution)/shard_map/ppermute | solution.py:918
  529.1 30.6 %collective-permute-start.62 = (bf16[512,768]{1,0:T(8,128)(2,1)}, bf16[512,768]{1,0:T(8,128)(2,1)}, u32[]{:S(2)}, u32[]{:S(2)}) collective-permute-start(bf16[512,768]{1,0:T(8,128)(2,1)} %side_by_side.1.refs_0_), channel_id=1, source_target_pairs={{0,4},{8,0},{16,8},{24,16},{28,24},{20,28},{12,20},{4,12},{1,5},{9... | collective-permute-start | bytes 2359304 | tf_op jit(solution)/shard_map/ppermute | solution.py:918
  559.7 33.5 %collective-permute-start.67 = (bf16[512,768]{1,0:T(8,128)(2,1)}, bf16[512,768]{1,0:T(8,128)(2,1)}, u32[]{:S(2)}, u32[]{:S(2)}) collective-permute-start(bf16[512,768]{1,0:T(8,128)(2,1)} %collective-permute-done.61.refs_2_), channel_id=1, source_target_pairs={{0,8},{8,16},{16,24},{24,28},{28,20},{20,12},{12,4},{4,0},{1,9},{9... | collective-permute-start | bytes 2359304 | tf_op jit(solution)/shard_map/ppermute | solution.py:918
  569.0 24.2 %collective-permute-start.68 = (bf16[512,768]{1,0:T(8,128)(2,1)}, bf16[512,768]{1,0:T(8,128)(2,1)}, u32[]{:S(2)}, u32[]{:S(2)}) collective-permute-start(bf16[512,768]{1,0:T(8,128)(2,1)} %collective-permute-done.62.refs_1_), channel_id=1, source_target_pairs={{0,4},{8,0},{16,8},{24,16},{28,24},{20,28},{12,20},{4,12},{1,5},{9... | collective-permute-start | bytes 2359304 | tf_op jit(solution)/shard_map/ppermute | solution.py:918
  571.0 20.1 %collective-permute-start.69 = (bf16[64,2048]{1,0:T(8,128)(2,1)}, bf16[64,2048]{1,0:T(8,128)(2,1)}, u32[]{:S(2)}, u32[]{:S(2)}) collective-permute-start(bf16[64,2048]{1,0:T(8,128)(2,1)} %pad_maximum_fusion.10), channel_id=1, source_target_pairs={{0,8},{8,16},{16,24},{24,28},{28,20},{20,12},{12,4},{4,0},{1,9},{9... | collective-permute-start | bytes 786440 | tf_op jit(solution)/shard_map/ppermute | solution.py:918
  573.7 19.5 %collective-permute-start.70 = (bf16[64,2048]{1,0:T(8,128)(2,1)}, bf16[64,2048]{1,0:T(8,128)(2,1)}, u32[]{:S(2)}, u32[]{:S(2)}) collective-permute-start(bf16[64,2048]{1,0:T(8,128)(2,1)} %pad_maximum_fusion.11), channel_id=1, source_target_pairs={{0,4},{8,0},{16,8},{24,16},{28,24},{20,28},{12,20},{4,12},{1,5},{9... | collective-permute-start | bytes 786440 | tf_op jit(solution)/shard_map/ppermute | solution.py:918
  585.8 14.1 %collective-permute-start.72 = (bf16[128,2048]{1,0:T(8,128)(2,1)S(1)}, bf16[128,2048]{1,0:T(8,128)(2,1)S(1)}, u32[]{:S(2)}, u32[]{:S(2)}) collective-permute-start(bf16[128,2048]{1,0:T(8,128)(2,1)S(1)} %get-tuple-element.733), channel_id=1, source_target_pairs={{0,1},{1,0},{2,3},{3,2},{4,5},{5,4},{6,7},{7,6},{8,9},{9,8},{10,11... | collective-permute-start | bytes 1572872 | tf_op jit(solution)/shard_map/ppermute | solution.py:906
  611.0 24.1 %collective-permute-start.80 = (bf16[512,768]{1,0:T(8,128)(2,1)}, bf16[512,768]{1,0:T(8,128)(2,1)S(1)}, u32[]{:S(2)}, u32[]{:S(2)}) collective-permute-start(bf16[512,768]{1,0:T(8,128)(2,1)} %collective-permute-done.67.refs_0_), channel_id=1, source_target_pairs={{0,8},{8,16},{16,24},{24,28},{28,20},{20,12},{12,4},{4,0},{1,9},{9... | collective-permute-start | bytes 2359304 | tf_op jit(solution)/shard_map/ppermute | solution.py:918
  612.0 23.8 %collective-permute-start.81 = (bf16[512,768]{1,0:T(8,128)(2,1)}, bf16[512,768]{1,0:T(8,128)(2,1)S(1)}, u32[]{:S(2)}, u32[]{:S(2)}) collective-permute-start(bf16[512,768]{1,0:T(8,128)(2,1)} %collective-permute-done.68.refs_3_), channel_id=1, source_target_pairs={{0,4},{8,0},{16,8},{24,16},{28,24},{20,28},{12,20},{4,12},{1,5},{9... | collective-permute-start | bytes 2359304 | tf_op jit(solution)/shard_map/ppermute | solution.py:918
  623.1 21.8 %collective-permute-start.82 = (bf16[80,2048]{1,0:T(8,128)(2,1)S(1)}, bf16[80,2048]{1,0:T(8,128)(2,1)S(1)}, u32[]{:S(2)}, u32[]{:S(2)}) collective-permute-start(bf16[80,2048]{1,0:T(8,128)(2,1)S(1)} %pack_gains.1.refs_0_), channel_id=1, source_target_pairs={{0,8},{8,16},{16,24},{24,28},{28,20},{20,12},{12,4},{4,0},{1,9},{9... | collective-permute-start | bytes 983048 | tf_op jit(solution)/shard_map/ppermute | solution.py:918
  624.2 20.6 %collective-permute-start.83 = (bf16[80,2048]{1,0:T(8,128)(2,1)S(1)}, bf16[80,2048]{1,0:T(8,128)(2,1)S(1)}, u32[]{:S(2)}, u32[]{:S(2)}) collective-permute-start(bf16[80,2048]{1,0:T(8,128)(2,1)S(1)} %pack_gains.1.refs_0_), channel_id=1, source_target_pairs={{0,4},{8,0},{16,8},{24,16},{28,24},{20,28},{12,20},{4,12},{1,5},{9... | collective-permute-start | bytes 983048 | tf_op jit(solution)/shard_map/ppermute | solution.py:918
  635.9 14.6 %collective-permute-start.84 = (bf16[256,768]{1,0:T(8,128)(2,1)S(1)}, bf16[256,768]{1,0:T(8,128)(2,1)S(1)}, u32[]{:S(2)}, u32[]{:S(2)}) collective-permute-start(bf16[256,768]{1,0:T(8,128)(2,1)S(1)} %slice.278), channel_id=1, source_target_pairs={{0,8},{8,16},{16,24},{24,28},{28,20},{20,12},{12,4},{4,0},{1,9},{9... | collective-permute-start | bytes 1179656 | tf_op jit(solution)/shard_map/ppermute | solution.py:918
  636.5 14.9 %collective-permute-start.85 = (bf16[256,768]{1,0:T(8,128)(2,1)S(1)}, bf16[256,768]{1,0:T(8,128)(2,1)}, u32[]{:S(2)}, u32[]{:S(2)}) collective-permute-start(bf16[256,768]{1,0:T(8,128)(2,1)S(1)} %slice.279), channel_id=1, source_target_pairs={{0,4},{8,0},{16,8},{24,16},{28,24},{20,28},{12,20},{4,12},{1,5},{9... | collective-permute-start | bytes 1179656 | tf_op jit(solution)/shard_map/ppermute | solution.py:918
  (137 other events, 1313.8 us)
Sparse Core Ops, SparseCore 0:
  43.0 57.5 all-gather.3
  102.7 58.2 all-gather.5
  163.2 58.2 all-gather.7
  422.0 89.5 reduce-scatter.3
  514.2 73.6 reduce-scatter.5
  590.4 71.8 reduce-scatter.7
